TPU v7x, 32 devices: a whole 2x2x4 slice. The times are simulated.
32 devices in a mesh: pipe: 4 (over y, core), seq: 8 (over z, x).
Axes of the slice: x: 2, y: 2, z: 4, core: 2. Of those that a mesh axis runs over, the one named last changes fastest.
Arguments:
- hidden: bfloat16 [2, 192, 3072], P(None, 'seq'), may hold values from -8 to 8
- mod_shift: float32 [4, 3072], P('pipe'), may hold values from -0.3 to 0.3
- mod_scale: float32 [4, 3072], P('pipe'), may hold values from -3 to 3
- mod_gate: float32 [4, 3072], P('pipe'), may hold values from 0.5 to 2.5
- norm_gain: float32 [4, 2, 128], P('pipe'), may hold values from 0.5 to 1.5
- input_proj: bfloat16 [4, 3072, 3, 2048], P('pipe', None, None, 'seq'), may hold values from -0.109375 to 0.109375
- output_proj: bfloat16 [4, 2048, 3072], P('pipe', 'seq'), may hold values from -0.5 to 0.5
- stale_cache: bfloat16 [4, 2, 192, 2, 2048], P('pipe', None, 'seq'), may hold values from -6 to 6
Outputs:
- block_output: bfloat16 [4, 2, 192, 3072], P('pipe', None, 'seq')
- fresh_cache: bfloat16 [4, 2, 192, 2, 2048], P('pipe', None, 'seq')
All inputs are finite; a program needn't handle non-finite values.
Results may differ from a plain program's by a relative error of at most 0.019.
Values may be sent and summed in bfloat16 or wider, within the bound.
No kernel may reach another device: no remote copies, remote signals or barrier semaphores. Data moves between devices by JAX's collectives and lax.ppermute only.
A program may use at most 64 MiB of HBM per device.

v0:
```python
import functools
import math

import jax
import jax.numpy as jnp
from jax import lax
from jax.experimental import pallas as pl
from jax.experimental.pallas import tpu as pltpu
from jax.sharding import PartitionSpec as P

AXES = ("pipe", "seq")
VMEM = pl.BlockSpec(memory_space=pltpu.VMEM)
ANY = pl.BlockSpec(memory_space=pl.ANY)


def ring_order(count):
    fast = 1
    while fast * fast * 4 <= count and count % (fast * 2) == 0:
        fast *= 2
    slow = count // fast
    if fast == 1 or slow % 2:
        return list(range(count))
    cells = [(0, 0)]
    for row in range(slow):
        columns = range(1, fast) if row % 2 == 0 else range(fast - 1, 0, -1)
        cells += [(row, column) for column in columns]
    cells += [(row, 0) for row in range(slow - 1, 0, -1)]
    return [row * fast + column for row, column in cells]


def normalise(values, shift_row, scale_row):
    centered = values - jnp.mean(values, axis=-1, keepdims=True)
    spread = jnp.mean(centered * centered, axis=-1, keepdims=True)
    return (centered * lax.rsqrt(spread + 1e-06) * (1.0 + scale_row) + shift_row).astype(
        jnp.bfloat16
    )


def norm_kernel(params_ref, x_ref, normed_ref):
    normed_ref[...] = normalise(
        x_ref[...].astype(jnp.float32), params_ref[0:1, :], params_ref[1:2, :]
    )


def finish_kernel(params_ref, next_ref, x_ref, own_ref, last_ref, out_ref, normed_ref):
    update = own_ref[...] + last_ref[...].astype(jnp.float32)
    result = (x_ref[...].astype(jnp.float32) + params_ref[2:3, :] * update).astype(jnp.bfloat16)
    out_ref[...] = result
    normed_ref[...] = normalise(
        result.astype(jnp.float32), next_ref[0:1, :], next_ref[1:2, :]
    )


def load_kernel(turn, own_ref, other_ref, out_ref, sem):
    mine = lax.rem(lax.axis_index("pipe"), 2) == turn

    @pl.when(mine)
    def _():
        pltpu.make_async_copy(own_ref, out_ref, sem).start()

    @pl.when(jnp.logical_not(mine))
    def _():
        pltpu.make_async_copy(other_ref, out_ref, sem).start()

    pltpu.make_async_copy(own_ref, out_ref, sem).wait()


def split_kernel(cache_ref, out_ref):
    channels = out_ref.shape[3]
    for kind in range(2):
        rows = cache_ref[:, kind, :]
        for shard in range(out_ref.shape[0]):
            out_ref[shard, kind] = rows[:, shard * channels : (shard + 1) * channels]


def project_kernel(head_size, gain_ref, weights_ref, *refs):
    groups, (q_ref, kv_ref, tokens_ref) = refs[:-3], refs[-3:]
    rows = groups[0].shape[0]
    for index, group in enumerate(groups):
        tokens_ref[index * rows : (index + 1) * rows, :] = group[...]
    tokens = tokens_ref[...]
    channels = weights_ref.shape[2]
    for part in (1, 2, 0):
        projected = jnp.dot(tokens, weights_ref[part], preferred_element_type=jnp.float32)
        if part == 2:
            kv_ref[1] = projected.astype(jnp.bfloat16)
            continue
        for start in range(0, channels, head_size):
            head = projected[:, start : start + head_size]
            square = jnp.mean(head * head, axis=-1, keepdims=True)
            head = (head * lax.rsqrt(square + 1e-06) * gain_ref[part : part + 1, :]).astype(
                jnp.bfloat16
            )
            if part == 0:
                q_ref[:, start : start + head_size] = head
            else:
                kv_ref[0, :, start : start + head_size] = head


def attend_kernel(turn, head_size, own_ref, other_ref, q_ref, kv_ref, stale_ref, fresh_ref, *refs):
    parts, (weights, sem) = refs[:-2], refs[-2:]
    early = lax.rem(lax.axis_index("pipe"), 2) == 0
    mine = lax.rem(lax.axis_index("pipe"), 2) == turn

    @pl.when(mine)
    def _():
        pltpu.make_async_copy(own_ref, weights, sem).start()

    @pl.when(jnp.logical_not(mine))
    def _():
        pltpu.make_async_copy(other_ref, weights, sem).start()

    factor = 1.0 / math.sqrt(head_size)
    tokens, channels = q_ref.shape
    heads = []
    across = (((1,), (1,)), ((), ()))

    def far_of(kind, cut):
        stale = stale_ref[:, kind, :, cut].astype(jnp.float32).reshape(tokens, head_size)
        return jnp.where(early, stale, fresh_ref[kind, :, cut].astype(jnp.float32)).astype(
            jnp.bfloat16
        )

    for start in range(0, channels, head_size):
        cut = slice(start, start + head_size)
        query = q_ref[:, cut]
        near = lax.dot_general(query, kv_ref[0, :, cut], across, preferred_element_type=jnp.float32)
        far = lax.dot_general(query, far_of(0, cut), across, preferred_element_type=jnp.float32)
        near = jnp.exp(near * factor)
        far = jnp.exp(far * factor)
        total = jnp.sum(near, axis=-1, keepdims=True) + jnp.sum(far, axis=-1, keepdims=True)
        near = (near / total).astype(jnp.bfloat16)
        far = (far / total).astype(jnp.bfloat16)
        mixed = jnp.dot(near, kv_ref[1, :, cut], preferred_element_type=jnp.float32)
        mixed = mixed + jnp.dot(far, far_of(1, cut), preferred_element_type=jnp.float32)
        heads.append(mixed.astype(jnp.bfloat16))
    attended = jnp.concatenate(heads, axis=1)
    pltpu.make_async_copy(own_ref, weights, sem).wait()
    rows = parts[0].shape[0]
    update = jnp.dot(attended, weights[...], preferred_element_type=jnp.float32)
    for index, part in enumerate(parts):
        part[...] = update[index * rows : (index + 1) * rows, :].astype(jnp.bfloat16)


def params_of(limit):
    return pltpu.CompilerParams(vmem_limit_bytes=limit << 20)


def body(hidden, mod_shift, mod_scale, mod_gate, norm_gain, input_proj, output_proj, stale_cache):
    sections = lax.axis_size("pipe")
    seq = lax.axis_size("seq")
    pipe = lax.axis_index("pipe")
    core = lax.rem(pipe, 2)
    plane = pipe // 2
    ring = ring_order(seq)
    half = seq // 2
    rows, width = hidden.shape[1:]
    head_size = norm_gain.shape[2]
    channels = input_proj.shape[3]
    tokens = rows * seq

    place = lambda row, position: row * seq + position
    swap = [(place(row, s), place(row ^ 1, s)) for row in range(sections) for s in range(seq)]

    def exchange(value, level, side):
        pairs = []
        for row in (2 * level, 2 * level + 1):
            for i in range((side + row) % 2, seq, 2):
                one, two = place(row, ring[i]), place(row, ring[(i + 1) % seq])
                pairs += [(one, two), (two, one)]
        return lax.ppermute(value, AXES, pairs)

    def upward(value, level):
        pairs = [
            (place(row, s), place(row + 2, s))
            for row in (2 * level, 2 * level + 1)
            for s in range(seq)
        ]
        return lax.ppermute(value, AXES, pairs)

    def gather(block, level, turn):
        groups = [jnp.concatenate([block, exchange(block, level, 0)], axis=0)]
        for step in range(1, half):
            if step == half - 1:
                groups[-1], late = lax.optimization_barrier((groups[-1], own_in))
            groups.append(exchange(groups[-1], level, step % 2))
        return groups, load(late, turn)

    def scatter(parts, level):
        wide = lambda value: value.astype(jnp.float32)
        got = exchange(parts[-1], level, (half - 1) % 2)
        for step in range(half - 2, 0, -1):
            got = exchange((wide(parts[step]) + wide(got)).astype(jnp.bfloat16), level, step % 2)
        own = wide(parts[0][:rows]) + wide(got[:rows])
        sent = (wide(parts[0][rows:]) + wide(got[rows:])).astype(jnp.bfloat16)
        return own, exchange(sent, level, 0)

    gains = jnp.pad(norm_gain[0].reshape(1, -1), ((0, 0), (0, width - 2 * head_size)))
    own_params = jnp.concatenate([mod_shift, mod_scale, mod_gate, gains], axis=0)
    own_in = jnp.transpose(input_proj[0], (1, 0, 2))
    own_out = output_proj[0]
    other_params = lax.ppermute(own_params, AXES, swap)
    own_in, own_out, other_params = lax.optimization_barrier((own_in, own_out, other_params))
    other_in = lax.ppermute(own_in, AXES, swap)
    other_out = lax.ppermute(own_out, AXES, swap)
    params = [jnp.where(core == turn, own_params, other_params) for turn in range(2)]
    gain_rows = [p[3, : 2 * head_size].reshape(2, head_size) for p in params]

    stale = pl.pallas_call(
        split_kernel,
        out_shape=jax.ShapeDtypeStruct((seq, 2, rows, channels), jnp.bfloat16),
        in_specs=[VMEM], out_specs=VMEM, compiler_params=params_of(16),
    )(stale_cache[0, 1])
    stale, hidden = lax.optimization_barrier((stale, hidden))
    stale = lax.all_to_all(stale, "seq", split_axis=0, concat_axis=0, tiled=True)
    stale_pair = [stale, lax.ppermute(stale, AXES, swap)]

    block_shape = jax.ShapeDtypeStruct((rows, width), jnp.bfloat16)

    def norm(x, turn):
        return pl.pallas_call(
            norm_kernel, out_shape=block_shape, in_specs=[VMEM] * 2, out_specs=VMEM,
            compiler_params=params_of(16),
        )(params[turn], x)

    def load(late, turn):
        return pl.pallas_call(
            functools.partial(load_kernel, turn),
            out_shape=jax.ShapeDtypeStruct(own_in.shape, jnp.bfloat16),
            in_specs=[ANY, ANY], out_specs=VMEM,
            scratch_shapes=[pltpu.SemaphoreType.DMA],
            compiler_params=params_of(16),
        )(late, other_in)

    def project(groups, weights, turn):
        return pl.pallas_call(
            functools.partial(project_kernel, head_size),
            out_shape=(
                jax.ShapeDtypeStruct((tokens, channels), jnp.bfloat16),
                jax.ShapeDtypeStruct((2, tokens, channels), jnp.bfloat16),
            ),
            in_specs=[VMEM] * (2 + half),
            out_specs=(VMEM, VMEM),
            scratch_shapes=[pltpu.VMEM((tokens, width), jnp.bfloat16)],
            compiler_params=params_of(32),
        )(gain_rows[turn], weights, *groups)

    def attend(queries, pair, fresh, turn):
        return pl.pallas_call(
            functools.partial(attend_kernel, turn, head_size),
            out_shape=(jax.ShapeDtypeStruct((2 * rows, width), jnp.bfloat16),) * half,
            in_specs=[ANY, ANY] + [VMEM] * 4,
            out_specs=(VMEM,) * half,
            scratch_shapes=[pltpu.VMEM(own_out.shape, jnp.bfloat16), pltpu.SemaphoreType.DMA],
            compiler_params=params_of(32),
        )(own_out, other_out, queries, pair, stale_pair[turn], fresh)

    def finish(x, own, last, turn):
        return pl.pallas_call(
            finish_kernel, out_shape=(block_shape,) * 2, in_specs=[VMEM] * 5, out_specs=(VMEM,) * 2,
            compiler_params=params_of(16),
        )(params[turn], params[1 - turn], x, own, last)

    outputs = [None, None]
    pairs = [None, None]
    freshes = [None, None]
    x = lax.dynamic_index_in_dim(hidden, core, 0, keepdims=False)
    for level in range(sections // 2):
        if level:
            x = upward(x, level - 1)
        normed = norm(x, 0)
        for turn in range(2):
            groups, weights = gather(normed, level, turn)
            queries, pair = project(groups, weights, turn)
            fresh = lax.ppermute(pair, AXES, swap)
            parts = attend(queries, pair, fresh, turn)
            own, last = scatter(parts, level)
            x, normed = finish(x, own, last, turn)
            here = plane == level
            keep = lambda new, old: new if old is None else jnp.where(here, new, old)
            outputs[turn] = keep(x, outputs[turn])
            pairs[turn] = keep(pair, pairs[turn])
            freshes[turn] = keep(fresh, freshes[turn])

    mine = jnp.where(core == 0, outputs[0], outputs[1])
    theirs = lax.ppermute(jnp.where(core == 0, outputs[1], outputs[0]), AXES, swap)
    block_output = jnp.stack(
        [jnp.where(core == 0, mine, theirs), jnp.where(core == 0, theirs, mine)]
    )
    cache = jnp.stack(
        [jnp.where(core == 0, pairs[0], freshes[1]), jnp.where(core == 0, freshes[0], pairs[1])]
    )
    cache = cache.reshape(2, 2, seq, rows, channels)
    spot = [0] * seq
    for index, position in enumerate(ring):
        spot[position] = index
    spot = jnp.array(spot, jnp.int32)
    steps = [0, 1]
    for group in range(1, half):
        steps += [-group, -group - 1] if group % 2 else [group, group + 1]
    held = [0] * seq
    for index, step in enumerate(steps):
        held[step % seq] = index
    held = jnp.array(held, jnp.int32)
    me = spot[lax.axis_index("seq")]
    cache = jnp.stack(
        [
            jnp.take(
                cache[patch],
                held[jnp.remainder((spot - me) * (1 - 2 * lax.rem(me + patch, 2)), seq)],
                axis=1,
            )
            for patch in range(2)
        ]
    )
    cache = lax.all_to_all(cache, "seq", split_axis=2, concat_axis=4, tiled=True)
    cache = jnp.transpose(cache[:, :, 0], (0, 2, 1, 3))
    return block_output[None], cache[None]


def solution(mesh):
    in_specs = (
        P(None, "seq", None),
        P("pipe", None),
        P("pipe", None),
        P("pipe", None),
        P("pipe", None, None),
        P("pipe", None, None, "seq"),
        P("pipe", "seq", None),
        P("pipe", None, "seq", None, None),
    )
    out_specs = (P("pipe", None, "seq", None), P("pipe", None, "seq", None, None))
    return jax.shard_map(body, mesh=mesh, in_specs=in_specs, out_specs=out_specs, check_vma=False)
```

profile of v0, /device:TPU:4, one launch (start us, length us, event | category | flops | bytes accessed | tf_op | source)
XLA Modules:
  0.0 338.4 jit_solution(12691093336323904596)
XLA Ops:
  11.6 5.8 %all-to-all-start = ((bf16[8,2,24,256]{3,2,1,0:T(8,128)(2,1)}), bf16[8,2,24,256]{3,2,1,0:T(8,128)(2,1)}, u32[]{:S(2)}, u32[]{:S(2)}) async-start(bf16[8,2,24,256]{3,2,1,0:T(8,128)(2,1)} %shard_map.113), calls=%async_computation | async-start | bytes 393216 | tf_op jit(solution)/shard_map/all_to_all | solution.py:215
  17.5 2.3 copy-done.1
  21.7 2.8 shard_map.116
  25.2 1.5 collective-permute-start.7
  26.7 1.4 collective-permute-done.7.fresh_ref
  29.0 2.3 shard_map.117
  38.0 2.3 copy-done.2
  40.3 2.3 shard_map.119.weights_ref
  44.0 1.4 collective-permute-done.17.fresh_ref
  52.1 113.6 %collective-permute-done.22.x_ref = bf16[24,3072]{1,0:T(8,128)(2,1)S(1)} collective-permute-done((bf16[24,3072]{1,0:T(8,128)(2,1)S(1)}, bf16[24,3072]{1,0:T(8,128)(2,1)S(1)}, u32[]{:S(2)}, u32[]{:S(2)}) %collective-permute-start.22) | collective-permute-done | bytes 147488 | tf_op jit(solution)/shard_map/ppermute | solution.py:179
  165.9 3.8 %collective-permute-start.23 = (bf16[24,3072]{1,0:T(8,128)(2,1)S(1)}, bf16[24,3072]{1,0:T(8,128)(2,1)S(1)}, u32[]{:S(2)}, u32[]{:S(2)}) collective-permute-start(bf16[24,3072]{1,0:T(8,128)(2,1)S(1)} %shard_map.123), channel_id=1, source_target_pairs={{16,17},{17,16},{19,21},{21,19},{23,22},{22,23},{20,18},{18,20},{2... | collective-permute-start | bytes 442376 | tf_op jit(solution)/shard_map/ppermute | solution.py:171
  169.8 4.2 %collective-permute-done.23 = bf16[24,3072]{1,0:T(8,128)(2,1)S(1)} collective-permute-done((bf16[24,3072]{1,0:T(8,128)(2,1)S(1)}, bf16[24,3072]{1,0:T(8,128)(2,1)S(1)}, u32[]{:S(2)}, u32[]{:S(2)}) %collective-permute-start.23) | collective-permute-done | bytes 147488 | tf_op jit(solution)/shard_map/ppermute | solution.py:171
  173.9 4.0 %collective-permute-start.24 = (bf16[48,3072]{1,0:T(8,128)(2,1)S(1)}, bf16[48,3072]{1,0:T(8,128)(2,1)S(1)}, u32[]{:S(2)}, u32[]{:S(2)}) collective-permute-start(bf16[48,3072]{1,0:T(8,128)(2,1)S(1)} %pad_maximum_fusion.2.refs_0_), channel_id=1, source_target_pairs={{17,19},{19,17},{21,23},{23,21},{22,20},{20,22},{18,16},{16,18},{2... | collective-permute-start | bytes 884744 | tf_op jit(solution)/shard_map/ppermute | solution.py:171
  178.0 6.7 %collective-permute-done.24.refs_1_ = bf16[48,3072]{1,0:T(8,128)(2,1)S(1)} collective-permute-done((bf16[48,3072]{1,0:T(8,128)(2,1)S(1)}, bf16[48,3072]{1,0:T(8,128)(2,1)S(1)}, u32[]{:S(2)}, u32[]{:S(2)}) %collective-permute-start.24) | collective-permute-done | bytes 294944 | tf_op jit(solution)/shard_map/ppermute | solution.py:171
  184.7 4.2 %collective-permute-start.25 = (bf16[48,3072]{1,0:T(8,128)(2,1)S(1)}, bf16[48,3072]{1,0:T(8,128)(2,1)S(1)}, u32[]{:S(2)}, u32[]{:S(2)}) collective-permute-start(bf16[48,3072]{1,0:T(8,128)(2,1)S(1)} %collective-permute-done.24.refs_1_), channel_id=1, source_target_pairs={{16,17},{17,16},{19,21},{21,19},{23,22},{22,23},{20,18},{18,20},{2... | collective-permute-start | bytes 884744 | tf_op jit(solution)/shard_map/ppermute | solution.py:171
  188.9 7.8 %collective-permute-done.25.refs_2_ = bf16[48,3072]{1,0:T(8,128)(2,1)S(1)} collective-permute-done((bf16[48,3072]{1,0:T(8,128)(2,1)S(1)}, bf16[48,3072]{1,0:T(8,128)(2,1)S(1)}, u32[]{:S(2)}, u32[]{:S(2)}) %collective-permute-start.25) | collective-permute-done | bytes 294944 | tf_op jit(solution)/shard_map/ppermute | solution.py:171
  196.8 3.6 %collective-permute-start.26 = (bf16[48,3072]{1,0:T(8,128)(2,1)S(1)}, bf16[48,3072]{1,0:T(8,128)(2,1)S(1)}, u32[]{:S(2)}, u32[]{:S(2)}) collective-permute-start(bf16[48,3072]{1,0:T(8,128)(2,1)S(1)} %collective-permute-done.25.refs_2_), channel_id=1, source_target_pairs={{17,19},{19,17},{21,23},{23,21},{22,20},{20,22},{18,16},{16,18},{2... | collective-permute-start | bytes 884744 | tf_op jit(solution)/shard_map/ppermute | solution.py:171
  200.8 4.6 %collective-permute-done.26.refs_3_ = bf16[48,3072]{1,0:T(8,128)(2,1)S(1)} collective-permute-done((bf16[48,3072]{1,0:T(8,128)(2,1)S(1)}, bf16[48,3072]{1,0:T(8,128)(2,1)S(1)}, u32[]{:S(2)}, u32[]{:S(2)}) %collective-permute-start.26) | collective-permute-done | bytes 294944 | tf_op jit(solution)/shard_map/ppermute | solution.py:171
  206.7 1.4 collective-permute-done.27.fresh_ref
  208.1 2.2 shard_map.126
  210.3 3.6 %collective-permute-start.28 = (bf16[48,3072]{1,0:T(8,128)(2,1)S(1)}, bf16[48,3072]{1,0:T(8,128)(2,1)S(1)}, u32[]{:S(2)}, u32[]{:S(2)}) collective-permute-start(bf16[48,3072]{1,0:T(8,128)(2,1)S(1)} %get-tuple-element.77), channel_id=1, source_target_pairs={{17,19},{19,17},{21,23},{23,21},{22,20},{20,22},{18,16},{16,18},{2... | collective-permute-start | bytes 884744 | tf_op jit(solution)/shard_map/ppermute | solution.py:171
  214.0 5.0 %collective-permute-done.28 = bf16[48,3072]{1,0:T(8,128)(2,1)S(1)} collective-permute-done((bf16[48,3072]{1,0:T(8,128)(2,1)S(1)}, bf16[48,3072]{1,0:T(8,128)(2,1)S(1)}, u32[]{:S(2)}, u32[]{:S(2)}) %collective-permute-start.28) | collective-permute-done | bytes 294944 | tf_op jit(solution)/shard_map/ppermute | solution.py:171
  219.0 3.6 %collective-permute-start.29 = (bf16[48,3072]{1,0:T(8,128)(2,1)S(1)}, bf16[48,3072]{1,0:T(8,128)(2,1)S(1)}, u32[]{:S(2)}, u32[]{:S(2)}) collective-permute-start(bf16[48,3072]{1,0:T(8,128)(2,1)S(1)} %add_convert_fusion.3), channel_id=1, source_target_pairs={{16,17},{17,16},{19,21},{21,19},{23,22},{22,23},{20,18},{18,20},{2... | collective-permute-start | bytes 884744 | tf_op jit(solution)/shard_map/ppermute | solution.py:171
  222.7 5.0 %collective-permute-done.29 = bf16[48,3072]{1,0:T(8,128)(2,1)S(1)} collective-permute-done((bf16[48,3072]{1,0:T(8,128)(2,1)S(1)}, bf16[48,3072]{1,0:T(8,128)(2,1)S(1)}, u32[]{:S(2)}, u32[]{:S(2)}) %collective-permute-start.29) | collective-permute-done | bytes 294944 | tf_op jit(solution)/shard_map/ppermute | solution.py:171
  227.7 3.6 %collective-permute-start.30 = (bf16[48,3072]{1,0:T(8,128)(2,1)S(1)}, bf16[48,3072]{1,0:T(8,128)(2,1)S(1)}, u32[]{:S(2)}, u32[]{:S(2)}) collective-permute-start(bf16[48,3072]{1,0:T(8,128)(2,1)S(1)} %add_convert_fusion.2), channel_id=1, source_target_pairs={{17,19},{19,17},{21,23},{23,21},{22,20},{20,22},{18,16},{16,18},{2... | collective-permute-start | bytes 884744 | tf_op jit(solution)/shard_map/ppermute | solution.py:171
  231.4 5.0 %collective-permute-done.30 = bf16[48,3072]{1,0:T(8,128)(2,1)S(1)} collective-permute-done((bf16[48,3072]{1,0:T(8,128)(2,1)S(1)}, bf16[48,3072]{1,0:T(8,128)(2,1)S(1)}, u32[]{:S(2)}, u32[]{:S(2)}) %collective-permute-start.30) | collective-permute-done | bytes 294944 | tf_op jit(solution)/shard_map/ppermute | solution.py:171
  236.4 3.6 %collective-permute-start.31 = (bf16[24,3072]{1,0:T(8,128)(2,1)S(1)}, bf16[24,3072]{1,0:T(8,128)(2,1)S(1)}, u32[]{:S(2)}, u32[]{:S(2)}) collective-permute-start(bf16[24,3072]{1,0:T(8,128)(2,1)S(1)} %get-tuple-element.96), channel_id=1, source_target_pairs={{16,17},{17,16},{19,21},{21,19},{23,22},{22,23},{20,18},{18,20},{2... | collective-permute-start | bytes 442376 | tf_op jit(solution)/shard_map/ppermute | solution.py:171
  240.1 3.4 %collective-permute-done.31.last_ref = bf16[24,3072]{1,0:T(8,128)(2,1)S(1)} collective-permute-done((bf16[24,3072]{1,0:T(8,128)(2,1)S(1)}, bf16[24,3072]{1,0:T(8,128)(2,1)S(1)}, u32[]{:S(2)}, u32[]{:S(2)}) %collective-permute-start.31) | collective-permute-done | bytes 147488 | tf_op jit(solution)/shard_map/ppermute | solution.py:171
  244.5 3.6 %collective-permute-start.32 = (bf16[24,3072]{1,0:T(8,128)(2,1)S(1)}, bf16[24,3072]{1,0:T(8,128)(2,1)S(1)}, u32[]{:S(2)}, u32[]{:S(2)}) collective-permute-start(bf16[24,3072]{1,0:T(8,128)(2,1)S(1)} %get-tuple-element.79), channel_id=1, source_target_pairs={{16,17},{17,16},{19,21},{21,19},{23,22},{22,23},{20,18},{18,20},{2... | collective-permute-start | bytes 442376 | tf_op jit(solution)/shard_map/ppermute | solution.py:171
  248.8 2.7 collective-permute-done.32
  252.2 3.6 %collective-permute-start.33 = (bf16[48,3072]{1,0:T(8,128)(2,1)}, bf16[48,3072]{1,0:T(8,128)(2,1)}, u32[]{:S(2)}, u32[]{:S(2)}) collective-permute-start(bf16[48,3072]{1,0:T(8,128)(2,1)} %constant_dynamic-update-slice_fusion.2.refs_0_), channel_id=1, source_target_pairs={{17,19},{19,17},{21,23},{23,21},{22,20},{20,22},{18,16},{16,18},{2... | collective-permute-start | bytes 884744 | tf_op jit(solution)/shard_map/ppermute | solution.py:171
  258.9 3.0 collective-permute-done.33.refs_1_
  261.9 3.8 %collective-permute-start.34 = (bf16[48,3072]{1,0:T(8,128)(2,1)}, bf16[48,3072]{1,0:T(8,128)(2,1)}, u32[]{:S(2)}, u32[]{:S(2)}) collective-permute-start(bf16[48,3072]{1,0:T(8,128)(2,1)} %collective-permute-done.33.refs_1_), channel_id=1, source_target_pairs={{16,17},{17,16},{19,21},{21,19},{23,22},{22,23},{20,18},{18,20},{2... | collective-permute-start | bytes 884744 | tf_op jit(solution)/shard_map/ppermute | solution.py:171
  267.6 5.4 %collective-permute-done.34.refs_2_ = bf16[48,3072]{1,0:T(8,128)(2,1)} collective-permute-done((bf16[48,3072]{1,0:T(8,128)(2,1)}, bf16[48,3072]{1,0:T(8,128)(2,1)}, u32[]{:S(2)}, u32[]{:S(2)}) %collective-permute-start.34) | collective-permute-done | bytes 294944 | tf_op jit(solution)/shard_map/ppermute | solution.py:171
  273.0 3.8 %collective-permute-start.35 = (bf16[48,3072]{1,0:T(8,128)(2,1)}, bf16[48,3072]{1,0:T(8,128)(2,1)}, u32[]{:S(2)}, u32[]{:S(2)}) collective-permute-start(bf16[48,3072]{1,0:T(8,128)(2,1)} %collective-permute-done.34.refs_2_), channel_id=1, source_target_pairs={{17,19},{19,17},{21,23},{23,21},{22,20},{20,22},{18,16},{16,18},{2... | collective-permute-start | bytes 884744 | tf_op jit(solution)/shard_map/ppermute | solution.py:171
  279.3 2.3 copy-done.3
  281.6 2.3 shard_map.128.weights_ref
  284.0 2.4 shard_map.129
  286.6 1.4 collective-permute-done.36.fresh_ref
  290.0 2.1 collective-permute-start.37
  292.2 6.6 %collective-permute-done.37 = bf16[48,3072]{1,0:T(8,128)(2,1)S(1)} collective-permute-done((bf16[48,3072]{1,0:T(8,128)(2,1)S(1)}, bf16[48,3072]{1,0:T(8,128)(2,1)S(1)}, u32[]{:S(2)}, u32[]{:S(2)}) %collective-permute-start.37) | collective-permute-done | bytes 294944 | tf_op jit(solution)/shard_map/ppermute | solution.py:171
  298.8 3.4 collective-permute-start.38
  303.9 3.6 %collective-permute-done.38 = bf16[48,3072]{1,0:T(8,128)(2,1)S(1)} collective-permute-done((bf16[48,3072]{1,0:T(8,128)(2,1)S(1)}, bf16[48,3072]{1,0:T(8,128)(2,1)S(1)}, u32[]{:S(2)}, u32[]{:S(2)}) %collective-permute-start.38) | collective-permute-done | bytes 294944 | tf_op jit(solution)/shard_map/ppermute | solution.py:171
  308.5 2.8 collective-permute-start.39
  313.0 4.0 %collective-permute-done.39 = bf16[48,3072]{1,0:T(8,128)(2,1)S(1)} collective-permute-done((bf16[48,3072]{1,0:T(8,128)(2,1)S(1)}, bf16[48,3072]{1,0:T(8,128)(2,1)S(1)}, u32[]{:S(2)}, u32[]{:S(2)}) %collective-permute-start.39) | collective-permute-done | bytes 294944 | tf_op jit(solution)/shard_map/ppermute | solution.py:171
  318.1 3.4 collective-permute-start.40
  322.4 3.7 %all-to-all-start.1 = ((bf16[2,2,8,24,256]{4,3,1,0,2:T(8,128)(2,1)}), bf16[2,2,8,24,256]{4,3,1,0,2:T(8,128)(2,1)S(1)}, u32[]{:S(2)}, u32[]{:S(2)}) async-start(bf16[2,2,8,24,256]{4,3,1,0,2:T(8,128)(2,1)} %pad_maximum_fusion), calls=%async_computation.1 | async-start | bytes 786432 | tf_op jit(solution)/shard_map/all_to_all | solution.py:316
  327.2 8.9 %all-to-all-done.1 = bf16[2,2,8,24,256]{4,3,1,0,2:T(8,128)(2,1)S(1)} async-done(((bf16[2,2,8,24,256]{4,3,1,0,2:T(8,128)(2,1)}), bf16[2,2,8,24,256]{4,3,1,0,2:T(8,128)(2,1)S(1)}, u32[]{:S(2)}, u32[]{:S(2)}) %all-to-all-start.1) | async-done | bytes 393248 | tf_op jit(solution)/shard_map/all_to_all | solution.py:316
  (176 shorter events, 50.0 us)
Async XLA Ops:
  1.5 1.3 collective-permute-start
  2.8 14.6 %collective-permute-start.5 = (bf16[3,3072,256]{2,1,0:T(8,128)(2,1)}, bf16[3,3072,256]{2,1,0:T(8,128)(2,1)}, u32[]{:S(2)}, u32[]{:S(2)}) collective-permute-start(bf16[3,3072,256]{2,1,0:T(8,128)(2,1)} %bitcast.38), channel_id=1, source_target_pairs={{0,8},{1,9},{2,10},{3,11},{4,12},{5,13},{6,14},{7,15},{8,0},{9,1},... | collective-permute-start | bytes 14155784 | tf_op jit(solution)/shard_map/ppermute | solution.py:204
  5.2 21.4 %collective-permute-start.1 = (bf16[256,3072]{1,0:T(8,128)(2,1)}, bf16[256,3072]{1,0:T(8,128)(2,1)S(1)}, u32[]{:S(2)}, u32[]{:S(2)}) collective-permute-start(bf16[256,3072]{1,0:T(8,128)(2,1)} %bitcast.45), channel_id=1, source_target_pairs={{0,8},{1,9},{2,10},{3,11},{4,12},{5,13},{6,14},{7,15},{8,0},{9,1},... | collective-permute-start | bytes 4718600 | tf_op jit(solution)/shard_map/ppermute | solution.py:205
  6.7 0.7 collective-permute-start.2
  7.4 0.7 collective-permute-start.3
  8.1 2.1 collective-permute-start.4
  10.2 9.9 %collective-permute-start.6 = (bf16[48,3072]{1,0:T(8,128)(2,1)}, bf16[48,3072]{1,0:T(8,128)(2,1)}, u32[]{:S(2)}, u32[]{:S(2)}) collective-permute-start(bf16[48,3072]{1,0:T(8,128)(2,1)} %collective-permute-done.4.refs_2_), channel_id=1, source_target_pairs={{1,3},{3,1},{5,7},{7,5},{6,4},{4,6},{2,0},{0,2},{8,9},{9,8},{11,13... | collective-permute-start | bytes 884744 | tf_op jit(solution)/shard_map/ppermute | solution.py:171
  11.6 15.0 %all-to-all-start = ((bf16[8,2,24,256]{3,2,1,0:T(8,128)(2,1)}), bf16[8,2,24,256]{3,2,1,0:T(8,128)(2,1)}, u32[]{:S(2)}, u32[]{:S(2)}) async-start(bf16[8,2,24,256]{3,2,1,0:T(8,128)(2,1)} %shard_map.113), calls=%async_computation | async-start | bytes 393216 | tf_op jit(solution)/shard_map/all_to_all | solution.py:215
  25.2 2.9 collective-permute-start.7
  31.3 0.7 collective-permute-start.8
  32.1 0.7 collective-permute-start.9
  32.9 0.7 collective-permute-start.10
  33.6 0.7 collective-permute-start.11
  34.7 0.7 collective-permute-start.12
  35.4 0.7 collective-permute-start.13
  36.1 0.7 collective-permute-start.14
  36.8 5.8 %collective-permute-start.15 = (bf16[48,3072]{1,0:T(8,128)(2,1)S(1)}, bf16[48,3072]{1,0:T(8,128)(2,1)S(1)}, u32[]{:S(2)}, u32[]{:S(2)}) collective-permute-start(bf16[48,3072]{1,0:T(8,128)(2,1)S(1)} %collective-permute-done.14.refs_2_), channel_id=1, source_target_pairs={{1,3},{3,1},{5,7},{7,5},{6,4},{4,6},{2,0},{0,2},{8,9},{9,8},{11,13... | collective-permute-start | bytes 884744 | tf_op jit(solution)/shard_map/ppermute | solution.py:171
  37.5 6.4 %collective-permute-start.16 = (bf16[8,2,24,256]{3,2,1,0:T(8,128)(2,1)}, bf16[8,2,24,256]{3,2,1,0:T(8,128)(2,1)S(1)}, u32[]{:S(2)}, u32[]{:S(2)}) collective-permute-start(bf16[8,2,24,256]{3,2,1,0:T(8,128)(2,1)} %all-to-all-done.stale_ref), channel_id=1, source_target_pairs={{0,8},{1,9},{2,10},{3,11},{4,12},{5,13},{6,14},{7,15},{8,0},{9,1},... | collective-permute-start | bytes 589832 | tf_op jit(solution)/shard_map/ppermute | solution.py:216
  42.7 157.7 %slice-start = ((s8[4718592]{0:T(1024)(128)(4,1)}), s8[524288]{0:T(1024)(128)(4,1)S(1)}, s32[]{:S(2)}) async-start(s8[4718592]{0:T(1024)(128)(4,1)} %bitcast.41), calls=%async_computation.2 | async-start | bytes 1048576
  43.9 152.9 %copy-start.10 = (bf16[2,192,256]{2,1,0:T(8,128)(2,1)}, bf16[2,192,256]{2,1,0:T(8,128)(2,1)S(1)}, u32[]{:S(2)}) copy-start(bf16[2,192,256]{2,1,0:T(8,128)(2,1)S(1)} %get-tuple-element.64.kv_ref) | copy-start | bytes 589828
  43.9 1.5 collective-permute-start.17
  44.0 152.8 %copy-start.15 = (bf16[8,2,24,256]{3,2,1,0:T(8,128)(2,1)}, bf16[8,2,24,256]{3,2,1,0:T(8,128)(2,1)S(1)}, u32[]{:S(2)}) copy-start(bf16[8,2,24,256]{3,2,1,0:T(8,128)(2,1)S(1)} %collective-permute-done.16.stale_ref) | copy-start | bytes 589828
  45.4 155.0 %slice-start.1 = ((s8[4718592]{0:T(1024)(128)(4,1)}), s8[4194304]{0:T(1024)(128)(4,1)S(1)}, s32[]{:S(2)}) async-start(s8[4718592]{0:T(1024)(128)(4,1)} %bitcast.41), calls=%async_computation.3 | async-start | bytes 8388608
  46.6 0.8 collective-permute-start.18
  47.5 0.7 collective-permute-start.19
  48.3 0.7 collective-permute-start.20
  49.1 0.7 collective-permute-start.21
  50.8 114.9 %collective-permute-start.22 = (bf16[24,3072]{1,0:T(8,128)(2,1)S(1)}, bf16[24,3072]{1,0:T(8,128)(2,1)S(1)}, u32[]{:S(2)}, u32[]{:S(2)}) collective-permute-start(bf16[24,3072]{1,0:T(8,128)(2,1)S(1)} %get-tuple-element.69), channel_id=1, source_target_pairs={{0,16},{1,17},{2,18},{3,19},{4,20},{5,21},{6,22},{7,23},{8,24},{9,... | collective-permute-start | bytes 442376 | tf_op jit(solution)/shard_map/ppermute | solution.py:179
  165.9 8.0 %collective-permute-start.23 = (bf16[24,3072]{1,0:T(8,128)(2,1)S(1)}, bf16[24,3072]{1,0:T(8,128)(2,1)S(1)}, u32[]{:S(2)}, u32[]{:S(2)}) collective-permute-start(bf16[24,3072]{1,0:T(8,128)(2,1)S(1)} %shard_map.123), channel_id=1, source_target_pairs={{16,17},{17,16},{19,21},{21,19},{23,22},{22,23},{20,18},{18,20},{2... | collective-permute-start | bytes 442376 | tf_op jit(solution)/shard_map/ppermute | solution.py:171
  173.9 10.7 %collective-permute-start.24 = (bf16[48,3072]{1,0:T(8,128)(2,1)S(1)}, bf16[48,3072]{1,0:T(8,128)(2,1)S(1)}, u32[]{:S(2)}, u32[]{:S(2)}) collective-permute-start(bf16[48,3072]{1,0:T(8,128)(2,1)S(1)} %pad_maximum_fusion.2.refs_0_), channel_id=1, source_target_pairs={{17,19},{19,17},{21,23},{23,21},{22,20},{20,22},{18,16},{16,18},{2... | collective-permute-start | bytes 884744 | tf_op jit(solution)/shard_map/ppermute | solution.py:171
  184.7 12.1 %collective-permute-start.25 = (bf16[48,3072]{1,0:T(8,128)(2,1)S(1)}, bf16[48,3072]{1,0:T(8,128)(2,1)S(1)}, u32[]{:S(2)}, u32[]{:S(2)}) collective-permute-start(bf16[48,3072]{1,0:T(8,128)(2,1)S(1)} %collective-permute-done.24.refs_1_), channel_id=1, source_target_pairs={{16,17},{17,16},{19,21},{21,19},{23,22},{22,23},{20,18},{18,20},{2... | collective-permute-start | bytes 884744 | tf_op jit(solution)/shard_map/ppermute | solution.py:171
  196.8 8.6 %collective-permute-start.26 = (bf16[48,3072]{1,0:T(8,128)(2,1)S(1)}, bf16[48,3072]{1,0:T(8,128)(2,1)S(1)}, u32[]{:S(2)}, u32[]{:S(2)}) collective-permute-start(bf16[48,3072]{1,0:T(8,128)(2,1)S(1)} %collective-permute-done.25.refs_2_), channel_id=1, source_target_pairs={{17,19},{19,17},{21,23},{23,21},{22,20},{20,22},{18,16},{16,18},{2... | collective-permute-start | bytes 884744 | tf_op jit(solution)/shard_map/ppermute | solution.py:171
  206.6 1.5 collective-permute-start.27
  210.3 8.6 %collective-permute-start.28 = (bf16[48,3072]{1,0:T(8,128)(2,1)S(1)}, bf16[48,3072]{1,0:T(8,128)(2,1)S(1)}, u32[]{:S(2)}, u32[]{:S(2)}) collective-permute-start(bf16[48,3072]{1,0:T(8,128)(2,1)S(1)} %get-tuple-element.77), channel_id=1, source_target_pairs={{17,19},{19,17},{21,23},{23,21},{22,20},{20,22},{18,16},{16,18},{2... | collective-permute-start | bytes 884744 | tf_op jit(solution)/shard_map/ppermute | solution.py:171
  219.0 8.6 %collective-permute-start.29 = (bf16[48,3072]{1,0:T(8,128)(2,1)S(1)}, bf16[48,3072]{1,0:T(8,128)(2,1)S(1)}, u32[]{:S(2)}, u32[]{:S(2)}) collective-permute-start(bf16[48,3072]{1,0:T(8,128)(2,1)S(1)} %add_convert_fusion.3), channel_id=1, source_target_pairs={{16,17},{17,16},{19,21},{21,19},{23,22},{22,23},{20,18},{18,20},{2... | collective-permute-start | bytes 884744 | tf_op jit(solution)/shard_map/ppermute | solution.py:171
  227.7 8.6 %collective-permute-start.30 = (bf16[48,3072]{1,0:T(8,128)(2,1)S(1)}, bf16[48,3072]{1,0:T(8,128)(2,1)S(1)}, u32[]{:S(2)}, u32[]{:S(2)}) collective-permute-start(bf16[48,3072]{1,0:T(8,128)(2,1)S(1)} %add_convert_fusion.2), channel_id=1, source_target_pairs={{17,19},{19,17},{21,23},{23,21},{22,20},{20,22},{18,16},{16,18},{2... | collective-permute-start | bytes 884744 | tf_op jit(solution)/shard_map/ppermute | solution.py:171
  236.4 7.0 %collective-permute-start.31 = (bf16[24,3072]{1,0:T(8,128)(2,1)S(1)}, bf16[24,3072]{1,0:T(8,128)(2,1)S(1)}, u32[]{:S(2)}, u32[]{:S(2)}) collective-permute-start(bf16[24,3072]{1,0:T(8,128)(2,1)S(1)} %get-tuple-element.96), channel_id=1, source_target_pairs={{16,17},{17,16},{19,21},{21,19},{23,22},{22,23},{20,18},{18,20},{2... | collective-permute-start | bytes 442376 | tf_op jit(solution)/shard_map/ppermute | solution.py:171
  244.5 7.0 %collective-permute-start.32 = (bf16[24,3072]{1,0:T(8,128)(2,1)S(1)}, bf16[24,3072]{1,0:T(8,128)(2,1)S(1)}, u32[]{:S(2)}, u32[]{:S(2)}) collective-permute-start(bf16[24,3072]{1,0:T(8,128)(2,1)S(1)} %get-tuple-element.79), channel_id=1, source_target_pairs={{16,17},{17,16},{19,21},{21,19},{23,22},{22,23},{20,18},{18,20},{2... | collective-permute-start | bytes 442376 | tf_op jit(solution)/shard_map/ppermute | solution.py:171
  252.2 9.8 %collective-permute-start.33 = (bf16[48,3072]{1,0:T(8,128)(2,1)}, bf16[48,3072]{1,0:T(8,128)(2,1)}, u32[]{:S(2)}, u32[]{:S(2)}) collective-permute-start(bf16[48,3072]{1,0:T(8,128)(2,1)} %constant_dynamic-update-slice_fusion.2.refs_0_), channel_id=1, source_target_pairs={{17,19},{19,17},{21,23},{23,21},{22,20},{20,22},{18,16},{16,18},{2... | collective-permute-start | bytes 884744 | tf_op jit(solution)/shard_map/ppermute | solution.py:171
  261.9 11.0 %collective-permute-start.34 = (bf16[48,3072]{1,0:T(8,128)(2,1)}, bf16[48,3072]{1,0:T(8,128)(2,1)}, u32[]{:S(2)}, u32[]{:S(2)}) collective-permute-start(bf16[48,3072]{1,0:T(8,128)(2,1)} %collective-permute-done.33.refs_1_), channel_id=1, source_target_pairs={{16,17},{17,16},{19,21},{21,19},{23,22},{22,23},{20,18},{18,20},{2... | collective-permute-start | bytes 884744 | tf_op jit(solution)/shard_map/ppermute | solution.py:171
  273.0 11.1 %collective-permute-start.35 = (bf16[48,3072]{1,0:T(8,128)(2,1)}, bf16[48,3072]{1,0:T(8,128)(2,1)}, u32[]{:S(2)}, u32[]{:S(2)}) collective-permute-start(bf16[48,3072]{1,0:T(8,128)(2,1)} %collective-permute-done.34.refs_2_), channel_id=1, source_target_pairs={{17,19},{19,17},{21,23},{23,21},{22,20},{20,22},{18,16},{16,18},{2... | collective-permute-start | bytes 884744 | tf_op jit(solution)/shard_map/ppermute | solution.py:171
  286.5 1.5 collective-permute-start.36
  290.0 8.7 %collective-permute-start.37 = (bf16[48,3072]{1,0:T(8,128)(2,1)S(1)}, bf16[48,3072]{1,0:T(8,128)(2,1)S(1)}, u32[]{:S(2)}, u32[]{:S(2)}) collective-permute-start(bf16[48,3072]{1,0:T(8,128)(2,1)S(1)} %get-tuple-element.87), channel_id=1, source_target_pairs={{17,19},{19,17},{21,23},{23,21},{22,20},{20,22},{18,16},{16,18},{2... | collective-permute-start | bytes 884744 | tf_op jit(solution)/shard_map/ppermute | solution.py:171
  298.8 8.6 %collective-permute-start.38 = (bf16[48,3072]{1,0:T(8,128)(2,1)S(1)}, bf16[48,3072]{1,0:T(8,128)(2,1)S(1)}, u32[]{:S(2)}, u32[]{:S(2)}) collective-permute-start(bf16[48,3072]{1,0:T(8,128)(2,1)S(1)} %add_convert_fusion.1), channel_id=1, source_target_pairs={{16,17},{17,16},{19,21},{21,19},{23,22},{22,23},{20,18},{18,20},{2... | collective-permute-start | bytes 884744 | tf_op jit(solution)/shard_map/ppermute | solution.py:171
  308.5 8.6 %collective-permute-start.39 = (bf16[48,3072]{1,0:T(8,128)(2,1)S(1)}, bf16[48,3072]{1,0:T(8,128)(2,1)S(1)}, u32[]{:S(2)}, u32[]{:S(2)}) collective-permute-start(bf16[48,3072]{1,0:T(8,128)(2,1)S(1)} %add_convert_fusion), channel_id=1, source_target_pairs={{17,19},{19,17},{21,23},{23,21},{22,20},{20,22},{18,16},{16,18},{2... | collective-permute-start | bytes 884744 | tf_op jit(solution)/shard_map/ppermute | solution.py:171
  318.1 7.9 %collective-permute-start.40 = (bf16[24,3072]{1,0:T(8,128)(2,1)S(1)}, bf16[24,3072]{1,0:T(8,128)(2,1)S(1)}, u32[]{:S(2)}, u32[]{:S(2)}) collective-permute-start(bf16[24,3072]{1,0:T(8,128)(2,1)S(1)} %get-tuple-element.94), channel_id=1, source_target_pairs={{16,17},{17,16},{19,21},{21,19},{23,22},{22,23},{20,18},{18,20},{2... | collective-permute-start | bytes 442376 | tf_op jit(solution)/shard_map/ppermute | solution.py:171
  322.4 13.7 %all-to-all-start.1 = ((bf16[2,2,8,24,256]{4,3,1,0,2:T(8,128)(2,1)}), bf16[2,2,8,24,256]{4,3,1,0,2:T(8,128)(2,1)S(1)}, u32[]{:S(2)}, u32[]{:S(2)}) async-start(bf16[2,2,8,24,256]{4,3,1,0,2:T(8,128)(2,1)} %pad_maximum_fusion), calls=%async_computation.1 | async-start | bytes 786432 | tf_op jit(solution)/shard_map/all_to_all | solution.py:316
  327.1 10.5 %collective-permute-start.41 = (bf16[24,3072]{1,0:T(8,128)(2,1)S(1)}, bf16[24,3072]{1,0:T(8,128)(2,1)S(1)}, u32[]{:S(2)}, u32[]{:S(2)}) collective-permute-start(bf16[24,3072]{1,0:T(8,128)(2,1)S(1)} %get-tuple-element.91), channel_id=1, source_target_pairs={{0,8},{1,9},{2,10},{3,11},{4,12},{5,13},{6,14},{7,15},{8,0},{9,1},... | collective-permute-start | bytes 442376 | tf_op jit(solution)/shard_map/ppermute | solution.py:286
  (30 other events, 669.4 us)
where the time goes:
time: 340 us; the launch traced here: 338 us
  waiting for transfers between devices  196 us (58%)
  starting transfers between devices  82.7 us (24%)
  Pallas kernels  24.4 us (7%)
  local copies, waits for them, and re-layouts  20.4 us (6%)
  other arithmetic  10.4 us (3%)
  between operations  4.2 us (1%)
    ppermute x1, waiting for transfers between devices, upward(): return lax.ppermute(value, AXES, pairs)  114 us
    ppermute x32, starting transfers between devices, exchange(): return lax.ppermute(value, AXES, pairs)  69.2 us
    ppermute x32, waiting for transfers between devices, exchange(): return lax.ppermute(value, AXES, pairs)  66.9 us
    unnamed x71, local copies, waits for them, and re-layouts  14.1 us
    all_to_all x1, waiting for transfers between devices, body(): lax.all_to_all(cache, 'seq', split_axis=2, concat_axis=4, tiled=True)  8.88 us
    pallas_call x4, Pallas kernels, project(): pl.pallas_call(functools.partial(project_kernel, head_size), out_shape=(j...  7.61 us
    pallas_call x4, Pallas kernels, attend(): pl.pallas_call(functools.partial(attend_kernel, turn, head_size), out_sha...  7.05 us
  transfers between devices with their start and end apart: 44, of which 21 were waited for; matrix products, arithmetic and copies ran while one was open for 4% of the time, Pallas kernels for 3%

commit v1 on v0

--- a/solution.py
+++ b/solution.py
@@ -13,21 +13,6 @@
 ANY = pl.BlockSpec(memory_space=pl.ANY)
 
 
-def ring_order(count):
-    fast = 1
-    while fast * fast * 4 <= count and count % (fast * 2) == 0:
-        fast *= 2
-    slow = count // fast
-    if fast == 1 or slow % 2:
-        return list(range(count))
-    cells = [(0, 0)]
-    for row in range(slow):
-        columns = range(1, fast) if row % 2 == 0 else range(fast - 1, 0, -1)
-        cells += [(row, column) for column in columns]
-    cells += [(row, 0) for row in range(slow - 1, 0, -1)]
-    return [row * fast + column for row, column in cells]
-
-
 def normalise(values, shift_row, scale_row):
     centered = values - jnp.mean(values, axis=-1, keepdims=True)
     spread = jnp.mean(centered * centered, axis=-1, keepdims=True)
@@ -42,8 +27,8 @@
     )
 
 
-def finish_kernel(params_ref, next_ref, x_ref, own_ref, last_ref, out_ref, normed_ref):
-    update = own_ref[...] + last_ref[...].astype(jnp.float32)
+def finish_kernel(params_ref, next_ref, x_ref, parts_ref, out_ref, normed_ref):
+    update = jnp.sum(parts_ref[...].astype(jnp.float32), axis=0)
     result = (x_ref[...].astype(jnp.float32) + params_ref[2:3, :] * update).astype(jnp.bfloat16)
     out_ref[...] = result
     normed_ref[...] = normalise(
@@ -73,12 +58,9 @@
             out_ref[shard, kind] = rows[:, shard * channels : (shard + 1) * channels]
 
 
-def project_kernel(head_size, gain_ref, weights_ref, *refs):
-    groups, (q_ref, kv_ref, tokens_ref) = refs[:-3], refs[-3:]
-    rows = groups[0].shape[0]
-    for index, group in enumerate(groups):
-        tokens_ref[index * rows : (index + 1) * rows, :] = group[...]
-    tokens = tokens_ref[...]
+def project_kernel(head_size, gain_ref, weights_ref, blocks_ref, q_ref, kv_ref):
+    count, rows, width = blocks_ref.shape
+    tokens = blocks_ref[...].astype(jnp.float32).reshape(count * rows, width).astype(jnp.bfloat16)
     channels = weights_ref.shape[2]
     for part in (1, 2, 0):
         projected = jnp.dot(tokens, weights_ref[part], preferred_element_type=jnp.float32)
@@ -97,8 +79,7 @@
                 kv_ref[0, :, start : start + head_size] = head
 
 
-def attend_kernel(turn, head_size, own_ref, other_ref, q_ref, kv_ref, stale_ref, fresh_ref, *refs):
-    parts, (weights, sem) = refs[:-2], refs[-2:]
+def attend_kernel(turn, head_size, own_ref, other_ref, q_ref, kv_ref, stale_ref, fresh_ref, parts_ref, weights, sem):
     early = lax.rem(lax.axis_index("pipe"), 2) == 0
     mine = lax.rem(lax.axis_index("pipe"), 2) == turn
 
@@ -136,10 +117,8 @@
         heads.append(mixed.astype(jnp.bfloat16))
     attended = jnp.concatenate(heads, axis=1)
     pltpu.make_async_copy(own_ref, weights, sem).wait()
-    rows = parts[0].shape[0]
     update = jnp.dot(attended, weights[...], preferred_element_type=jnp.float32)
-    for index, part in enumerate(parts):
-        part[...] = update[index * rows : (index + 1) * rows, :].astype(jnp.bfloat16)
+    parts_ref[...] = update.reshape(parts_ref.shape).astype(jnp.bfloat16)
 
 
 def params_of(limit):
@@ -152,8 +131,6 @@
     pipe = lax.axis_index("pipe")
     core = lax.rem(pipe, 2)
     plane = pipe // 2
-    ring = ring_order(seq)
-    half = seq // 2
     rows, width = hidden.shape[1:]
     head_size = norm_gain.shape[2]
     channels = input_proj.shape[3]
@@ -162,13 +139,8 @@
     place = lambda row, position: row * seq + position
     swap = [(place(row, s), place(row ^ 1, s)) for row in range(sections) for s in range(seq)]
 
-    def exchange(value, level, side):
-        pairs = []
-        for row in (2 * level, 2 * level + 1):
-            for i in range((side + row) % 2, seq, 2):
-                one, two = place(row, ring[i]), place(row, ring[(i + 1) % seq])
-                pairs += [(one, two), (two, one)]
-        return lax.ppermute(value, AXES, pairs)
+    def across(blocks):
+        return lax.all_to_all(blocks, "seq", split_axis=0, concat_axis=0, tiled=True)
 
     def upward(value, level):
         pairs = [
@@ -177,23 +149,6 @@
             for s in range(seq)
         ]
         return lax.ppermute(value, AXES, pairs)
-
-    def gather(block, level, turn):
-        groups = [jnp.concatenate([block, exchange(block, level, 0)], axis=0)]
-        for step in range(1, half):
-            if step == half - 1:
-                groups[-1], late = lax.optimization_barrier((groups[-1], own_in))
-            groups.append(exchange(groups[-1], level, step % 2))
-        return groups, load(late, turn)
-
-    def scatter(parts, level):
-        wide = lambda value: value.astype(jnp.float32)
-        got = exchange(parts[-1], level, (half - 1) % 2)
-        for step in range(half - 2, 0, -1):
-            got = exchange((wide(parts[step]) + wide(got)).astype(jnp.bfloat16), level, step % 2)
-        own = wide(parts[0][:rows]) + wide(got[:rows])
-        sent = (wide(parts[0][rows:]) + wide(got[rows:])).astype(jnp.bfloat16)
-        return own, exchange(sent, level, 0)
 
     gains = jnp.pad(norm_gain[0].reshape(1, -1), ((0, 0), (0, width - 2 * head_size)))
     own_params = jnp.concatenate([mod_shift, mod_scale, mod_gate, gains], axis=0)
@@ -212,7 +167,7 @@
         in_specs=[VMEM], out_specs=VMEM, compiler_params=params_of(16),
     )(stale_cache[0, 1])
     stale, hidden = lax.optimization_barrier((stale, hidden))
-    stale = lax.all_to_all(stale, "seq", split_axis=0, concat_axis=0, tiled=True)
+    stale = across(stale)
     stale_pair = [stale, lax.ppermute(stale, AXES, swap)]
 
     block_shape = jax.ShapeDtypeStruct((rows, width), jnp.bfloat16)
@@ -223,43 +178,42 @@
             compiler_params=params_of(16),
         )(params[turn], x)
 
-    def load(late, turn):
+    def load(turn):
         return pl.pallas_call(
             functools.partial(load_kernel, turn),
             out_shape=jax.ShapeDtypeStruct(own_in.shape, jnp.bfloat16),
             in_specs=[ANY, ANY], out_specs=VMEM,
             scratch_shapes=[pltpu.SemaphoreType.DMA],
             compiler_params=params_of(16),
-        )(late, other_in)
-
-    def project(groups, weights, turn):
+        )(own_in, other_in)
+
+    def project(blocks, weights, turn):
         return pl.pallas_call(
             functools.partial(project_kernel, head_size),
             out_shape=(
                 jax.ShapeDtypeStruct((tokens, channels), jnp.bfloat16),
                 jax.ShapeDtypeStruct((2, tokens, channels), jnp.bfloat16),
             ),
-            in_specs=[VMEM] * (2 + half),
+            in_specs=[VMEM] * 3,
             out_specs=(VMEM, VMEM),
-            scratch_shapes=[pltpu.VMEM((tokens, width), jnp.bfloat16)],
             compiler_params=params_of(32),
-        )(gain_rows[turn], weights, *groups)
+        )(gain_rows[turn], weights, blocks)
 
     def attend(queries, pair, fresh, turn):
         return pl.pallas_call(
             functools.partial(attend_kernel, turn, head_size),
-            out_shape=(jax.ShapeDtypeStruct((2 * rows, width), jnp.bfloat16),) * half,
+            out_shape=jax.ShapeDtypeStruct((seq, rows, width), jnp.bfloat16),
             in_specs=[ANY, ANY] + [VMEM] * 4,
-            out_specs=(VMEM,) * half,
+            out_specs=VMEM,
             scratch_shapes=[pltpu.VMEM(own_out.shape, jnp.bfloat16), pltpu.SemaphoreType.DMA],
             compiler_params=params_of(32),
         )(own_out, other_out, queries, pair, stale_pair[turn], fresh)
 
-    def finish(x, own, last, turn):
-        return pl.pallas_call(
-            finish_kernel, out_shape=(block_shape,) * 2, in_specs=[VMEM] * 5, out_specs=(VMEM,) * 2,
+    def finish(x, parts, turn):
+        return pl.pallas_call(
+            finish_kernel, out_shape=(block_shape,) * 2, in_specs=[VMEM] * 4, out_specs=(VMEM,) * 2,
             compiler_params=params_of(16),
-        )(params[turn], params[1 - turn], x, own, last)
+        )(params[turn], params[1 - turn], x, parts)
 
     outputs = [None, None]
     pairs = [None, None]
@@ -270,12 +224,11 @@
             x = upward(x, level - 1)
         normed = norm(x, 0)
         for turn in range(2):
-            groups, weights = gather(normed, level, turn)
-            queries, pair = project(groups, weights, turn)
+            blocks = across(jnp.broadcast_to(normed, (seq,) + normed.shape))
+            queries, pair = project(blocks, load(turn), turn)
             fresh = lax.ppermute(pair, AXES, swap)
             parts = attend(queries, pair, fresh, turn)
-            own, last = scatter(parts, level)
-            x, normed = finish(x, own, last, turn)
+            x, normed = finish(x, across(parts), turn)
             here = plane == level
             keep = lambda new, old: new if old is None else jnp.where(here, new, old)
             outputs[turn] = keep(x, outputs[turn])
@@ -291,28 +244,6 @@
         [jnp.where(core == 0, pairs[0], freshes[1]), jnp.where(core == 0, freshes[0], pairs[1])]
     )
     cache = cache.reshape(2, 2, seq, rows, channels)
-    spot = [0] * seq
-    for index, position in enumerate(ring):
-        spot[position] = index
-    spot = jnp.array(spot, jnp.int32)
-    steps = [0, 1]
-    for group in range(1, half):
-        steps += [-group, -group - 1] if group % 2 else [group, group + 1]
-    held = [0] * seq
-    for index, step in enumerate(steps):
-        held[step % seq] = index
-    held = jnp.array(held, jnp.int32)
-    me = spot[lax.axis_index("seq")]
-    cache = jnp.stack(
-        [
-            jnp.take(
-                cache[patch],
-                held[jnp.remainder((spot - me) * (1 - 2 * lax.rem(me + patch, 2)), seq)],
-                axis=1,
-            )
-            for patch in range(2)
-        ]
-    )
     cache = lax.all_to_all(cache, "seq", split_axis=2, concat_axis=4, tiled=True)
     cache = jnp.transpose(cache[:, :, 0], (0, 2, 1, 3))
     return block_output[None], cache[None]

time: 340 us -> 341 us (level)
  the two profiles are of different devices: /device:TPU:4 before, /device:TPU:0 now
where the time goes in v1:
time: 341 us; the launch traced here: 340 us
  blocking collectives  163 us (48%)
  waiting for transfers between devices  96.2 us (28%)
  starting transfers between devices  28.8 us (8%)
  Pallas kernels  25 us (7%)
  local copies, waits for them, and re-layouts  22.2 us (7%)
  other arithmetic  3.7 us (1%)
    all_to_all x5, blocking collectives, across(): lax.all_to_all(blocks, 'seq', split_axis=0, concat_axis=0, tiled=True)  163 us
    all_to_all x4, waiting for transfers between devices, across(): lax.all_to_all(blocks, 'seq', split_axis=0, concat_axis=0, tiled=True)  76.4 us
    all_to_all x4, starting transfers between devices, across(): lax.all_to_all(blocks, 'seq', split_axis=0, concat_axis=0, tiled=True)  19.1 us
    unnamed x77, local copies, waits for them, and re-layouts  17.3 us
    all_to_all x1, waiting for transfers between devices, body(): lax.all_to_all(cache, 'seq', split_axis=2, concat_axis=4, tiled=True)  10.6 us
    pallas_call x4, Pallas kernels, attend(): pl.pallas_call(functools.partial(attend_kernel, turn, head_size), out_sha...  9.31 us
    pallas_call x4, Pallas kernels, project(): pl.pallas_call(functools.partial(project_kernel, head_size), out_shape=(j...  8.69 us
  transfers between devices with their start and end apart: 15, of which 10 were waited for; matrix products, arithmetic and copies ran while one was open for 2% of the time, Pallas kernels for 3%

profile of v1, /device:TPU:0, one launch (start us, length us, event | category | flops | bytes accessed | tf_op | source)
XLA Modules:
  0.0 340.0 jit_solution(4731427260739393241)
XLA Ops:
  0.7 0.8 select_maximum_fusion
  2.0 0.9 collective-permute-done
  3.3 1.1 slice_bitcast_fusion.cache_ref
  6.2 1.2 broadcast_in_dim.18
  7.4 7.1 %all-to-all-start = ((bf16[8,24,3072]{2,1,0:T(8,128)(2,1)}), bf16[8,24,3072]{2,1,0:T(8,128)(2,1)}, u32[]{:S(2)}, u32[]{:S(2)}) async-start(bf16[8,24,3072]{2,1,0:T(8,128)(2,1)} %broadcast_in_dim.18), calls=%async_computation | async-start | bytes 2359296 | tf_op jit(solution)/shard_map/all_to_all | solution.py:143
  14.7 29.1 %all-to-all-done.blocks_ref = bf16[8,24,3072]{2,1,0:T(8,128)(2,1)} async-done(((bf16[8,24,3072]{2,1,0:T(8,128)(2,1)}), bf16[8,24,3072]{2,1,0:T(8,128)(2,1)}, u32[]{:S(2)}, u32[]{:S(2)}) %all-to-all-start) | async-done | bytes 1179680 | tf_op jit(solution)/shard_map/all_to_all | solution.py:143
  43.7 4.0 %all-to-all-start.1 = ((bf16[8,2,24,256]{3,2,1,0:T(8,128)(2,1)}), bf16[8,2,24,256]{3,2,1,0:T(8,128)(2,1)}, u32[]{:S(2)}, u32[]{:S(2)}) async-start(bf16[8,2,24,256]{3,2,1,0:T(8,128)(2,1)} %copy-done.20), calls=%async_computation.1 | async-start | bytes 393216 | tf_op jit(solution)/shard_map/all_to_all | solution.py:143
  47.8 2.3 copy-done.5
  50.4 3.9 %shard_map.98 = (bf16[192,256]{1,0:T(8,128)(2,1)S(1)}, bf16[2,192,256]{2,1,0:T(8,128)(2,1)}) custom-call(f32[2,128]{1,0:T(2,128)S(1)} %bitcast.41, bf16[3,3072,256]{2,1,0:T(8,128)(2,1)S(1)} %shard_map.96.weights_ref, bf16[8,24,3072]{2,1,0:T(8,128)(2,1)} %all-to-all-done.blocks_ref), custom_call_target="tpu_custom_call" | custom-call | tf_op jit(solution)/shard_map/pallas_call | solution.py:191
  55.0 1.4 collective-permute-start.3
  56.4 1.4 collective-permute-done.3.fresh_ref
  57.8 0.9 copy-done.29
  58.7 2.4 shard_map.99
  61.0 35.1 %all_to_all.60.parts_ref = bf16[8,24,3072]{2,1,0:T(8,128)(2,1)S(1)} all-to-all(bf16[8,24,3072]{2,1,0:T(8,128)(2,1)S(1)} %shard_map.99), channel_id=1, replica_groups=mesh['pipe'=4,'seq'=8] {'seq'}, dimensions={0} | all-to-all | bytes 2359296 | tf_op jit(solution)/shard_map/all_to_all | solution.py:143
  97.3 1.2 broadcast_in_dim.19
  98.5 4.3 %all-to-all-start.3 = ((bf16[8,24,3072]{2,1,0:T(8,128)(2,1)}), bf16[8,24,3072]{2,1,0:T(8,128)(2,1)}, u32[]{:S(2)}, u32[]{:S(2)}) async-start(bf16[8,24,3072]{2,1,0:T(8,128)(2,1)} %broadcast_in_dim.19), calls=%async_computation.3 | async-start | bytes 2359296 | tf_op jit(solution)/shard_map/all_to_all | solution.py:143
  102.8 2.3 copy-done.6
  105.2 2.3 shard_map.101.weights_ref
  107.5 2.2 copy-done.2
  109.7 21.1 %all-to-all-done.3.blocks_ref = bf16[8,24,3072]{2,1,0:T(8,128)(2,1)} async-done(((bf16[8,24,3072]{2,1,0:T(8,128)(2,1)}), bf16[8,24,3072]{2,1,0:T(8,128)(2,1)}, u32[]{:S(2)}, u32[]{:S(2)}) %all-to-all-start.3) | async-done | bytes 1179680 | tf_op jit(solution)/shard_map/all_to_all | solution.py:143
  130.8 2.3 copy-done.3
  133.1 2.4 shard_map.102
  135.7 1.4 collective-permute-done.5.fresh_ref
  137.1 2.3 shard_map.103
  140.1 32.5 %all_to_all.61.parts_ref = bf16[8,24,3072]{2,1,0:T(8,128)(2,1)S(1)} all-to-all(bf16[8,24,3072]{2,1,0:T(8,128)(2,1)S(1)} %shard_map.103), channel_id=1, replica_groups=mesh['pipe'=4,'seq'=8] {'seq'}, dimensions={0} | all-to-all | bytes 2359296 | tf_op jit(solution)/shard_map/all_to_all | solution.py:143
  172.6 1.2 shard_map.104
  173.8 3.4 %collective-permute-start.6 = (bf16[24,3072]{1,0:T(8,128)(2,1)S(1)}, bf16[24,3072]{1,0:T(8,128)(2,1)S(1)}, u32[]{:S(2)}, u32[]{:S(2)}) collective-permute-start(bf16[24,3072]{1,0:T(8,128)(2,1)S(1)} %get-tuple-element.32), channel_id=1, source_target_pairs={{0,16},{1,17},{2,18},{3,19},{4,20},{5,21},{6,22},{7,23},{8,24},{9,... | collective-permute-start | bytes 442376 | tf_op jit(solution)/shard_map/ppermute | solution.py:151
  177.2 2.6 collective-permute-done.6.x_ref
  180.3 31.2 %all_to_all.62.blocks_ref = bf16[8,24,3072]{2,1,0:T(8,128)(2,1)S(1)} all-to-all(bf16[8,24,3072]{2,1,0:T(8,128)(2,1)S(1)} %broadcast_in_dim.20), channel_id=1, replica_groups=mesh['pipe'=4,'seq'=8] {'seq'}, dimensions={0} | all-to-all | bytes 2359296 | tf_op jit(solution)/shard_map/all_to_all | solution.py:143
  211.5 1.2 shard_map.106
  212.8 1.4 collective-permute-done.7.fresh_ref
  214.2 2.3 shard_map.107
  216.5 32.2 %all_to_all.63.parts_ref = bf16[8,24,3072]{2,1,0:T(8,128)(2,1)S(1)} all-to-all(bf16[8,24,3072]{2,1,0:T(8,128)(2,1)S(1)} %shard_map.107), channel_id=1, replica_groups=mesh['pipe'=4,'seq'=8] {'seq'}, dimensions={0} | all-to-all | bytes 2359296 | tf_op jit(solution)/shard_map/all_to_all | solution.py:143
  250.0 31.8 %all_to_all.64.blocks_ref = bf16[8,24,3072]{2,1,0:T(8,128)(2,1)S(1)} all-to-all(bf16[8,24,3072]{2,1,0:T(8,128)(2,1)S(1)} %broadcast_in_dim.21), channel_id=1, replica_groups=mesh['pipe'=4,'seq'=8] {'seq'}, dimensions={0} | all-to-all | bytes 2359296 | tf_op jit(solution)/shard_map/all_to_all | solution.py:143
  281.9 1.2 shard_map.109
  283.1 1.4 collective-permute-done.8.fresh_ref
  284.6 2.3 shard_map.110
  286.9 1.0 copy-done.7
  289.3 3.7 %all-to-all-start.8 = ((bf16[8,24,3072]{2,1,0:T(8,128)(2,1)}), bf16[8,24,3072]{2,1,0:T(8,128)(2,1)S(1)}, u32[]{:S(2)}, u32[]{:S(2)}) async-start(bf16[8,24,3072]{2,1,0:T(8,128)(2,1)} %copy-done.7), calls=%async_computation.8 | async-start | bytes 2359296 | tf_op jit(solution)/shard_map/all_to_all | solution.py:143
  293.1 1.0 select_select_fusion
  294.1 1.0 select_select_fusion.1
  295.1 0.8 copy.17
  295.9 26.2 %all-to-all-done.8.parts_ref = bf16[8,24,3072]{2,1,0:T(8,128)(2,1)S(1)} async-done(((bf16[8,24,3072]{2,1,0:T(8,128)(2,1)}), bf16[8,24,3072]{2,1,0:T(8,128)(2,1)S(1)}, u32[]{:S(2)}, u32[]{:S(2)}) %all-to-all-start.8) | async-done | bytes 1179680 | tf_op jit(solution)/shard_map/all_to_all | solution.py:143
  322.1 3.6 %all-to-all-start.9 = ((bf16[2,2,8,24,256]{4,3,1,0,2:T(8,128)(2,1)}), bf16[2,2,8,24,256]{4,3,1,0,2:T(8,128)(2,1)S(1)}, u32[]{:S(2)}, u32[]{:S(2)}) async-start(bf16[2,2,8,24,256]{4,3,1,0,2:T(8,128)(2,1)} %copy.17), calls=%async_computation.9 | async-start | bytes 786432 | tf_op jit(solution)/shard_map/all_to_all | solution.py:247
  325.8 1.2 shard_map.111
  327.0 10.6 %all-to-all-done.9 = bf16[2,2,8,24,256]{4,3,1,0,2:T(8,128)(2,1)S(1)} async-done(((bf16[2,2,8,24,256]{4,3,1,0,2:T(8,128)(2,1)}), bf16[2,2,8,24,256]{4,3,1,0,2:T(8,128)(2,1)S(1)}, u32[]{:S(2)}, u32[]{:S(2)}) %all-to-all-start.9) | async-done | bytes 393248 | tf_op jit(solution)/shard_map/all_to_all | solution.py:247
  338.0 1.2 copy.16
  339.2 0.7 maximum_bitcast_fusion
  (102 shorter events, 9.6 us)
Async XLA Ops:
  0.6 4.9 %copy-start = (bf16[2,24,3072]{2,1,0:T(8,128)(2,1)S(1)}, bf16[2,24,3072]{2,1,0:T(8,128)(2,1)}, u32[]{:S(2)}) copy-start(bf16[2,24,3072]{2,1,0:T(8,128)(2,1)} %param.8) | copy-start | bytes 884740
  0.6 4.9 %copy-start.33 = (f32[1,2,128]{2,1,0:T(2,128)S(1)}, f32[1,2,128]{2,1,0:T(2,128)}, u32[]{:S(2)}) copy-start(f32[1,2,128]{2,1,0:T(2,128)} %param.12) | copy-start | bytes 3076
  0.7 4.9 %copy-start.30 = (f32[1,3072]{1,0:T(1,128)S(1)}, f32[1,3072]{1,0:T(1,128)}, u32[]{:S(2)}) copy-start(f32[1,3072]{1,0:T(1,128)} %param.11) | copy-start | bytes 36868
  0.7 4.9 %copy-start.31 = (f32[1,3072]{1,0:T(1,128)S(1)}, f32[1,3072]{1,0:T(1,128)}, u32[]{:S(2)}) copy-start(f32[1,3072]{1,0:T(1,128)} %param.10) | copy-start | bytes 36868
  0.7 4.9 %copy-start.32 = (f32[1,3072]{1,0:T(1,128)S(1)}, f32[1,3072]{1,0:T(1,128)}, u32[]{:S(2)}) copy-start(f32[1,3072]{1,0:T(1,128)} %param.9) | copy-start | bytes 36868
  1.5 1.4 collective-permute-start
  2.9 44.8 %collective-permute-start.2 = (bf16[3,3072,256]{2,1,0:T(8,128)(2,1)}, bf16[3,3072,256]{2,1,0:T(8,128)(2,1)}, u32[]{:S(2)}, u32[]{:S(2)}) collective-permute-start(bf16[3,3072,256]{2,1,0:T(8,128)(2,1)} %bitcast.38), channel_id=1, source_target_pairs={{0,8},{1,9},{2,10},{3,11},{4,12},{5,13},{6,14},{7,15},{8,0},{9,1},... | collective-permute-start | bytes 14155784 | tf_op jit(solution)/shard_map/ppermute | solution.py:159
  4.8 0.7 copy-start.20
  7.4 7.1 %copy-start.4 = (bf16[1,256,3072]{2,1,0:T(8,128)(2,1)S(1)}, bf16[1,256,3072]{2,1,0:T(8,128)(2,1)}, u32[]{:S(2)}) copy-start(bf16[1,256,3072]{2,1,0:T(8,128)(2,1)} %param.14) | copy-start | bytes 4718596
  7.4 36.3 %all-to-all-start = ((bf16[8,24,3072]{2,1,0:T(8,128)(2,1)}), bf16[8,24,3072]{2,1,0:T(8,128)(2,1)}, u32[]{:S(2)}, u32[]{:S(2)}) async-start(bf16[8,24,3072]{2,1,0:T(8,128)(2,1)} %broadcast_in_dim.18), calls=%async_computation | async-start | bytes 2359296 | tf_op jit(solution)/shard_map/all_to_all | solution.py:143
  14.5 41.9 %collective-permute-start.1 = (bf16[256,3072]{1,0:T(8,128)(2,1)S(1)}, bf16[256,3072]{1,0:T(8,128)(2,1)S(1)}, u32[]{:S(2)}, u32[]{:S(2)}) collective-permute-start(bf16[256,3072]{1,0:T(8,128)(2,1)S(1)} %bitcast.33), channel_id=1, source_target_pairs={{0,8},{1,9},{2,10},{3,11},{4,12},{5,13},{6,14},{7,15},{8,0},{9,1},... | collective-permute-start | bytes 4718600 | tf_op jit(solution)/shard_map/ppermute | solution.py:160
  43.7 12.7 %all-to-all-start.1 = ((bf16[8,2,24,256]{3,2,1,0:T(8,128)(2,1)}), bf16[8,2,24,256]{3,2,1,0:T(8,128)(2,1)}, u32[]{:S(2)}, u32[]{:S(2)}) async-start(bf16[8,2,24,256]{3,2,1,0:T(8,128)(2,1)} %copy-done.20), calls=%async_computation.1 | async-start | bytes 393216 | tf_op jit(solution)/shard_map/all_to_all | solution.py:143
  47.8 2.3 copy-start.5
  50.4 3.9 %copy-start.1 = (bf16[3,3072,256]{2,1,0:T(8,128)(2,1)}, bf16[3,3072,256]{2,1,0:T(8,128)(2,1)S(1)}, u32[]{:S(2)}) copy-start(bf16[3,3072,256]{2,1,0:T(8,128)(2,1)S(1)} %shard_map.96.weights_ref) | copy-start | bytes 14155780
  55.0 2.8 collective-permute-start.3
  57.8 0.9 copy-start.29
  61.0 35.1 %copy-start.9 = (bf16[24,3072]{1,0:T(8,128)(2,1)S(1)}, bf16[24,3072]{1,0:T(8,128)(2,1)}, u32[]{:S(2)}) copy-start(bf16[24,3072]{1,0:T(8,128)(2,1)} %copy-done.8) | copy-start | bytes 442372
  98.5 32.3 %all-to-all-start.3 = ((bf16[8,24,3072]{2,1,0:T(8,128)(2,1)}), bf16[8,24,3072]{2,1,0:T(8,128)(2,1)}, u32[]{:S(2)}, u32[]{:S(2)}) async-start(bf16[8,24,3072]{2,1,0:T(8,128)(2,1)} %broadcast_in_dim.19), calls=%async_computation.3 | async-start | bytes 2359296 | tf_op jit(solution)/shard_map/all_to_all | solution.py:143
  102.7 32.9 %collective-permute-start.4 = (bf16[8,2,24,256]{3,2,1,0:T(8,128)(2,1)}, bf16[8,2,24,256]{3,2,1,0:T(8,128)(2,1)}, u32[]{:S(2)}, u32[]{:S(2)}) collective-permute-start(bf16[8,2,24,256]{3,2,1,0:T(8,128)(2,1)} %all-to-all-done.1.stale_ref), channel_id=1, source_target_pairs={{0,8},{1,9},{2,10},{3,11},{4,12},{5,13},{6,14},{7,15},{8,0},{9,1},... | collective-permute-start | bytes 589832 | tf_op jit(solution)/shard_map/ppermute | solution.py:171
  102.8 2.3 copy-start.6
  107.5 2.2 copy-start.2
  130.8 2.3 copy-start.3
  135.6 1.5 collective-permute-start.5
  137.1 2.3 copy-start.12
  137.1 74.4 %slice-start = ((s8[4718592]{0:T(1024)(128)(4,1)}), s8[4194304]{0:T(1024)(128)(4,1)S(1)}, s32[]{:S(2)}) async-start(s8[4718592]{0:T(1024)(128)(4,1)} %bitcast.29), calls=%async_computation.10 | async-start | bytes 8388608
  139.4 0.7 copy-start.10
  140.1 32.5 %copy-start.22 = (bf16[24,3072]{1,0:T(8,128)(2,1)S(1)}, bf16[24,3072]{1,0:T(8,128)(2,1)}, u32[]{:S(2)}) copy-start(bf16[24,3072]{1,0:T(8,128)(2,1)} %copy-done.21) | copy-start | bytes 442372
  140.1 71.3 %slice-start.1 = ((s8[4718592]{0:T(1024)(128)(4,1)}), s8[524288]{0:T(1024)(128)(4,1)S(1)}, s32[]{:S(2)}) async-start(s8[4718592]{0:T(1024)(128)(4,1)} %bitcast.29), calls=%async_computation.11 | async-start | bytes 1048576
  173.8 37.7 %copy-start.26 = (bf16[24,3072]{1,0:T(8,128)(2,1)}, bf16[24,3072]{1,0:T(8,128)(2,1)S(1)}, u32[]{:S(2)}) copy-start(bf16[24,3072]{1,0:T(8,128)(2,1)S(1)} %get-tuple-element.32) | copy-start | bytes 442372
  173.8 6.1 %collective-permute-start.6 = (bf16[24,3072]{1,0:T(8,128)(2,1)S(1)}, bf16[24,3072]{1,0:T(8,128)(2,1)S(1)}, u32[]{:S(2)}, u32[]{:S(2)}) collective-permute-start(bf16[24,3072]{1,0:T(8,128)(2,1)S(1)} %get-tuple-element.32), channel_id=1, source_target_pairs={{0,16},{1,17},{2,18},{3,19},{4,20},{5,21},{6,22},{7,23},{8,24},{9,... | collective-permute-start | bytes 442376 | tf_op jit(solution)/shard_map/ppermute | solution.py:151
  211.5 70.4 %slice-start.2 = ((s8[4718592]{0:T(1024)(128)(4,1)}), s8[524288]{0:T(1024)(128)(4,1)S(1)}, s32[]{:S(2)}) async-start(s8[4718592]{0:T(1024)(128)(4,1)} %bitcast.31), calls=%async_computation.12 | async-start | bytes 1048576
  212.7 3.8 %copy-start.14 = (bf16[2,192,256]{2,1,0:T(8,128)(2,1)}, bf16[2,192,256]{2,1,0:T(8,128)(2,1)S(1)}, u32[]{:S(2)}) copy-start(bf16[2,192,256]{2,1,0:T(8,128)(2,1)S(1)} %get-tuple-element.34.kv_ref) | copy-start | bytes 589828
  212.7 1.5 collective-permute-start.7
  214.2 2.3 copy-start.16
  214.2 67.7 %slice-start.3 = ((s8[4718592]{0:T(1024)(128)(4,1)}), s8[4194304]{0:T(1024)(128)(4,1)S(1)}, s32[]{:S(2)}) async-start(s8[4718592]{0:T(1024)(128)(4,1)} %bitcast.31), calls=%async_computation.13 | async-start | bytes 8388608
  283.1 1.5 collective-permute-start.8
  286.9 1.0 copy-start.7
  288.6 0.7 copy-start.19
  289.3 3.7 %copy-start.11 = (bf16[2,192,256]{2,1,0:T(8,128)(2,1)S(1)}, bf16[2,192,256]{2,1,0:T(8,128)(2,1)}, u32[]{:S(2)}) copy-start(bf16[2,192,256]{2,1,0:T(8,128)(2,1)} %copy-done.10) | copy-start | bytes 589828
  289.3 3.8 %copy-start.17 = (bf16[2,192,256]{2,1,0:T(8,128)(2,1)S(1)}, bf16[2,192,256]{2,1,0:T(8,128)(2,1)}, u32[]{:S(2)}) copy-start(bf16[2,192,256]{2,1,0:T(8,128)(2,1)} %copy-done.16) | copy-start | bytes 589828
  289.3 4.7 %copy-start.13 = (bf16[2,192,256]{2,1,0:T(8,128)(2,1)S(1)}, bf16[2,192,256]{2,1,0:T(8,128)(2,1)}, u32[]{:S(2)}) copy-start(bf16[2,192,256]{2,1,0:T(8,128)(2,1)} %copy-done.12) | copy-start | bytes 589828
  289.3 4.8 %copy-start.15 = (bf16[2,192,256]{2,1,0:T(8,128)(2,1)S(1)}, bf16[2,192,256]{2,1,0:T(8,128)(2,1)}, u32[]{:S(2)}) copy-start(bf16[2,192,256]{2,1,0:T(8,128)(2,1)} %copy-done.14) | copy-start | bytes 589828
  289.3 32.8 %all-to-all-start.8 = ((bf16[8,24,3072]{2,1,0:T(8,128)(2,1)}), bf16[8,24,3072]{2,1,0:T(8,128)(2,1)S(1)}, u32[]{:S(2)}, u32[]{:S(2)}) async-start(bf16[8,24,3072]{2,1,0:T(8,128)(2,1)} %copy-done.7), calls=%async_computation.8 | async-start | bytes 2359296 | tf_op jit(solution)/shard_map/all_to_all | solution.py:143
  295.1 30.7 %copy-start.25 = (bf16[24,3072]{1,0:T(8,128)(2,1)S(1)}, bf16[24,3072]{1,0:T(8,128)(2,1)}, u32[]{:S(2)}) copy-start(bf16[24,3072]{1,0:T(8,128)(2,1)} %copy-done.24) | copy-start | bytes 442372
  295.9 31.0 %copy-start.23 = (bf16[24,3072]{1,0:T(8,128)(2,1)S(1)}, bf16[24,3072]{1,0:T(8,128)(2,1)}, u32[]{:S(2)}) copy-start(bf16[24,3072]{1,0:T(8,128)(2,1)} %copy-done.21) | copy-start | bytes 442372
  295.9 31.0 %copy-start.27 = (bf16[24,3072]{1,0:T(8,128)(2,1)S(1)}, bf16[24,3072]{1,0:T(8,128)(2,1)}, u32[]{:S(2)}) copy-start(bf16[24,3072]{1,0:T(8,128)(2,1)} %copy-done.26) | copy-start | bytes 442372
  322.1 15.5 %all-to-all-start.9 = ((bf16[2,2,8,24,256]{4,3,1,0,2:T(8,128)(2,1)}), bf16[2,2,8,24,256]{4,3,1,0,2:T(8,128)(2,1)S(1)}, u32[]{:S(2)}, u32[]{:S(2)}) async-start(bf16[2,2,8,24,256]{4,3,1,0,2:T(8,128)(2,1)} %copy.17), calls=%async_computation.9 | async-start | bytes 786432 | tf_op jit(solution)/shard_map/all_to_all | solution.py:247
  327.0 12.2 %collective-permute-start.9 = (bf16[24,3072]{1,0:T(8,128)(2,1)S(1)}, bf16[24,3072]{1,0:T(8,128)(2,1)S(1)}, u32[]{:S(2)}, u32[]{:S(2)}) collective-permute-start(bf16[24,3072]{1,0:T(8,128)(2,1)S(1)} %get-tuple-element.42), channel_id=1, source_target_pairs={{0,8},{1,9},{2,10},{3,11},{4,12},{5,13},{6,14},{7,15},{8,0},{9,1},... | collective-permute-start | bytes 442376 | tf_op jit(solution)/shard_map/ppermute | solution.py:239
  (5 other events, 3.3 us)

commit v2 on v1

v2 whole, which is shorter than its diff:
```python
import functools
import math

import jax
import jax.numpy as jnp
from jax import lax
from jax.experimental import pallas as pl
from jax.experimental.pallas import tpu as pltpu
from jax.sharding import PartitionSpec as P

AXES = ("pipe", "seq")
VMEM = pl.BlockSpec(memory_space=pltpu.VMEM)
ANY = pl.BlockSpec(memory_space=pl.ANY)


def normalise(values, params_ref):
    centered = values - jnp.mean(values, axis=-1, keepdims=True)
    spread = jnp.mean(centered * centered, axis=-1, keepdims=True)
    return (
        centered * lax.rsqrt(spread + 1e-06) * (1.0 + params_ref[1:2, :]) + params_ref[0:1, :]
    ).astype(jnp.bfloat16)


def norm_kernel(params_ref, x_ref, out_ref):
    block = normalise(x_ref[...].astype(jnp.float32), params_ref)
    for shard in range(out_ref.shape[0]):
        out_ref[shard] = block


def pack_kernel(params_ref, x_ref, cache_ref, out_ref):
    count, _, total = out_ref.shape
    width = x_ref.shape[1]
    channels = (total - width) // 2
    block = normalise(x_ref[...].astype(jnp.float32), params_ref)
    sides = [cache_ref[:, kind, :] for kind in range(2)]
    for shard in range(count):
        out_ref[shard, :, :width] = block
        for kind in range(2):
            begin = width + kind * channels
            out_ref[shard, :, begin : begin + channels] = sides[kind][
                :, shard * channels : (shard + 1) * channels
            ]


def start_copies(turn, own_ref, other_ref, buffer, sems):
    mine = lax.rem(lax.axis_index("pipe"), 2) == turn
    parts = buffer.shape[0]

    @pl.when(mine)
    def _():
        for part in range(parts):
            pltpu.make_async_copy(own_ref.at[part], buffer.at[part], sems.at[part]).start()

    @pl.when(jnp.logical_not(mine))
    def _():
        for part in range(parts):
            pltpu.make_async_copy(other_ref.at[part], buffer.at[part], sems.at[part]).start()


def project_kernel(turn, head_size, gain_ref, own_ref, other_ref, blocks_ref, q_ref, kv_ref, weights, sems):
    start_copies(turn, own_ref, other_ref, weights, sems)
    count, rows, _ = blocks_ref.shape
    width = weights.shape[1]
    tokens = (
        blocks_ref[:, :, :width].astype(jnp.float32).reshape(count * rows, width).astype(jnp.bfloat16)
    )
    channels = weights.shape[2]
    for part in (0, 1, 2):
        pltpu.make_async_copy(own_ref.at[part], weights.at[part], sems.at[part]).wait()
        projected = jnp.dot(tokens, weights[part], preferred_element_type=jnp.float32)
        if part == 2:
            kv_ref[1] = projected.astype(jnp.bfloat16)
            continue
        for start in range(0, channels, head_size):
            head = projected[:, start : start + head_size]
            square = jnp.mean(head * head, axis=-1, keepdims=True)
            head = (head * lax.rsqrt(square + 1e-06) * gain_ref[part : part + 1, :]).astype(
                jnp.bfloat16
            )
            if part == 0:
                q_ref[:, start : start + head_size] = head
            else:
                kv_ref[0, :, start : start + head_size] = head


def attention(head_size, q_ref, kv_ref, far_ref):
    factor = 1.0 / math.sqrt(head_size)
    tokens, channels = q_ref.shape
    heads = []
    across = (((1,), (1,)), ((), ()))

    def far_of(kind, start):
        if far_ref.shape[2] == channels:
            return far_ref[kind, :, start : start + head_size]
        begin = kind * channels + start
        blocks = far_ref[:, :, begin : begin + head_size].astype(jnp.float32)
        return blocks.reshape(tokens, head_size).astype(jnp.bfloat16)

    for start in range(0, channels, head_size):
        cut = slice(start, start + head_size)
        query = q_ref[:, cut]
        near = lax.dot_general(query, kv_ref[0, :, cut], across, preferred_element_type=jnp.float32)
        far = lax.dot_general(query, far_of(0, start), across, preferred_element_type=jnp.float32)
        near = jnp.exp(near * factor)
        far = jnp.exp(far * factor)
        total = jnp.sum(near, axis=-1, keepdims=True) + jnp.sum(far, axis=-1, keepdims=True)
        near = (near / total).astype(jnp.bfloat16)
        far = (far / total).astype(jnp.bfloat16)
        mixed = jnp.dot(near, kv_ref[1, :, cut], preferred_element_type=jnp.float32)
        mixed = mixed + jnp.dot(far, far_of(1, start), preferred_element_type=jnp.float32)
        heads.append(mixed.astype(jnp.bfloat16))
    return jnp.concatenate(heads, axis=1)


def put_cache(caches, out_ref, offset):
    count, rows, _ = out_ref.shape
    channels = caches[0].shape[2] if caches else 0
    for patch, cache in enumerate(caches):
        for kind in range(2):
            begin = offset + (2 * patch + kind) * channels
            out_ref[:, :, begin : begin + channels] = (
                cache[kind].astype(jnp.float32).reshape(count, rows, channels).astype(jnp.bfloat16)
            )


def cache_kernel(*refs):
    put_cache(refs[:-1], refs[-1], 0)


def partial_kernel(turn, head_size, own_ref, other_ref, q_ref, kv_ref, far_ref, *refs):
    extra, (parts_ref, weights, sems) = refs[:-3], refs[-3:]
    start_copies(turn, own_ref, other_ref, weights, sems)
    count, rows, _ = parts_ref.shape
    width = weights.shape[2]
    put_cache(extra, parts_ref, width)
    attended = attention(head_size, q_ref, kv_ref, far_ref)
    pltpu.make_async_copy(own_ref.at[0], weights.at[0], sems.at[0]).wait()
    update = jnp.dot(attended, weights[0], preferred_element_type=jnp.float32)
    parts_ref[:, :, :width] = update.reshape(count, rows, width).astype(jnp.bfloat16)


def finish_kernel(params_ref, next_ref, x_ref, parts_ref, out_ref, *normed):
    width = x_ref.shape[1]
    update = jnp.sum(parts_ref[:, :, :width].astype(jnp.float32), axis=0)
    result = (x_ref[...].astype(jnp.float32) + params_ref[2:3, :] * update).astype(jnp.bfloat16)
    out_ref[...] = result
    for blocks_ref in normed:
        block = normalise(result.astype(jnp.float32), next_ref)
        for shard in range(blocks_ref.shape[0]):
            blocks_ref[shard] = block


def blank_kernel(*refs):
    pass


def params_of(limit):
    return pltpu.CompilerParams(vmem_limit_bytes=limit << 20)


def body(hidden, mod_shift, mod_scale, mod_gate, norm_gain, input_proj, output_proj, stale_cache):
    sections = lax.axis_size("pipe")
    planes = sections // 2
    seq = lax.axis_size("seq")
    pipe = lax.axis_index("pipe")
    core = lax.rem(pipe, 2)
    plane = pipe // 2
    rows, width = hidden.shape[1:]
    head_size = norm_gain.shape[2]
    channels = input_proj.shape[3]
    tokens = rows * seq
    bf16 = lambda *shape: jax.ShapeDtypeStruct(shape, jnp.bfloat16)

    place = lambda row, position: row * seq + position

    def swap(value):
        pairs = [(place(row, s), place(row ^ 1, s)) for row in range(sections) for s in range(seq)]
        return lax.ppermute(value, AXES, pairs)

    def upward(value, level, side):
        row = 2 * level + side
        return lax.ppermute(value, AXES, [(place(row, s), place(row + 2, s)) for s in range(seq)])

    def across(blocks):
        return lax.all_to_all(blocks, "seq", split_axis=0, concat_axis=0, tiled=True)

    def blank(*shapes):
        return pl.pallas_call(blank_kernel, out_shape=shapes, out_specs=(ANY,) * len(shapes))()

    gains = jnp.pad(norm_gain[0].reshape(1, -1), ((0, 0), (0, width - 2 * head_size)))
    own_params = jnp.concatenate([mod_shift, mod_scale, mod_gate, gains], axis=0)
    own_in = jnp.transpose(input_proj[0], (1, 0, 2))
    own_out = output_proj
    x = lax.dynamic_index_in_dim(hidden, core, 0, keepdims=False)
    packed = pl.pallas_call(
        pack_kernel, out_shape=bf16(seq, rows, width + 2 * channels),
        in_specs=[VMEM] * 3, out_specs=VMEM, compiler_params=params_of(16),
    )(own_params, x, stale_cache[0, 1])

    other_params = swap(own_params)
    own_in, own_out, other_params, packed = lax.optimization_barrier(
        (own_in, own_out, other_params, packed)
    )
    other_in = swap(own_in)
    other_out = swap(own_out)
    params = [jnp.where(core == turn, own_params, other_params) for turn in range(2)]
    gain_rows = [p[3, : 2 * head_size].reshape(2, head_size) for p in params]
    blocks_shape = bf16(seq, rows, width)

    def norm(x, turn):
        return pl.pallas_call(
            norm_kernel, out_shape=blocks_shape, in_specs=[VMEM] * 2, out_specs=VMEM,
            compiler_params=params_of(16),
        )(params[turn], x)

    def project(blocks, turn):
        return pl.pallas_call(
            functools.partial(project_kernel, turn, head_size),
            out_shape=(bf16(tokens, channels), bf16(2, tokens, channels)),
            in_specs=[VMEM, ANY, ANY, VMEM],
            out_specs=(VMEM, VMEM),
            scratch_shapes=[
                pltpu.VMEM(own_in.shape, jnp.bfloat16), pltpu.SemaphoreType.DMA((3,)),
            ],
            compiler_params=params_of(56),
        )(gain_rows[turn], own_in, other_in, blocks)

    def partial(blocks, far, turn, extra=lambda pair: ()):
        queries, pair = project(blocks, turn)
        caches = extra(pair)
        parts = pl.pallas_call(
            functools.partial(partial_kernel, turn, head_size),
            out_shape=bf16(seq, rows, width + 2 * channels * len(caches)),
            in_specs=[ANY, ANY] + [VMEM] * (3 + len(caches)),
            out_specs=VMEM,
            scratch_shapes=[
                pltpu.VMEM(own_out.shape, jnp.bfloat16), pltpu.SemaphoreType.DMA((1,)),
            ],
            compiler_params=params_of(32),
        )(own_out, other_out, queries, pair, far, *caches)
        return parts, pair

    def finish(x, parts, turn, onward):
        shapes = (bf16(rows, width),) + (blocks_shape,) * onward
        return pl.pallas_call(
            finish_kernel, out_shape=shapes, in_specs=[VMEM] * 4, out_specs=(VMEM,) * len(shapes),
            compiler_params=params_of(16),
        )(params[turn], params[1 - turn], x, parts)

    early = core == 0
    either = lambda on_early, on_late: lax.cond(early, on_early, on_late)

    def first_early():
        value = across(packed)
        return value, value[:, :, width:]

    def first_late():
        return blank(bf16(*packed.shape))[0], across(packed[:, :, width:])

    received, stale = either(first_early, first_late)
    stale_pair = [stale, swap(stale)]
    pair = None
    blocks_out, sources = {}, {}
    for layer in range(sections):
        turn, level = layer % 2, layer // 2
        crossing = layer > 0 and turn == 0

        def early_scatter():
            parts, fresh = partial(received, stale_pair[turn], turn)
            return parts, fresh, x

        def late_gather():
            old = blank(bf16(2, tokens, channels))[0] if pair is None else pair
            if layer == 0 or crossing:
                return norm(x, turn), old, x
            result, normed = finish(x, received, 1 - turn, 1)
            return normed, old, result

        if crossing:
            x = either(lambda: x, lambda: finish(x, received, 1 - turn, 0)[0])
            blocks_out[layer - 1, 1] = x
            x = jnp.where(early, x, upward(x, level - 1, 1))
        payload, pair, x = either(early_scatter, late_gather)
        if layer > 0 and not crossing:
            blocks_out[layer - 1, 1] = x
        sources[layer, 0] = pair
        got = swap(pair)
        sources[layer, 2] = got
        received = across(payload)
        if layer == sections - 1:
            break

        crossing = turn == 1

        def early_gather():
            if crossing:
                return norm(x, 1 - turn), pair, x
            result, normed = finish(x, received, turn, 1)
            return normed, pair, result

        def late_scatter():
            parts, fresh = partial(received, got, turn)
            return parts, fresh, x

        if crossing:
            x = either(lambda: finish(x, received, turn, 0)[0], lambda: x)
            blocks_out[layer, 0] = x
            x = jnp.where(early, upward(x, level, 0), x)
        payload, pair, x = either(early_gather, late_scatter)
        if not crossing:
            blocks_out[layer, 0] = x
        sources[layer, 1] = pair
        if crossing:
            active = pipe == jnp.where(early, 2 * level + 2, 2 * level + 1)
            received = lax.cond(active, across, lambda _: blank(blocks_shape)[0], payload)
        else:
            received = across(payload)

    def by_plane(values):
        chosen = values[0]
        for level in range(1, planes):
            chosen = jnp.where(plane == level, values[level], chosen)
        return chosen

    last = sections - 1
    first_cache = by_plane(
        [jnp.where(early, sources[2 * m, 0], sources[2 * m + 1, 2]) for m in range(planes)]
    )
    second_cache = by_plane(
        [
            jnp.where(early, sources[2 * m + 1, 2], sources[2 * m + 1, int(m < planes - 1)])
            for m in range(planes)
        ]
    )

    def last_early():
        result = finish(x, received, last % 2, 0)[0]
        packed = pl.pallas_call(
            cache_kernel, out_shape=bf16(seq, rows, 4 * channels),
            in_specs=[VMEM] * 2, out_specs=VMEM, compiler_params=params_of(16),
        )(first_cache, second_cache)
        return result, across(packed)

    def last_late():
        extra = lambda fresh: (first_cache, jnp.where(plane == planes - 1, fresh, second_cache))
        parts, _ = partial(received, got, last % 2, extra)
        parts = across(parts)
        return finish(x, parts, last % 2, 0)[0], parts[:, :, width:]

    x, cache = either(last_early, last_late)
    blocks_out[last, 0] = blocks_out[last, 1] = x
    mine = by_plane(
        [jnp.where(early, blocks_out[2 * m, 0], blocks_out[2 * m + 1, 1]) for m in range(planes)]
    )
    theirs = swap(
        by_plane(
            [jnp.where(early, blocks_out[2 * m + 1, 0], blocks_out[2 * m, 1]) for m in range(planes)]
        )
    )
    block_output = jnp.stack([jnp.where(early, mine, theirs), jnp.where(early, theirs, mine)])
    cache = cache.reshape(seq, rows, 2, 2, channels)
    cache = jnp.transpose(cache, (2, 1, 3, 0, 4)).reshape(2, rows, 2, seq * channels)
    return block_output[None], cache[None]


def solution(mesh):
    in_specs = (
        P(None, "seq", None),
        P("pipe", None),
        P("pipe", None),
        P("pipe", None),
        P("pipe", None, None),
        P("pipe", None, None, "seq"),
        P("pipe", "seq", None),
        P("pipe", None, "seq", None, None),
    )
    out_specs = (P("pipe", None, "seq", None), P("pipe", None, "seq", None, None))
    return jax.shard_map(body, mesh=mesh, in_specs=in_specs, out_specs=out_specs, check_vma=False)
```

time: 341 us -> 295 us (0.87)
  blocking collectives: 163 us -> 60.8 us
  starting transfers between devices: 28.8 us -> 55.5 us
  waiting for transfers between devices: 96.2 us -> 111 us
  Pallas kernels: 25 us -> 37 us
    all_to_all x5 -> x2, blocking collectives: 163 us -> 60.8 us  [across(): lax.all_to_all(blocks, 'seq', split_axis=0, concat_axis=0, tiled=True)]
    all_to_all x4 -> x6, waiting for transfers between devices: 76.4 us -> 107 us  [across(): lax.all_to_all(blocks, 'seq', split_axis=0, concat_axis=0, tiled=True)]
    ppermute x10 -> x11, starting transfers between devices: 6.15 us -> 29.9 us  [the longest x9 25.2 us: swap(): return lax.ppermute(value, AXES, pairs)]
    pallas_call x17 -> x16, Pallas kernels: 25 us -> 37 us  [the longest x4 18.6 us: project(): pl.pallas_call(functools.partial(project_kernel, turn, head_size), out_sh...]
    all_to_all x1 -> x0, waiting for transfers between devices: 10.6 us -> none  [body(): lax.all_to_all(cache, 'seq', split_axis=2, concat_axis=4, tiled=True)]
    unnamed x77 -> x34, local copies, waits for them, and re-layouts: 17.3 us -> 8.01 us
    cond x0 -> x22, local copies, waits for them, and re-layouts: none -> 8.43 us
    all_to_all x4 -> x6, starting transfers between devices: 19.1 us -> 25.5 us  [across(): lax.all_to_all(blocks, 'seq', split_axis=0, concat_axis=0, tiled=True)]
  transfers between devices with their start and end apart: 15 -> 17, of which waited for: 10 -> 8; matrix products, arithmetic and copies ran while one was open for 2% -> 2% of each run, Pallas kernels for 3% -> 1%
where the time goes in v2:
time: 295 us; the launch traced here: 293 us
  waiting for transfers between devices  111 us (38%)
  blocking collectives  60.8 us (21%)
  starting transfers between devices  55.5 us (19%)
  Pallas kernels  37 us (13%)
  local copies, waits for them, and re-layouts  21.2 us (7%)
  other arithmetic  6.6 us (2%)
    all_to_all x6, waiting for transfers between devices, across(): lax.all_to_all(blocks, 'seq', split_axis=0, concat_axis=0, tiled=True)  107 us
    all_to_all x2, blocking collectives, across(): lax.all_to_all(blocks, 'seq', split_axis=0, concat_axis=0, tiled=True)  60.8 us
    all_to_all x6, starting transfers between devices, across(): lax.all_to_all(blocks, 'seq', split_axis=0, concat_axis=0, tiled=True)  25.5 us
    ppermute x9, starting transfers between devices, swap(): return lax.ppermute(value, AXES, pairs)  25.2 us
    pallas_call x4, Pallas kernels, project(): pl.pallas_call(functools.partial(project_kernel, turn, head_size), out_sh...  18.6 us
    pallas_call x4, Pallas kernels, partial(): pl.pallas_call(functools.partial(partial_kernel, turn, head_size), out_sh...  10.4 us
    cond x22, local copies, waits for them, and re-layouts  8.43 us
    unnamed x34, local copies, waits for them, and re-layouts  8.01 us
  transfers between devices with their start and end apart: 17, of which 8 were waited for; matrix products, arithmetic and copies ran while one was open for 2% of the time, Pallas kernels for 1%

profile of v2, /device:TPU:0, one launch (start us, length us, event | category | flops | bytes accessed | tf_op | source)
XLA Modules:
  0.0 293.4 jit_solution(1653835277629536409)
XLA Ops:
  2.0 1.2 slice_bitcast_fusion.cache_ref
  3.3 1.9 shard_map.95
  5.7 30.4 %conditional.12 = (bf16[8,24,3584]{2,1,0:T(8,128)(2,1)}, bf16[8,24,512]{2,1,0:T(8,128)(2,1)S(1)}) conditional(s32[]{:T(128)} %convert_element_type.6, bf16[8,24,3584]{2,1,0:T(8,128)(2,1)} %shard_map.95, bf16[8,24,3584]{2,1,0:T(8,128)(2,1)} %shard_map.95), branch_computations={%region_0.1_spmd, %region_1.2_spmd} | conditional | bytes 3145744 | solution.py:251
  5.7 29.5 %all_to_all.50 = bf16[8,24,3584]{2,1,0:T(8,128)(2,1)} all-to-all(bf16[8,24,3584]{2,1,0:T(8,128)(2,1)} %param.1), channel_id=1, replica_groups=mesh['pipe'=4,'seq'=8] {'seq'}, dimensions={0} | all-to-all | bytes 2752512 | tf_op jit(solution)/shard_map/cond/branch_1_fun/all_to_all | solution.py:185
  36.8 8.9 %conditional.13 = (bf16[8,24,3072]{2,1,0:T(8,128)(2,1)S(1)}, bf16[2,192,256]{2,1,0:T(8,128)(2,1)}) conditional(s32[]{:T(128)} %convert_element_type.6, (f32[4,3072]{1,0:T(4,128)S(1)}, bf16[24,3072]{1,0:T(8,128)(2,1)S(1)}) %tuple.104, (f32[2,128]{1,0:T(2,128)S(1)}, bf16[3,3072,256]{2,1,0:T(8,128)(2,1)}, bf16[3,3072,256]{2,1,0:T(8,128)(2,1)}, ...), branch_computations={%region_2.3_spmd, %region_3.4_spmd} | conditional | bytes 1179720 | solution.py:251
  36.8 5.7 %branch_1_fun.14 = (bf16[192,256]{1,0:T(8,128)(2,1)}, bf16[2,192,256]{2,1,0:T(8,128)(2,1)}) custom-call(f32[2,128]{1,0:T(2,128)S(1)} %get-tuple-element.235.gain_ref, bf16[3,3072,256]{2,1,0:T(8,128)(2,1)} %get-tuple-element.236.own_ref, bf16[3,3072,256]{2,1,0:T(8,128)(2,1)} %get-tuple-element.237.other_ref, bf16[8,24,3584]{2,1,0:T(8,128)(2,1)} %get-tuple-element.238.blocks_ref), custom_call_target="tpu_custom_call" | custom-call | tf_op jit(solution)/shard_map/cond/branch_1_fun/pallas_call | solution.py:217
  43.4 2.3 branch_1_fun.15
  45.7 1.1 copy-done.11
  46.8 6.4 %all-to-all-start.5 = ((bf16[8,24,3072]{2,1,0:T(8,128)(2,1)}), bf16[8,24,3072]{2,1,0:T(8,128)(2,1)S(1)}, u32[]{:S(2)}, u32[]{:S(2)}) async-start(bf16[8,24,3072]{2,1,0:T(8,128)(2,1)} %copy-done.11), calls=%async_computation.5 | async-start | bytes 2359296 | tf_op jit(solution)/shard_map/all_to_all | solution.py:185
  53.2 17.8 %all-to-all-done.5 = bf16[8,24,3072]{2,1,0:T(8,128)(2,1)S(1)} async-done(((bf16[8,24,3072]{2,1,0:T(8,128)(2,1)}), bf16[8,24,3072]{2,1,0:T(8,128)(2,1)S(1)}, u32[]{:S(2)}, u32[]{:S(2)}) %all-to-all-start.5) | async-done | bytes 1179680 | tf_op jit(solution)/shard_map/all_to_all | solution.py:185
  71.1 3.3 %conditional.14 = (bf16[8,24,3072]{2,1,0:T(8,128)(2,1)}, bf16[2,192,256]{2,1,0:T(8,128)(2,1)}, bf16[24,3072]{1,0:T(8,128)(2,1)S(1)}) conditional(s32[]{:T(128)} %convert_element_type.6, (f32[2,128]{1,0:T(2,128)S(1)}, bf16[3,3072,256]{2,1,0:T(8,128)(2,1)}, bf16[3,3072,256]{2,1,0:T(8,128)(2,1)}, bf16[8,24,3072]{2,1,0:T(8,128)(2,1)S(1)}, ...), branch_computations={%region_4.5_spmd, %region_5.6_spmd} | conditional | bytes 688152 | solution.py:251
  71.1 1.7 branch_1_fun.16
  72.8 1.6 copy.25
  74.4 3.6 %all-to-all-start.6 = ((bf16[8,24,3072]{2,1,0:T(8,128)(2,1)}), bf16[8,24,3072]{2,1,0:T(8,128)(2,1)S(1)}, u32[]{:S(2)}, u32[]{:S(2)}) async-start(bf16[8,24,3072]{2,1,0:T(8,128)(2,1)} %get-tuple-element.400), calls=%async_computation.6 | async-start | bytes 2359296 | tf_op jit(solution)/shard_map/all_to_all | solution.py:185
  78.0 21.4 %all-to-all-done.6 = bf16[8,24,3072]{2,1,0:T(8,128)(2,1)S(1)} async-done(((bf16[8,24,3072]{2,1,0:T(8,128)(2,1)}), bf16[8,24,3072]{2,1,0:T(8,128)(2,1)S(1)}, u32[]{:S(2)}, u32[]{:S(2)}) %all-to-all-start.6) | async-done | bytes 1179680 | tf_op jit(solution)/shard_map/all_to_all | solution.py:185
  99.4 8.2 %conditional.15 = (bf16[8,24,3072]{2,1,0:T(8,128)(2,1)S(1)}, bf16[2,192,256]{2,1,0:T(8,128)(2,1)}, bf16[24,3072]{1,0:T(8,128)(2,1)S(1)}) conditional(s32[]{:T(128)} %convert_element_type.6, (f32[4,3072]{1,0:T(4,128)S(1)}, f32[4,3072]{1,0:T(4,128)S(1)}, bf16[24,3072]{1,0:T(8,128)(2,1)S(1)}, bf16[8,24,3072]{2,1,0:T(8,128)(2,1)S(1)}, ...), branch_computations={%region_6.7_spmd, %region_7.8_spmd} | conditional | bytes 688180 | solution.py:251
  99.4 4.3 %branch_1_fun.17 = (bf16[192,256]{1,0:T(8,128)(2,1)}, bf16[2,192,256]{2,1,0:T(8,128)(2,1)}) custom-call(f32[2,128]{1,0:T(2,128)S(1)} %get-tuple-element.268.gain_ref, bf16[3,3072,256]{2,1,0:T(8,128)(2,1)} %get-tuple-element.269.own_ref, bf16[3,3072,256]{2,1,0:T(8,128)(2,1)} %get-tuple-element.270.other_ref, ...), custom_call_target="tpu_custom_call" | custom-call | tf_op jit(solution)/shard_map/cond/branch_1_fun/pallas_call | solution.py:217
  104.6 3.0 %branch_1_fun.18 = bf16[8,24,3072]{2,1,0:T(8,128)(2,1)S(1)} custom-call(bf16[1,256,3072]{2,1,0:T(8,128)(2,1)S(1)} %get-tuple-element.266.own_ref, bf16[1,256,3072]{2,1,0:T(8,128)(2,1)} %get-tuple-element.267.other_ref, bf16[192,256]{1,0:T(8,128)(2,1)S(1)} %copy-done.3, bf16[2,192,256]{2,1,0:T(8,128)(2,1)} %get-tuple-element.441.kv_ref, ...), custom_call_target="tpu_custom_call" | custom-call | tf_op jit(solution)/shard_map/cond/branch_1_fun/pallas_call | solution.py:231
  107.6 1.1 copy-done.26
  108.7 3.6 %all-to-all-start.7 = ((bf16[8,24,3072]{2,1,0:T(8,128)(2,1)}), bf16[8,24,3072]{2,1,0:T(8,128)(2,1)S(1)}, u32[]{:S(2)}, u32[]{:S(2)}) async-start(bf16[8,24,3072]{2,1,0:T(8,128)(2,1)} %copy-done.26), calls=%async_computation.7 | async-start | bytes 2359296 | tf_op jit(solution)/shard_map/all_to_all | solution.py:185
  112.4 18.2 %all-to-all-done.7 = bf16[8,24,3072]{2,1,0:T(8,128)(2,1)S(1)} async-done(((bf16[8,24,3072]{2,1,0:T(8,128)(2,1)}), bf16[8,24,3072]{2,1,0:T(8,128)(2,1)S(1)}, u32[]{:S(2)}, u32[]{:S(2)}) %all-to-all-start.7) | async-done | bytes 1179680 | tf_op jit(solution)/shard_map/all_to_all | solution.py:185
  131.4 4.1 %collective-permute-start.5 = (bf16[24,3072]{1,0:T(8,128)(2,1)}, bf16[24,3072]{1,0:T(8,128)(2,1)}, u32[]{:S(2)}, u32[]{:S(2)}) collective-permute-start(bf16[24,3072]{1,0:T(8,128)(2,1)} %get-tuple-element.467), channel_id=1, source_target_pairs={{0,16},{1,17},{2,18},{3,19},{4,20},{5,21},{6,22},{7,23}} | collective-permute-start | bytes 442376 | tf_op jit(solution)/shard_map/ppermute | solution.py:182
  135.5 2.3 collective-permute-done.5
  139.4 1.3 conditional.17
  144.5 7.4 %conditional.20 = (bf16[8,24,3072]{2,1,0:T(8,128)(2,1)S(1)}, bf16[2,192,256]{2,1,0:T(8,128)(2,1)}) conditional(s32[]{:T(128)} %convert_element_type.6, (f32[4,3072]{1,0:T(4,128)S(1)}, bf16[24,3072]{1,0:T(8,128)(2,1)S(1)}, bf16[2,192,256]{2,1,0:T(8,128)(2,1)}) %tuple.169, (f32[2,128]{1,0:T(2,128)S(1)}, bf16[3,3072,256]{2,1,0:T(8,128)(2,1)}, ...), branch_computations={%region_16.17_spmd, %region_17.18_spmd} | conditional | bytes 1179720 | solution.py:251
  144.5 4.3 %branch_1_fun.21 = (bf16[192,256]{1,0:T(8,128)(2,1)}, bf16[2,192,256]{2,1,0:T(8,128)(2,1)}) custom-call(f32[2,128]{1,0:T(2,128)S(1)} %get-tuple-element.301.gain_ref, bf16[3,3072,256]{2,1,0:T(8,128)(2,1)} %get-tuple-element.302.own_ref, bf16[3,3072,256]{2,1,0:T(8,128)(2,1)} %get-tuple-element.303.other_ref, ...), custom_call_target="tpu_custom_call" | custom-call | tf_op jit(solution)/shard_map/cond/branch_1_fun/pallas_call | solution.py:217
  149.8 2.2 branch_1_fun.22
  152.0 1.1 copy-done.12
  153.1 3.6 %all-to-all-start.8 = ((bf16[8,24,3072]{2,1,0:T(8,128)(2,1)}), bf16[8,24,3072]{2,1,0:T(8,128)(2,1)S(1)}, u32[]{:S(2)}, u32[]{:S(2)}) async-start(bf16[8,24,3072]{2,1,0:T(8,128)(2,1)} %copy-done.12), calls=%async_computation.8 | async-start | bytes 2359296 | tf_op jit(solution)/shard_map/all_to_all | solution.py:185
  156.6 6.2 %collective-permute-start.8 = (bf16[2,192,256]{2,1,0:T(8,128)(2,1)}, bf16[2,192,256]{2,1,0:T(8,128)(2,1)}, u32[]{:S(2)}, u32[]{:S(2)}) collective-permute-start(bf16[2,192,256]{2,1,0:T(8,128)(2,1)} %get-tuple-element.408), channel_id=1, source_target_pairs={{0,8},{1,9},{2,10},{3,11},{4,12},{5,13},{6,14},{7,15},{8,0},{9,1},... | collective-permute-start | bytes 589832 | tf_op jit(solution)/shard_map/ppermute | solution.py:178
  162.8 21.1 %all-to-all-done.8 = bf16[8,24,3072]{2,1,0:T(8,128)(2,1)S(1)} async-done(((bf16[8,24,3072]{2,1,0:T(8,128)(2,1)}), bf16[8,24,3072]{2,1,0:T(8,128)(2,1)S(1)}, u32[]{:S(2)}, u32[]{:S(2)}) %all-to-all-start.8) | async-done | bytes 1179680 | tf_op jit(solution)/shard_map/all_to_all | solution.py:185
  183.9 2.2 conditional.21
  184.5 1.6 copy.51
  186.1 31.4 %all_to_all.53 = bf16[8,24,3072]{2,1,0:T(8,128)(2,1)S(1)} all-to-all(bf16[8,24,3072]{2,1,0:T(8,128)(2,1)S(1)} %get-tuple-element.410), channel_id=1, replica_groups=mesh['pipe'=4,'seq'=8] {'seq'}, dimensions={0} | all-to-all | bytes 2359296 | tf_op jit(solution)/shard_map/all_to_all | solution.py:185
  217.5 8.2 %conditional.22 = (bf16[8,24,3072]{2,1,0:T(8,128)(2,1)S(1)}, bf16[2,192,256]{2,1,0:T(8,128)(2,1)}, bf16[24,3072]{1,0:T(8,128)(2,1)S(1)}) conditional(s32[]{:T(128)} %convert_element_type.6, (f32[4,3072]{1,0:T(4,128)S(1)}, f32[4,3072]{1,0:T(4,128)S(1)}, bf16[24,3072]{1,0:T(8,128)(2,1)S(1)}, bf16[8,24,3072]{2,1,0:T(8,128)(2,1)S(1)}, ...), branch_computations={%region_20.21_spmd, %region_21.22_spmd} | conditional | bytes 688180 | solution.py:251
  217.5 4.3 %branch_1_fun.24 = (bf16[192,256]{1,0:T(8,128)(2,1)}, bf16[2,192,256]{2,1,0:T(8,128)(2,1)}) custom-call(f32[2,128]{1,0:T(2,128)S(1)} %get-tuple-element.334.gain_ref, bf16[3,3072,256]{2,1,0:T(8,128)(2,1)} %get-tuple-element.335.own_ref, bf16[3,3072,256]{2,1,0:T(8,128)(2,1)} %get-tuple-element.336.other_ref, ...), custom_call_target="tpu_custom_call" | custom-call | tf_op jit(solution)/shard_map/cond/branch_1_fun/pallas_call | solution.py:217
  222.7 3.0 %branch_1_fun.25 = bf16[8,24,3072]{2,1,0:T(8,128)(2,1)S(1)} custom-call(bf16[1,256,3072]{2,1,0:T(8,128)(2,1)S(1)} %get-tuple-element.332.own_ref, bf16[1,256,3072]{2,1,0:T(8,128)(2,1)} %get-tuple-element.333.other_ref, bf16[192,256]{1,0:T(8,128)(2,1)S(1)} %copy-done.4, bf16[2,192,256]{2,1,0:T(8,128)(2,1)} %get-tuple-element.461.kv_ref, ...), custom_call_target="tpu_custom_call" | custom-call | tf_op jit(solution)/shard_map/cond/branch_1_fun/pallas_call | solution.py:231
  225.7 1.1 copy-done.27
  227.4 4.4 %all-to-all-start.10 = ((bf16[8,24,3072]{2,1,0:T(8,128)(2,1)}), bf16[8,24,3072]{2,1,0:T(8,128)(2,1)S(1)}, u32[]{:S(2)}, u32[]{:S(2)}) async-start(bf16[8,24,3072]{2,1,0:T(8,128)(2,1)} %copy-done.27), calls=%async_computation.10 | async-start | bytes 2359296 | tf_op jit(solution)/shard_map/all_to_all | solution.py:185
  231.8 1.8 collective-permute-done.9
  233.6 2.0 select_select_fusion
  235.6 20.2 %all-to-all-done.10 = bf16[8,24,3072]{2,1,0:T(8,128)(2,1)S(1)} async-done(((bf16[8,24,3072]{2,1,0:T(8,128)(2,1)}), bf16[8,24,3072]{2,1,0:T(8,128)(2,1)S(1)}, u32[]{:S(2)}, u32[]{:S(2)}) %all-to-all-start.10) | async-done | bytes 1179680 | tf_op jit(solution)/shard_map/all_to_all | solution.py:185
  255.8 15.3 %conditional.23 = (bf16[24,3072]{1,0:T(8,128)(2,1)}, bf16[8,24,1024]{2,1,0:T(8,128)(2,1)}) conditional(s32[]{:T(128)} %convert_element_type.6, (f32[2,128]{1,0:T(2,128)S(1)}, bf16[3,3072,256]{2,1,0:T(8,128)(2,1)}, bf16[3,3072,256]{2,1,0:T(8,128)(2,1)}, bf16[8,24,3072]{2,1,0:T(8,128)(2,1)S(1)}, s32[]{:T(128)}, ...), branch_computations={%region_22.23_spmd, %region_23.24_spmd} | conditional | flops 98305 | bytes 7864486 | solution.py:251
  255.8 1.8 branch_1_fun.27
  257.6 4.1 %all-to-all-start.3 = ((bf16[8,24,1024]{2,1,0:T(8,128)(2,1)}), bf16[8,24,1024]{2,1,0:T(8,128)(2,1)}, u32[]{:S(2)}, u32[]{:S(2)}) async-start(bf16[8,24,1024]{2,1,0:T(8,128)(2,1)} %branch_1_fun.27), calls=%async_computation.3 | async-start | bytes 786432 | tf_op jit(solution)/shard_map/cond/branch_1_fun/all_to_all | solution.py:185
  262.6 8.5 %all-to-all-done.3 = bf16[8,24,1024]{2,1,0:T(8,128)(2,1)} async-done(((bf16[8,24,1024]{2,1,0:T(8,128)(2,1)}), bf16[8,24,1024]{2,1,0:T(8,128)(2,1)}, u32[]{:S(2)}, u32[]{:S(2)}) %all-to-all-start.3) | async-done | bytes 393248 | tf_op jit(solution)/shard_map/cond/branch_1_fun/all_to_all | solution.py:185
  272.1 17.8 %collective-permute-start.10 = (bf16[24,3072]{1,0:T(8,128)(2,1)S(1)}, bf16[24,3072]{1,0:T(8,128)(2,1)S(1)}, u32[]{:S(2)}, u32[]{:S(2)}) collective-permute-start(bf16[24,3072]{1,0:T(8,128)(2,1)S(1)} %select_select_fusion.2), channel_id=1, source_target_pairs={{0,8},{1,9},{2,10},{3,11},{4,12},{5,13},{6,14},{7,15},{8,0},{9,1},... | collective-permute-start | bytes 442376 | tf_op jit(solution)/shard_map/ppermute | solution.py:178
  289.9 1.3 reshape.7
  (89 shorter events, 21.5 us)
Async XLA Ops:
  0.6 2.6 copy-start
  1.5 3.6 %collective-permute-start = (f32[4,3072]{1,0:T(4,128)S(1)}, f32[4,3072]{1,0:T(4,128)S(1)}, u32[]{:S(2)}, u32[]{:S(2)}) collective-permute-start(f32[4,3072]{1,0:T(4,128)S(1)} %select_maximum_fusion.params_ref), channel_id=1, source_target_pairs={{0,8},{1,9},{2,10},{3,11},{4,12},{5,13},{6,14},{7,15},{8,0},{9,1},... | collective-permute-start | bytes 147464 | tf_op jit(solution)/shard_map/ppermute | solution.py:178
  2.0 3.2 %copy-start.10 = (bf16[1,256,3072]{2,1,0:T(8,128)(2,1)S(1)}, bf16[1,256,3072]{2,1,0:T(8,128)(2,1)}, u32[]{:S(2)}) copy-start(bf16[1,256,3072]{2,1,0:T(8,128)(2,1)} %param.38) | copy-start | bytes 4718596
  2.0 3.6 %copy-start.28 = (f32[1,3072]{1,0:T(1,128)S(1)}, f32[1,3072]{1,0:T(1,128)}, u32[]{:S(2)}) copy-start(f32[1,3072]{1,0:T(1,128)} %param.35) | copy-start | bytes 36868
  2.0 3.6 %copy-start.29 = (f32[1,3072]{1,0:T(1,128)S(1)}, f32[1,3072]{1,0:T(1,128)}, u32[]{:S(2)}) copy-start(f32[1,3072]{1,0:T(1,128)} %param.34) | copy-start | bytes 36868
  2.0 3.6 %copy-start.30 = (f32[1,3072]{1,0:T(1,128)S(1)}, f32[1,3072]{1,0:T(1,128)}, u32[]{:S(2)}) copy-start(f32[1,3072]{1,0:T(1,128)} %param.33) | copy-start | bytes 36868
  2.0 3.6 %copy-start.31 = (f32[1,2,128]{2,1,0:T(2,128)S(1)}, f32[1,2,128]{2,1,0:T(2,128)}, u32[]{:S(2)}) copy-start(f32[1,2,128]{2,1,0:T(2,128)} %param.36) | copy-start | bytes 3076
  5.1 31.1 %collective-permute-start.1 = (bf16[3,3072,256]{2,1,0:T(8,128)(2,1)}, bf16[3,3072,256]{2,1,0:T(8,128)(2,1)}, u32[]{:S(2)}, u32[]{:S(2)}) collective-permute-start(bf16[3,3072,256]{2,1,0:T(8,128)(2,1)} %bitcast.21), channel_id=1, source_target_pairs={{0,8},{1,9},{2,10},{3,11},{4,12},{5,13},{6,14},{7,15},{8,0},{9,1},... | collective-permute-start | bytes 14155784 | tf_op jit(solution)/shard_map/ppermute | solution.py:178
  5.2 31.0 %collective-permute-start.2 = (bf16[1,256,3072]{2,1,0:T(8,128)(2,1)S(1)}, bf16[1,256,3072]{2,1,0:T(8,128)(2,1)}, u32[]{:S(2)}, u32[]{:S(2)}) collective-permute-start(bf16[1,256,3072]{2,1,0:T(8,128)(2,1)S(1)} %copy-done.10), channel_id=1, source_target_pairs={{0,8},{1,9},{2,10},{3,11},{4,12},{5,13},{6,14},{7,15},{8,0},{9,1},... | collective-permute-start | bytes 4718600 | tf_op jit(solution)/shard_map/ppermute | solution.py:178
  36.1 0.7 copy-start.15
  36.8 5.7 %copy-start.16 = (bf16[8,24,512]{2,1,0:T(8,128)(2,1)}, bf16[8,24,512]{2,1,0:T(8,128)(2,1)S(1)}, u32[]{:S(2)}) copy-start(bf16[8,24,512]{2,1,0:T(8,128)(2,1)S(1)} %get-tuple-element.241.far_ref) | copy-start | bytes 589828 | tf_op jit(solution)/shard_map/cond
  42.5 0.9 copy-start.5
  45.7 1.1 copy-start.11
  46.8 24.2 %all-to-all-start.5 = ((bf16[8,24,3072]{2,1,0:T(8,128)(2,1)}), bf16[8,24,3072]{2,1,0:T(8,128)(2,1)S(1)}, u32[]{:S(2)}, u32[]{:S(2)}) async-start(bf16[8,24,3072]{2,1,0:T(8,128)(2,1)} %copy-done.11), calls=%async_computation.5 | async-start | bytes 2359296 | tf_op jit(solution)/shard_map/all_to_all | solution.py:185
  53.2 17.9 %collective-permute-start.3 = (bf16[2,192,256]{2,1,0:T(8,128)(2,1)}, bf16[2,192,256]{2,1,0:T(8,128)(2,1)}, u32[]{:S(2)}, u32[]{:S(2)}) collective-permute-start(bf16[2,192,256]{2,1,0:T(8,128)(2,1)} %get-tuple-element.398), channel_id=1, source_target_pairs={{0,8},{1,9},{2,10},{3,11},{4,12},{5,13},{6,14},{7,15},{8,0},{9,1},... | collective-permute-start | bytes 589832 | tf_op jit(solution)/shard_map/ppermute | solution.py:178
  74.4 25.0 %all-to-all-start.6 = ((bf16[8,24,3072]{2,1,0:T(8,128)(2,1)}), bf16[8,24,3072]{2,1,0:T(8,128)(2,1)S(1)}, u32[]{:S(2)}, u32[]{:S(2)}) async-start(bf16[8,24,3072]{2,1,0:T(8,128)(2,1)} %get-tuple-element.400), calls=%async_computation.6 | async-start | bytes 2359296 | tf_op jit(solution)/shard_map/all_to_all | solution.py:185
  77.9 21.5 %collective-permute-start.4 = (bf16[8,24,512]{2,1,0:T(8,128)(2,1)}, bf16[8,24,512]{2,1,0:T(8,128)(2,1)}, u32[]{:S(2)}, u32[]{:S(2)}) collective-permute-start(bf16[8,24,512]{2,1,0:T(8,128)(2,1)} %copy-done.15), channel_id=1, source_target_pairs={{0,8},{1,9},{2,10},{3,11},{4,12},{5,13},{6,14},{7,15},{8,0},{9,1},... | collective-permute-start | bytes 589832 | tf_op jit(solution)/shard_map/ppermute | solution.py:178
  103.7 0.9 copy-start.3
  107.6 1.1 copy-start.26
  108.7 21.8 %copy-start.22 = (bf16[24,3072]{1,0:T(8,128)(2,1)}, bf16[24,3072]{1,0:T(8,128)(2,1)S(1)}, u32[]{:S(2)}) copy-start(bf16[24,3072]{1,0:T(8,128)(2,1)S(1)} %get-tuple-element.402) | copy-start | bytes 442372
  108.7 21.8 %all-to-all-start.7 = ((bf16[8,24,3072]{2,1,0:T(8,128)(2,1)}), bf16[8,24,3072]{2,1,0:T(8,128)(2,1)S(1)}, u32[]{:S(2)}, u32[]{:S(2)}) async-start(bf16[8,24,3072]{2,1,0:T(8,128)(2,1)} %copy-done.26), calls=%async_computation.7 | async-start | bytes 2359296 | tf_op jit(solution)/shard_map/all_to_all | solution.py:185
  112.3 23.2 %collective-permute-start.6 = (bf16[2,192,256]{2,1,0:T(8,128)(2,1)}, bf16[2,192,256]{2,1,0:T(8,128)(2,1)}, u32[]{:S(2)}, u32[]{:S(2)}) collective-permute-start(bf16[2,192,256]{2,1,0:T(8,128)(2,1)} %get-tuple-element.404), channel_id=1, source_target_pairs={{0,8},{1,9},{2,10},{3,11},{4,12},{5,13},{6,14},{7,15},{8,0},{9,1},... | collective-permute-start | bytes 589832 | tf_op jit(solution)/shard_map/ppermute | solution.py:178
  131.4 6.4 %collective-permute-start.5 = (bf16[24,3072]{1,0:T(8,128)(2,1)}, bf16[24,3072]{1,0:T(8,128)(2,1)}, u32[]{:S(2)}, u32[]{:S(2)}) collective-permute-start(bf16[24,3072]{1,0:T(8,128)(2,1)} %get-tuple-element.467), channel_id=1, source_target_pairs={{0,16},{1,17},{2,18},{3,19},{4,20},{5,21},{6,22},{7,23}} | collective-permute-start | bytes 442376 | tf_op jit(solution)/shard_map/ppermute | solution.py:182
  138.7 0.7 copy-start.13
  140.6 0.7 copy-start.19
  141.3 0.9 copy-start.14
  142.9 0.7 collective-permute-start.7
  144.5 4.3 %copy-start.17 = (bf16[8,24,512]{2,1,0:T(8,128)(2,1)S(1)}, bf16[8,24,512]{2,1,0:T(8,128)(2,1)}, u32[]{:S(2)}) copy-start(bf16[8,24,512]{2,1,0:T(8,128)(2,1)} %get-tuple-element.307.far_ref) | copy-start | bytes 589828 | tf_op jit(solution)/shard_map/cond
  148.9 0.9 copy-start.8
  151.9 1.1 copy-start.12
  153.1 30.8 %all-to-all-start.8 = ((bf16[8,24,3072]{2,1,0:T(8,128)(2,1)}), bf16[8,24,3072]{2,1,0:T(8,128)(2,1)S(1)}, u32[]{:S(2)}, u32[]{:S(2)}) async-start(bf16[8,24,3072]{2,1,0:T(8,128)(2,1)} %copy-done.12), calls=%async_computation.8 | async-start | bytes 2359296 | tf_op jit(solution)/shard_map/all_to_all | solution.py:185
  156.6 27.3 %collective-permute-start.8 = (bf16[2,192,256]{2,1,0:T(8,128)(2,1)}, bf16[2,192,256]{2,1,0:T(8,128)(2,1)}, u32[]{:S(2)}, u32[]{:S(2)}) collective-permute-start(bf16[2,192,256]{2,1,0:T(8,128)(2,1)} %get-tuple-element.408), channel_id=1, source_target_pairs={{0,8},{1,9},{2,10},{3,11},{4,12},{5,13},{6,14},{7,15},{8,0},{9,1},... | collective-permute-start | bytes 589832 | tf_op jit(solution)/shard_map/ppermute | solution.py:178
  221.8 0.9 copy-start.4
  225.7 1.1 copy-start.27
  226.8 0.7 copy-start.23
  227.4 28.3 %all-to-all-start.10 = ((bf16[8,24,3072]{2,1,0:T(8,128)(2,1)}), bf16[8,24,3072]{2,1,0:T(8,128)(2,1)S(1)}, u32[]{:S(2)}, u32[]{:S(2)}) async-start(bf16[8,24,3072]{2,1,0:T(8,128)(2,1)} %copy-done.27), calls=%async_computation.10 | async-start | bytes 2359296 | tf_op jit(solution)/shard_map/all_to_all | solution.py:185
  231.8 1.8 collective-permute-start.9
  255.8 6.0 %copy-start.25 = (bf16[24,3072]{1,0:T(8,128)(2,1)S(1)}, bf16[24,3072]{1,0:T(8,128)(2,1)}, u32[]{:S(2)}) copy-start(bf16[24,3072]{1,0:T(8,128)(2,1)} %get-tuple-element.359.x_ref) | copy-start | bytes 442372 | tf_op jit(solution)/shard_map/cond
  257.6 13.5 %all-to-all-start.3 = ((bf16[8,24,1024]{2,1,0:T(8,128)(2,1)}), bf16[8,24,1024]{2,1,0:T(8,128)(2,1)}, u32[]{:S(2)}, u32[]{:S(2)}) async-start(bf16[8,24,1024]{2,1,0:T(8,128)(2,1)} %branch_1_fun.27), calls=%async_computation.3 | async-start | bytes 786432 | tf_op jit(solution)/shard_map/cond/branch_1_fun/all_to_all | solution.py:185
  272.1 20.4 %collective-permute-start.10 = (bf16[24,3072]{1,0:T(8,128)(2,1)S(1)}, bf16[24,3072]{1,0:T(8,128)(2,1)S(1)}, u32[]{:S(2)}, u32[]{:S(2)}) collective-permute-start(bf16[24,3072]{1,0:T(8,128)(2,1)S(1)} %select_select_fusion.2), channel_id=1, source_target_pairs={{0,8},{1,9},{2,10},{3,11},{4,12},{5,13},{6,14},{7,15},{8,0},{9,1},... | collective-permute-start | bytes 442376 | tf_op jit(solution)/shard_map/ppermute | solution.py:178
  289.9 2.6 copy-start.21

commit v3 on v2

v3 whole, which is shorter than its diff:
```python
import functools
import math

import jax
import jax.numpy as jnp
from jax import lax
from jax.experimental import pallas as pl
from jax.experimental.pallas import tpu as pltpu
from jax.sharding import PartitionSpec as P

AXES = ("pipe", "seq")
VMEM = pl.BlockSpec(memory_space=pltpu.VMEM)
ANY = pl.BlockSpec(memory_space=pl.ANY)
HBM = pl.BlockSpec(memory_space=pltpu.HBM)


def normalise(values, params_ref):
    centered = values - jnp.mean(values, axis=-1, keepdims=True)
    spread = jnp.mean(centered * centered, axis=-1, keepdims=True)
    return (
        centered * lax.rsqrt(spread + 1e-06) * (1.0 + params_ref[1:2, :]) + params_ref[0:1, :]
    ).astype(jnp.bfloat16)


def spread_block(block, buffer, out_ref, sems):
    width = buffer.shape[1]
    buffer[...] = block
    copies = [
        pltpu.make_async_copy(buffer, out_ref.at[shard, :, :width], sems.at[shard])
        for shard in range(out_ref.shape[0])
    ]
    for copy in copies:
        copy.start()
    return copies


def norm_kernel(params_ref, x_ref, out_ref, buffer, sems):
    block = normalise(x_ref[...].astype(jnp.float32), params_ref)
    for copy in spread_block(block, buffer, out_ref, sems):
        copy.wait()


def pack_kernel(params_ref, x_ref, cache_ref, out_ref, buffer, sems, sides, sem):
    count, _, total = sides.shape
    width = x_ref.shape[1]
    channels = total // 2
    block = normalise(x_ref[...].astype(jnp.float32), params_ref)
    copies = spread_block(block, buffer, out_ref, sems)
    for kind in range(2):
        rows = cache_ref[:, kind, :]
        for shard in range(count):
            sides[shard, :, kind * channels : (kind + 1) * channels] = rows[
                :, shard * channels : (shard + 1) * channels
            ]
    copies.append(pltpu.make_async_copy(sides, out_ref.at[:, :, width:], sem))
    copies[-1].start()
    for copy in copies:
        copy.wait()


def attention(head_size, q_ref, kv_ref, far_ref):
    factor = 1.0 / math.sqrt(head_size)
    tokens, channels = q_ref.shape
    heads = []
    across = (((1,), (1,)), ((), ()))

    def far_of(kind, start):
        if far_ref.shape[2] == channels:
            return far_ref[kind, :, start : start + head_size]
        begin = kind * channels + start
        blocks = far_ref[:, :, begin : begin + head_size].astype(jnp.float32)
        return blocks.reshape(tokens, head_size).astype(jnp.bfloat16)

    for start in range(0, channels, head_size):
        cut = slice(start, start + head_size)
        query = q_ref[:, cut]
        near = lax.dot_general(query, kv_ref[0, :, cut], across, preferred_element_type=jnp.float32)
        far = lax.dot_general(query, far_of(0, start), across, preferred_element_type=jnp.float32)
        near = jnp.exp(near * factor)
        far = jnp.exp(far * factor)
        total = jnp.sum(near, axis=-1, keepdims=True) + jnp.sum(far, axis=-1, keepdims=True)
        near = (near / total).astype(jnp.bfloat16)
        far = (far / total).astype(jnp.bfloat16)
        mixed = jnp.dot(near, kv_ref[1, :, cut], preferred_element_type=jnp.float32)
        mixed = mixed + jnp.dot(far, far_of(1, start), preferred_element_type=jnp.float32)
        heads.append(mixed.astype(jnp.bfloat16))
    return jnp.concatenate(heads, axis=1)


def put_cache(caches, out_ref, offset):
    count, rows, _ = out_ref.shape
    channels = caches[0].shape[2]
    for patch, cache in enumerate(caches):
        for kind in range(2):
            begin = offset + (2 * patch + kind) * channels
            out_ref[:, :, begin : begin + channels] = (
                cache[kind].astype(jnp.float32).reshape(count, rows, channels).astype(jnp.bfloat16)
            )


def cache_kernel(*refs):
    put_cache(refs[:-1], refs[-1], 0)


def block_kernel(
    turn, head_size, planes, gain_ref, own_in, other_in, own_out, other_out, blocks_ref, far_ref, *refs
):
    caches, refs = refs[:-10], refs[-10:]
    parts_ref, kv_ref, blocks, w_in, w_out, parts, q_ref, in_sems, sems, part_sems = refs
    count, rows, width = blocks.shape
    channels = w_out.shape[0]
    pieces = in_sems.shape[1]
    depth = width // pieces
    mine = lax.rem(lax.axis_index("pipe"), 2) == turn

    def weight_copies(source_in, source_out):
        for part in (1, 2, 0):
            for piece in range(pieces):
                cut = pl.ds(piece * depth, depth)
                pltpu.make_async_copy(
                    source_in.at[part, cut], w_in.at[part, cut], in_sems.at[part, piece]
                ).start()
        pltpu.make_async_copy(source_out.at[0], w_out, sems.at[1]).start()

    fetch = pltpu.make_async_copy(blocks_ref.at[:, :, :width], blocks, sems.at[0])
    fetch.start()

    @pl.when(mine)
    def _():
        weight_copies(own_in, own_out)

    @pl.when(jnp.logical_not(mine))
    def _():
        weight_copies(other_in, other_out)

    fetch.wait()
    tokens = blocks[...].astype(jnp.float32).reshape(count * rows, width).astype(jnp.bfloat16)
    for part in (1, 2, 0):
        for piece in range(pieces):
            cut = pl.ds(piece * depth, depth)
            pltpu.make_async_copy(
                own_in.at[part, cut], w_in.at[part, cut], in_sems.at[part, piece]
            ).wait()
        projected = jnp.dot(tokens, w_in[part], preferred_element_type=jnp.float32)
        if part == 2:
            kv_ref[1] = projected.astype(jnp.bfloat16)
            continue
        for start in range(0, channels, head_size):
            head = projected[:, start : start + head_size]
            square = jnp.mean(head * head, axis=-1, keepdims=True)
            head = (head * lax.rsqrt(square + 1e-06) * gain_ref[part : part + 1, :]).astype(
                jnp.bfloat16
            )
            if part == 0:
                q_ref[:, start : start + head_size] = head
            else:
                kv_ref[0, :, start : start + head_size] = head

    sent = []

    def send(begin, size, sem):
        cut = pl.ds(begin, size)
        sent.append(
            pltpu.make_async_copy(parts.at[:, :, cut], parts_ref.at[:, :, cut], part_sems.at[sem])
        )
        sent[-1].start()

    steps = part_sems.shape[0] - 1
    if caches:
        last = lax.axis_index("pipe") // 2 == planes - 1
        first, second = caches
        put_cache((first, jnp.where(last, kv_ref[...], second[...])), parts, width)
        send(width, 4 * channels, steps)
    attended = attention(head_size, q_ref, kv_ref, far_ref)
    pltpu.make_async_copy(own_out.at[0], w_out, sems.at[1]).wait()
    tile = width // steps
    for step in range(steps):
        cut = slice(step * tile, (step + 1) * tile)
        update = jnp.dot(attended, w_out[:, cut], preferred_element_type=jnp.float32)
        parts[:, :, cut] = update.reshape(count, rows, tile).astype(jnp.bfloat16)
        send(step * tile, tile, step)
    for copy in sent:
        copy.wait()


def finish_kernel(params_ref, next_ref, x_ref, parts_ref, out_ref, *rest):
    width = x_ref.shape[1]
    update = jnp.sum(parts_ref[:, :, :width].astype(jnp.float32), axis=0)
    result = (x_ref[...].astype(jnp.float32) + params_ref[2:3, :] * update).astype(jnp.bfloat16)
    out_ref[...] = result
    if rest:
        blocks_ref, buffer, sems = rest
        block = normalise(result.astype(jnp.float32), next_ref)
        for copy in spread_block(block, buffer, blocks_ref, sems):
            copy.wait()


def blank_kernel(*refs):
    pass


def params_of(limit):
    return pltpu.CompilerParams(vmem_limit_bytes=limit << 20)


def body(hidden, mod_shift, mod_scale, mod_gate, norm_gain, input_proj, output_proj, stale_cache):
    sections = lax.axis_size("pipe")
    planes = sections // 2
    seq = lax.axis_size("seq")
    pipe = lax.axis_index("pipe")
    core = lax.rem(pipe, 2)
    plane = pipe // 2
    rows, width = hidden.shape[1:]
    head_size = norm_gain.shape[2]
    channels = input_proj.shape[3]
    tokens = rows * seq
    bf16 = lambda *shape: jax.ShapeDtypeStruct(shape, jnp.bfloat16)

    place = lambda row, position: row * seq + position

    def swap(value):
        pairs = [(place(row, s), place(row ^ 1, s)) for row in range(sections) for s in range(seq)]
        return lax.ppermute(value, AXES, pairs)

    def upward(value, level, side):
        row = 2 * level + side
        return lax.ppermute(value, AXES, [(place(row, s), place(row + 2, s)) for s in range(seq)])

    def across(blocks):
        return lax.all_to_all(blocks, "seq", split_axis=0, concat_axis=0, tiled=True)

    def blank(*shapes):
        return pl.pallas_call(blank_kernel, out_shape=shapes, out_specs=(ANY,) * len(shapes))()

    gains = jnp.pad(norm_gain[0].reshape(1, -1), ((0, 0), (0, width - 2 * head_size)))
    own_params = jnp.concatenate([mod_shift, mod_scale, mod_gate, gains], axis=0)
    own_in = jnp.transpose(input_proj[0], (1, 0, 2))
    own_out = output_proj
    x = lax.dynamic_index_in_dim(hidden, core, 0, keepdims=False)
    spreading = [pltpu.VMEM((rows, width), jnp.bfloat16), pltpu.SemaphoreType.DMA((seq,))]
    packed = pl.pallas_call(
        pack_kernel, out_shape=bf16(seq, rows, width + 2 * channels),
        in_specs=[VMEM] * 3, out_specs=HBM,
        scratch_shapes=spreading + [
            pltpu.VMEM((seq, rows, 2 * channels), jnp.bfloat16), pltpu.SemaphoreType.DMA,
        ],
        compiler_params=params_of(16),
    )(own_params, x, stale_cache[0, 1])

    other_params = swap(own_params)
    own_in, own_out, other_params, packed = lax.optimization_barrier(
        (own_in, own_out, other_params, packed)
    )
    other_in = swap(own_in)
    other_out = swap(own_out)
    params = [jnp.where(core == turn, own_params, other_params) for turn in range(2)]
    gain_rows = [p[3, : 2 * head_size].reshape(2, head_size) for p in params]
    blocks_shape = bf16(seq, rows, width)

    def norm(x, turn):
        return pl.pallas_call(
            norm_kernel, out_shape=blocks_shape, in_specs=[VMEM] * 2, out_specs=HBM,
            scratch_shapes=spreading, compiler_params=params_of(16),
        )(params[turn], x)

    def block(blocks, far, turn, caches=()):
        total = width + 2 * channels * len(caches)
        return pl.pallas_call(
            functools.partial(block_kernel, turn, head_size, planes),
            out_shape=(bf16(seq, rows, total), bf16(2, tokens, channels)),
            in_specs=[VMEM] + [HBM] * 4 + [ANY] + [VMEM] * (1 + len(caches)),
            out_specs=(HBM, VMEM),
            scratch_shapes=[
                pltpu.VMEM((seq, rows, width), jnp.bfloat16),
                pltpu.VMEM(own_in.shape, jnp.bfloat16),
                pltpu.VMEM(own_out.shape[1:], jnp.bfloat16),
                pltpu.VMEM((seq, rows, total), jnp.bfloat16),
                pltpu.VMEM((tokens, channels), jnp.bfloat16),
                pltpu.SemaphoreType.DMA((3, 2)),
                pltpu.SemaphoreType.DMA((2,)),
                pltpu.SemaphoreType.DMA((5,)),
            ],
            compiler_params=params_of(32),
        )(gain_rows[turn], own_in, other_in, own_out, other_out, blocks, far, *caches)

    def finish(x, parts, turn, onward):
        shapes = (bf16(rows, width),) + (blocks_shape,) * onward
        return pl.pallas_call(
            finish_kernel, out_shape=shapes, in_specs=[VMEM] * 4,
            out_specs=(VMEM,) + (HBM,) * onward,
            scratch_shapes=spreading * onward, compiler_params=params_of(16),
        )(params[turn], params[1 - turn], x, parts)

    early = core == 0
    either = lambda on_early, on_late: lax.cond(early, on_early, on_late)

    def first_early():
        value = across(packed)
        return value, value[:, :, width:]

    def first_late():
        return blank(bf16(*packed.shape))[0], across(packed[:, :, width:])

    received, stale = either(first_early, first_late)
    stale_pair = [stale, swap(stale)]
    pair_shape, block_shape = bf16(2, tokens, channels), bf16(rows, width)
    late_pair = None
    early_x, late_x = x, x
    blocks_out, sources = {}, {}
    for layer in range(sections):
        turn, level = layer % 2, layer // 2
        crossing = layer > 0 and turn == 0

        def early_scatter():
            parts, fresh = block(received, stale_pair[turn], turn)
            return parts, fresh, blank(block_shape)[0]

        def late_gather():
            old = late_pair if turn else blank(pair_shape)[0]
            if turn == 0:
                return norm(late_x, turn), old, blank(block_shape)[0]
            result, normed = finish(late_x, received, 1 - turn, 1)
            return normed, old, result

        if crossing:
            late_x = either(
                lambda: blank(block_shape)[0], lambda: finish(late_x, received, 1 - turn, 0)[0]
            )
            blocks_out[layer - 1, 1] = late_x
            late_x = upward(late_x, level - 1, 1)
        payload, pair, result = either(early_scatter, late_gather)
        if turn:
            late_x = blocks_out[layer - 1, 1] = result
        sources[layer, 0] = pair
        got = swap(pair)
        sources[layer, 2] = got
        received = across(payload)
        if layer == sections - 1:
            break

        crossing = turn == 1

        def early_gather():
            if crossing:
                return norm(early_x, 1 - turn), blank(pair_shape)[0], blank(block_shape)[0]
            result, normed = finish(early_x, received, turn, 1)
            return normed, blank(pair_shape)[0], result

        def late_scatter():
            parts, fresh = block(received, got, turn)
            return parts, fresh, blank(block_shape)[0]

        if crossing:
            early_x = either(
                lambda: finish(early_x, received, turn, 0)[0], lambda: blank(block_shape)[0]
            )
            blocks_out[layer, 0] = early_x
            early_x = upward(early_x, level, 0)
        payload, late_pair, result = either(early_gather, late_scatter)
        if not crossing:
            early_x = blocks_out[layer, 0] = result
        sources[layer, 1] = late_pair
        if crossing:
            active = pipe == jnp.where(early, 2 * level + 2, 2 * level + 1)
            received = lax.cond(active, across, lambda _: blank(blocks_shape)[0], payload)
        else:
            received = across(payload)

    def by_plane(values):
        chosen = values[0]
        for level in range(1, planes):
            chosen = jnp.where(plane == level, values[level], chosen)
        return chosen

    last = sections - 1
    first_cache = by_plane(
        [jnp.where(early, sources[2 * m, 0], sources[2 * m + 1, 2]) for m in range(planes)]
    )
    second_cache = by_plane(
        [
            jnp.where(early, sources[2 * m + 1, 2], sources[2 * m + 1, int(m < planes - 1)])
            for m in range(planes)
        ]
    )

    def last_early():
        result = finish(early_x, received, last % 2, 0)[0]
        packed = pl.pallas_call(
            cache_kernel, out_shape=bf16(seq, rows, 4 * channels),
            in_specs=[VMEM] * 2, out_specs=VMEM, compiler_params=params_of(16),
        )(first_cache, second_cache)
        return result, across(packed)

    def last_late():
        parts, _ = block(received, got, last % 2, (first_cache, second_cache))
        parts = across(parts)
        return finish(late_x, parts, last % 2, 0)[0], parts[:, :, width:]

    x, cache = either(last_early, last_late)
    blocks_out[last, 0] = blocks_out[last, 1] = x
    mine = by_plane(
        [jnp.where(early, blocks_out[2 * m, 0], blocks_out[2 * m + 1, 1]) for m in range(planes)]
    )
    theirs = swap(
        by_plane(
            [jnp.where(early, blocks_out[2 * m + 1, 0], blocks_out[2 * m, 1]) for m in range(planes)]
        )
    )
    block_output = jnp.stack([jnp.where(early, mine, theirs), jnp.where(early, theirs, mine)])
    cache = cache.reshape(seq, rows, 2, 2, channels)
    cache = jnp.transpose(cache, (2, 1, 3, 0, 4)).reshape(2, rows, 2, seq * channels)
    return block_output[None], cache[None]


def solution(mesh):
    in_specs = (
        P(None, "seq", None),
        P("pipe", None),
        P("pipe", None),
        P("pipe", None),
        P("pipe", None, None),
        P("pipe", None, None, "seq"),
        P("pipe", "seq", None),
        P("pipe", None, "seq", None, None),
    )
    out_specs = (P("pipe", None, "seq", None), P("pipe", None, "seq", None, None))
    return jax.shard_map(body, mesh=mesh, in_specs=in_specs, out_specs=out_specs, check_vma=False)
```

time: 295 us -> 303 us (1.027)
  the two profiles are of different devices: /device:TPU:0 before, /device:TPU:7 now
where the time goes in v3:
time: 303 us; the launch traced here: 302 us
  waiting for transfers between devices  93.5 us (31%)
  starting transfers between devices  92.4 us (30%)
  blocking collectives  59.5 us (20%)
  Pallas kernels  42.4 us (14%)
  local copies, waits for them, and re-layouts  7.34 us (2%)
  other arithmetic  4.73 us (2%)
    all_to_all x6, waiting for transfers between devices, across(): lax.all_to_all(blocks, 'seq', split_axis=0, concat_axis=0, tiled=True)  65.5 us
    ppermute x9, starting transfers between devices, swap(): return lax.ppermute(value, AXES, pairs)  59.6 us
    all_to_all x2, blocking collectives, across(): lax.all_to_all(blocks, 'seq', split_axis=0, concat_axis=0, tiled=True)  59.5 us
    pallas_call x4, Pallas kernels, block(): pl.pallas_call(functools.partial(block_kernel, turn, head_size, planes),...  31.1 us
    all_to_all x6, starting transfers between devices, across(): lax.all_to_all(blocks, 'seq', split_axis=0, concat_axis=0, tiled=True)  30.8 us
    ppermute x2, waiting for transfers between devices, upward(): lax.ppermute(value, AXES, [(place(row, s), place(row + 2, s)) for s in ra...  25.7 us
    pallas_call x4, Pallas kernels, finish(): pl.pallas_call(finish_kernel, out_shape=shapes, in_specs=[VMEM] * 4, out_...  6.19 us
  transfers between devices with their start and end apart: 17, of which 8 were waited for; matrix products, arithmetic and copies ran while one was open for 2% of the time, Pallas kernels for 0%

profile of v3, /device:TPU:7, one launch (start us, length us, event | category | flops | bytes accessed | tf_op | source)
XLA Modules:
  0.0 301.6 jit_solution(16803451179500246586)
XLA Ops:
  0.6 0.8 select_maximum_fusion.params_ref
  2.2 1.2 slice_bitcast_fusion.cache_ref
  3.5 1.4 shard_map.95
  6.3 13.4 %conditional.12 = (bf16[8,24,3584]{2,1,0:T(8,128)(2,1)}, bf16[8,24,512]{2,1,0:T(8,128)(2,1)}) conditional(s32[]{:T(128)} %convert_element_type.6, bf16[8,24,3584]{2,1,0:T(8,128)(2,1)S(1)} %shard_map.95, bf16[8,24,3584]{2,1,0:T(8,128)(2,1)S(1)} %shard_map.95), branch_computations={%region_0.1_spmd, %region_1.2_spmd} | conditional | bytes 3145744 | solution.py:295
  7.0 5.8 %all-to-all-start = ((bf16[8,24,512]{2,1,0:T(8,128)(2,1)}), bf16[8,24,512]{2,1,0:T(8,128)(2,1)}, u32[]{:S(2)}, u32[]{:S(2)}) async-start(bf16[8,24,512]{2,1,0:T(8,128)(2,1)} %slice.12), calls=%async_computation | async-start | bytes 393216 | tf_op jit(solution)/shard_map/cond/branch_0_fun/all_to_all | solution.py:230
  12.8 6.9 %all-to-all-done = bf16[8,24,512]{2,1,0:T(8,128)(2,1)} async-done(((bf16[8,24,512]{2,1,0:T(8,128)(2,1)}), bf16[8,24,512]{2,1,0:T(8,128)(2,1)}, u32[]{:S(2)}, u32[]{:S(2)}) %all-to-all-start) | async-done | bytes 196640 | tf_op jit(solution)/shard_map/cond/branch_0_fun/all_to_all | solution.py:230
  19.7 1.4 conditional.13
  19.7 1.4 branch_0_fun.18
  21.1 6.9 %all-to-all-start.5 = ((bf16[8,24,3072]{2,1,0:T(8,128)(2,1)}), bf16[8,24,3072]{2,1,0:T(8,128)(2,1)S(1)}, u32[]{:S(2)}, u32[]{:S(2)}) async-start(bf16[8,24,3072]{2,1,0:T(8,128)(2,1)} %get-tuple-element.365), calls=%async_computation.5 | async-start | bytes 2359296 | tf_op jit(solution)/shard_map/all_to_all | solution.py:230
  28.0 25.4 %collective-permute-start.3 = (bf16[2,192,256]{2,1,0:T(8,128)(2,1)S(1)}, bf16[2,192,256]{2,1,0:T(8,128)(2,1)}, u32[]{:S(2)}, u32[]{:S(2)}) collective-permute-start(bf16[2,192,256]{2,1,0:T(8,128)(2,1)S(1)} %get-tuple-element.366), channel_id=1, source_target_pairs={{0,8},{1,9},{2,10},{3,11},{4,12},{5,13},{6,14},{7,15},{8,0},{9,1},... | collective-permute-start | bytes 589832 | tf_op jit(solution)/shard_map/ppermute | solution.py:223
  53.3 1.2 collective-permute-done.3
  54.5 8.0 %conditional.14 = (bf16[8,24,3072]{2,1,0:T(8,128)(2,1)}, bf16[2,192,256]{2,1,0:T(8,128)(2,1)}, bf16[24,3072]{1,0:T(8,128)(2,1)S(1)}) conditional(s32[]{:T(128)} %convert_element_type.6, (f32[2,128]{1,0:T(2,128)S(1)}, bf16[3,3072,256]{2,1,0:T(8,128)(2,1)}, bf16[3,3072,256]{2,1,0:T(8,128)(2,1)}, bf16[1,256,3072]{2,1,0:T(8,128)(2,1)S(1)}, ...), branch_computations={%region_4.5_spmd, %region_5.6_spmd} | conditional | bytes 24 | solution.py:295
  54.5 8.0 %branch_0_fun.20 = (bf16[8,24,3072]{2,1,0:T(8,128)(2,1)}, bf16[2,192,256]{2,1,0:T(8,128)(2,1)}) custom-call(f32[2,128]{1,0:T(2,128)S(1)} %get-tuple-element.222.gain_ref, bf16[3,3072,256]{2,1,0:T(8,128)(2,1)} %get-tuple-element.223.own_in, bf16[3,3072,256]{2,1,0:T(8,128)(2,1)} %get-tuple-element.224.other_in, ...), custom_call_target="tpu_custom_call" | custom-call | tf_op jit(solution)/shard_map/cond/branch_0_fun/pallas_call | solution.py:268
  62.6 5.5 %all-to-all-start.6 = ((bf16[8,24,3072]{2,1,0:T(8,128)(2,1)}), bf16[8,24,3072]{2,1,0:T(8,128)(2,1)S(1)}, u32[]{:S(2)}, u32[]{:S(2)}) async-start(bf16[8,24,3072]{2,1,0:T(8,128)(2,1)} %get-tuple-element.367), calls=%async_computation.6 | async-start | bytes 2359296 | tf_op jit(solution)/shard_map/all_to_all | solution.py:230
  68.0 8.3 %collective-permute-start.4 = (bf16[8,24,512]{2,1,0:T(8,128)(2,1)}, bf16[8,24,512]{2,1,0:T(8,128)(2,1)}, u32[]{:S(2)}, u32[]{:S(2)}) collective-permute-start(bf16[8,24,512]{2,1,0:T(8,128)(2,1)} %get-tuple-element.364), channel_id=1, source_target_pairs={{0,8},{1,9},{2,10},{3,11},{4,12},{5,13},{6,14},{7,15},{8,0},{9,1},... | collective-permute-start | bytes 589832 | tf_op jit(solution)/shard_map/ppermute | solution.py:223
  76.4 15.9 %all-to-all-done.6 = bf16[8,24,3072]{2,1,0:T(8,128)(2,1)S(1)} async-done(((bf16[8,24,3072]{2,1,0:T(8,128)(2,1)}), bf16[8,24,3072]{2,1,0:T(8,128)(2,1)S(1)}, u32[]{:S(2)}, u32[]{:S(2)}) %all-to-all-start.6) | async-done | bytes 1179680 | tf_op jit(solution)/shard_map/all_to_all | solution.py:230
  92.2 2.3 conditional.15
  92.2 2.3 branch_0_fun.22
  94.6 4.6 %all-to-all-start.7 = ((bf16[8,24,3072]{2,1,0:T(8,128)(2,1)}), bf16[8,24,3072]{2,1,0:T(8,128)(2,1)S(1)}, u32[]{:S(2)}, u32[]{:S(2)}) async-start(bf16[8,24,3072]{2,1,0:T(8,128)(2,1)} %get-tuple-element.370), calls=%async_computation.7 | async-start | bytes 2359296 | tf_op jit(solution)/shard_map/all_to_all | solution.py:230
  99.2 10.3 %collective-permute-start.5 = (bf16[2,192,256]{2,1,0:T(8,128)(2,1)}, bf16[2,192,256]{2,1,0:T(8,128)(2,1)}, u32[]{:S(2)}, u32[]{:S(2)}) collective-permute-start(bf16[2,192,256]{2,1,0:T(8,128)(2,1)} %get-tuple-element.371), channel_id=1, source_target_pairs={{0,8},{1,9},{2,10},{3,11},{4,12},{5,13},{6,14},{7,15},{8,0},{9,1},... | collective-permute-start | bytes 589832 | tf_op jit(solution)/shard_map/ppermute | solution.py:223
  109.5 10.7 %all-to-all-done.7 = bf16[8,24,3072]{2,1,0:T(8,128)(2,1)S(1)} async-done(((bf16[8,24,3072]{2,1,0:T(8,128)(2,1)}), bf16[8,24,3072]{2,1,0:T(8,128)(2,1)S(1)}, u32[]{:S(2)}, u32[]{:S(2)}) %all-to-all-start.7) | async-done | bytes 1179680 | tf_op jit(solution)/shard_map/all_to_all | solution.py:230
  121.7 8.0 %conditional.17 = (bf16[2,192,256]{2,1,0:T(8,128)(2,1)}, bf16[8,24,3072]{2,1,0:T(8,128)(2,1)S(1)}) conditional(s32[]{:T(128)} %convert_element_type.6, (f32[2,128]{1,0:T(2,128)S(1)}, bf16[3,3072,256]{2,1,0:T(8,128)(2,1)}, bf16[3,3072,256]{2,1,0:T(8,128)(2,1)}, bf16[1,256,3072]{2,1,0:T(8,128)(2,1)S(1)}, bf16[1,256,3072]{2,1,0:T(8,128)(2,1)}, ...), branch_computations={%region_10.11_spmd, %region_11.12_spmd} | conditional | bytes 16 | solution.py:295
  121.7 7.8 %branch_0_fun.24 = (bf16[8,24,3072]{2,1,0:T(8,128)(2,1)S(1)}, bf16[2,192,256]{2,1,0:T(8,128)(2,1)}) custom-call(f32[2,128]{1,0:T(2,128)S(1)} %get-tuple-element.257.gain_ref, bf16[3,3072,256]{2,1,0:T(8,128)(2,1)} %get-tuple-element.258.own_in, bf16[3,3072,256]{2,1,0:T(8,128)(2,1)} %get-tuple-element.259.other_in, ...), custom_call_target="tpu_custom_call" | custom-call | tf_op jit(solution)/shard_map/cond/branch_0_fun/pallas_call | solution.py:268
  129.7 1.1 conditional.19
  129.7 1.1 branch_0_fun.26
  130.8 1.3 collective-permute-start.7
  132.1 25.7 %collective-permute-done.7 = bf16[24,3072]{1,0:T(8,128)(2,1)} collective-permute-done((bf16[24,3072]{1,0:T(8,128)(2,1)S(1)}, bf16[24,3072]{1,0:T(8,128)(2,1)}, u32[]{:S(2)}, u32[]{:S(2)}) %collective-permute-start.7) | collective-permute-done | bytes 147488 | tf_op jit(solution)/shard_map/ppermute | solution.py:227
  157.8 2.4 conditional.20
  157.8 2.4 branch_0_fun.27
  160.2 4.3 %all-to-all-start.8 = ((bf16[8,24,3072]{2,1,0:T(8,128)(2,1)}), bf16[8,24,3072]{2,1,0:T(8,128)(2,1)S(1)}, u32[]{:S(2)}, u32[]{:S(2)}) async-start(bf16[8,24,3072]{2,1,0:T(8,128)(2,1)} %get-tuple-element.374), calls=%async_computation.8 | async-start | bytes 2359296 | tf_op jit(solution)/shard_map/all_to_all | solution.py:230
  164.5 7.8 %collective-permute-start.8 = (bf16[2,192,256]{2,1,0:T(8,128)(2,1)S(1)}, bf16[2,192,256]{2,1,0:T(8,128)(2,1)}, u32[]{:S(2)}, u32[]{:S(2)}) collective-permute-start(bf16[2,192,256]{2,1,0:T(8,128)(2,1)S(1)} %get-tuple-element.375), channel_id=1, source_target_pairs={{0,8},{1,9},{2,10},{3,11},{4,12},{5,13},{6,14},{7,15},{8,0},{9,1},... | collective-permute-start | bytes 589832 | tf_op jit(solution)/shard_map/ppermute | solution.py:223
  172.3 16.4 %all-to-all-done.8 = bf16[8,24,3072]{2,1,0:T(8,128)(2,1)S(1)} async-done(((bf16[8,24,3072]{2,1,0:T(8,128)(2,1)}), bf16[8,24,3072]{2,1,0:T(8,128)(2,1)S(1)}, u32[]{:S(2)}, u32[]{:S(2)}) %all-to-all-start.8) | async-done | bytes 1179680 | tf_op jit(solution)/shard_map/all_to_all | solution.py:230
  188.7 7.3 %conditional.21 = (bf16[8,24,3072]{2,1,0:T(8,128)(2,1)}, bf16[2,192,256]{2,1,0:T(8,128)(2,1)S(1)}, bf16[24,3072]{1,0:T(8,128)(2,1)}) conditional(s32[]{:T(128)} %convert_element_type.6, (f32[2,128]{1,0:T(2,128)S(1)}, bf16[3,3072,256]{2,1,0:T(8,128)(2,1)}, bf16[3,3072,256]{2,1,0:T(8,128)(2,1)}, bf16[1,256,3072]{2,1,0:T(8,128)(2,1)S(1)}, ...), branch_computations={%region_18.19_spmd, %region_19.20_spmd} | conditional | bytes 24 | solution.py:295
  188.7 7.3 %branch_0_fun.29 = (bf16[8,24,3072]{2,1,0:T(8,128)(2,1)}, bf16[2,192,256]{2,1,0:T(8,128)(2,1)S(1)}) custom-call(f32[2,128]{1,0:T(2,128)S(1)} %get-tuple-element.281.gain_ref, bf16[3,3072,256]{2,1,0:T(8,128)(2,1)} %get-tuple-element.282.own_in, bf16[3,3072,256]{2,1,0:T(8,128)(2,1)} %get-tuple-element.283.other_in, ...), custom_call_target="tpu_custom_call" | custom-call | tf_op jit(solution)/shard_map/cond/branch_0_fun/pallas_call | solution.py:268
  196.1 33.1 %all_to_all.53 = bf16[8,24,3072]{2,1,0:T(8,128)(2,1)S(1)} all-to-all(bf16[8,24,3072]{2,1,0:T(8,128)(2,1)} %get-tuple-element.377), channel_id=1, replica_groups=mesh['pipe'=4,'seq'=8] {'seq'}, dimensions={0} | all-to-all | bytes 2359296 | tf_op jit(solution)/shard_map/all_to_all | solution.py:230
  229.2 2.6 conditional.22
  229.2 2.6 branch_0_fun.31
  232.4 3.8 %all-to-all-start.10 = ((bf16[8,24,3072]{2,1,0:T(8,128)(2,1)}), bf16[8,24,3072]{2,1,0:T(8,128)(2,1)S(1)}, u32[]{:S(2)}, u32[]{:S(2)}) async-start(bf16[8,24,3072]{2,1,0:T(8,128)(2,1)} %get-tuple-element.379), calls=%async_computation.10 | async-start | bytes 2359296 | tf_op jit(solution)/shard_map/all_to_all | solution.py:230
  236.3 6.4 %collective-permute-start.9 = (bf16[2,192,256]{2,1,0:T(8,128)(2,1)S(1)}, bf16[2,192,256]{2,1,0:T(8,128)(2,1)S(1)}, u32[]{:S(2)}, u32[]{:S(2)}) collective-permute-start(bf16[2,192,256]{2,1,0:T(8,128)(2,1)S(1)} %copy-done.19), channel_id=1, source_target_pairs={{0,8},{1,9},{2,10},{3,11},{4,12},{5,13},{6,14},{7,15},{8,0},{9,1},... | collective-permute-start | bytes 589832 | tf_op jit(solution)/shard_map/ppermute | solution.py:223
  242.6 1.1 collective-permute-done.9
  244.4 1.3 select_select_fusion
  245.7 15.6 %all-to-all-done.10 = bf16[8,24,3072]{2,1,0:T(8,128)(2,1)S(1)} async-done(((bf16[8,24,3072]{2,1,0:T(8,128)(2,1)}), bf16[8,24,3072]{2,1,0:T(8,128)(2,1)S(1)}, u32[]{:S(2)}, u32[]{:S(2)}) %all-to-all-start.10) | async-done | bytes 1179680 | tf_op jit(solution)/shard_map/all_to_all | solution.py:230
  261.3 35.7 %conditional.23 = (bf16[24,3072]{1,0:T(8,128)(2,1)S(1)}, bf16[8,24,1024]{2,1,0:T(8,128)(2,1)}) conditional(s32[]{:T(128)} %convert_element_type.6, (f32[2,128]{1,0:T(2,128)S(1)}, bf16[3,3072,256]{2,1,0:T(8,128)(2,1)}, bf16[3,3072,256]{2,1,0:T(8,128)(2,1)}, bf16[1,256,3072]{2,1,0:T(8,128)(2,1)S(1)}, bf16[1,256,3072]{2,1,0:T(8,128)(2,1)}, ...), branch_computations={%region_22.23_spmd, %region_23.24_spmd} | conditional | bytes 4522028 | solution.py:295
  261.3 8.0 %branch_0_fun.32 = (bf16[8,24,4096]{2,1,0:T(8,128)(2,1)S(1)}, bf16[2,192,256]{2,1,0:T(8,128)(2,1)}) custom-call(f32[2,128]{1,0:T(2,128)S(1)} %get-tuple-element.315.gain_ref, bf16[3,3072,256]{2,1,0:T(8,128)(2,1)} %get-tuple-element.316.own_in, bf16[3,3072,256]{2,1,0:T(8,128)(2,1)} %get-tuple-element.317.other_in, ...), custom_call_target="tpu_custom_call" | custom-call | tf_op jit(solution)/shard_map/cond/branch_0_fun/pallas_call | solution.py:268
  269.3 26.4 %all_to_all.52.parts_ref = bf16[8,24,4096]{2,1,0:T(8,128)(2,1)S(1)} all-to-all(bf16[8,24,4096]{2,1,0:T(8,128)(2,1)S(1)} %get-tuple-element.324), channel_id=1, replica_groups=mesh['pipe'=4,'seq'=8] {'seq'}, dimensions={0} | all-to-all | bytes 3145728 | tf_op jit(solution)/shard_map/cond/branch_0_fun/all_to_all | solution.py:230
  297.0 1.0 select_select_fusion.2
  298.1 1.3 reshape.7
  299.9 0.8 broadcast_in_dim_reshape.3
  (76 shorter events, 7.8 us)
Async XLA Ops:
  0.6 2.8 copy-start
  1.5 3.4 %collective-permute-start = (f32[4,3072]{1,0:T(4,128)S(1)}, f32[4,3072]{1,0:T(4,128)S(1)}, u32[]{:S(2)}, u32[]{:S(2)}) collective-permute-start(f32[4,3072]{1,0:T(4,128)S(1)} %select_maximum_fusion.params_ref), channel_id=1, source_target_pairs={{0,8},{1,9},{2,10},{3,11},{4,12},{5,13},{6,14},{7,15},{8,0},{9,1},... | collective-permute-start | bytes 147464 | tf_op jit(solution)/shard_map/ppermute | solution.py:223
  2.2 2.8 copy-start.1
  2.2 3.2 %copy-start.20 = (f32[1,3072]{1,0:T(1,128)S(1)}, f32[1,3072]{1,0:T(1,128)}, u32[]{:S(2)}) copy-start(f32[1,3072]{1,0:T(1,128)} %param.35) | copy-start | bytes 36868
  2.2 3.2 %copy-start.21 = (f32[1,2,128]{2,1,0:T(2,128)S(1)}, f32[1,2,128]{2,1,0:T(2,128)}, u32[]{:S(2)}) copy-start(f32[1,2,128]{2,1,0:T(2,128)} %param.36) | copy-start | bytes 3076
  3.5 1.4 copy-start.2
  4.9 14.8 %collective-permute-start.1 = (bf16[3,3072,256]{2,1,0:T(8,128)(2,1)}, bf16[3,3072,256]{2,1,0:T(8,128)(2,1)}, u32[]{:S(2)}, u32[]{:S(2)}) collective-permute-start(bf16[3,3072,256]{2,1,0:T(8,128)(2,1)} %bitcast.21), channel_id=1, source_target_pairs={{0,8},{1,9},{2,10},{3,11},{4,12},{5,13},{6,14},{7,15},{8,0},{9,1},... | collective-permute-start | bytes 14155784 | tf_op jit(solution)/shard_map/ppermute | solution.py:223
  5.0 14.7 %collective-permute-start.2 = (bf16[1,256,3072]{2,1,0:T(8,128)(2,1)S(1)}, bf16[1,256,3072]{2,1,0:T(8,128)(2,1)}, u32[]{:S(2)}, u32[]{:S(2)}) collective-permute-start(bf16[1,256,3072]{2,1,0:T(8,128)(2,1)S(1)} %copy-done.1), channel_id=1, source_target_pairs={{0,8},{1,9},{2,10},{3,11},{4,12},{5,13},{6,14},{7,15},{8,0},{9,1},... | collective-permute-start | bytes 4718600 | tf_op jit(solution)/shard_map/ppermute | solution.py:223
  6.3 13.4 %copy-start.3 = (bf16[24,3072]{1,0:T(8,128)(2,1)S(1)}, bf16[24,3072]{1,0:T(8,128)(2,1)}, u32[]{:S(2)}) copy-start(bf16[24,3072]{1,0:T(8,128)(2,1)} %copy-done.2) | copy-start | bytes 442372
  7.0 12.7 %all-to-all-start = ((bf16[8,24,512]{2,1,0:T(8,128)(2,1)}), bf16[8,24,512]{2,1,0:T(8,128)(2,1)}, u32[]{:S(2)}, u32[]{:S(2)}) async-start(bf16[8,24,512]{2,1,0:T(8,128)(2,1)} %slice.12), calls=%async_computation | async-start | bytes 393216 | tf_op jit(solution)/shard_map/cond/branch_0_fun/all_to_all | solution.py:230
  21.1 6.9 %copy-start.9 = (bf16[2,192,256]{2,1,0:T(8,128)(2,1)}, bf16[2,192,256]{2,1,0:T(8,128)(2,1)S(1)}, u32[]{:S(2)}) copy-start(bf16[2,192,256]{2,1,0:T(8,128)(2,1)S(1)} %get-tuple-element.366) | copy-start | bytes 589828
  21.1 32.2 %all-to-all-start.5 = ((bf16[8,24,3072]{2,1,0:T(8,128)(2,1)}), bf16[8,24,3072]{2,1,0:T(8,128)(2,1)S(1)}, u32[]{:S(2)}, u32[]{:S(2)}) async-start(bf16[8,24,3072]{2,1,0:T(8,128)(2,1)} %get-tuple-element.365), calls=%async_computation.5 | async-start | bytes 2359296 | tf_op jit(solution)/shard_map/all_to_all | solution.py:230
  28.0 26.6 %collective-permute-start.3 = (bf16[2,192,256]{2,1,0:T(8,128)(2,1)S(1)}, bf16[2,192,256]{2,1,0:T(8,128)(2,1)}, u32[]{:S(2)}, u32[]{:S(2)}) collective-permute-start(bf16[2,192,256]{2,1,0:T(8,128)(2,1)S(1)} %get-tuple-element.366), channel_id=1, source_target_pairs={{0,8},{1,9},{2,10},{3,11},{4,12},{5,13},{6,14},{7,15},{8,0},{9,1},... | collective-permute-start | bytes 589832 | tf_op jit(solution)/shard_map/ppermute | solution.py:223
  62.5 57.7 %copy-start.4 = (bf16[24,3072]{1,0:T(8,128)(2,1)}, bf16[24,3072]{1,0:T(8,128)(2,1)S(1)}, u32[]{:S(2)}) copy-start(bf16[24,3072]{1,0:T(8,128)(2,1)S(1)} %get-tuple-element.372) | copy-start | bytes 442372
  62.6 29.7 %all-to-all-start.6 = ((bf16[8,24,3072]{2,1,0:T(8,128)(2,1)}), bf16[8,24,3072]{2,1,0:T(8,128)(2,1)S(1)}, u32[]{:S(2)}, u32[]{:S(2)}) async-start(bf16[8,24,3072]{2,1,0:T(8,128)(2,1)} %get-tuple-element.367), calls=%async_computation.6 | async-start | bytes 2359296 | tf_op jit(solution)/shard_map/all_to_all | solution.py:230
  68.0 24.2 %collective-permute-start.4 = (bf16[8,24,512]{2,1,0:T(8,128)(2,1)}, bf16[8,24,512]{2,1,0:T(8,128)(2,1)}, u32[]{:S(2)}, u32[]{:S(2)}) collective-permute-start(bf16[8,24,512]{2,1,0:T(8,128)(2,1)} %get-tuple-element.364), channel_id=1, source_target_pairs={{0,8},{1,9},{2,10},{3,11},{4,12},{5,13},{6,14},{7,15},{8,0},{9,1},... | collective-permute-start | bytes 589832 | tf_op jit(solution)/shard_map/ppermute | solution.py:223
  94.6 25.7 %all-to-all-start.7 = ((bf16[8,24,3072]{2,1,0:T(8,128)(2,1)}), bf16[8,24,3072]{2,1,0:T(8,128)(2,1)S(1)}, u32[]{:S(2)}, u32[]{:S(2)}) async-start(bf16[8,24,3072]{2,1,0:T(8,128)(2,1)} %get-tuple-element.370), calls=%async_computation.7 | async-start | bytes 2359296 | tf_op jit(solution)/shard_map/all_to_all | solution.py:230
  99.2 21.8 %collective-permute-start.5 = (bf16[2,192,256]{2,1,0:T(8,128)(2,1)}, bf16[2,192,256]{2,1,0:T(8,128)(2,1)}, u32[]{:S(2)}, u32[]{:S(2)}) collective-permute-start(bf16[2,192,256]{2,1,0:T(8,128)(2,1)} %get-tuple-element.371), channel_id=1, source_target_pairs={{0,8},{1,9},{2,10},{3,11},{4,12},{5,13},{6,14},{7,15},{8,0},{9,1},... | collective-permute-start | bytes 589832 | tf_op jit(solution)/shard_map/ppermute | solution.py:223
  120.3 0.7 copy-start.13
  120.3 0.7 collective-permute-start.6
  121.0 0.7 copy-start.14
  130.8 27.0 %copy-start.11 = (bf16[24,3072]{1,0:T(8,128)(2,1)}, bf16[24,3072]{1,0:T(8,128)(2,1)S(1)}, u32[]{:S(2)}) copy-start(bf16[24,3072]{1,0:T(8,128)(2,1)S(1)} %get-tuple-element.438) | copy-start | bytes 442372
  130.8 27.0 %collective-permute-start.7 = (bf16[24,3072]{1,0:T(8,128)(2,1)S(1)}, bf16[24,3072]{1,0:T(8,128)(2,1)}, u32[]{:S(2)}, u32[]{:S(2)}) collective-permute-start(bf16[24,3072]{1,0:T(8,128)(2,1)S(1)} %get-tuple-element.438), channel_id=1, source_target_pairs={{8,24},{9,25},{10,26},{11,27},{12,28},{13,29},{14,30},{15,31}} | collective-permute-start | bytes 442376 | tf_op jit(solution)/shard_map/ppermute | solution.py:227
  160.2 4.3 %copy-start.10 = (bf16[2,192,256]{2,1,0:T(8,128)(2,1)}, bf16[2,192,256]{2,1,0:T(8,128)(2,1)S(1)}, u32[]{:S(2)}) copy-start(bf16[2,192,256]{2,1,0:T(8,128)(2,1)S(1)} %get-tuple-element.375) | copy-start | bytes 589828
  160.2 28.5 %copy-start.15 = (bf16[24,3072]{1,0:T(8,128)(2,1)S(1)}, bf16[24,3072]{1,0:T(8,128)(2,1)}, u32[]{:S(2)}) copy-start(bf16[24,3072]{1,0:T(8,128)(2,1)} %copy-done.14) | copy-start | bytes 442372
  160.2 28.5 %all-to-all-start.8 = ((bf16[8,24,3072]{2,1,0:T(8,128)(2,1)}), bf16[8,24,3072]{2,1,0:T(8,128)(2,1)S(1)}, u32[]{:S(2)}, u32[]{:S(2)}) async-start(bf16[8,24,3072]{2,1,0:T(8,128)(2,1)} %get-tuple-element.374), calls=%async_computation.8 | async-start | bytes 2359296 | tf_op jit(solution)/shard_map/all_to_all | solution.py:230
  164.5 24.2 %collective-permute-start.8 = (bf16[2,192,256]{2,1,0:T(8,128)(2,1)S(1)}, bf16[2,192,256]{2,1,0:T(8,128)(2,1)}, u32[]{:S(2)}, u32[]{:S(2)}) collective-permute-start(bf16[2,192,256]{2,1,0:T(8,128)(2,1)S(1)} %get-tuple-element.375), channel_id=1, source_target_pairs={{0,8},{1,9},{2,10},{3,11},{4,12},{5,13},{6,14},{7,15},{8,0},{9,1},... | collective-permute-start | bytes 589832 | tf_op jit(solution)/shard_map/ppermute | solution.py:223
  196.1 33.1 %copy-start.18 = (bf16[2,192,256]{2,1,0:T(8,128)(2,1)}, bf16[2,192,256]{2,1,0:T(8,128)(2,1)S(1)}, u32[]{:S(2)}) copy-start(bf16[2,192,256]{2,1,0:T(8,128)(2,1)S(1)} %get-tuple-element.378) | copy-start | bytes 589828
  231.8 0.7 copy-start.16
  231.8 4.5 %copy-start.19 = (bf16[2,192,256]{2,1,0:T(8,128)(2,1)S(1)}, bf16[2,192,256]{2,1,0:T(8,128)(2,1)}, u32[]{:S(2)}) copy-start(bf16[2,192,256]{2,1,0:T(8,128)(2,1)} %get-tuple-element.380) | copy-start | bytes 589828
  232.4 28.9 %all-to-all-start.10 = ((bf16[8,24,3072]{2,1,0:T(8,128)(2,1)}), bf16[8,24,3072]{2,1,0:T(8,128)(2,1)S(1)}, u32[]{:S(2)}, u32[]{:S(2)}) async-start(bf16[8,24,3072]{2,1,0:T(8,128)(2,1)} %get-tuple-element.379), calls=%async_computation.10 | async-start | bytes 2359296 | tf_op jit(solution)/shard_map/all_to_all | solution.py:230
  236.3 7.4 %collective-permute-start.9 = (bf16[2,192,256]{2,1,0:T(8,128)(2,1)S(1)}, bf16[2,192,256]{2,1,0:T(8,128)(2,1)S(1)}, u32[]{:S(2)}, u32[]{:S(2)}) collective-permute-start(bf16[2,192,256]{2,1,0:T(8,128)(2,1)S(1)} %copy-done.19), channel_id=1, source_target_pairs={{0,8},{1,9},{2,10},{3,11},{4,12},{5,13},{6,14},{7,15},{8,0},{9,1},... | collective-permute-start | bytes 589832 | tf_op jit(solution)/shard_map/ppermute | solution.py:223
  243.7 0.7 copy-start.8
  269.3 27.2 %copy-start.17 = (bf16[24,3072]{1,0:T(8,128)(2,1)S(1)}, bf16[24,3072]{1,0:T(8,128)(2,1)}, u32[]{:S(2)}) copy-start(bf16[24,3072]{1,0:T(8,128)(2,1)} %get-tuple-element.314.x_ref) | copy-start | bytes 442372 | tf_op jit(solution)/shard_map/cond
  298.0 2.7 collective-permute-start.10
  298.1 2.6 copy-start.5
  298.1 2.6 copy-start.6
  298.1 2.6 copy-start.12

commit v4 on v3

--- a/solution.py
+++ b/solution.py
@@ -60,16 +60,14 @@
 
 def attention(head_size, q_ref, kv_ref, far_ref):
     factor = 1.0 / math.sqrt(head_size)
-    tokens, channels = q_ref.shape
+    channels = q_ref.shape[1]
     heads = []
     across = (((1,), (1,)), ((), ()))
 
     def far_of(kind, start):
-        if far_ref.shape[2] == channels:
+        if len(far_ref.shape) == 3:
             return far_ref[kind, :, start : start + head_size]
-        begin = kind * channels + start
-        blocks = far_ref[:, :, begin : begin + head_size].astype(jnp.float32)
-        return blocks.reshape(tokens, head_size).astype(jnp.bfloat16)
+        return far_ref[:, kind * channels + start : kind * channels + start + head_size]
 
     for start in range(0, channels, head_size):
         cut = slice(start, start + head_size)
@@ -88,14 +86,11 @@
 
 
 def put_cache(caches, out_ref, offset):
-    count, rows, _ = out_ref.shape
     channels = caches[0].shape[2]
     for patch, cache in enumerate(caches):
         for kind in range(2):
             begin = offset + (2 * patch + kind) * channels
-            out_ref[:, :, begin : begin + channels] = (
-                cache[kind].astype(jnp.float32).reshape(count, rows, channels).astype(jnp.bfloat16)
-            )
+            out_ref[:, begin : begin + channels] = cache[kind]
 
 
 def cache_kernel(*refs):
@@ -105,9 +100,9 @@
 def block_kernel(
     turn, head_size, planes, gain_ref, own_in, other_in, own_out, other_out, blocks_ref, far_ref, *refs
 ):
-    caches, refs = refs[:-10], refs[-10:]
-    parts_ref, kv_ref, blocks, w_in, w_out, parts, q_ref, in_sems, sems, part_sems = refs
-    count, rows, width = blocks.shape
+    caches, refs = refs[:-11], refs[-11:]
+    out_ref, kv_ref, blocks, far, w_in, w_out, parts, q_ref, in_sems, sems, part_sems = refs
+    width = blocks.shape[1]
     channels = w_out.shape[0]
     pieces = in_sems.shape[1]
     depth = width // pieces
@@ -122,8 +117,14 @@
                 ).start()
         pltpu.make_async_copy(source_out.at[0], w_out, sems.at[1]).start()
 
-    fetch = pltpu.make_async_copy(blocks_ref.at[:, :, :width], blocks, sems.at[0])
+    fetch = pltpu.make_async_copy(blocks_ref.at[:, :width], blocks, sems.at[0])
     fetch.start()
+    if len(far.shape) == 3:
+        fetch_far = pltpu.make_async_copy(far_ref, far, sems.at[2])
+    else:
+        begin = far_ref.shape[1] - far.shape[1]
+        fetch_far = pltpu.make_async_copy(far_ref.at[:, begin:], far, sems.at[2])
+    fetch_far.start()
 
     @pl.when(mine)
     def _():
@@ -134,7 +135,7 @@
         weight_copies(other_in, other_out)
 
     fetch.wait()
-    tokens = blocks[...].astype(jnp.float32).reshape(count * rows, width).astype(jnp.bfloat16)
+    tokens = blocks[...]
     for part in (1, 2, 0):
         for piece in range(pieces):
             cut = pl.ds(piece * depth, depth)
@@ -156,12 +157,13 @@
             else:
                 kv_ref[0, :, start : start + head_size] = head
 
+    fetch_far.wait()
     sent = []
 
     def send(begin, size, sem):
         cut = pl.ds(begin, size)
         sent.append(
-            pltpu.make_async_copy(parts.at[:, :, cut], parts_ref.at[:, :, cut], part_sems.at[sem])
+            pltpu.make_async_copy(parts.at[:, cut], out_ref.at[:, cut], part_sems.at[sem])
         )
         sent[-1].start()
 
@@ -171,13 +173,13 @@
         first, second = caches
         put_cache((first, jnp.where(last, kv_ref[...], second[...])), parts, width)
         send(width, 4 * channels, steps)
-    attended = attention(head_size, q_ref, kv_ref, far_ref)
+    attended = attention(head_size, q_ref, kv_ref, far)
     pltpu.make_async_copy(own_out.at[0], w_out, sems.at[1]).wait()
     tile = width // steps
     for step in range(steps):
         cut = slice(step * tile, (step + 1) * tile)
         update = jnp.dot(attended, w_out[:, cut], preferred_element_type=jnp.float32)
-        parts[:, :, cut] = update.reshape(count, rows, tile).astype(jnp.bfloat16)
+        parts[:, cut] = update.astype(jnp.bfloat16)
         send(step * tile, tile, step)
     for copy in sent:
         copy.wait()
@@ -263,25 +265,33 @@
             scratch_shapes=spreading, compiler_params=params_of(16),
         )(params[turn], x)
 
+    flat = lambda blocks: blocks.reshape(tokens, blocks.shape[2])
+    apart = lambda values: values.reshape(seq, rows, values.shape[1])
+
     def block(blocks, far, turn, caches=()):
         total = width + 2 * channels * len(caches)
-        return pl.pallas_call(
+        side = (2, tokens, channels) if far.ndim == 3 else (tokens, 2 * channels)
+        out, pair = pl.pallas_call(
             functools.partial(block_kernel, turn, head_size, planes),
-            out_shape=(bf16(seq, rows, total), bf16(2, tokens, channels)),
-            in_specs=[VMEM] + [HBM] * 4 + [ANY] + [VMEM] * (1 + len(caches)),
+            out_shape=(bf16(tokens, total), bf16(2, tokens, channels)),
+            in_specs=[VMEM] + [HBM] * 4 + [ANY] * 2 + [VMEM] * len(caches),
             out_specs=(HBM, VMEM),
             scratch_shapes=[
-                pltpu.VMEM((seq, rows, width), jnp.bfloat16),
+                pltpu.VMEM((tokens, width), jnp.bfloat16),
+                pltpu.VMEM(side, jnp.bfloat16),
                 pltpu.VMEM(own_in.shape, jnp.bfloat16),
                 pltpu.VMEM(own_out.shape[1:], jnp.bfloat16),
-                pltpu.VMEM((seq, rows, total), jnp.bfloat16),
+                pltpu.VMEM((tokens, total), jnp.bfloat16),
                 pltpu.VMEM((tokens, channels), jnp.bfloat16),
                 pltpu.SemaphoreType.DMA((3, 2)),
-                pltpu.SemaphoreType.DMA((2,)),
+                pltpu.SemaphoreType.DMA((3,)),
                 pltpu.SemaphoreType.DMA((5,)),
             ],
             compiler_params=params_of(32),
-        )(gain_rows[turn], own_in, other_in, own_out, other_out, blocks, far, *caches)
+        )(
+            gain_rows[turn], own_in, other_in, own_out, other_out, flat(blocks), far, *caches
+        )
+        return apart(out), pair
 
     def finish(x, parts, turn, onward):
         shapes = (bf16(rows, width),) + (blocks_shape,) * onward
@@ -295,14 +305,13 @@
     either = lambda on_early, on_late: lax.cond(early, on_early, on_late)
 
     def first_early():
-        value = across(packed)
-        return value, value[:, :, width:]
+        return across(packed), blank(bf16(tokens, 2 * channels))[0]
 
     def first_late():
-        return blank(bf16(*packed.shape))[0], across(packed[:, :, width:])
+        return blank(bf16(*packed.shape))[0], flat(across(packed[:, :, width:]))
 
     received, stale = either(first_early, first_late)
-    stale_pair = [stale, swap(stale)]
+    stales = [flat(received), swap(stale)]
     pair_shape, block_shape = bf16(2, tokens, channels), bf16(rows, width)
     late_pair = None
     early_x, late_x = x, x
@@ -312,7 +321,7 @@
         crossing = layer > 0 and turn == 0
 
         def early_scatter():
-            parts, fresh = block(received, stale_pair[turn], turn)
+            parts, fresh = block(received, stales[turn], turn)
             return parts, fresh, blank(block_shape)[0]
 
         def late_gather():
@@ -386,10 +395,10 @@
     def last_early():
         result = finish(early_x, received, last % 2, 0)[0]
         packed = pl.pallas_call(
-            cache_kernel, out_shape=bf16(seq, rows, 4 * channels),
+            cache_kernel, out_shape=bf16(tokens, 4 * channels),
             in_specs=[VMEM] * 2, out_specs=VMEM, compiler_params=params_of(16),
         )(first_cache, second_cache)
-        return result, across(packed)
+        return result, across(apart(packed))
 
     def last_late():
         parts, _ = block(received, got, last % 2, (first_cache, second_cache))

time: 303 us -> 288 us (0.950)
  the two profiles are of different devices: /device:TPU:7 before, /device:TPU:0 now
where the time goes in v4:
time: 288 us; the launch traced here: 287 us
  waiting for transfers between devices  139 us (48%)
  starting transfers between devices  63.2 us (22%)
  Pallas kernels  40.1 us (14%)
  blocking collectives  32.7 us (11%)
  local copies, waits for them, and re-layouts  7.19 us (2%)
  other arithmetic  3.92 us (1%)
    all_to_all x7, waiting for transfers between devices, across(): lax.all_to_all(blocks, 'seq', split_axis=0, concat_axis=0, tiled=True)  135 us
    all_to_all x7, starting transfers between devices, across(): lax.all_to_all(blocks, 'seq', split_axis=0, concat_axis=0, tiled=True)  34.4 us
    all_to_all x1, blocking collectives, across(): lax.all_to_all(blocks, 'seq', split_axis=0, concat_axis=0, tiled=True)  32.7 us
    pallas_call x4, Pallas kernels, block(): pl.pallas_call(functools.partial(block_kernel, turn, head_size, planes),...  27.7 us
    ppermute x9, starting transfers between devices, swap(): return lax.ppermute(value, AXES, pairs)  24 us
    pallas_call x4, Pallas kernels, finish(): pl.pallas_call(finish_kernel, out_shape=shapes, in_specs=[VMEM] * 4, out_...  8.13 us
  transfers between devices with their start and end apart: 18, of which 9 were waited for; matrix products, arithmetic and copies ran while one was open for 2% of the time, Pallas kernels for 1%

profile of v4, /device:TPU:0, one launch (start us, length us, event | category | flops | bytes accessed | tf_op | source)
XLA Modules:
  0.0 287.1 jit_solution(11503816303589471480)
XLA Ops:
  0.6 0.8 select_maximum_fusion.params_ref
  2.0 1.2 slice_bitcast_fusion.cache_ref
  3.3 1.5 shard_map.95
  5.5 33.2 %conditional.12 = (bf16[8,24,3584]{2,1,0:T(8,128)(2,1)}, bf16[192,512]{1,0:T(8,128)(2,1)}, bf16[192,3584]{1,0:T(8,128)(2,1)S(1)}) conditional(s32[]{:T(128)} %convert_element_type.6, bf16[8,24,3584]{2,1,0:T(8,128)(2,1)} %shard_map.95, bf16[8,24,3584]{2,1,0:T(8,128)(2,1)} %shard_map.95), branch_computations={%region_0.1_spmd, %region_1.2_spmd} | conditional | bytes 6881336 | solution.py:305
  5.5 6.9 %all-to-all-start.1 = ((bf16[8,24,3584]{2,1,0:T(8,128)(2,1)}), bf16[8,24,3584]{2,1,0:T(8,128)(2,1)}, u32[]{:S(2)}, u32[]{:S(2)}) async-start(bf16[8,24,3584]{2,1,0:T(8,128)(2,1)} %param.1), calls=%async_computation.1 | async-start | bytes 2752512 | tf_op jit(solution)/shard_map/cond/branch_1_fun/all_to_all | solution.py:232
  12.4 25.0 %all-to-all-done.1 = bf16[8,24,3584]{2,1,0:T(8,128)(2,1)} async-done(((bf16[8,24,3584]{2,1,0:T(8,128)(2,1)}), bf16[8,24,3584]{2,1,0:T(8,128)(2,1)}, u32[]{:S(2)}, u32[]{:S(2)}) %all-to-all-start.1) | async-done | bytes 1376288 | tf_op jit(solution)/shard_map/cond/branch_1_fun/all_to_all | solution.py:232
  37.3 1.3 copy.18
  38.7 7.3 %conditional.13 = (bf16[8,24,3072]{2,1,0:T(8,128)(2,1)}, bf16[2,192,256]{2,1,0:T(8,128)(2,1)}) conditional(s32[]{:T(128)} %convert_element_type.6, (f32[4,3072]{1,0:T(4,128)S(1)}, bf16[24,3072]{1,0:T(8,128)(2,1)S(1)}) %tuple.106, (bf16[8,24,3584]{2,1,0:T(8,128)(2,1)}, f32[2,128]{1,0:T(2,128)S(1)}, bf16[3,3072,256]{2,1,0:T(8,128)(2,1)}, ...), branch_computations={%region_2.3_spmd, %region_3.4_spmd} | conditional | bytes 16 | solution.py:305
  38.7 7.3 %branch_1_fun.18 = (bf16[192,3072]{1,0:T(8,128)(2,1)}, bf16[2,192,256]{2,1,0:T(8,128)(2,1)}) custom-call(f32[2,128]{1,0:T(2,128)S(1)} %get-tuple-element.214.gain_ref, bf16[3,3072,256]{2,1,0:T(8,128)(2,1)} %get-tuple-element.215.own_in, bf16[3,3072,256]{2,1,0:T(8,128)(2,1)} %get-tuple-element.216.other_in, ...), custom_call_target="tpu_custom_call" | custom-call | tf_op jit(solution)/shard_map/cond/branch_1_fun/pallas_call | solution.py:274
  46.0 6.6 %all-to-all-start.5 = ((bf16[8,24,3072]{2,1,0:T(8,128)(2,1)}), bf16[8,24,3072]{2,1,0:T(8,128)(2,1)}, u32[]{:S(2)}, u32[]{:S(2)}) async-start(bf16[8,24,3072]{2,1,0:T(8,128)(2,1)} %get-tuple-element.369), calls=%async_computation.5 | async-start | bytes 2359296 | tf_op jit(solution)/shard_map/all_to_all | solution.py:232
  52.6 18.0 %all-to-all-done.5 = bf16[8,24,3072]{2,1,0:T(8,128)(2,1)} async-done(((bf16[8,24,3072]{2,1,0:T(8,128)(2,1)}), bf16[8,24,3072]{2,1,0:T(8,128)(2,1)}, u32[]{:S(2)}, u32[]{:S(2)}) %all-to-all-start.5) | async-done | bytes 1179680 | tf_op jit(solution)/shard_map/all_to_all | solution.py:232
  70.5 3.5 %conditional.14 = (bf16[8,24,3072]{2,1,0:T(8,128)(2,1)}, bf16[2,192,256]{2,1,0:T(8,128)(2,1)}, bf16[24,3072]{1,0:T(8,128)(2,1)}) conditional(s32[]{:T(128)} %convert_element_type.6, (bf16[8,24,3072]{2,1,0:T(8,128)(2,1)}, f32[2,128]{1,0:T(2,128)S(1)}, bf16[3,3072,256]{2,1,0:T(8,128)(2,1)}, bf16[3,3072,256]{2,1,0:T(8,128)(2,1)}, ...), branch_computations={%region_4.5_spmd, %region_5.6_spmd} | conditional | bytes 24 | solution.py:305
  70.5 3.5 %branch_1_fun.19 = (bf16[24,3072]{1,0:T(8,128)(2,1)}, bf16[8,24,3072]{2,1,0:T(8,128)(2,1)}) custom-call(f32[4,3072]{1,0:T(4,128)S(1)} %get-tuple-element.232.params_ref, f32[4,3072]{1,0:T(4,128)S(1)} %get-tuple-element.233.next_ref, bf16[24,3072]{1,0:T(8,128)(2,1)S(1)} %get-tuple-element.234.x_ref, bf16[8,24,3072]{2,1,0:T(8,128)(2,1)} %get-tuple-element.235.parts_ref), custom_call_target="tpu_custom_call" | custom-call | tf_op jit(solution)/shard_map/cond/branch_1_fun/pallas_call | solution.py:298
  74.1 4.3 %all-to-all-start.6 = ((bf16[8,24,3072]{2,1,0:T(8,128)(2,1)}), bf16[8,24,3072]{2,1,0:T(8,128)(2,1)}, u32[]{:S(2)}, u32[]{:S(2)}) async-start(bf16[8,24,3072]{2,1,0:T(8,128)(2,1)} %get-tuple-element.371), calls=%async_computation.6 | async-start | bytes 2359296 | tf_op jit(solution)/shard_map/all_to_all | solution.py:232
  78.4 18.5 %all-to-all-done.6 = bf16[8,24,3072]{2,1,0:T(8,128)(2,1)} async-done(((bf16[8,24,3072]{2,1,0:T(8,128)(2,1)}), bf16[8,24,3072]{2,1,0:T(8,128)(2,1)}, u32[]{:S(2)}, u32[]{:S(2)}) %all-to-all-start.6) | async-done | bytes 1179680 | tf_op jit(solution)/shard_map/all_to_all | solution.py:232
  96.9 7.3 %conditional.15 = (bf16[8,24,3072]{2,1,0:T(8,128)(2,1)}, bf16[2,192,256]{2,1,0:T(8,128)(2,1)}, bf16[24,3072]{1,0:T(8,128)(2,1)}) conditional(s32[]{:T(128)} %convert_element_type.6, (f32[4,3072]{1,0:T(4,128)S(1)}, f32[4,3072]{1,0:T(4,128)S(1)}, bf16[24,3072]{1,0:T(8,128)(2,1)S(1)}, bf16[8,24,3072]{2,1,0:T(8,128)(2,1)}, ...), branch_computations={%region_6.7_spmd, %region_7.8_spmd} | conditional | bytes 24 | solution.py:305
  96.9 7.3 %branch_1_fun.21 = (bf16[192,3072]{1,0:T(8,128)(2,1)}, bf16[2,192,256]{2,1,0:T(8,128)(2,1)}) custom-call(f32[2,128]{1,0:T(2,128)S(1)} %get-tuple-element.245.gain_ref, bf16[3,3072,256]{2,1,0:T(8,128)(2,1)} %get-tuple-element.246.own_in, bf16[3,3072,256]{2,1,0:T(8,128)(2,1)} %get-tuple-element.247.other_in, ...), custom_call_target="tpu_custom_call" | custom-call | tf_op jit(solution)/shard_map/cond/branch_1_fun/pallas_call | solution.py:274
  104.2 4.4 %all-to-all-start.7 = ((bf16[8,24,3072]{2,1,0:T(8,128)(2,1)}), bf16[8,24,3072]{2,1,0:T(8,128)(2,1)}, u32[]{:S(2)}, u32[]{:S(2)}) async-start(bf16[8,24,3072]{2,1,0:T(8,128)(2,1)} %get-tuple-element.375), calls=%async_computation.7 | async-start | bytes 2359296 | tf_op jit(solution)/shard_map/all_to_all | solution.py:232
  108.7 18.0 %all-to-all-done.7 = bf16[8,24,3072]{2,1,0:T(8,128)(2,1)} async-done(((bf16[8,24,3072]{2,1,0:T(8,128)(2,1)}), bf16[8,24,3072]{2,1,0:T(8,128)(2,1)}, u32[]{:S(2)}, u32[]{:S(2)}) %all-to-all-start.7) | async-done | bytes 1179680 | tf_op jit(solution)/shard_map/all_to_all | solution.py:232
  126.7 2.1 conditional.16
  126.7 2.1 branch_1_fun.23
  128.8 3.4 %collective-permute-start.6 = (bf16[24,3072]{1,0:T(8,128)(2,1)}, bf16[24,3072]{1,0:T(8,128)(2,1)S(1)}, u32[]{:S(2)}, u32[]{:S(2)}) collective-permute-start(bf16[24,3072]{1,0:T(8,128)(2,1)} %get-tuple-element.442), channel_id=1, source_target_pairs={{0,16},{1,17},{2,18},{3,19},{4,20},{5,21},{6,22},{7,23}} | collective-permute-start | bytes 442376 | tf_op jit(solution)/shard_map/ppermute | solution.py:229
  132.3 2.9 %collective-permute-done.6 = bf16[24,3072]{1,0:T(8,128)(2,1)S(1)} collective-permute-done((bf16[24,3072]{1,0:T(8,128)(2,1)}, bf16[24,3072]{1,0:T(8,128)(2,1)S(1)}, u32[]{:S(2)}, u32[]{:S(2)}) %collective-permute-start.6) | collective-permute-done | bytes 147488 | tf_op jit(solution)/shard_map/ppermute | solution.py:229
  135.8 1.9 conditional.17
  135.8 1.9 branch_1_fun.25
  137.8 1.3 collective-permute-start.7
  139.1 6.6 %conditional.20 = (bf16[8,24,3072]{2,1,0:T(8,128)(2,1)}, bf16[2,192,256]{2,1,0:T(8,128)(2,1)S(1)}) conditional(s32[]{:T(128)} %convert_element_type.6, (f32[4,3072]{1,0:T(4,128)S(1)}, bf16[24,3072]{1,0:T(8,128)(2,1)}) %tuple.119, (bf16[8,24,3072]{2,1,0:T(8,128)(2,1)}, f32[2,128]{1,0:T(2,128)S(1)}, bf16[3,3072,256]{2,1,0:T(8,128)(2,1)}, ...), branch_computations={%region_16.17_spmd, %region_17.18_spmd} | conditional | bytes 16 | solution.py:305
  139.1 6.6 %branch_1_fun.27 = (bf16[192,3072]{1,0:T(8,128)(2,1)}, bf16[2,192,256]{2,1,0:T(8,128)(2,1)S(1)}) custom-call(f32[2,128]{1,0:T(2,128)S(1)} %get-tuple-element.275.gain_ref, bf16[3,3072,256]{2,1,0:T(8,128)(2,1)} %get-tuple-element.276.own_in, bf16[3,3072,256]{2,1,0:T(8,128)(2,1)} %get-tuple-element.277.other_in, ...), custom_call_target="tpu_custom_call" | custom-call | tf_op jit(solution)/shard_map/cond/branch_1_fun/pallas_call | solution.py:274
  145.7 3.7 %all-to-all-start.8 = ((bf16[8,24,3072]{2,1,0:T(8,128)(2,1)}), bf16[8,24,3072]{2,1,0:T(8,128)(2,1)S(1)}, u32[]{:S(2)}, u32[]{:S(2)}) async-start(bf16[8,24,3072]{2,1,0:T(8,128)(2,1)} %get-tuple-element.379), calls=%async_computation.8 | async-start | bytes 2359296 | tf_op jit(solution)/shard_map/all_to_all | solution.py:232
  149.5 4.9 %collective-permute-start.8 = (bf16[2,192,256]{2,1,0:T(8,128)(2,1)S(1)}, bf16[2,192,256]{2,1,0:T(8,128)(2,1)}, u32[]{:S(2)}, u32[]{:S(2)}) collective-permute-start(bf16[2,192,256]{2,1,0:T(8,128)(2,1)S(1)} %get-tuple-element.380), channel_id=1, source_target_pairs={{0,8},{1,9},{2,10},{3,11},{4,12},{5,13},{6,14},{7,15},{8,0},{9,1},... | collective-permute-start | bytes 589832 | tf_op jit(solution)/shard_map/ppermute | solution.py:225
  154.4 22.9 %all-to-all-done.8 = bf16[8,24,3072]{2,1,0:T(8,128)(2,1)S(1)} async-done(((bf16[8,24,3072]{2,1,0:T(8,128)(2,1)}), bf16[8,24,3072]{2,1,0:T(8,128)(2,1)S(1)}, u32[]{:S(2)}, u32[]{:S(2)}) %all-to-all-start.8) | async-done | bytes 1179680 | tf_op jit(solution)/shard_map/all_to_all | solution.py:232
  177.3 2.3 conditional.21
  177.3 2.3 branch_1_fun.28
  179.6 32.7 %all_to_all.52 = bf16[8,24,3072]{2,1,0:T(8,128)(2,1)S(1)} all-to-all(bf16[8,24,3072]{2,1,0:T(8,128)(2,1)} %get-tuple-element.382), channel_id=1, replica_groups=mesh['pipe'=4,'seq'=8] {'seq'}, dimensions={0} | all-to-all | bytes 2359296 | tf_op jit(solution)/shard_map/all_to_all | solution.py:232
  212.3 6.6 %conditional.22 = (bf16[8,24,3072]{2,1,0:T(8,128)(2,1)}, bf16[2,192,256]{2,1,0:T(8,128)(2,1)S(1)}, bf16[24,3072]{1,0:T(8,128)(2,1)S(1)}) conditional(s32[]{:T(128)} %convert_element_type.6, (f32[4,3072]{1,0:T(4,128)S(1)}, f32[4,3072]{1,0:T(4,128)S(1)}, bf16[24,3072]{1,0:T(8,128)(2,1)}, bf16[8,24,3072]{2,1,0:T(8,128)(2,1)S(1)}, ...), branch_computations={%region_20.21_spmd, %region_21.22_spmd} | conditional | bytes 24 | solution.py:305
  212.3 6.6 %branch_1_fun.30 = (bf16[192,3072]{1,0:T(8,128)(2,1)}, bf16[2,192,256]{2,1,0:T(8,128)(2,1)S(1)}) custom-call(f32[2,128]{1,0:T(2,128)S(1)} %get-tuple-element.306.gain_ref, bf16[3,3072,256]{2,1,0:T(8,128)(2,1)} %get-tuple-element.307.own_in, bf16[3,3072,256]{2,1,0:T(8,128)(2,1)} %get-tuple-element.308.other_in, ...), custom_call_target="tpu_custom_call" | custom-call | tf_op jit(solution)/shard_map/cond/branch_1_fun/pallas_call | solution.py:274
  219.6 4.5 %all-to-all-start.10 = ((bf16[8,24,3072]{2,1,0:T(8,128)(2,1)}), bf16[8,24,3072]{2,1,0:T(8,128)(2,1)S(1)}, u32[]{:S(2)}, u32[]{:S(2)}) async-start(bf16[8,24,3072]{2,1,0:T(8,128)(2,1)} %get-tuple-element.384), calls=%async_computation.10 | async-start | bytes 2359296 | tf_op jit(solution)/shard_map/all_to_all | solution.py:232
  224.1 1.4 collective-permute-done.9
  226.2 1.3 select_select_fusion
  227.5 23.2 %all-to-all-done.10 = bf16[8,24,3072]{2,1,0:T(8,128)(2,1)S(1)} async-done(((bf16[8,24,3072]{2,1,0:T(8,128)(2,1)}), bf16[8,24,3072]{2,1,0:T(8,128)(2,1)S(1)}, u32[]{:S(2)}, u32[]{:S(2)}) %all-to-all-start.10) | async-done | bytes 1179680 | tf_op jit(solution)/shard_map/all_to_all | solution.py:232
  250.7 14.2 %conditional.23 = (bf16[24,3072]{1,0:T(8,128)(2,1)S(1)}, bf16[8,24,1024]{2,1,0:T(8,128)(2,1)}) conditional(s32[]{:T(128)} %convert_element_type.6, (bf16[8,24,3072]{2,1,0:T(8,128)(2,1)S(1)}, f32[2,128]{1,0:T(2,128)S(1)}, bf16[3,3072,256]{2,1,0:T(8,128)(2,1)}, bf16[3,3072,256]{2,1,0:T(8,128)(2,1)}, bf16[1,256,3072]{2,1,0:T(8,128)(2,1)S(1)}, ...), branch_computations={%region_22.23_spmd, %region_23.24_spmd} | conditional | bytes 4522028 | solution.py:305
  250.7 0.8 branch_1_fun.33
  251.5 4.1 %all-to-all-start.4 = ((bf16[8,24,1024]{2,1,0:T(8,128)(2,1)}), bf16[8,24,1024]{2,1,0:T(8,128)(2,1)}, u32[]{:S(2)}, u32[]{:S(2)}) async-start(bf16[8,24,1024]{2,1,0:T(8,128)(2,1)} %bitcast.19), calls=%async_computation.4 | async-start | bytes 786432 | tf_op jit(solution)/shard_map/cond/branch_1_fun/all_to_all | solution.py:232
  255.8 9.1 %all-to-all-done.4 = bf16[8,24,1024]{2,1,0:T(8,128)(2,1)} async-done(((bf16[8,24,1024]{2,1,0:T(8,128)(2,1)}), bf16[8,24,1024]{2,1,0:T(8,128)(2,1)}, u32[]{:S(2)}, u32[]{:S(2)}) %all-to-all-start.4) | async-done | bytes 393248 | tf_op jit(solution)/shard_map/cond/branch_1_fun/all_to_all | solution.py:232
  264.9 0.9 select_select_fusion.2
  265.9 17.7 %collective-permute-start.10 = (bf16[24,3072]{1,0:T(8,128)(2,1)S(1)}, bf16[24,3072]{1,0:T(8,128)(2,1)S(1)}, u32[]{:S(2)}, u32[]{:S(2)}) collective-permute-start(bf16[24,3072]{1,0:T(8,128)(2,1)S(1)} %select_select_fusion.2), channel_id=1, source_target_pairs={{0,8},{1,9},{2,10},{3,11},{4,12},{5,13},{6,14},{7,15},{8,0},{9,1},... | collective-permute-start | bytes 442376 | tf_op jit(solution)/shard_map/ppermute | solution.py:225
  283.6 1.3 reshape.68
  285.4 0.8 broadcast_in_dim_reshape.3
  (71 shorter events, 4.9 us)
Async XLA Ops:
  0.6 2.6 copy-start
  1.5 3.3 %collective-permute-start = (f32[4,3072]{1,0:T(4,128)S(1)}, f32[4,3072]{1,0:T(4,128)S(1)}, u32[]{:S(2)}, u32[]{:S(2)}) collective-permute-start(f32[4,3072]{1,0:T(4,128)S(1)} %select_maximum_fusion.params_ref), channel_id=1, source_target_pairs={{0,8},{1,9},{2,10},{3,11},{4,12},{5,13},{6,14},{7,15},{8,0},{9,1},... | collective-permute-start | bytes 147464 | tf_op jit(solution)/shard_map/ppermute | solution.py:225
  2.0 2.9 %copy-start.1 = (bf16[1,256,3072]{2,1,0:T(8,128)(2,1)S(1)}, bf16[1,256,3072]{2,1,0:T(8,128)(2,1)}, u32[]{:S(2)}) copy-start(bf16[1,256,3072]{2,1,0:T(8,128)(2,1)} %param.38) | copy-start | bytes 4718596
  2.0 3.4 %copy-start.15 = (f32[1,3072]{1,0:T(1,128)S(1)}, f32[1,3072]{1,0:T(1,128)}, u32[]{:S(2)}) copy-start(f32[1,3072]{1,0:T(1,128)} %param.35) | copy-start | bytes 36868
  2.0 3.4 %copy-start.16 = (f32[1,3072]{1,0:T(1,128)S(1)}, f32[1,3072]{1,0:T(1,128)}, u32[]{:S(2)}) copy-start(f32[1,3072]{1,0:T(1,128)} %param.34) | copy-start | bytes 36868
  2.0 3.4 %copy-start.17 = (f32[1,3072]{1,0:T(1,128)S(1)}, f32[1,3072]{1,0:T(1,128)}, u32[]{:S(2)}) copy-start(f32[1,3072]{1,0:T(1,128)} %param.33) | copy-start | bytes 36868
  2.0 3.4 %copy-start.18 = (f32[1,2,128]{2,1,0:T(2,128)S(1)}, f32[1,2,128]{2,1,0:T(2,128)}, u32[]{:S(2)}) copy-start(f32[1,2,128]{2,1,0:T(2,128)} %param.36) | copy-start | bytes 3076
  4.8 33.9 %collective-permute-start.1 = (bf16[3,3072,256]{2,1,0:T(8,128)(2,1)}, bf16[3,3072,256]{2,1,0:T(8,128)(2,1)}, u32[]{:S(2)}, u32[]{:S(2)}) collective-permute-start(bf16[3,3072,256]{2,1,0:T(8,128)(2,1)} %bitcast.42), channel_id=1, source_target_pairs={{0,8},{1,9},{2,10},{3,11},{4,12},{5,13},{6,14},{7,15},{8,0},{9,1},... | collective-permute-start | bytes 14155784 | tf_op jit(solution)/shard_map/ppermute | solution.py:225
  4.9 33.8 %collective-permute-start.2 = (bf16[1,256,3072]{2,1,0:T(8,128)(2,1)S(1)}, bf16[1,256,3072]{2,1,0:T(8,128)(2,1)}, u32[]{:S(2)}, u32[]{:S(2)}) collective-permute-start(bf16[1,256,3072]{2,1,0:T(8,128)(2,1)S(1)} %copy-done.1), channel_id=1, source_target_pairs={{0,8},{1,9},{2,10},{3,11},{4,12},{5,13},{6,14},{7,15},{8,0},{9,1},... | collective-permute-start | bytes 4718600 | tf_op jit(solution)/shard_map/ppermute | solution.py:225
  5.5 31.9 %all-to-all-start.1 = ((bf16[8,24,3584]{2,1,0:T(8,128)(2,1)}), bf16[8,24,3584]{2,1,0:T(8,128)(2,1)}, u32[]{:S(2)}, u32[]{:S(2)}) async-start(bf16[8,24,3584]{2,1,0:T(8,128)(2,1)} %param.1), calls=%async_computation.1 | async-start | bytes 2752512 | tf_op jit(solution)/shard_map/cond/branch_1_fun/all_to_all | solution.py:232
  46.0 24.6 %all-to-all-start.5 = ((bf16[8,24,3072]{2,1,0:T(8,128)(2,1)}), bf16[8,24,3072]{2,1,0:T(8,128)(2,1)}, u32[]{:S(2)}, u32[]{:S(2)}) async-start(bf16[8,24,3072]{2,1,0:T(8,128)(2,1)} %get-tuple-element.369), calls=%async_computation.5 | async-start | bytes 2359296 | tf_op jit(solution)/shard_map/all_to_all | solution.py:232
  52.6 18.0 %collective-permute-start.3 = (bf16[2,192,256]{2,1,0:T(8,128)(2,1)}, bf16[2,192,256]{2,1,0:T(8,128)(2,1)}, u32[]{:S(2)}, u32[]{:S(2)}) collective-permute-start(bf16[2,192,256]{2,1,0:T(8,128)(2,1)} %get-tuple-element.370), channel_id=1, source_target_pairs={{0,8},{1,9},{2,10},{3,11},{4,12},{5,13},{6,14},{7,15},{8,0},{9,1},... | collective-permute-start | bytes 589832 | tf_op jit(solution)/shard_map/ppermute | solution.py:225
  74.1 22.8 %all-to-all-start.6 = ((bf16[8,24,3072]{2,1,0:T(8,128)(2,1)}), bf16[8,24,3072]{2,1,0:T(8,128)(2,1)}, u32[]{:S(2)}, u32[]{:S(2)}) async-start(bf16[8,24,3072]{2,1,0:T(8,128)(2,1)} %get-tuple-element.371), calls=%async_computation.6 | async-start | bytes 2359296 | tf_op jit(solution)/shard_map/all_to_all | solution.py:232
  78.3 18.6 %collective-permute-start.4 = (bf16[192,512]{1,0:T(8,128)(2,1)}, bf16[192,512]{1,0:T(8,128)(2,1)}, u32[]{:S(2)}, u32[]{:S(2)}) collective-permute-start(bf16[192,512]{1,0:T(8,128)(2,1)} %get-tuple-element.373), channel_id=1, source_target_pairs={{0,8},{1,9},{2,10},{3,11},{4,12},{5,13},{6,14},{7,15},{8,0},{9,1},... | collective-permute-start | bytes 589832 | tf_op jit(solution)/shard_map/ppermute | solution.py:225
  104.2 22.5 %copy-start.2 = (bf16[24,3072]{1,0:T(8,128)(2,1)S(1)}, bf16[24,3072]{1,0:T(8,128)(2,1)}, u32[]{:S(2)}) copy-start(bf16[24,3072]{1,0:T(8,128)(2,1)} %get-tuple-element.377) | copy-start | bytes 442372
  104.2 22.5 %all-to-all-start.7 = ((bf16[8,24,3072]{2,1,0:T(8,128)(2,1)}), bf16[8,24,3072]{2,1,0:T(8,128)(2,1)}, u32[]{:S(2)}, u32[]{:S(2)}) async-start(bf16[8,24,3072]{2,1,0:T(8,128)(2,1)} %get-tuple-element.375), calls=%async_computation.7 | async-start | bytes 2359296 | tf_op jit(solution)/shard_map/all_to_all | solution.py:232
  108.6 23.6 %collective-permute-start.5 = (bf16[2,192,256]{2,1,0:T(8,128)(2,1)}, bf16[2,192,256]{2,1,0:T(8,128)(2,1)}, u32[]{:S(2)}, u32[]{:S(2)}) collective-permute-start(bf16[2,192,256]{2,1,0:T(8,128)(2,1)} %get-tuple-element.376), channel_id=1, source_target_pairs={{0,8},{1,9},{2,10},{3,11},{4,12},{5,13},{6,14},{7,15},{8,0},{9,1},... | collective-permute-start | bytes 589832 | tf_op jit(solution)/shard_map/ppermute | solution.py:225
  128.8 6.4 %collective-permute-start.6 = (bf16[24,3072]{1,0:T(8,128)(2,1)}, bf16[24,3072]{1,0:T(8,128)(2,1)S(1)}, u32[]{:S(2)}, u32[]{:S(2)}) collective-permute-start(bf16[24,3072]{1,0:T(8,128)(2,1)} %get-tuple-element.442), channel_id=1, source_target_pairs={{0,16},{1,17},{2,18},{3,19},{4,20},{5,21},{6,22},{7,23}} | collective-permute-start | bytes 442376 | tf_op jit(solution)/shard_map/ppermute | solution.py:229
  135.2 0.6 copy-start.10
  137.8 1.4 copy-start.8
  137.8 1.3 collective-permute-start.7
  145.7 3.7 %copy-start.7 = (bf16[2,192,256]{2,1,0:T(8,128)(2,1)}, bf16[2,192,256]{2,1,0:T(8,128)(2,1)S(1)}, u32[]{:S(2)}) copy-start(bf16[2,192,256]{2,1,0:T(8,128)(2,1)S(1)} %get-tuple-element.380) | copy-start | bytes 589828
  145.7 31.5 %copy-start.11 = (bf16[24,3072]{1,0:T(8,128)(2,1)S(1)}, bf16[24,3072]{1,0:T(8,128)(2,1)}, u32[]{:S(2)}) copy-start(bf16[24,3072]{1,0:T(8,128)(2,1)} %copy-done.10) | copy-start | bytes 442372
  145.7 31.5 %all-to-all-start.8 = ((bf16[8,24,3072]{2,1,0:T(8,128)(2,1)}), bf16[8,24,3072]{2,1,0:T(8,128)(2,1)S(1)}, u32[]{:S(2)}, u32[]{:S(2)}) async-start(bf16[8,24,3072]{2,1,0:T(8,128)(2,1)} %get-tuple-element.379), calls=%async_computation.8 | async-start | bytes 2359296 | tf_op jit(solution)/shard_map/all_to_all | solution.py:232
  149.5 27.8 %collective-permute-start.8 = (bf16[2,192,256]{2,1,0:T(8,128)(2,1)S(1)}, bf16[2,192,256]{2,1,0:T(8,128)(2,1)}, u32[]{:S(2)}, u32[]{:S(2)}) collective-permute-start(bf16[2,192,256]{2,1,0:T(8,128)(2,1)S(1)} %get-tuple-element.380), channel_id=1, source_target_pairs={{0,8},{1,9},{2,10},{3,11},{4,12},{5,13},{6,14},{7,15},{8,0},{9,1},... | collective-permute-start | bytes 589832 | tf_op jit(solution)/shard_map/ppermute | solution.py:225
  218.9 0.7 copy-start.12
  218.9 5.1 %copy-start.14 = (bf16[2,192,256]{2,1,0:T(8,128)(2,1)}, bf16[2,192,256]{2,1,0:T(8,128)(2,1)S(1)}, u32[]{:S(2)}) copy-start(bf16[2,192,256]{2,1,0:T(8,128)(2,1)S(1)} %get-tuple-element.385) | copy-start | bytes 589828
  219.6 31.2 %all-to-all-start.10 = ((bf16[8,24,3072]{2,1,0:T(8,128)(2,1)}), bf16[8,24,3072]{2,1,0:T(8,128)(2,1)S(1)}, u32[]{:S(2)}, u32[]{:S(2)}) async-start(bf16[8,24,3072]{2,1,0:T(8,128)(2,1)} %get-tuple-element.384), calls=%async_computation.10 | async-start | bytes 2359296 | tf_op jit(solution)/shard_map/all_to_all | solution.py:232
  224.0 1.5 collective-permute-start.9
  225.5 0.7 copy-start.6
  250.7 4.9 %copy-start.5 = (bf16[24,3072]{1,0:T(8,128)(2,1)S(1)}, bf16[24,3072]{1,0:T(8,128)(2,1)}, u32[]{:S(2)}) copy-start(bf16[24,3072]{1,0:T(8,128)(2,1)} %get-tuple-element.330.x_ref) | copy-start | bytes 442372 | tf_op jit(solution)/shard_map/cond
  251.5 13.4 %all-to-all-start.4 = ((bf16[8,24,1024]{2,1,0:T(8,128)(2,1)}), bf16[8,24,1024]{2,1,0:T(8,128)(2,1)}, u32[]{:S(2)}, u32[]{:S(2)}) async-start(bf16[8,24,1024]{2,1,0:T(8,128)(2,1)} %bitcast.19), calls=%async_computation.4 | async-start | bytes 786432 | tf_op jit(solution)/shard_map/cond/branch_1_fun/all_to_all | solution.py:232
  265.9 20.4 %collective-permute-start.10 = (bf16[24,3072]{1,0:T(8,128)(2,1)S(1)}, bf16[24,3072]{1,0:T(8,128)(2,1)S(1)}, u32[]{:S(2)}, u32[]{:S(2)}) collective-permute-start(bf16[24,3072]{1,0:T(8,128)(2,1)S(1)} %select_select_fusion.2), channel_id=1, source_target_pairs={{0,8},{1,9},{2,10},{3,11},{4,12},{5,13},{6,14},{7,15},{8,0},{9,1},... | collective-permute-start | bytes 442376 | tf_op jit(solution)/shard_map/ppermute | solution.py:225
  283.6 2.6 copy-start.3
  283.6 2.6 copy-start.4
  283.6 2.6 copy-start.9

commit v5 on v4

--- a/solution.py
+++ b/solution.py
@@ -98,7 +98,7 @@
 
 
 def block_kernel(
-    turn, head_size, planes, gain_ref, own_in, other_in, own_out, other_out, blocks_ref, far_ref, *refs
+    head_size, planes, gain_ref, in_ref, out_weights_ref, blocks_ref, far_ref, *refs
 ):
     caches, refs = refs[:-11], refs[-11:]
     out_ref, kv_ref, blocks, far, w_in, w_out, parts, q_ref, in_sems, sems, part_sems = refs
@@ -106,17 +106,6 @@
     channels = w_out.shape[0]
     pieces = in_sems.shape[1]
     depth = width // pieces
-    mine = lax.rem(lax.axis_index("pipe"), 2) == turn
-
-    def weight_copies(source_in, source_out):
-        for part in (1, 2, 0):
-            for piece in range(pieces):
-                cut = pl.ds(piece * depth, depth)
-                pltpu.make_async_copy(
-                    source_in.at[part, cut], w_in.at[part, cut], in_sems.at[part, piece]
-                ).start()
-        pltpu.make_async_copy(source_out.at[0], w_out, sems.at[1]).start()
-
     fetch = pltpu.make_async_copy(blocks_ref.at[:, :width], blocks, sems.at[0])
     fetch.start()
     if len(far.shape) == 3:
@@ -126,21 +115,20 @@
         fetch_far = pltpu.make_async_copy(far_ref.at[:, begin:], far, sems.at[2])
     fetch_far.start()
 
-    @pl.when(mine)
-    def _():
-        weight_copies(own_in, own_out)
-
-    @pl.when(jnp.logical_not(mine))
-    def _():
-        weight_copies(other_in, other_out)
-
+    for part in (1, 2, 0):
+        for piece in range(pieces):
+            cut = pl.ds(piece * depth, depth)
+            pltpu.make_async_copy(
+                in_ref.at[part, cut], w_in.at[part, cut], in_sems.at[part, piece]
+            ).start()
+    pltpu.make_async_copy(out_weights_ref.at[0], w_out, sems.at[1]).start()
     fetch.wait()
     tokens = blocks[...]
     for part in (1, 2, 0):
         for piece in range(pieces):
             cut = pl.ds(piece * depth, depth)
             pltpu.make_async_copy(
-                own_in.at[part, cut], w_in.at[part, cut], in_sems.at[part, piece]
+                in_ref.at[part, cut], w_in.at[part, cut], in_sems.at[part, piece]
             ).wait()
         projected = jnp.dot(tokens, w_in[part], preferred_element_type=jnp.float32)
         if part == 2:
@@ -174,7 +162,7 @@
         put_cache((first, jnp.where(last, kv_ref[...], second[...])), parts, width)
         send(width, 4 * channels, steps)
     attended = attention(head_size, q_ref, kv_ref, far)
-    pltpu.make_async_copy(own_out.at[0], w_out, sems.at[1]).wait()
+    pltpu.make_async_copy(out_weights_ref.at[0], w_out, sems.at[1]).wait()
     tile = width // steps
     for step in range(steps):
         cut = slice(step * tile, (step + 1) * tile)
@@ -185,16 +173,53 @@
         copy.wait()
 
 
-def finish_kernel(params_ref, next_ref, x_ref, parts_ref, out_ref, *rest):
+def finish_kernel(shards, cached, params_ref, next_ref, x_ref, parts_ref, out_ref, *refs):
+    parts, part_sems, refs = refs[-2], refs[-1], refs[:-2]
     width = x_ref.shape[1]
-    update = jnp.sum(parts_ref[:, :, :width].astype(jnp.float32), axis=0)
+    fetches = [
+        pltpu.make_async_copy(parts_ref.at[shard, :, :width], parts.at[shard], part_sems.at[shard])
+        for shard in range(shards)
+    ]
+    for fetch in fetches:
+        fetch.start()
+    if cached:
+        cache_ref, caches, cache_sem = refs
+        fetch = pltpu.make_async_copy(parts_ref.at[:, :, width:], caches, cache_sem)
+        fetch.start()
+    update = jnp.zeros(x_ref.shape, jnp.float32)
+    for shard in range(shards):
+        fetches[shard].wait()
+        update = update + parts[shard].astype(jnp.float32)
     result = (x_ref[...].astype(jnp.float32) + params_ref[2:3, :] * update).astype(jnp.bfloat16)
     out_ref[...] = result
-    if rest:
-        blocks_ref, buffer, sems = rest
+    if cached:
+        fetch.wait()
+        place_cache(caches, cache_ref)
+    elif refs:
+        blocks_ref, buffer, sems = refs
         block = normalise(result.astype(jnp.float32), next_ref)
         for copy in spread_block(block, buffer, blocks_ref, sems):
             copy.wait()
+
+
+def place_cache(caches, out_ref):
+    channels = caches.shape[2] // 4
+    for patch in range(2):
+        for shard in range(caches.shape[0]):
+            begin = 2 * patch * channels
+            sides = [
+                caches[shard, :, begin + kind * channels : begin + (kind + 1) * channels].astype(
+                    jnp.float32
+                )
+                for kind in range(2)
+            ]
+            out_ref[patch, :, :, shard * channels : (shard + 1) * channels] = jnp.stack(
+                sides, axis=1
+            ).astype(jnp.bfloat16)
+
+
+def place_kernel(caches_ref, out_ref):
+    place_cache(caches_ref, out_ref)
 
 
 def blank_kernel(*refs):
@@ -255,6 +280,7 @@
     )
     other_in = swap(own_in)
     other_out = swap(own_out)
+    own, other = (own_in, own_out), (other_in, other_out)
     params = [jnp.where(core == turn, own_params, other_params) for turn in range(2)]
     gain_rows = [p[3, : 2 * head_size].reshape(2, head_size) for p in params]
     blocks_shape = bf16(seq, rows, width)
@@ -268,13 +294,13 @@
     flat = lambda blocks: blocks.reshape(tokens, blocks.shape[2])
     apart = lambda values: values.reshape(seq, rows, values.shape[1])
 
-    def block(blocks, far, turn, caches=()):
+    def block(blocks, far, turn, weights, caches=()):
         total = width + 2 * channels * len(caches)
         side = (2, tokens, channels) if far.ndim == 3 else (tokens, 2 * channels)
         out, pair = pl.pallas_call(
-            functools.partial(block_kernel, turn, head_size, planes),
+            functools.partial(block_kernel, head_size, planes),
             out_shape=(bf16(tokens, total), bf16(2, tokens, channels)),
-            in_specs=[VMEM] + [HBM] * 4 + [ANY] * 2 + [VMEM] * len(caches),
+            in_specs=[VMEM] + [HBM] * 2 + [ANY] * 2 + [VMEM] * len(caches),
             out_specs=(HBM, VMEM),
             scratch_shapes=[
                 pltpu.VMEM((tokens, width), jnp.bfloat16),
@@ -289,30 +315,48 @@
             ],
             compiler_params=params_of(32),
         )(
-            gain_rows[turn], own_in, other_in, own_out, other_out, flat(blocks), far, *caches
+            gain_rows[turn], *weights, flat(blocks), far, *caches
         )
         return apart(out), pair
 
-    def finish(x, parts, turn, onward):
-        shapes = (bf16(rows, width),) + (blocks_shape,) * onward
+    cache_shape = bf16(2, rows, 2, seq * channels)
+
+    def finish(x, parts, turn, onward, cached=False):
+        shapes = (bf16(rows, width),) + (blocks_shape,) * onward + (cache_shape,) * cached
+        scratch = spreading * onward
+        if cached:
+            scratch = [
+                pltpu.VMEM((seq, rows, 4 * channels), jnp.bfloat16), pltpu.SemaphoreType.DMA,
+            ]
         return pl.pallas_call(
-            finish_kernel, out_shape=shapes, in_specs=[VMEM] * 4,
-            out_specs=(VMEM,) + (HBM,) * onward,
-            scratch_shapes=spreading * onward, compiler_params=params_of(16),
+            functools.partial(finish_kernel, seq, cached),
+            out_shape=shapes, in_specs=[VMEM] * 3 + [ANY],
+            out_specs=(VMEM,) + (HBM,) * onward + (VMEM,) * cached,
+            scratch_shapes=scratch + [
+                pltpu.VMEM((seq, rows, width), jnp.bfloat16), pltpu.SemaphoreType.DMA((seq,)),
+            ],
+            compiler_params=params_of(16),
         )(params[turn], params[1 - turn], x, parts)
 
     early = core == 0
     either = lambda on_early, on_late: lax.cond(early, on_early, on_late)
 
+    pair_shape, block_shape = bf16(2, tokens, channels), bf16(rows, width)
+    side_shape = bf16(tokens, 2 * channels)
+
     def first_early():
-        return across(packed), blank(bf16(tokens, 2 * channels))[0]
+        received = across(packed)
+        side = flat(received)
+        parts, fresh = block(received, side, 0, own)
+        kept = lax.cond(
+            plane == 0, lambda: blank(side_shape)[0], lambda: side[:, width:]
+        )
+        return parts, fresh, kept
 
     def first_late():
-        return blank(bf16(*packed.shape))[0], flat(across(packed[:, :, width:]))
-
-    received, stale = either(first_early, first_late)
-    stales = [flat(received), swap(stale)]
-    pair_shape, block_shape = bf16(2, tokens, channels), bf16(rows, width)
+        side = flat(across(packed[:, :, width:]))
+        return norm(x, 0), blank(pair_shape)[0], side
+
     late_pair = None
     early_x, late_x = x, x
     blocks_out, sources = {}, {}
@@ -321,7 +365,7 @@
         crossing = layer > 0 and turn == 0
 
         def early_scatter():
-            parts, fresh = block(received, stales[turn], turn)
+            parts, fresh = block(received, stales[turn], turn, other if turn else own)
             return parts, fresh, blank(block_shape)[0]
 
         def late_gather():
@@ -337,7 +381,11 @@
             )
             blocks_out[layer - 1, 1] = late_x
             late_x = upward(late_x, level - 1, 1)
-        payload, pair, result = either(early_scatter, late_gather)
+        if layer == 0:
+            payload, pair, side = either(first_early, first_late)
+            stales = [side, swap(side)]
+        else:
+            payload, pair, result = either(early_scatter, late_gather)
         if turn:
             late_x = blocks_out[layer - 1, 1] = result
         sources[layer, 0] = pair
@@ -356,7 +404,7 @@
             return normed, blank(pair_shape)[0], result
 
         def late_scatter():
-            parts, fresh = block(received, got, turn)
+            parts, fresh = block(received, got, turn, own if turn else other)
             return parts, fresh, blank(block_shape)[0]
 
         if crossing:
@@ -398,12 +446,15 @@
             cache_kernel, out_shape=bf16(tokens, 4 * channels),
             in_specs=[VMEM] * 2, out_specs=VMEM, compiler_params=params_of(16),
         )(first_cache, second_cache)
-        return result, across(apart(packed))
+        cache = pl.pallas_call(
+            place_kernel, out_shape=cache_shape, in_specs=[VMEM], out_specs=VMEM,
+            compiler_params=params_of(16),
+        )(across(apart(packed)))
+        return result, cache
 
     def last_late():
-        parts, _ = block(received, got, last % 2, (first_cache, second_cache))
-        parts = across(parts)
-        return finish(late_x, parts, last % 2, 0)[0], parts[:, :, width:]
+        parts, _ = block(received, got, last % 2, own if last % 2 else other, (first_cache, second_cache))
+        return finish(late_x, across(parts), last % 2, 0, True)
 
     x, cache = either(last_early, last_late)
     blocks_out[last, 0] = blocks_out[last, 1] = x
@@ -416,8 +467,6 @@
         )
     )
     block_output = jnp.stack([jnp.where(early, mine, theirs), jnp.where(early, theirs, mine)])
-    cache = cache.reshape(seq, rows, 2, 2, channels)
-    cache = jnp.transpose(cache, (2, 1, 3, 0, 4)).reshape(2, rows, 2, seq * channels)
     return block_output[None], cache[None]
 
 

time: 288 us -> 307 us (1.066)
  the two profiles are of different devices: /device:TPU:0 before, /device:TPU:5 now
where the time goes in v5:
time: 307 us; the launch traced here: 306 us
  waiting for transfers between devices  102 us (33%)
  starting transfers between devices  89.6 us (29%)
  blocking collectives  57.6 us (19%)
  Pallas kernels  45.5 us (15%)
  other arithmetic  5.12 us (2%)
  local copies, waits for them, and re-layouts  4.15 us (1%)
    all_to_all x6, waiting for transfers between devices, across(): lax.all_to_all(blocks, 'seq', split_axis=0, concat_axis=0, tiled=True)  74.7 us
    ppermute x9, starting transfers between devices, swap(): return lax.ppermute(value, AXES, pairs)  59.3 us
    all_to_all x2, blocking collectives, across(): lax.all_to_all(blocks, 'seq', split_axis=0, concat_axis=0, tiled=True)  57.6 us
    all_to_all x6, starting transfers between devices, across(): lax.all_to_all(blocks, 'seq', split_axis=0, concat_axis=0, tiled=True)  28.4 us
    pallas_call x4, Pallas kernels, block(): pl.pallas_call(functools.partial(block_kernel, head_size, planes), out_sh...  27.7 us
    ppermute x2, waiting for transfers between devices, upward(): lax.ppermute(value, AXES, [(place(row, s), place(row + 2, s)) for s in ra...  21.8 us
    pallas_call x4, Pallas kernels, finish(): pl.pallas_call(functools.partial(finish_kernel, seq, cached), out_shape=s...  12.5 us
  transfers between devices with their start and end apart: 17, of which 9 were waited for; matrix products, arithmetic and copies ran while one was open for 1% of the time, Pallas kernels for 1%

profile of v5, /device:TPU:5, one launch (start us, length us, event | category | flops | bytes accessed | tf_op | source)
XLA Modules:
  0.0 305.8 jit_solution(11617733841649706231)
XLA Ops:
  2.2 1.1 slice_bitcast_fusion.cache_ref
  3.4 1.5 shard_map.95
  5.2 15.1 %conditional.12 = (bf16[8,24,3072]{2,1,0:T(8,128)(2,1)}, bf16[2,192,256]{2,1,0:T(8,128)(2,1)S(1)}, bf16[192,512]{1,0:T(8,128)(2,1)}) conditional(s32[]{:T(128)} %convert_element_type.9, (f32[4,3072]{1,0:T(4,128)S(1)}, bf16[24,3072]{1,0:T(8,128)(2,1)S(1)}, bf16[8,24,3584]{2,1,0:T(8,128)(2,1)}) %tuple.111, (bf16[8,24,3584]{2,1,0:T(8,128)(2,1)}, ...), branch_computations={%region_0.1_spmd, %region_1.4_spmd} | conditional | flops 2 | bytes 4522062 | solution.py:342
  5.2 1.6 slice.10
  6.8 5.5 %all-to-all-start = ((bf16[8,24,512]{2,1,0:T(8,128)(2,1)}), bf16[8,24,512]{2,1,0:T(8,128)(2,1)}, u32[]{:S(2)}, u32[]{:S(2)}) async-start(bf16[8,24,512]{2,1,0:T(8,128)(2,1)} %slice.10), calls=%async_computation | async-start | bytes 393216 | tf_op jit(solution)/shard_map/cond/branch_0_fun/all_to_all | solution.py:257
  12.3 1.4 branch_0_fun.16
  13.7 6.6 %all-to-all-done = bf16[8,24,512]{2,1,0:T(8,128)(2,1)} async-done(((bf16[8,24,512]{2,1,0:T(8,128)(2,1)}), bf16[8,24,512]{2,1,0:T(8,128)(2,1)}, u32[]{:S(2)}, u32[]{:S(2)}) %all-to-all-start) | async-done | bytes 196640 | tf_op jit(solution)/shard_map/cond/branch_0_fun/all_to_all | solution.py:257
  20.3 5.5 %all-to-all-start.5 = ((bf16[8,24,3072]{2,1,0:T(8,128)(2,1)}), bf16[8,24,3072]{2,1,0:T(8,128)(2,1)S(1)}, u32[]{:S(2)}, u32[]{:S(2)}) async-start(bf16[8,24,3072]{2,1,0:T(8,128)(2,1)} %get-tuple-element.331), calls=%async_computation.5 | async-start | bytes 2359296 | tf_op jit(solution)/shard_map/all_to_all | solution.py:257
  25.8 29.0 %collective-permute-start.2 = (bf16[1,256,3072]{2,1,0:T(8,128)(2,1)S(1)}, bf16[1,256,3072]{2,1,0:T(8,128)(2,1)}, u32[]{:S(2)}, u32[]{:S(2)}) collective-permute-start(bf16[1,256,3072]{2,1,0:T(8,128)(2,1)S(1)} %copy-done.1), channel_id=1, source_target_pairs={{0,8},{1,9},{2,10},{3,11},{4,12},{5,13},{6,14},{7,15},{8,0},{9,1},... | collective-permute-start | bytes 4718600 | tf_op jit(solution)/shard_map/ppermute | solution.py:250
  54.9 3.4 %collective-permute-done.3 = bf16[2,192,256]{2,1,0:T(8,128)(2,1)} collective-permute-done((bf16[2,192,256]{2,1,0:T(8,128)(2,1)S(1)}, bf16[2,192,256]{2,1,0:T(8,128)(2,1)}, u32[]{:S(2)}, u32[]{:S(2)}) %collective-permute-start.3) | collective-permute-done | bytes 196640 | tf_op jit(solution)/shard_map/ppermute | solution.py:250
  58.3 7.2 %conditional.13 = (bf16[8,24,3072]{2,1,0:T(8,128)(2,1)}, bf16[2,192,256]{2,1,0:T(8,128)(2,1)}, bf16[24,3072]{1,0:T(8,128)(2,1)S(1)}) conditional(s32[]{:T(128)} %convert_element_type.9, (bf16[8,24,3072]{2,1,0:T(8,128)(2,1)S(1)}, f32[2,128]{1,0:T(2,128)S(1)}, bf16[3,3072,256]{2,1,0:T(8,128)(2,1)}, bf16[1,256,3072]{2,1,0:T(8,128)(2,1)}, ...), branch_computations={%region_4.5_spmd, %region_5.6_spmd} | conditional | bytes 24 | solution.py:342
  58.3 7.2 %branch_0_fun.18 = (bf16[192,3072]{1,0:T(8,128)(2,1)}, bf16[2,192,256]{2,1,0:T(8,128)(2,1)}) custom-call(f32[2,128]{1,0:T(2,128)S(1)} %get-tuple-element.203.gain_ref, bf16[3,3072,256]{2,1,0:T(8,128)(2,1)} %get-tuple-element.204.in_ref, bf16[1,256,3072]{2,1,0:T(8,128)(2,1)} %get-tuple-element.205.out_weights_ref, bf16[192,3072]{1,0:T(8,128)(2,1)S(1)} %bitcast.43, ...), custom_call_target="tpu_custom_call" | custom-call | tf_op jit(solution)/shard_map/cond/branch_0_fun/pallas_call | solution.py:300
  65.5 5.7 %all-to-all-start.6 = ((bf16[8,24,3072]{2,1,0:T(8,128)(2,1)}), bf16[8,24,3072]{2,1,0:T(8,128)(2,1)S(1)}, u32[]{:S(2)}, u32[]{:S(2)}) async-start(bf16[8,24,3072]{2,1,0:T(8,128)(2,1)} %get-tuple-element.333), calls=%async_computation.6 | async-start | bytes 2359296 | tf_op jit(solution)/shard_map/all_to_all | solution.py:257
  71.2 8.5 %collective-permute-start.4 = (bf16[192,512]{1,0:T(8,128)(2,1)}, bf16[192,512]{1,0:T(8,128)(2,1)}, u32[]{:S(2)}, u32[]{:S(2)}) collective-permute-start(bf16[192,512]{1,0:T(8,128)(2,1)} %get-tuple-element.335), channel_id=1, source_target_pairs={{0,8},{1,9},{2,10},{3,11},{4,12},{5,13},{6,14},{7,15},{8,0},{9,1},... | collective-permute-start | bytes 589832 | tf_op jit(solution)/shard_map/ppermute | solution.py:250
  79.7 16.4 %all-to-all-done.6 = bf16[8,24,3072]{2,1,0:T(8,128)(2,1)S(1)} async-done(((bf16[8,24,3072]{2,1,0:T(8,128)(2,1)}), bf16[8,24,3072]{2,1,0:T(8,128)(2,1)S(1)}, u32[]{:S(2)}, u32[]{:S(2)}) %all-to-all-start.6) | async-done | bytes 1179680 | tf_op jit(solution)/shard_map/all_to_all | solution.py:257
  96.1 4.0 %conditional.14 = (bf16[8,24,3072]{2,1,0:T(8,128)(2,1)}, bf16[2,192,256]{2,1,0:T(8,128)(2,1)}, bf16[24,3072]{1,0:T(8,128)(2,1)}) conditional(s32[]{:T(128)} %convert_element_type.9, (f32[4,3072]{1,0:T(4,128)S(1)}, f32[4,3072]{1,0:T(4,128)S(1)}, bf16[24,3072]{1,0:T(8,128)(2,1)S(1)}, bf16[8,24,3072]{2,1,0:T(8,128)(2,1)S(1)}, ...), branch_computations={%region_6.7_spmd, %region_7.8_spmd} | conditional | bytes 24 | solution.py:342
  96.1 4.0 %branch_0_fun.20 = (bf16[24,3072]{1,0:T(8,128)(2,1)}, bf16[8,24,3072]{2,1,0:T(8,128)(2,1)}) custom-call(f32[4,3072]{1,0:T(4,128)S(1)} %get-tuple-element.216.params_ref, f32[4,3072]{1,0:T(4,128)S(1)} %get-tuple-element.217.next_ref, bf16[24,3072]{1,0:T(8,128)(2,1)S(1)} %get-tuple-element.218.x_ref, bf16[8,24,3072]{2,1,0:T(8,128)(2,1)S(1)} %get-tuple-element.219.parts_ref), custom_call_target="tpu_custom_call" | custom-call | tf_op jit(solution)/shard_map/cond/branch_0_fun/pallas_call | solution.py:331
  100.1 4.0 %all-to-all-start.7 = ((bf16[8,24,3072]{2,1,0:T(8,128)(2,1)}), bf16[8,24,3072]{2,1,0:T(8,128)(2,1)S(1)}, u32[]{:S(2)}, u32[]{:S(2)}) async-start(bf16[8,24,3072]{2,1,0:T(8,128)(2,1)} %get-tuple-element.337), calls=%async_computation.7 | async-start | bytes 2359296 | tf_op jit(solution)/shard_map/all_to_all | solution.py:257
  104.1 7.7 %collective-permute-start.5 = (bf16[2,192,256]{2,1,0:T(8,128)(2,1)}, bf16[2,192,256]{2,1,0:T(8,128)(2,1)}, u32[]{:S(2)}, u32[]{:S(2)}) collective-permute-start(bf16[2,192,256]{2,1,0:T(8,128)(2,1)} %get-tuple-element.338), channel_id=1, source_target_pairs={{0,8},{1,9},{2,10},{3,11},{4,12},{5,13},{6,14},{7,15},{8,0},{9,1},... | collective-permute-start | bytes 589832 | tf_op jit(solution)/shard_map/ppermute | solution.py:250
  111.8 17.1 %all-to-all-done.7 = bf16[8,24,3072]{2,1,0:T(8,128)(2,1)S(1)} async-done(((bf16[8,24,3072]{2,1,0:T(8,128)(2,1)}), bf16[8,24,3072]{2,1,0:T(8,128)(2,1)S(1)}, u32[]{:S(2)}, u32[]{:S(2)}) %all-to-all-start.7) | async-done | bytes 1179680 | tf_op jit(solution)/shard_map/all_to_all | solution.py:257
  129.7 7.2 %conditional.16 = (bf16[2,192,256]{2,1,0:T(8,128)(2,1)}, bf16[8,24,3072]{2,1,0:T(8,128)(2,1)S(1)}) conditional(s32[]{:T(128)} %convert_element_type.9, (bf16[8,24,3072]{2,1,0:T(8,128)(2,1)S(1)}, f32[2,128]{1,0:T(2,128)S(1)}, bf16[3,3072,256]{2,1,0:T(8,128)(2,1)}, bf16[1,256,3072]{2,1,0:T(8,128)(2,1)S(1)}, ...), branch_computations={%region_10.11_spmd, %region_11.12_spmd} | conditional | bytes 16 | solution.py:342
  129.8 7.0 %branch_0_fun.22 = (bf16[192,3072]{1,0:T(8,128)(2,1)S(1)}, bf16[2,192,256]{2,1,0:T(8,128)(2,1)}) custom-call(f32[2,128]{1,0:T(2,128)S(1)} %get-tuple-element.234.gain_ref, bf16[3,3072,256]{2,1,0:T(8,128)(2,1)} %get-tuple-element.235.in_ref, bf16[1,256,3072]{2,1,0:T(8,128)(2,1)S(1)} %get-tuple-element.236.out_weights_ref, bf16[192,3072]{1,0:T(8,128)(2,1)S(1)} %bitcast.42, ...), custom_call_target="tpu_custom_call" | custom-call | tf_op jit(solution)/shard_map/cond/branch_0_fun/pallas_call | solution.py:300
  136.9 2.8 conditional.18
  136.9 2.7 branch_0_fun.24
  139.6 1.3 collective-permute-start.7
  140.9 21.8 %collective-permute-done.7 = bf16[24,3072]{1,0:T(8,128)(2,1)} collective-permute-done((bf16[24,3072]{1,0:T(8,128)(2,1)S(1)}, bf16[24,3072]{1,0:T(8,128)(2,1)}, u32[]{:S(2)}, u32[]{:S(2)}) %collective-permute-start.7) | collective-permute-done | bytes 147488 | tf_op jit(solution)/shard_map/ppermute | solution.py:254
  162.7 2.4 conditional.19
  162.7 2.4 branch_0_fun.25
  165.1 3.6 %all-to-all-start.8 = ((bf16[8,24,3072]{2,1,0:T(8,128)(2,1)}), bf16[8,24,3072]{2,1,0:T(8,128)(2,1)S(1)}, u32[]{:S(2)}, u32[]{:S(2)}) async-start(bf16[8,24,3072]{2,1,0:T(8,128)(2,1)} %get-tuple-element.341), calls=%async_computation.8 | async-start | bytes 2359296 | tf_op jit(solution)/shard_map/all_to_all | solution.py:257
  168.7 8.4 %collective-permute-start.8 = (bf16[2,192,256]{2,1,0:T(8,128)(2,1)S(1)}, bf16[2,192,256]{2,1,0:T(8,128)(2,1)}, u32[]{:S(2)}, u32[]{:S(2)}) collective-permute-start(bf16[2,192,256]{2,1,0:T(8,128)(2,1)S(1)} %get-tuple-element.342), channel_id=1, source_target_pairs={{0,8},{1,9},{2,10},{3,11},{4,12},{5,13},{6,14},{7,15},{8,0},{9,1},... | collective-permute-start | bytes 589832 | tf_op jit(solution)/shard_map/ppermute | solution.py:250
  177.1 16.3 %all-to-all-done.8 = bf16[8,24,3072]{2,1,0:T(8,128)(2,1)S(1)} async-done(((bf16[8,24,3072]{2,1,0:T(8,128)(2,1)}), bf16[8,24,3072]{2,1,0:T(8,128)(2,1)S(1)}, u32[]{:S(2)}, u32[]{:S(2)}) %all-to-all-start.8) | async-done | bytes 1179680 | tf_op jit(solution)/shard_map/all_to_all | solution.py:257
  193.4 6.5 %conditional.20 = (bf16[8,24,3072]{2,1,0:T(8,128)(2,1)}, bf16[2,192,256]{2,1,0:T(8,128)(2,1)S(1)}, bf16[24,3072]{1,0:T(8,128)(2,1)}) conditional(s32[]{:T(128)} %convert_element_type.9, (bf16[8,24,3072]{2,1,0:T(8,128)(2,1)S(1)}, f32[2,128]{1,0:T(2,128)S(1)}, bf16[3,3072,256]{2,1,0:T(8,128)(2,1)}, bf16[1,256,3072]{2,1,0:T(8,128)(2,1)}, ...), branch_computations={%region_18.19_spmd, %region_19.20_spmd} | conditional | bytes 24 | solution.py:342
  193.4 6.5 %branch_0_fun.27 = (bf16[192,3072]{1,0:T(8,128)(2,1)}, bf16[2,192,256]{2,1,0:T(8,128)(2,1)S(1)}) custom-call(f32[2,128]{1,0:T(2,128)S(1)} %get-tuple-element.256.gain_ref, bf16[3,3072,256]{2,1,0:T(8,128)(2,1)} %get-tuple-element.257.in_ref, bf16[1,256,3072]{2,1,0:T(8,128)(2,1)} %get-tuple-element.258.out_weights_ref, bf16[192,3072]{1,0:T(8,128)(2,1)S(1)} %bitcast.44, ...), custom_call_target="tpu_custom_call" | custom-call | tf_op jit(solution)/shard_map/cond/branch_0_fun/pallas_call | solution.py:300
  200.0 31.6 %all_to_all.52 = bf16[8,24,3072]{2,1,0:T(8,128)(2,1)S(1)} all-to-all(bf16[8,24,3072]{2,1,0:T(8,128)(2,1)} %get-tuple-element.344), channel_id=1, replica_groups=mesh['pipe'=4,'seq'=8] {'seq'}, dimensions={0} | all-to-all | bytes 2359296 | tf_op jit(solution)/shard_map/all_to_all | solution.py:257
  231.5 4.4 %conditional.21 = (bf16[8,24,3072]{2,1,0:T(8,128)(2,1)}, bf16[2,192,256]{2,1,0:T(8,128)(2,1)}, bf16[24,3072]{1,0:T(8,128)(2,1)S(1)}) conditional(s32[]{:T(128)} %convert_element_type.9, (f32[4,3072]{1,0:T(4,128)S(1)}, f32[4,3072]{1,0:T(4,128)S(1)}, bf16[24,3072]{1,0:T(8,128)(2,1)}, bf16[8,24,3072]{2,1,0:T(8,128)(2,1)S(1)}, ...), branch_computations={%region_20.21_spmd, %region_21.22_spmd} | conditional | bytes 24 | solution.py:342
  231.5 4.2 %branch_0_fun.29 = (bf16[24,3072]{1,0:T(8,128)(2,1)S(1)}, bf16[8,24,3072]{2,1,0:T(8,128)(2,1)}) custom-call(f32[4,3072]{1,0:T(4,128)S(1)} %get-tuple-element.269.params_ref, f32[4,3072]{1,0:T(4,128)S(1)} %get-tuple-element.270.next_ref, bf16[24,3072]{1,0:T(8,128)(2,1)} %get-tuple-element.271.x_ref, bf16[8,24,3072]{2,1,0:T(8,128)(2,1)S(1)} %get-tuple-element.272.parts_ref), custom_call_target="tpu_custom_call" | custom-call | tf_op jit(solution)/shard_map/cond/branch_0_fun/pallas_call | solution.py:331
  236.6 4.1 %all-to-all-start.10 = ((bf16[8,24,3072]{2,1,0:T(8,128)(2,1)}), bf16[8,24,3072]{2,1,0:T(8,128)(2,1)S(1)}, u32[]{:S(2)}, u32[]{:S(2)}) async-start(bf16[8,24,3072]{2,1,0:T(8,128)(2,1)} %get-tuple-element.346), calls=%async_computation.10 | async-start | bytes 2359296 | tf_op jit(solution)/shard_map/all_to_all | solution.py:257
  240.8 4.6 %collective-permute-start.9 = (bf16[2,192,256]{2,1,0:T(8,128)(2,1)S(1)}, bf16[2,192,256]{2,1,0:T(8,128)(2,1)S(1)}, u32[]{:S(2)}, u32[]{:S(2)}) collective-permute-start(bf16[2,192,256]{2,1,0:T(8,128)(2,1)S(1)} %copy-done.12), channel_id=1, source_target_pairs={{0,8},{1,9},{2,10},{3,11},{4,12},{5,13},{6,14},{7,15},{8,0},{9,1},... | collective-permute-start | bytes 589832 | tf_op jit(solution)/shard_map/ppermute | solution.py:250
  245.4 1.1 collective-permute-done.9
  247.1 1.3 select_select_fusion
  248.4 18.3 %all-to-all-done.10 = bf16[8,24,3072]{2,1,0:T(8,128)(2,1)S(1)} async-done(((bf16[8,24,3072]{2,1,0:T(8,128)(2,1)}), bf16[8,24,3072]{2,1,0:T(8,128)(2,1)S(1)}, u32[]{:S(2)}, u32[]{:S(2)}) %all-to-all-start.10) | async-done | bytes 1179680 | tf_op jit(solution)/shard_map/all_to_all | solution.py:257
  266.7 34.7 %conditional.22 = ((bf16[24,3072]{1,0:T(8,128)(2,1)}, bf16[2,24,2,2048]{3,2,1,0:T(2,128)(2,1)S(1)})) conditional(s32[]{:T(128)} %convert_element_type.9, (bf16[8,24,3072]{2,1,0:T(8,128)(2,1)S(1)}, f32[2,128]{1,0:T(2,128)S(1)}, bf16[3,3072,256]{2,1,0:T(8,128)(2,1)}, bf16[1,256,3072]{2,1,0:T(8,128)(2,1)S(1)}, bf16[2,192,256]{2,1,0:T(8,128)(2,1)}, ...), branch_computations={%region_22.23_spmd, %region_23.24_spmd} | conditional | bytes 3735588 | solution.py:342
  266.7 7.1 %branch_0_fun.30 = (bf16[192,4096]{1,0:T(8,128)(2,1)S(1)}, bf16[2,192,256]{2,1,0:T(8,128)(2,1)}) custom-call(f32[2,128]{1,0:T(2,128)S(1)} %get-tuple-element.286.gain_ref, bf16[3,3072,256]{2,1,0:T(8,128)(2,1)} %get-tuple-element.287.in_ref, bf16[1,256,3072]{2,1,0:T(8,128)(2,1)S(1)} %get-tuple-element.288.out_weights_ref, bf16[192,3072]{1,0:T(8,128)(2,1)S(1)} %bitcast.41, ...), custom_call_target="tpu_custom_call" | custom-call | tf_op jit(solution)/shard_map/cond/branch_0_fun/pallas_call | solution.py:300
  273.8 26.1 %all_to_all.51.parts_ref = bf16[8,24,4096]{2,1,0:T(8,128)(2,1)S(1)} all-to-all(bf16[8,24,4096]{2,1,0:T(8,128)(2,1)S(1)} %bitcast.35), channel_id=1, replica_groups=mesh['pipe'=4,'seq'=8] {'seq'}, dimensions={0} | all-to-all | bytes 3145728 | tf_op jit(solution)/shard_map/cond/branch_0_fun/all_to_all | solution.py:257
  299.8 1.6 branch_0_fun.31
  301.4 1.2 select_select_fusion.2
  302.7 1.4 collective-permute-done.10
  304.0 1.0 select_bitcast_fusion.1
  (62 shorter events, 4.8 us)
Async XLA Ops:
  0.6 2.8 copy-start
  1.5 3.4 %collective-permute-start = (f32[4,3072]{1,0:T(4,128)S(1)}, f32[4,3072]{1,0:T(4,128)S(1)}, u32[]{:S(2)}, u32[]{:S(2)}) collective-permute-start(f32[4,3072]{1,0:T(4,128)S(1)} %select_maximum_fusion.params_ref), channel_id=1, source_target_pairs={{0,8},{1,9},{2,10},{3,11},{4,12},{5,13},{6,14},{7,15},{8,0},{9,1},... | collective-permute-start | bytes 147464 | tf_op jit(solution)/shard_map/ppermute | solution.py:250
  2.2 2.8 copy-start.13
  2.2 2.8 copy-start.14
  2.2 2.8 copy-start.15
  2.2 2.8 copy-start.16
  3.4 1.8 copy-start.1
  4.9 53.3 %collective-permute-start.1 = (bf16[3,3072,256]{2,1,0:T(8,128)(2,1)}, bf16[3,3072,256]{2,1,0:T(8,128)(2,1)}, u32[]{:S(2)}, u32[]{:S(2)}) collective-permute-start(bf16[3,3072,256]{2,1,0:T(8,128)(2,1)} %bitcast.36), channel_id=1, source_target_pairs={{0,8},{1,9},{2,10},{3,11},{4,12},{5,13},{6,14},{7,15},{8,0},{9,1},... | collective-permute-start | bytes 14155784 | tf_op jit(solution)/shard_map/ppermute | solution.py:250
  6.8 13.5 %all-to-all-start = ((bf16[8,24,512]{2,1,0:T(8,128)(2,1)}), bf16[8,24,512]{2,1,0:T(8,128)(2,1)}, u32[]{:S(2)}, u32[]{:S(2)}) async-start(bf16[8,24,512]{2,1,0:T(8,128)(2,1)} %slice.10), calls=%async_computation | async-start | bytes 393216 | tf_op jit(solution)/shard_map/cond/branch_0_fun/all_to_all | solution.py:257
  20.3 34.5 %copy-start.4 = (bf16[2,192,256]{2,1,0:T(8,128)(2,1)}, bf16[2,192,256]{2,1,0:T(8,128)(2,1)S(1)}, u32[]{:S(2)}) copy-start(bf16[2,192,256]{2,1,0:T(8,128)(2,1)S(1)} %get-tuple-element.332) | copy-start | bytes 589828
  20.3 34.6 %all-to-all-start.5 = ((bf16[8,24,3072]{2,1,0:T(8,128)(2,1)}), bf16[8,24,3072]{2,1,0:T(8,128)(2,1)S(1)}, u32[]{:S(2)}, u32[]{:S(2)}) async-start(bf16[8,24,3072]{2,1,0:T(8,128)(2,1)} %get-tuple-element.331), calls=%async_computation.5 | async-start | bytes 2359296 | tf_op jit(solution)/shard_map/all_to_all | solution.py:257
  25.8 32.5 %collective-permute-start.2 = (bf16[1,256,3072]{2,1,0:T(8,128)(2,1)S(1)}, bf16[1,256,3072]{2,1,0:T(8,128)(2,1)}, u32[]{:S(2)}, u32[]{:S(2)}) collective-permute-start(bf16[1,256,3072]{2,1,0:T(8,128)(2,1)S(1)} %copy-done.1), channel_id=1, source_target_pairs={{0,8},{1,9},{2,10},{3,11},{4,12},{5,13},{6,14},{7,15},{8,0},{9,1},... | collective-permute-start | bytes 4718600 | tf_op jit(solution)/shard_map/ppermute | solution.py:250
  54.8 3.4 %collective-permute-start.3 = (bf16[2,192,256]{2,1,0:T(8,128)(2,1)S(1)}, bf16[2,192,256]{2,1,0:T(8,128)(2,1)}, u32[]{:S(2)}, u32[]{:S(2)}) collective-permute-start(bf16[2,192,256]{2,1,0:T(8,128)(2,1)S(1)} %get-tuple-element.332), channel_id=1, source_target_pairs={{0,8},{1,9},{2,10},{3,11},{4,12},{5,13},{6,14},{7,15},{8,0},{9,1},... | collective-permute-start | bytes 589832 | tf_op jit(solution)/shard_map/ppermute | solution.py:250
  65.5 63.5 %copy-start.2 = (bf16[24,3072]{1,0:T(8,128)(2,1)}, bf16[24,3072]{1,0:T(8,128)(2,1)S(1)}, u32[]{:S(2)}) copy-start(bf16[24,3072]{1,0:T(8,128)(2,1)S(1)} %get-tuple-element.339) | copy-start | bytes 442372
  65.5 30.6 %all-to-all-start.6 = ((bf16[8,24,3072]{2,1,0:T(8,128)(2,1)}), bf16[8,24,3072]{2,1,0:T(8,128)(2,1)S(1)}, u32[]{:S(2)}, u32[]{:S(2)}) async-start(bf16[8,24,3072]{2,1,0:T(8,128)(2,1)} %get-tuple-element.333), calls=%async_computation.6 | async-start | bytes 2359296 | tf_op jit(solution)/shard_map/all_to_all | solution.py:257
  71.2 24.9 %collective-permute-start.4 = (bf16[192,512]{1,0:T(8,128)(2,1)}, bf16[192,512]{1,0:T(8,128)(2,1)}, u32[]{:S(2)}, u32[]{:S(2)}) collective-permute-start(bf16[192,512]{1,0:T(8,128)(2,1)} %get-tuple-element.335), channel_id=1, source_target_pairs={{0,8},{1,9},{2,10},{3,11},{4,12},{5,13},{6,14},{7,15},{8,0},{9,1},... | collective-permute-start | bytes 589832 | tf_op jit(solution)/shard_map/ppermute | solution.py:250
  100.1 28.8 %all-to-all-start.7 = ((bf16[8,24,3072]{2,1,0:T(8,128)(2,1)}), bf16[8,24,3072]{2,1,0:T(8,128)(2,1)S(1)}, u32[]{:S(2)}, u32[]{:S(2)}) async-start(bf16[8,24,3072]{2,1,0:T(8,128)(2,1)} %get-tuple-element.337), calls=%async_computation.7 | async-start | bytes 2359296 | tf_op jit(solution)/shard_map/all_to_all | solution.py:257
  104.1 25.6 %collective-permute-start.5 = (bf16[2,192,256]{2,1,0:T(8,128)(2,1)}, bf16[2,192,256]{2,1,0:T(8,128)(2,1)}, u32[]{:S(2)}, u32[]{:S(2)}) collective-permute-start(bf16[2,192,256]{2,1,0:T(8,128)(2,1)} %get-tuple-element.338), channel_id=1, source_target_pairs={{0,8},{1,9},{2,10},{3,11},{4,12},{5,13},{6,14},{7,15},{8,0},{9,1},... | collective-permute-start | bytes 589832 | tf_op jit(solution)/shard_map/ppermute | solution.py:250
  128.9 0.7 copy-start.10
  128.9 0.7 collective-permute-start.6
  139.6 23.1 %copy-start.7 = (bf16[24,3072]{1,0:T(8,128)(2,1)}, bf16[24,3072]{1,0:T(8,128)(2,1)S(1)}, u32[]{:S(2)}) copy-start(bf16[24,3072]{1,0:T(8,128)(2,1)S(1)} %get-tuple-element.408) | copy-start | bytes 442372
  139.6 23.1 %collective-permute-start.7 = (bf16[24,3072]{1,0:T(8,128)(2,1)S(1)}, bf16[24,3072]{1,0:T(8,128)(2,1)}, u32[]{:S(2)}, u32[]{:S(2)}) collective-permute-start(bf16[24,3072]{1,0:T(8,128)(2,1)S(1)} %get-tuple-element.408), channel_id=1, source_target_pairs={{8,24},{9,25},{10,26},{11,27},{12,28},{13,29},{14,30},{15,31}} | collective-permute-start | bytes 442376 | tf_op jit(solution)/shard_map/ppermute | solution.py:254
  165.1 3.6 %copy-start.5 = (bf16[2,192,256]{2,1,0:T(8,128)(2,1)}, bf16[2,192,256]{2,1,0:T(8,128)(2,1)S(1)}, u32[]{:S(2)}) copy-start(bf16[2,192,256]{2,1,0:T(8,128)(2,1)S(1)} %get-tuple-element.342) | copy-start | bytes 589828
  165.1 28.3 %all-to-all-start.8 = ((bf16[8,24,3072]{2,1,0:T(8,128)(2,1)}), bf16[8,24,3072]{2,1,0:T(8,128)(2,1)S(1)}, u32[]{:S(2)}, u32[]{:S(2)}) async-start(bf16[8,24,3072]{2,1,0:T(8,128)(2,1)} %get-tuple-element.341), calls=%async_computation.8 | async-start | bytes 2359296 | tf_op jit(solution)/shard_map/all_to_all | solution.py:257
  168.7 24.7 %collective-permute-start.8 = (bf16[2,192,256]{2,1,0:T(8,128)(2,1)S(1)}, bf16[2,192,256]{2,1,0:T(8,128)(2,1)}, u32[]{:S(2)}, u32[]{:S(2)}) collective-permute-start(bf16[2,192,256]{2,1,0:T(8,128)(2,1)S(1)} %get-tuple-element.342), channel_id=1, source_target_pairs={{0,8},{1,9},{2,10},{3,11},{4,12},{5,13},{6,14},{7,15},{8,0},{9,1},... | collective-permute-start | bytes 589832 | tf_op jit(solution)/shard_map/ppermute | solution.py:250
  200.0 31.6 %copy-start.11 = (bf16[2,192,256]{2,1,0:T(8,128)(2,1)}, bf16[2,192,256]{2,1,0:T(8,128)(2,1)S(1)}, u32[]{:S(2)}) copy-start(bf16[2,192,256]{2,1,0:T(8,128)(2,1)S(1)} %get-tuple-element.345) | copy-start | bytes 589828
  236.0 0.7 copy-start.8
  236.0 4.8 %copy-start.12 = (bf16[2,192,256]{2,1,0:T(8,128)(2,1)S(1)}, bf16[2,192,256]{2,1,0:T(8,128)(2,1)}, u32[]{:S(2)}) copy-start(bf16[2,192,256]{2,1,0:T(8,128)(2,1)} %get-tuple-element.347) | copy-start | bytes 589828
  236.6 30.0 %all-to-all-start.10 = ((bf16[8,24,3072]{2,1,0:T(8,128)(2,1)}), bf16[8,24,3072]{2,1,0:T(8,128)(2,1)S(1)}, u32[]{:S(2)}, u32[]{:S(2)}) async-start(bf16[8,24,3072]{2,1,0:T(8,128)(2,1)} %get-tuple-element.346), calls=%async_computation.10 | async-start | bytes 2359296 | tf_op jit(solution)/shard_map/all_to_all | solution.py:257
  240.8 5.7 %collective-permute-start.9 = (bf16[2,192,256]{2,1,0:T(8,128)(2,1)S(1)}, bf16[2,192,256]{2,1,0:T(8,128)(2,1)S(1)}, u32[]{:S(2)}, u32[]{:S(2)}) collective-permute-start(bf16[2,192,256]{2,1,0:T(8,128)(2,1)S(1)} %copy-done.12), channel_id=1, source_target_pairs={{0,8},{1,9},{2,10},{3,11},{4,12},{5,13},{6,14},{7,15},{8,0},{9,1},... | collective-permute-start | bytes 589832 | tf_op jit(solution)/shard_map/ppermute | solution.py:250
  246.5 0.7 copy-start.6
  273.8 26.1 %copy-start.9 = (bf16[24,3072]{1,0:T(8,128)(2,1)S(1)}, bf16[24,3072]{1,0:T(8,128)(2,1)}, u32[]{:S(2)}) copy-start(bf16[24,3072]{1,0:T(8,128)(2,1)} %get-tuple-element.285.x_ref) | copy-start | bytes 442372 | tf_op jit(solution)/shard_map/cond
  301.4 4.4 %copy-start.17 = (bf16[2,24,2,2048]{3,2,1,0:T(2,128)(2,1)}, bf16[2,24,2,2048]{3,2,1,0:T(2,128)(2,1)S(1)}, u32[]{:S(2)}) copy-start(bf16[2,24,2,2048]{3,2,1,0:T(2,128)(2,1)S(1)} %get-tuple-element.356) | copy-start | bytes 1179652
  302.6 1.4 collective-permute-start.10

commit v6 on v4

--- a/solution.py
+++ b/solution.py
@@ -230,6 +230,22 @@
 
     def across(blocks):
         return lax.all_to_all(blocks, "seq", split_axis=0, concat_axis=0, tiled=True)
+
+    fast = 1
+    while fast * fast * 4 <= seq and seq % (fast * 2) == 0:
+        fast *= 2
+    columns = [list(range(start, seq, fast)) for start in range(fast)]
+    stepwise = fast == 2
+
+    def gather_stepwise(copies):
+        ours = lax.all_to_all(
+            copies, "seq", split_axis=0, concat_axis=0, tiled=True, axis_index_groups=columns
+        )
+        pairs = [(place(row, s), place(row, s ^ 1)) for row in range(0, sections, 2) for s in range(seq)]
+        theirs = lax.ppermute(ours, AXES, pairs)
+        lower = lax.rem(lax.axis_index("seq"), 2) == 0
+        both = [jnp.where(lower, ours, theirs), jnp.where(lower, theirs, ours)]
+        return jnp.stack(both, axis=1).reshape(seq, rows, width)
 
     def blank(*shapes):
         return pl.pallas_call(blank_kernel, out_shape=shapes, out_specs=(ANY,) * len(shapes))()
@@ -293,8 +309,8 @@
         )
         return apart(out), pair
 
-    def finish(x, parts, turn, onward):
-        shapes = (bf16(rows, width),) + (blocks_shape,) * onward
+    def finish(x, parts, turn, onward, copies=seq):
+        shapes = (bf16(rows, width),) + (bf16(copies, rows, width),) * onward
         return pl.pallas_call(
             finish_kernel, out_shape=shapes, in_specs=[VMEM] * 4,
             out_specs=(VMEM,) + (HBM,) * onward,
@@ -352,12 +368,15 @@
         def early_gather():
             if crossing:
                 return norm(early_x, 1 - turn), blank(pair_shape)[0], blank(block_shape)[0]
+            if stepwise:
+                result, normed = finish(early_x, received, turn, 1, seq // fast)
+                return gather_stepwise(normed), blank(pair_shape)[0], result
             result, normed = finish(early_x, received, turn, 1)
-            return normed, blank(pair_shape)[0], result
+            return across(normed), blank(pair_shape)[0], result
 
         def late_scatter():
             parts, fresh = block(received, got, turn)
-            return parts, fresh, blank(block_shape)[0]
+            return (parts if crossing else across(parts)), fresh, blank(block_shape)[0]
 
         if crossing:
             early_x = either(
@@ -373,7 +392,7 @@
             active = pipe == jnp.where(early, 2 * level + 2, 2 * level + 1)
             received = lax.cond(active, across, lambda _: blank(blocks_shape)[0], payload)
         else:
-            received = across(payload)
+            received = payload
 
     def by_plane(values):
         chosen = values[0]

time: 288 us -> 310 us (1.076)
  the two profiles are of different devices: /device:TPU:0 before, /device:TPU:7 now
where the time goes in v6:
time: 310 us; the launch traced here: 309 us
  starting transfers between devices  140 us (45%)
  waiting for transfers between devices  78.6 us (25%)
  Pallas kernels  43.5 us (14%)
  blocking collectives  29.5 us (10%)
  local copies, waits for them, and re-layouts  9.63 us (3%)
  other arithmetic  5.58 us (2%)
    ppermute x9, starting transfers between devices, swap(): return lax.ppermute(value, AXES, pairs)  104 us
    all_to_all x7, waiting for transfers between devices, across(): lax.all_to_all(blocks, 'seq', split_axis=0, concat_axis=0, tiled=True)  50.1 us
    all_to_all x7, starting transfers between devices, across(): lax.all_to_all(blocks, 'seq', split_axis=0, concat_axis=0, tiled=True)  34.7 us
    pallas_call x4, Pallas kernels, block(): pl.pallas_call(functools.partial(block_kernel, turn, head_size, planes),...  29.9 us
    all_to_all x1, blocking collectives, across(): lax.all_to_all(blocks, 'seq', split_axis=0, concat_axis=0, tiled=True)  29.5 us
    ppermute x2, waiting for transfers between devices, upward(): lax.ppermute(value, AXES, [(place(row, s), place(row + 2, s)) for s in ra...  24.1 us
    pallas_call x4, Pallas kernels, finish(): pl.pallas_call(finish_kernel, out_shape=shapes, in_specs=[VMEM] * 4, out_...  8.44 us
  transfers between devices with their start and end apart: 18, of which 8 were waited for; matrix products, arithmetic and copies ran while one was open for 3% of the time, Pallas kernels for 3%

profile of v6, /device:TPU:7, one launch (start us, length us, event | category | flops | bytes accessed | tf_op | source)
XLA Modules:
  0.0 308.6 jit_solution(17243906362824076221)
XLA Ops:
  0.6 0.8 select_maximum_fusion.params_ref
  2.3 1.2 slice_bitcast_fusion.cache_ref
  3.5 1.5 shard_map.95
  5.7 16.0 %conditional.12 = (bf16[8,24,3584]{2,1,0:T(8,128)(2,1)}, bf16[192,512]{1,0:T(8,128)(2,1)}, bf16[192,3584]{1,0:T(8,128)(2,1)S(1)}) conditional(s32[]{:T(128)} %convert_element_type.6, bf16[8,24,3584]{2,1,0:T(8,128)(2,1)} %shard_map.95, bf16[8,24,3584]{2,1,0:T(8,128)(2,1)} %shard_map.95), branch_computations={%region_0.1_spmd, %region_1.2_spmd} | conditional | bytes 6881336 | solution.py:321
  5.7 1.6 slice.10
  7.3 5.8 %all-to-all-start = ((bf16[8,24,512]{2,1,0:T(8,128)(2,1)}), bf16[8,24,512]{2,1,0:T(8,128)(2,1)}, u32[]{:S(2)}, u32[]{:S(2)}) async-start(bf16[8,24,512]{2,1,0:T(8,128)(2,1)} %slice.10), calls=%async_computation | async-start | bytes 393216 | tf_op jit(solution)/shard_map/cond/branch_0_fun/all_to_all | solution.py:232
  13.1 1.3 copy.18
  14.4 7.3 %all-to-all-done = bf16[8,24,512]{2,1,0:T(8,128)(2,1)} async-done(((bf16[8,24,512]{2,1,0:T(8,128)(2,1)}), bf16[8,24,512]{2,1,0:T(8,128)(2,1)}, u32[]{:S(2)}, u32[]{:S(2)}) %all-to-all-start) | async-done | bytes 196640 | tf_op jit(solution)/shard_map/cond/branch_0_fun/all_to_all | solution.py:232
  21.7 1.4 conditional.13
  21.7 1.4 branch_0_fun.18
  23.1 4.5 %all-to-all-start.9 = ((bf16[8,24,3072]{2,1,0:T(8,128)(2,1)}), bf16[8,24,3072]{2,1,0:T(8,128)(2,1)}, u32[]{:S(2)}, u32[]{:S(2)}) async-start(bf16[8,24,3072]{2,1,0:T(8,128)(2,1)} %get-tuple-element.369), calls=%async_computation.9 | async-start | bytes 2359296 | tf_op jit(solution)/shard_map/all_to_all | solution.py:232
  27.6 24.7 %collective-permute-start.5 = (bf16[2,192,256]{2,1,0:T(8,128)(2,1)}, bf16[2,192,256]{2,1,0:T(8,128)(2,1)}, u32[]{:S(2)}, u32[]{:S(2)}) collective-permute-start(bf16[2,192,256]{2,1,0:T(8,128)(2,1)} %get-tuple-element.370), channel_id=1, source_target_pairs={{0,8},{1,9},{2,10},{3,11},{4,12},{5,13},{6,14},{7,15},{8,0},{9,1},... | collective-permute-start | bytes 589832 | tf_op jit(solution)/shard_map/ppermute | solution.py:225
  52.3 1.4 collective-permute-done.5
  53.7 34.2 %conditional.14 = (bf16[8,24,3072]{2,1,0:T(8,128)(2,1)}, bf16[2,192,256]{2,1,0:T(8,128)(2,1)}, bf16[24,3072]{1,0:T(8,128)(2,1)}) conditional(s32[]{:T(128)} %convert_element_type.6, (bf16[8,24,3072]{2,1,0:T(8,128)(2,1)}, f32[2,128]{1,0:T(2,128)S(1)}, bf16[3,3072,256]{2,1,0:T(8,128)(2,1)}, bf16[3,3072,256]{2,1,0:T(8,128)(2,1)}, ...), branch_computations={%region_4.5_spmd, %region_5.6_spmd} | conditional | flops 1179657 | bytes 10616989 | solution.py:321
  53.7 7.3 %branch_0_fun.20 = (bf16[192,3072]{1,0:T(8,128)(2,1)}, bf16[2,192,256]{2,1,0:T(8,128)(2,1)}) custom-call(f32[2,128]{1,0:T(2,128)S(1)} %get-tuple-element.223.gain_ref, bf16[3,3072,256]{2,1,0:T(8,128)(2,1)} %get-tuple-element.224.own_in, bf16[3,3072,256]{2,1,0:T(8,128)(2,1)} %get-tuple-element.225.other_in, ...), custom_call_target="tpu_custom_call" | custom-call | tf_op jit(solution)/shard_map/cond/branch_0_fun/pallas_call | solution.py:290
  61.0 5.4 %all-to-all-start.2 = ((bf16[8,24,3072]{2,1,0:T(8,128)(2,1)}), bf16[8,24,3072]{2,1,0:T(8,128)(2,1)}, u32[]{:S(2)}, u32[]{:S(2)}) async-start(bf16[8,24,3072]{2,1,0:T(8,128)(2,1)} %bitcast.6), calls=%async_computation.2 | async-start | bytes 2359296 | tf_op jit(solution)/shard_map/cond/branch_0_fun/all_to_all | solution.py:232
  66.5 21.4 %all-to-all-done.2 = bf16[8,24,3072]{2,1,0:T(8,128)(2,1)} async-done(((bf16[8,24,3072]{2,1,0:T(8,128)(2,1)}), bf16[8,24,3072]{2,1,0:T(8,128)(2,1)}, u32[]{:S(2)}, u32[]{:S(2)}) %all-to-all-start.2) | async-done | bytes 1179680 | tf_op jit(solution)/shard_map/cond/branch_0_fun/all_to_all | solution.py:232
  87.9 3.5 %conditional.15 = (bf16[8,24,3072]{2,1,0:T(8,128)(2,1)}, bf16[2,192,256]{2,1,0:T(8,128)(2,1)}, bf16[24,3072]{1,0:T(8,128)(2,1)}) conditional(s32[]{:T(128)} %convert_element_type.6, (f32[4,3072]{1,0:T(4,128)S(1)}, f32[4,3072]{1,0:T(4,128)S(1)}, bf16[24,3072]{1,0:T(8,128)(2,1)S(1)}, bf16[8,24,3072]{2,1,0:T(8,128)(2,1)}, ...), branch_computations={%region_6.7_spmd, %region_7.8_spmd} | conditional | bytes 24 | solution.py:321
  87.9 3.5 %branch_0_fun.22 = (bf16[24,3072]{1,0:T(8,128)(2,1)}, bf16[8,24,3072]{2,1,0:T(8,128)(2,1)}) custom-call(f32[4,3072]{1,0:T(4,128)S(1)} %get-tuple-element.238.params_ref, f32[4,3072]{1,0:T(4,128)S(1)} %get-tuple-element.239.next_ref, bf16[24,3072]{1,0:T(8,128)(2,1)S(1)} %get-tuple-element.240.x_ref, bf16[8,24,3072]{2,1,0:T(8,128)(2,1)} %get-tuple-element.241.parts_ref), custom_call_target="tpu_custom_call" | custom-call | tf_op jit(solution)/shard_map/cond/branch_0_fun/pallas_call | solution.py:314
  91.4 4.9 %all-to-all-start.10 = ((bf16[8,24,3072]{2,1,0:T(8,128)(2,1)}), bf16[8,24,3072]{2,1,0:T(8,128)(2,1)}, u32[]{:S(2)}, u32[]{:S(2)}) async-start(bf16[8,24,3072]{2,1,0:T(8,128)(2,1)} %get-tuple-element.375), calls=%async_computation.10 | async-start | bytes 2359296 | tf_op jit(solution)/shard_map/all_to_all | solution.py:232
  96.3 25.3 %collective-permute-start.7 = (bf16[2,192,256]{2,1,0:T(8,128)(2,1)}, bf16[2,192,256]{2,1,0:T(8,128)(2,1)}, u32[]{:S(2)}, u32[]{:S(2)}) collective-permute-start(bf16[2,192,256]{2,1,0:T(8,128)(2,1)} %get-tuple-element.376), channel_id=1, source_target_pairs={{0,8},{1,9},{2,10},{3,11},{4,12},{5,13},{6,14},{7,15},{8,0},{9,1},... | collective-permute-start | bytes 589832 | tf_op jit(solution)/shard_map/ppermute | solution.py:225
  123.7 7.1 %conditional.17 = (bf16[2,192,256]{2,1,0:T(8,128)(2,1)}, bf16[8,24,3072]{2,1,0:T(8,128)(2,1)S(1)}) conditional(s32[]{:T(128)} %convert_element_type.6, (bf16[8,24,3072]{2,1,0:T(8,128)(2,1)}, f32[2,128]{1,0:T(2,128)S(1)}, bf16[3,3072,256]{2,1,0:T(8,128)(2,1)}, bf16[3,3072,256]{2,1,0:T(8,128)(2,1)}, bf16[1,256,3072]{2,1,0:T(8,128)(2,1)S(1)}, ...), branch_computations={%region_10.11_spmd, %region_11.12_spmd} | conditional | bytes 16 | solution.py:321
  123.7 7.1 %branch_0_fun.24 = (bf16[192,3072]{1,0:T(8,128)(2,1)S(1)}, bf16[2,192,256]{2,1,0:T(8,128)(2,1)}) custom-call(f32[2,128]{1,0:T(2,128)S(1)} %get-tuple-element.258.gain_ref, bf16[3,3072,256]{2,1,0:T(8,128)(2,1)} %get-tuple-element.259.own_in, bf16[3,3072,256]{2,1,0:T(8,128)(2,1)} %get-tuple-element.260.other_in, ...), custom_call_target="tpu_custom_call" | custom-call | tf_op jit(solution)/shard_map/cond/branch_0_fun/pallas_call | solution.py:290
  130.9 1.6 conditional.19
  130.9 1.5 branch_0_fun.26
  132.5 1.3 collective-permute-start.9
  133.8 24.1 %collective-permute-done.9 = bf16[24,3072]{1,0:T(8,128)(2,1)} collective-permute-done((bf16[24,3072]{1,0:T(8,128)(2,1)S(1)}, bf16[24,3072]{1,0:T(8,128)(2,1)}, u32[]{:S(2)}, u32[]{:S(2)}) %collective-permute-start.9) | collective-permute-done | bytes 147488 | tf_op jit(solution)/shard_map/ppermute | solution.py:229
  157.9 2.3 conditional.20
  157.9 2.3 branch_0_fun.27
  160.2 4.1 %all-to-all-start.11 = ((bf16[8,24,3072]{2,1,0:T(8,128)(2,1)}), bf16[8,24,3072]{2,1,0:T(8,128)(2,1)S(1)}, u32[]{:S(2)}, u32[]{:S(2)}) async-start(bf16[8,24,3072]{2,1,0:T(8,128)(2,1)} %get-tuple-element.379), calls=%async_computation.11 | async-start | bytes 2359296 | tf_op jit(solution)/shard_map/all_to_all | solution.py:232
  164.3 28.0 %collective-permute-start.10 = (bf16[2,192,256]{2,1,0:T(8,128)(2,1)S(1)}, bf16[2,192,256]{2,1,0:T(8,128)(2,1)S(1)}, u32[]{:S(2)}, u32[]{:S(2)}) collective-permute-start(bf16[2,192,256]{2,1,0:T(8,128)(2,1)S(1)} %get-tuple-element.380), channel_id=1, source_target_pairs={{0,8},{1,9},{2,10},{3,11},{4,12},{5,13},{6,14},{7,15},{8,0},{9,1},... | collective-permute-start | bytes 589832 | tf_op jit(solution)/shard_map/ppermute | solution.py:225
  192.4 1.1 collective-permute-done.10
  193.4 34.2 %conditional.21 = (bf16[8,24,3072]{2,1,0:T(8,128)(2,1)S(1)}, bf16[2,192,256]{2,1,0:T(8,128)(2,1)}, bf16[24,3072]{1,0:T(8,128)(2,1)S(1)}) conditional(s32[]{:T(128)} %convert_element_type.6, (bf16[8,24,3072]{2,1,0:T(8,128)(2,1)S(1)}, f32[2,128]{1,0:T(2,128)S(1)}, bf16[3,3072,256]{2,1,0:T(8,128)(2,1)}, bf16[3,3072,256]{2,1,0:T(8,128)(2,1)}, ...), branch_computations={%region_18.19_spmd, %region_19.20_spmd} | conditional | flops 1179657 | bytes 10616989 | solution.py:321
  193.4 7.4 %branch_0_fun.29 = (bf16[192,3072]{1,0:T(8,128)(2,1)}, bf16[2,192,256]{2,1,0:T(8,128)(2,1)}) custom-call(f32[2,128]{1,0:T(2,128)S(1)} %get-tuple-element.284.gain_ref, bf16[3,3072,256]{2,1,0:T(8,128)(2,1)} %get-tuple-element.285.own_in, bf16[3,3072,256]{2,1,0:T(8,128)(2,1)} %get-tuple-element.286.other_in, ...), custom_call_target="tpu_custom_call" | custom-call | tf_op jit(solution)/shard_map/cond/branch_0_fun/pallas_call | solution.py:290
  200.8 5.5 %all-to-all-start.4 = ((bf16[8,24,3072]{2,1,0:T(8,128)(2,1)}), bf16[8,24,3072]{2,1,0:T(8,128)(2,1)S(1)}, u32[]{:S(2)}, u32[]{:S(2)}) async-start(bf16[8,24,3072]{2,1,0:T(8,128)(2,1)} %bitcast.17), calls=%async_computation.4 | async-start | bytes 2359296 | tf_op jit(solution)/shard_map/cond/branch_0_fun/all_to_all | solution.py:232
  206.3 21.3 %all-to-all-done.4 = bf16[8,24,3072]{2,1,0:T(8,128)(2,1)S(1)} async-done(((bf16[8,24,3072]{2,1,0:T(8,128)(2,1)}), bf16[8,24,3072]{2,1,0:T(8,128)(2,1)S(1)}, u32[]{:S(2)}, u32[]{:S(2)}) %all-to-all-start.4) | async-done | bytes 1179680 | tf_op jit(solution)/shard_map/cond/branch_0_fun/all_to_all | solution.py:232
  227.6 2.8 conditional.22
  227.6 2.5 branch_0_fun.31
  231.0 4.5 %all-to-all-start.12 = ((bf16[8,24,3072]{2,1,0:T(8,128)(2,1)}), bf16[8,24,3072]{2,1,0:T(8,128)(2,1)S(1)}, u32[]{:S(2)}, u32[]{:S(2)}) async-start(bf16[8,24,3072]{2,1,0:T(8,128)(2,1)} %get-tuple-element.384), calls=%async_computation.12 | async-start | bytes 2359296 | tf_op jit(solution)/shard_map/all_to_all | solution.py:232
  235.5 24.3 %collective-permute-start.11 = (bf16[2,192,256]{2,1,0:T(8,128)(2,1)}, bf16[2,192,256]{2,1,0:T(8,128)(2,1)S(1)}, u32[]{:S(2)}, u32[]{:S(2)}) collective-permute-start(bf16[2,192,256]{2,1,0:T(8,128)(2,1)} %get-tuple-element.385), channel_id=1, source_target_pairs={{0,8},{1,9},{2,10},{3,11},{4,12},{5,13},{6,14},{7,15},{8,0},{9,1},... | collective-permute-start | bytes 589832 | tf_op jit(solution)/shard_map/ppermute | solution.py:225
  259.8 1.3 collective-permute-done.11
  261.8 2.0 select_select_fusion
  263.8 39.3 %conditional.23 = (bf16[24,3072]{1,0:T(8,128)(2,1)}, bf16[8,24,1024]{2,1,0:T(8,128)(2,1)}) conditional(s32[]{:T(128)} %convert_element_type.6, (bf16[8,24,3072]{2,1,0:T(8,128)(2,1)S(1)}, f32[2,128]{1,0:T(2,128)S(1)}, bf16[3,3072,256]{2,1,0:T(8,128)(2,1)}, bf16[3,3072,256]{2,1,0:T(8,128)(2,1)}, bf16[1,256,3072]{2,1,0:T(8,128)(2,1)S(1)}, ...), branch_computations={%region_22.23_spmd, %region_23.24_spmd} | conditional | bytes 4522028 | solution.py:321
  263.8 8.1 %branch_0_fun.32 = (bf16[192,4096]{1,0:T(8,128)(2,1)S(1)}, bf16[2,192,256]{2,1,0:T(8,128)(2,1)}) custom-call(f32[2,128]{1,0:T(2,128)S(1)} %get-tuple-element.318.gain_ref, bf16[3,3072,256]{2,1,0:T(8,128)(2,1)} %get-tuple-element.319.own_in, bf16[3,3072,256]{2,1,0:T(8,128)(2,1)} %get-tuple-element.320.other_in, ...), custom_call_target="tpu_custom_call" | custom-call | tf_op jit(solution)/shard_map/cond/branch_0_fun/pallas_call | solution.py:290
  271.9 29.5 %all_to_all.59.parts_ref = bf16[8,24,4096]{2,1,0:T(8,128)(2,1)S(1)} all-to-all(bf16[8,24,4096]{2,1,0:T(8,128)(2,1)S(1)} %bitcast.51), channel_id=1, replica_groups=mesh['pipe'=4,'seq'=8] {'seq'}, dimensions={0} | all-to-all | bytes 3145728 | tf_op jit(solution)/shard_map/cond/branch_0_fun/all_to_all | solution.py:232
  303.1 1.0 select_select_fusion.2
  304.2 1.3 reshape.74
  306.8 1.0 select_bitcast_fusion.5
  (70 shorter events, 8.6 us)
Async XLA Ops:
  0.6 2.8 copy-start
  1.5 3.5 %collective-permute-start.2 = (f32[4,3072]{1,0:T(4,128)S(1)}, f32[4,3072]{1,0:T(4,128)S(1)}, u32[]{:S(2)}, u32[]{:S(2)}) collective-permute-start(f32[4,3072]{1,0:T(4,128)S(1)} %select_maximum_fusion.params_ref), channel_id=1, source_target_pairs={{0,8},{1,9},{2,10},{3,11},{4,12},{5,13},{6,14},{7,15},{8,0},{9,1},... | collective-permute-start | bytes 147464 | tf_op jit(solution)/shard_map/ppermute | solution.py:225
  2.2 2.9 copy-start.1
  2.2 3.3 %copy-start.13 = (f32[1,3072]{1,0:T(1,128)S(1)}, f32[1,3072]{1,0:T(1,128)}, u32[]{:S(2)}) copy-start(f32[1,3072]{1,0:T(1,128)} %param.35) | copy-start | bytes 36868
  2.2 3.3 %copy-start.14 = (f32[1,3072]{1,0:T(1,128)S(1)}, f32[1,3072]{1,0:T(1,128)}, u32[]{:S(2)}) copy-start(f32[1,3072]{1,0:T(1,128)} %param.34) | copy-start | bytes 36868
  2.2 3.3 %copy-start.15 = (f32[1,3072]{1,0:T(1,128)S(1)}, f32[1,3072]{1,0:T(1,128)}, u32[]{:S(2)}) copy-start(f32[1,3072]{1,0:T(1,128)} %param.33) | copy-start | bytes 36868
  2.2 3.3 %copy-start.16 = (f32[1,2,128]{2,1,0:T(2,128)S(1)}, f32[1,2,128]{2,1,0:T(2,128)}, u32[]{:S(2)}) copy-start(f32[1,2,128]{2,1,0:T(2,128)} %param.36) | copy-start | bytes 3076
  5.0 16.7 %collective-permute-start.3 = (bf16[3,3072,256]{2,1,0:T(8,128)(2,1)}, bf16[3,3072,256]{2,1,0:T(8,128)(2,1)}, u32[]{:S(2)}, u32[]{:S(2)}) collective-permute-start(bf16[3,3072,256]{2,1,0:T(8,128)(2,1)} %bitcast.52), channel_id=1, source_target_pairs={{0,8},{1,9},{2,10},{3,11},{4,12},{5,13},{6,14},{7,15},{8,0},{9,1},... | collective-permute-start | bytes 14155784 | tf_op jit(solution)/shard_map/ppermute | solution.py:225
  5.1 16.6 %collective-permute-start.4 = (bf16[1,256,3072]{2,1,0:T(8,128)(2,1)S(1)}, bf16[1,256,3072]{2,1,0:T(8,128)(2,1)}, u32[]{:S(2)}, u32[]{:S(2)}) collective-permute-start(bf16[1,256,3072]{2,1,0:T(8,128)(2,1)S(1)} %copy-done.1), channel_id=1, source_target_pairs={{0,8},{1,9},{2,10},{3,11},{4,12},{5,13},{6,14},{7,15},{8,0},{9,1},... | collective-permute-start | bytes 4718600 | tf_op jit(solution)/shard_map/ppermute | solution.py:225
  7.3 14.4 %all-to-all-start = ((bf16[8,24,512]{2,1,0:T(8,128)(2,1)}), bf16[8,24,512]{2,1,0:T(8,128)(2,1)}, u32[]{:S(2)}, u32[]{:S(2)}) async-start(bf16[8,24,512]{2,1,0:T(8,128)(2,1)} %slice.10), calls=%async_computation | async-start | bytes 393216 | tf_op jit(solution)/shard_map/cond/branch_0_fun/all_to_all | solution.py:232
  23.1 29.2 %all-to-all-start.9 = ((bf16[8,24,3072]{2,1,0:T(8,128)(2,1)}), bf16[8,24,3072]{2,1,0:T(8,128)(2,1)}, u32[]{:S(2)}, u32[]{:S(2)}) async-start(bf16[8,24,3072]{2,1,0:T(8,128)(2,1)} %get-tuple-element.369), calls=%async_computation.9 | async-start | bytes 2359296 | tf_op jit(solution)/shard_map/all_to_all | solution.py:232
  27.6 26.1 %collective-permute-start.5 = (bf16[2,192,256]{2,1,0:T(8,128)(2,1)}, bf16[2,192,256]{2,1,0:T(8,128)(2,1)}, u32[]{:S(2)}, u32[]{:S(2)}) collective-permute-start(bf16[2,192,256]{2,1,0:T(8,128)(2,1)} %get-tuple-element.370), channel_id=1, source_target_pairs={{0,8},{1,9},{2,10},{3,11},{4,12},{5,13},{6,14},{7,15},{8,0},{9,1},... | collective-permute-start | bytes 589832 | tf_op jit(solution)/shard_map/ppermute | solution.py:225
  52.3 35.6 %collective-permute-start.6 = (bf16[192,512]{1,0:T(8,128)(2,1)}, bf16[192,512]{1,0:T(8,128)(2,1)}, u32[]{:S(2)}, u32[]{:S(2)}) collective-permute-start(bf16[192,512]{1,0:T(8,128)(2,1)} %get-tuple-element.373), channel_id=1, source_target_pairs={{0,8},{1,9},{2,10},{3,11},{4,12},{5,13},{6,14},{7,15},{8,0},{9,1},... | collective-permute-start | bytes 589832 | tf_op jit(solution)/shard_map/ppermute | solution.py:225
  61.0 26.9 %all-to-all-start.2 = ((bf16[8,24,3072]{2,1,0:T(8,128)(2,1)}), bf16[8,24,3072]{2,1,0:T(8,128)(2,1)}, u32[]{:S(2)}, u32[]{:S(2)}) async-start(bf16[8,24,3072]{2,1,0:T(8,128)(2,1)} %bitcast.6), calls=%async_computation.2 | async-start | bytes 2359296 | tf_op jit(solution)/shard_map/cond/branch_0_fun/all_to_all | solution.py:232
  91.4 30.2 %copy-start.2 = (bf16[24,3072]{1,0:T(8,128)(2,1)S(1)}, bf16[24,3072]{1,0:T(8,128)(2,1)}, u32[]{:S(2)}) copy-start(bf16[24,3072]{1,0:T(8,128)(2,1)} %get-tuple-element.377) | copy-start | bytes 442372
  91.4 30.2 %all-to-all-start.10 = ((bf16[8,24,3072]{2,1,0:T(8,128)(2,1)}), bf16[8,24,3072]{2,1,0:T(8,128)(2,1)}, u32[]{:S(2)}, u32[]{:S(2)}) async-start(bf16[8,24,3072]{2,1,0:T(8,128)(2,1)} %get-tuple-element.375), calls=%async_computation.10 | async-start | bytes 2359296 | tf_op jit(solution)/shard_map/all_to_all | solution.py:232
  96.3 26.7 %collective-permute-start.7 = (bf16[2,192,256]{2,1,0:T(8,128)(2,1)}, bf16[2,192,256]{2,1,0:T(8,128)(2,1)}, u32[]{:S(2)}, u32[]{:S(2)}) collective-permute-start(bf16[2,192,256]{2,1,0:T(8,128)(2,1)} %get-tuple-element.376), channel_id=1, source_target_pairs={{0,8},{1,9},{2,10},{3,11},{4,12},{5,13},{6,14},{7,15},{8,0},{9,1},... | collective-permute-start | bytes 589832 | tf_op jit(solution)/shard_map/ppermute | solution.py:225
  121.7 1.4 collective-permute-start.8
  123.1 0.7 copy-start.10
  132.5 25.4 %copy-start.8 = (bf16[24,3072]{1,0:T(8,128)(2,1)}, bf16[24,3072]{1,0:T(8,128)(2,1)S(1)}, u32[]{:S(2)}) copy-start(bf16[24,3072]{1,0:T(8,128)(2,1)S(1)} %get-tuple-element.448) | copy-start | bytes 442372
  132.5 25.4 %collective-permute-start.9 = (bf16[24,3072]{1,0:T(8,128)(2,1)S(1)}, bf16[24,3072]{1,0:T(8,128)(2,1)}, u32[]{:S(2)}, u32[]{:S(2)}) collective-permute-start(bf16[24,3072]{1,0:T(8,128)(2,1)S(1)} %get-tuple-element.448), channel_id=1, source_target_pairs={{8,24},{9,25},{10,26},{11,27},{12,28},{13,29},{14,30},{15,31}} | collective-permute-start | bytes 442376 | tf_op jit(solution)/shard_map/ppermute | solution.py:229
  160.2 4.1 %copy-start.7 = (bf16[2,192,256]{2,1,0:T(8,128)(2,1)}, bf16[2,192,256]{2,1,0:T(8,128)(2,1)S(1)}, u32[]{:S(2)}) copy-start(bf16[2,192,256]{2,1,0:T(8,128)(2,1)S(1)} %get-tuple-element.380) | copy-start | bytes 589828
  160.2 32.2 %all-to-all-start.11 = ((bf16[8,24,3072]{2,1,0:T(8,128)(2,1)}), bf16[8,24,3072]{2,1,0:T(8,128)(2,1)S(1)}, u32[]{:S(2)}, u32[]{:S(2)}) async-start(bf16[8,24,3072]{2,1,0:T(8,128)(2,1)} %get-tuple-element.379), calls=%async_computation.11 | async-start | bytes 2359296 | tf_op jit(solution)/shard_map/all_to_all | solution.py:232
  164.3 29.1 %collective-permute-start.10 = (bf16[2,192,256]{2,1,0:T(8,128)(2,1)S(1)}, bf16[2,192,256]{2,1,0:T(8,128)(2,1)S(1)}, u32[]{:S(2)}, u32[]{:S(2)}) collective-permute-start(bf16[2,192,256]{2,1,0:T(8,128)(2,1)S(1)} %get-tuple-element.380), channel_id=1, source_target_pairs={{0,8},{1,9},{2,10},{3,11},{4,12},{5,13},{6,14},{7,15},{8,0},{9,1},... | collective-permute-start | bytes 589832 | tf_op jit(solution)/shard_map/ppermute | solution.py:225
  200.8 26.8 %all-to-all-start.4 = ((bf16[8,24,3072]{2,1,0:T(8,128)(2,1)}), bf16[8,24,3072]{2,1,0:T(8,128)(2,1)S(1)}, u32[]{:S(2)}, u32[]{:S(2)}) async-start(bf16[8,24,3072]{2,1,0:T(8,128)(2,1)} %bitcast.17), calls=%async_computation.4 | async-start | bytes 2359296 | tf_op jit(solution)/shard_map/cond/branch_0_fun/all_to_all | solution.py:232
  227.6 36.2 %copy-start.4 = (bf16[24,3072]{1,0:T(8,128)(2,1)}, bf16[24,3072]{1,0:T(8,128)(2,1)S(1)}, u32[]{:S(2)}) copy-start(bf16[24,3072]{1,0:T(8,128)(2,1)S(1)} %get-tuple-element.381) | copy-start | bytes 442372
  230.4 0.7 copy-start.11
  231.0 32.7 %all-to-all-start.12 = ((bf16[8,24,3072]{2,1,0:T(8,128)(2,1)}), bf16[8,24,3072]{2,1,0:T(8,128)(2,1)S(1)}, u32[]{:S(2)}, u32[]{:S(2)}) async-start(bf16[8,24,3072]{2,1,0:T(8,128)(2,1)} %get-tuple-element.384), calls=%async_computation.12 | async-start | bytes 2359296 | tf_op jit(solution)/shard_map/all_to_all | solution.py:232
  235.5 25.6 %collective-permute-start.11 = (bf16[2,192,256]{2,1,0:T(8,128)(2,1)}, bf16[2,192,256]{2,1,0:T(8,128)(2,1)S(1)}, u32[]{:S(2)}, u32[]{:S(2)}) collective-permute-start(bf16[2,192,256]{2,1,0:T(8,128)(2,1)} %get-tuple-element.385), channel_id=1, source_target_pairs={{0,8},{1,9},{2,10},{3,11},{4,12},{5,13},{6,14},{7,15},{8,0},{9,1},... | collective-permute-start | bytes 589832 | tf_op jit(solution)/shard_map/ppermute | solution.py:225
  261.1 0.7 copy-start.6
  271.9 30.4 %copy-start.12 = (bf16[24,3072]{1,0:T(8,128)(2,1)S(1)}, bf16[24,3072]{1,0:T(8,128)(2,1)}, u32[]{:S(2)}) copy-start(bf16[24,3072]{1,0:T(8,128)(2,1)} %get-tuple-element.317.x_ref) | copy-start | bytes 442372 | tf_op jit(solution)/shard_map/cond
  304.1 2.7 collective-permute-start.12
  304.2 2.6 copy-start.3
  304.2 2.6 copy-start.5
  304.2 2.6 copy-start.9

commit v7 on v4

--- a/solution.py
+++ b/solution.py
@@ -98,7 +98,7 @@
 
 
 def block_kernel(
-    turn, head_size, planes, gain_ref, own_in, other_in, own_out, other_out, blocks_ref, far_ref, *refs
+    head_size, planes, gain_ref, in_ref, out_weights_ref, blocks_ref, far_ref, *refs
 ):
     caches, refs = refs[:-11], refs[-11:]
     out_ref, kv_ref, blocks, far, w_in, w_out, parts, q_ref, in_sems, sems, part_sems = refs
@@ -106,17 +106,6 @@
     channels = w_out.shape[0]
     pieces = in_sems.shape[1]
     depth = width // pieces
-    mine = lax.rem(lax.axis_index("pipe"), 2) == turn
-
-    def weight_copies(source_in, source_out):
-        for part in (1, 2, 0):
-            for piece in range(pieces):
-                cut = pl.ds(piece * depth, depth)
-                pltpu.make_async_copy(
-                    source_in.at[part, cut], w_in.at[part, cut], in_sems.at[part, piece]
-                ).start()
-        pltpu.make_async_copy(source_out.at[0], w_out, sems.at[1]).start()
-
     fetch = pltpu.make_async_copy(blocks_ref.at[:, :width], blocks, sems.at[0])
     fetch.start()
     if len(far.shape) == 3:
@@ -126,21 +115,20 @@
         fetch_far = pltpu.make_async_copy(far_ref.at[:, begin:], far, sems.at[2])
     fetch_far.start()
 
-    @pl.when(mine)
-    def _():
-        weight_copies(own_in, own_out)
-
-    @pl.when(jnp.logical_not(mine))
-    def _():
-        weight_copies(other_in, other_out)
-
+    for part in (1, 2, 0):
+        for piece in range(pieces):
+            cut = pl.ds(piece * depth, depth)
+            pltpu.make_async_copy(
+                in_ref.at[part, cut], w_in.at[part, cut], in_sems.at[part, piece]
+            ).start()
+    pltpu.make_async_copy(out_weights_ref.at[0], w_out, sems.at[1]).start()
     fetch.wait()
     tokens = blocks[...]
     for part in (1, 2, 0):
         for piece in range(pieces):
             cut = pl.ds(piece * depth, depth)
             pltpu.make_async_copy(
-                own_in.at[part, cut], w_in.at[part, cut], in_sems.at[part, piece]
+                in_ref.at[part, cut], w_in.at[part, cut], in_sems.at[part, piece]
             ).wait()
         projected = jnp.dot(tokens, w_in[part], preferred_element_type=jnp.float32)
         if part == 2:
@@ -174,7 +162,7 @@
         put_cache((first, jnp.where(last, kv_ref[...], second[...])), parts, width)
         send(width, 4 * channels, steps)
     attended = attention(head_size, q_ref, kv_ref, far)
-    pltpu.make_async_copy(own_out.at[0], w_out, sems.at[1]).wait()
+    pltpu.make_async_copy(out_weights_ref.at[0], w_out, sems.at[1]).wait()
     tile = width // steps
     for step in range(steps):
         cut = slice(step * tile, (step + 1) * tile)
@@ -255,6 +243,7 @@
     )
     other_in = swap(own_in)
     other_out = swap(own_out)
+    own, other = (own_in, own_out), (other_in, other_out)
     params = [jnp.where(core == turn, own_params, other_params) for turn in range(2)]
     gain_rows = [p[3, : 2 * head_size].reshape(2, head_size) for p in params]
     blocks_shape = bf16(seq, rows, width)
@@ -268,13 +257,13 @@
     flat = lambda blocks: blocks.reshape(tokens, blocks.shape[2])
     apart = lambda values: values.reshape(seq, rows, values.shape[1])
 
-    def block(blocks, far, turn, caches=()):
+    def block(blocks, far, turn, weights, caches=()):
         total = width + 2 * channels * len(caches)
         side = (2, tokens, channels) if far.ndim == 3 else (tokens, 2 * channels)
         out, pair = pl.pallas_call(
-            functools.partial(block_kernel, turn, head_size, planes),
+            functools.partial(block_kernel, head_size, planes),
             out_shape=(bf16(tokens, total), bf16(2, tokens, channels)),
-            in_specs=[VMEM] + [HBM] * 4 + [ANY] * 2 + [VMEM] * len(caches),
+            in_specs=[VMEM] + [HBM] * 2 + [ANY] * 2 + [VMEM] * len(caches),
             out_specs=(HBM, VMEM),
             scratch_shapes=[
                 pltpu.VMEM((tokens, width), jnp.bfloat16),
@@ -289,7 +278,7 @@
             ],
             compiler_params=params_of(32),
         )(
-            gain_rows[turn], own_in, other_in, own_out, other_out, flat(blocks), far, *caches
+            gain_rows[turn], *weights, flat(blocks), far, *caches
         )
         return apart(out), pair
 
@@ -304,15 +293,22 @@
     early = core == 0
     either = lambda on_early, on_late: lax.cond(early, on_early, on_late)
 
+    pair_shape, block_shape = bf16(2, tokens, channels), bf16(rows, width)
+    side_shape = bf16(tokens, 2 * channels)
+
     def first_early():
-        return across(packed), blank(bf16(tokens, 2 * channels))[0]
+        received = across(packed)
+        side = flat(received)
+        parts, fresh = block(received, side, 0, own)
+        kept = lax.cond(plane == 0, lambda: blank(side_shape)[0], lambda: side[:, width:])
+        return parts, fresh, kept
 
     def first_late():
-        return blank(bf16(*packed.shape))[0], flat(across(packed[:, :, width:]))
-
-    received, stale = either(first_early, first_late)
-    stales = [flat(received), swap(stale)]
-    pair_shape, block_shape = bf16(2, tokens, channels), bf16(rows, width)
+        side = flat(across(packed[:, :, width:]))
+        blocks, side = lax.optimization_barrier((norm(x, 0), side))
+        return across(blocks), blank(pair_shape)[0], side
+
+    gathered, pair, side = either(first_early, first_late)
     late_pair = None
     early_x, late_x = x, x
     blocks_out, sources = {}, {}
@@ -321,7 +317,7 @@
         crossing = layer > 0 and turn == 0
 
         def early_scatter():
-            parts, fresh = block(received, stales[turn], turn)
+            parts, fresh = block(received, stales[turn], turn, other if turn else own)
             return parts, fresh, blank(block_shape)[0]
 
         def late_gather():
@@ -337,13 +333,19 @@
             )
             blocks_out[layer - 1, 1] = late_x
             late_x = upward(late_x, level - 1, 1)
-        payload, pair, result = either(early_scatter, late_gather)
+        if layer:
+            payload, pair, result = either(early_scatter, late_gather)
         if turn:
             late_x = blocks_out[layer - 1, 1] = result
         sources[layer, 0] = pair
         got = swap(pair)
         sources[layer, 2] = got
-        received = across(payload)
+        if layer:
+            received = across(payload)
+        else:
+            gathered, got, side = lax.optimization_barrier((gathered, got, side))
+            stales = [side, swap(side)]
+            received = either(lambda: across(gathered), lambda: blank(blocks_shape)[0])
         if layer == sections - 1:
             break
 
@@ -356,7 +358,7 @@
             return normed, blank(pair_shape)[0], result
 
         def late_scatter():
-            parts, fresh = block(received, got, turn)
+            parts, fresh = block(gathered if layer == 0 else received, got, turn, own if turn else other)
             return parts, fresh, blank(block_shape)[0]
 
         if crossing:
@@ -401,7 +403,7 @@
         return result, across(apart(packed))
 
     def last_late():
-        parts, _ = block(received, got, last % 2, (first_cache, second_cache))
+        parts, _ = block(received, got, last % 2, own if last % 2 else other, (first_cache, second_cache))
         parts = across(parts)
         return finish(late_x, parts, last % 2, 0)[0], parts[:, :, width:]
 

time: 288 us -> 306 us (1.062)
  blocking collectives: 32.7 us -> 64.1 us
  starting transfers between devices: 63.2 us -> 56 us
  Pallas kernels: 40.1 us -> 36 us
  waiting for transfers between devices: 139 us -> 135 us
    all_to_all x1 -> x2, blocking collectives: 32.7 us -> 64.1 us  [across(): lax.all_to_all(blocks, 'seq', split_axis=0, concat_axis=0, tiled=True)]
    all_to_all x7 -> x6, starting transfers between devices: 34.4 us -> 27.3 us  [across(): lax.all_to_all(blocks, 'seq', split_axis=0, concat_axis=0, tiled=True)]
    all_to_all x7 -> x6, waiting for transfers between devices: 135 us -> 129 us  [across(): lax.all_to_all(blocks, 'seq', split_axis=0, concat_axis=0, tiled=True)]
    pallas_call x4, Pallas kernels: 8.13 us -> 5 us  [finish(): pl.pallas_call(finish_kernel, out_shape=shapes, in_specs=[VMEM] * 4, out_...]
  transfers between devices with their start and end apart: 18 -> 17, of which waited for: 9 -> 9; matrix products, arithmetic and copies ran while one was open for 2% -> 2% of each run, Pallas kernels for 1% -> 3%
where the time goes in v7:
time: 306 us; the launch traced here: 305 us
  waiting for transfers between devices  135 us (44%)
  blocking collectives  64.1 us (21%)
  starting transfers between devices  56 us (18%)
  Pallas kernels  36 us (12%)
  local copies, waits for them, and re-layouts  7.74 us (3%)
  other arithmetic  4.81 us (2%)
    all_to_all x6, waiting for transfers between devices, across(): lax.all_to_all(blocks, 'seq', split_axis=0, concat_axis=0, tiled=True)  129 us
    all_to_all x2, blocking collectives, across(): lax.all_to_all(blocks, 'seq', split_axis=0, concat_axis=0, tiled=True)  64.1 us
    all_to_all x6, starting transfers between devices, across(): lax.all_to_all(blocks, 'seq', split_axis=0, concat_axis=0, tiled=True)  27.3 us
    pallas_call x4, Pallas kernels, block(): pl.pallas_call(functools.partial(block_kernel, head_size, planes), out_sh...  27.3 us
    ppermute x9, starting transfers between devices, swap(): return lax.ppermute(value, AXES, pairs)  23.2 us
  transfers between devices with their start and end apart: 17, of which 9 were waited for; matrix products, arithmetic and copies ran while one was open for 2% of the time, Pallas kernels for 3%

profile of v7, /device:TPU:0, one launch (start us, length us, event | category | flops | bytes accessed | tf_op | source)
XLA Modules:
  0.0 304.8 jit_solution(6646630075136157604)
XLA Ops:
  0.6 0.8 select_maximum_fusion.params_ref
  2.0 1.2 slice_bitcast_fusion.cache_ref
  3.3 1.4 shard_map.95
  5.3 0.9 broadcast_select_fusion.1
  6.2 45.1 %conditional.13 = (bf16[8,24,3072]{2,1,0:T(8,128)(2,1)}, bf16[2,192,256]{2,1,0:T(8,128)(2,1)S(1)}, bf16[192,512]{1,0:T(8,128)(2,1)}) conditional(s32[]{:T(128)} %convert_element_type.9, (f32[4,3072]{1,0:T(4,128)S(1)}, bf16[24,3072]{1,0:T(8,128)(2,1)}, bf16[8,24,3584]{2,1,0:T(8,128)(2,1)S(1)}) %tuple.171, (bf16[8,24,3584]{2,1,0:T(8,128)(2,1)S(1)}, ...), branch_computations={%region_0.1_spmd, %region_1.4_spmd} | conditional | flops 2 | bytes 10027114 | solution.py:294
  6.2 1.2 copy-done.2
  7.4 6.9 %all-to-all-start.2 = ((bf16[8,24,3584]{2,1,0:T(8,128)(2,1)}), bf16[8,24,3584]{2,1,0:T(8,128)(2,1)S(1)}, u32[]{:S(2)}, u32[]{:S(2)}) async-start(bf16[8,24,3584]{2,1,0:T(8,128)(2,1)} %copy-done.2), calls=%async_computation.2 | async-start | bytes 2752512 | tf_op jit(solution)/shard_map/cond/branch_1_fun/all_to_all | solution.py:220
  14.2 30.7 %all-to-all-done.2 = bf16[8,24,3584]{2,1,0:T(8,128)(2,1)S(1)} async-done(((bf16[8,24,3584]{2,1,0:T(8,128)(2,1)}), bf16[8,24,3584]{2,1,0:T(8,128)(2,1)S(1)}, u32[]{:S(2)}, u32[]{:S(2)}) %all-to-all-start.2) | async-done | bytes 1376288 | tf_op jit(solution)/shard_map/cond/branch_1_fun/all_to_all | solution.py:220
  44.9 6.4 %branch_1_fun.18 = (bf16[192,3072]{1,0:T(8,128)(2,1)}, bf16[2,192,256]{2,1,0:T(8,128)(2,1)S(1)}) custom-call(f32[2,128]{1,0:T(2,128)S(1)} %get-tuple-element.192.gain_ref, bf16[3,3072,256]{2,1,0:T(8,128)(2,1)} %get-tuple-element.193.in_ref, bf16[1,256,3072]{2,1,0:T(8,128)(2,1)S(1)} %get-tuple-element.194.out_weights_ref, bf16[192,3584]{1,0:T(8,128)(2,1)S(1)} %bitcast.46, ...), custom_call_target="tpu_custom_call" | custom-call | tf_op jit(solution)/shard_map/cond/branch_1_fun/pallas_call | solution.py:263
  51.4 1.4 collective-permute-done.1
  53.5 30.4 %conditional.14 = (bf16[8,24,3072]{2,1,0:T(8,128)(2,1)S(1)}) conditional(s32[]{:T(128)} %convert_element_type.9, () %tuple.114, bf16[8,24,3072]{2,1,0:T(8,128)(2,1)} %get-tuple-element.333), branch_computations={%region_4.5_spmd, %region_5.6_spmd} | conditional | bytes 2359304 | solution.py:294
  53.5 30.4 %all_to_all.53 = bf16[8,24,3072]{2,1,0:T(8,128)(2,1)S(1)} all-to-all(bf16[8,24,3072]{2,1,0:T(8,128)(2,1)} %param.5), channel_id=1, replica_groups=mesh['pipe'=4,'seq'=8] {'seq'}, dimensions={0} | all-to-all | bytes 2359296 | tf_op jit(solution)/shard_map/cond/branch_1_fun/all_to_all | solution.py:220
  83.9 1.6 conditional.15
  83.9 1.6 branch_1_fun.19
  85.5 4.3 %all-to-all-start.7 = ((bf16[8,24,3072]{2,1,0:T(8,128)(2,1)}), bf16[8,24,3072]{2,1,0:T(8,128)(2,1)S(1)}, u32[]{:S(2)}, u32[]{:S(2)}) async-start(bf16[8,24,3072]{2,1,0:T(8,128)(2,1)} %get-tuple-element.335), calls=%async_computation.7 | async-start | bytes 2359296 | tf_op jit(solution)/shard_map/all_to_all | solution.py:220
  89.9 26.3 %all-to-all-done.7 = bf16[8,24,3072]{2,1,0:T(8,128)(2,1)S(1)} async-done(((bf16[8,24,3072]{2,1,0:T(8,128)(2,1)}), bf16[8,24,3072]{2,1,0:T(8,128)(2,1)S(1)}, u32[]{:S(2)}, u32[]{:S(2)}) %all-to-all-start.7) | async-done | bytes 1179680 | tf_op jit(solution)/shard_map/all_to_all | solution.py:220
  116.1 7.2 %conditional.16 = (bf16[8,24,3072]{2,1,0:T(8,128)(2,1)}, bf16[2,192,256]{2,1,0:T(8,128)(2,1)}, bf16[24,3072]{1,0:T(8,128)(2,1)}) conditional(s32[]{:T(128)} %convert_element_type.9, (f32[4,3072]{1,0:T(4,128)S(1)}, f32[4,3072]{1,0:T(4,128)S(1)}, bf16[24,3072]{1,0:T(8,128)(2,1)S(1)}, bf16[8,24,3072]{2,1,0:T(8,128)(2,1)S(1)}, ...), branch_computations={%region_8.9_spmd, %region_9.10_spmd} | conditional | bytes 24 | solution.py:294
  116.1 7.2 %branch_1_fun.21 = (bf16[192,3072]{1,0:T(8,128)(2,1)}, bf16[2,192,256]{2,1,0:T(8,128)(2,1)}) custom-call(f32[2,128]{1,0:T(2,128)S(1)} %get-tuple-element.219.gain_ref, bf16[3,3072,256]{2,1,0:T(8,128)(2,1)} %get-tuple-element.220.in_ref, bf16[1,256,3072]{2,1,0:T(8,128)(2,1)} %get-tuple-element.221.out_weights_ref, bf16[192,3072]{1,0:T(8,128)(2,1)S(1)} %bitcast.51, ...), custom_call_target="tpu_custom_call" | custom-call | tf_op jit(solution)/shard_map/cond/branch_1_fun/pallas_call | solution.py:263
  123.4 4.0 %all-to-all-start.8 = ((bf16[8,24,3072]{2,1,0:T(8,128)(2,1)}), bf16[8,24,3072]{2,1,0:T(8,128)(2,1)S(1)}, u32[]{:S(2)}, u32[]{:S(2)}) async-start(bf16[8,24,3072]{2,1,0:T(8,128)(2,1)} %get-tuple-element.339), calls=%async_computation.8 | async-start | bytes 2359296 | tf_op jit(solution)/shard_map/all_to_all | solution.py:220
  127.4 17.8 %all-to-all-done.8 = bf16[8,24,3072]{2,1,0:T(8,128)(2,1)S(1)} async-done(((bf16[8,24,3072]{2,1,0:T(8,128)(2,1)}), bf16[8,24,3072]{2,1,0:T(8,128)(2,1)S(1)}, u32[]{:S(2)}, u32[]{:S(2)}) %all-to-all-start.8) | async-done | bytes 1179680 | tf_op jit(solution)/shard_map/all_to_all | solution.py:220
  145.4 4.1 %collective-permute-start.6 = (bf16[24,3072]{1,0:T(8,128)(2,1)S(1)}, bf16[24,3072]{1,0:T(8,128)(2,1)S(1)}, u32[]{:S(2)}, u32[]{:S(2)}) collective-permute-start(bf16[24,3072]{1,0:T(8,128)(2,1)S(1)} %get-tuple-element.404), channel_id=1, source_target_pairs={{0,16},{1,17},{2,18},{3,19},{4,20},{5,21},{6,22},{7,23}} | collective-permute-start | bytes 442376 | tf_op jit(solution)/shard_map/ppermute | solution.py:217
  149.6 2.6 collective-permute-done.6
  152.9 1.5 conditional.18
  152.9 1.5 branch_1_fun.25
  154.4 1.3 collective-permute-start.7
  155.8 6.5 %conditional.21 = (bf16[8,24,3072]{2,1,0:T(8,128)(2,1)}, bf16[2,192,256]{2,1,0:T(8,128)(2,1)S(1)}) conditional(s32[]{:T(128)} %convert_element_type.9, (f32[4,3072]{1,0:T(4,128)S(1)}, bf16[24,3072]{1,0:T(8,128)(2,1)}) %tuple.125, (bf16[8,24,3072]{2,1,0:T(8,128)(2,1)S(1)}, f32[2,128]{1,0:T(2,128)S(1)}, bf16[3,3072,256]{2,1,0:T(8,128)(2,1)}, ...), branch_computations={%region_18.19_spmd, %region_19.20_spmd} | conditional | bytes 16 | solution.py:294
  155.8 6.5 %branch_1_fun.27 = (bf16[192,3072]{1,0:T(8,128)(2,1)}, bf16[2,192,256]{2,1,0:T(8,128)(2,1)S(1)}) custom-call(f32[2,128]{1,0:T(2,128)S(1)} %get-tuple-element.245.gain_ref, bf16[3,3072,256]{2,1,0:T(8,128)(2,1)} %get-tuple-element.246.in_ref, bf16[1,256,3072]{2,1,0:T(8,128)(2,1)S(1)} %get-tuple-element.247.out_weights_ref, bf16[192,3072]{1,0:T(8,128)(2,1)S(1)} %bitcast.53, ...), custom_call_target="tpu_custom_call" | custom-call | tf_op jit(solution)/shard_map/cond/branch_1_fun/pallas_call | solution.py:263
  162.3 3.7 %all-to-all-start.9 = ((bf16[8,24,3072]{2,1,0:T(8,128)(2,1)}), bf16[8,24,3072]{2,1,0:T(8,128)(2,1)S(1)}, u32[]{:S(2)}, u32[]{:S(2)}) async-start(bf16[8,24,3072]{2,1,0:T(8,128)(2,1)} %get-tuple-element.343), calls=%async_computation.9 | async-start | bytes 2359296 | tf_op jit(solution)/shard_map/all_to_all | solution.py:220
  166.1 4.2 %collective-permute-start.8 = (bf16[2,192,256]{2,1,0:T(8,128)(2,1)S(1)}, bf16[2,192,256]{2,1,0:T(8,128)(2,1)}, u32[]{:S(2)}, u32[]{:S(2)}) collective-permute-start(bf16[2,192,256]{2,1,0:T(8,128)(2,1)S(1)} %get-tuple-element.344), channel_id=1, source_target_pairs={{0,8},{1,9},{2,10},{3,11},{4,12},{5,13},{6,14},{7,15},{8,0},{9,1},... | collective-permute-start | bytes 589832 | tf_op jit(solution)/shard_map/ppermute | solution.py:213
  170.2 23.6 %all-to-all-done.9 = bf16[8,24,3072]{2,1,0:T(8,128)(2,1)S(1)} async-done(((bf16[8,24,3072]{2,1,0:T(8,128)(2,1)}), bf16[8,24,3072]{2,1,0:T(8,128)(2,1)S(1)}, u32[]{:S(2)}, u32[]{:S(2)}) %all-to-all-start.9) | async-done | bytes 1179680 | tf_op jit(solution)/shard_map/all_to_all | solution.py:220
  193.9 2.4 conditional.22
  193.9 2.4 branch_1_fun.28
  196.3 33.8 %all_to_all.56 = bf16[8,24,3072]{2,1,0:T(8,128)(2,1)S(1)} all-to-all(bf16[8,24,3072]{2,1,0:T(8,128)(2,1)} %get-tuple-element.346), channel_id=1, replica_groups=mesh['pipe'=4,'seq'=8] {'seq'}, dimensions={0} | all-to-all | bytes 2359296 | tf_op jit(solution)/shard_map/all_to_all | solution.py:220
  230.0 7.2 %conditional.23 = (bf16[8,24,3072]{2,1,0:T(8,128)(2,1)}, bf16[2,192,256]{2,1,0:T(8,128)(2,1)}, bf16[24,3072]{1,0:T(8,128)(2,1)S(1)}) conditional(s32[]{:T(128)} %convert_element_type.9, (f32[4,3072]{1,0:T(4,128)S(1)}, f32[4,3072]{1,0:T(4,128)S(1)}, bf16[24,3072]{1,0:T(8,128)(2,1)}, bf16[8,24,3072]{2,1,0:T(8,128)(2,1)S(1)}, ...), branch_computations={%region_22.23_spmd, %region_23.24_spmd} | conditional | bytes 24 | solution.py:294
  230.0 7.2 %branch_1_fun.30 = (bf16[192,3072]{1,0:T(8,128)(2,1)}, bf16[2,192,256]{2,1,0:T(8,128)(2,1)}) custom-call(f32[2,128]{1,0:T(2,128)S(1)} %get-tuple-element.272.gain_ref, bf16[3,3072,256]{2,1,0:T(8,128)(2,1)} %get-tuple-element.273.in_ref, bf16[1,256,3072]{2,1,0:T(8,128)(2,1)} %get-tuple-element.274.out_weights_ref, bf16[192,3072]{1,0:T(8,128)(2,1)S(1)} %bitcast.52, ...), custom_call_target="tpu_custom_call" | custom-call | tf_op jit(solution)/shard_map/cond/branch_1_fun/pallas_call | solution.py:263
  237.9 4.3 %all-to-all-start.11 = ((bf16[8,24,3072]{2,1,0:T(8,128)(2,1)}), bf16[8,24,3072]{2,1,0:T(8,128)(2,1)S(1)}, u32[]{:S(2)}, u32[]{:S(2)}) async-start(bf16[8,24,3072]{2,1,0:T(8,128)(2,1)} %get-tuple-element.348), calls=%async_computation.11 | async-start | bytes 2359296 | tf_op jit(solution)/shard_map/all_to_all | solution.py:220
  242.3 1.4 collective-permute-done.9
  244.4 1.3 select_select_fusion
  245.7 22.6 %all-to-all-done.11 = bf16[8,24,3072]{2,1,0:T(8,128)(2,1)S(1)} async-done(((bf16[8,24,3072]{2,1,0:T(8,128)(2,1)}), bf16[8,24,3072]{2,1,0:T(8,128)(2,1)S(1)}, u32[]{:S(2)}, u32[]{:S(2)}) %all-to-all-start.11) | async-done | bytes 1179680 | tf_op jit(solution)/shard_map/all_to_all | solution.py:220
  268.3 14.3 %conditional.24 = (bf16[24,3072]{1,0:T(8,128)(2,1)}, bf16[8,24,1024]{2,1,0:T(8,128)(2,1)}) conditional(s32[]{:T(128)} %convert_element_type.9, (bf16[8,24,3072]{2,1,0:T(8,128)(2,1)S(1)}, f32[2,128]{1,0:T(2,128)S(1)}, bf16[3,3072,256]{2,1,0:T(8,128)(2,1)}, bf16[1,256,3072]{2,1,0:T(8,128)(2,1)S(1)}, bf16[2,192,256]{2,1,0:T(8,128)(2,1)}, ...), branch_computations={%region_24.25_spmd, %region_25.26_spmd} | conditional | bytes 4522028 | solution.py:294
  268.3 0.8 branch_1_fun.33
  269.1 4.1 %all-to-all-start.6 = ((bf16[8,24,1024]{2,1,0:T(8,128)(2,1)}), bf16[8,24,1024]{2,1,0:T(8,128)(2,1)}, u32[]{:S(2)}, u32[]{:S(2)}) async-start(bf16[8,24,1024]{2,1,0:T(8,128)(2,1)} %bitcast.17), calls=%async_computation.6 | async-start | bytes 786432 | tf_op jit(solution)/shard_map/cond/branch_1_fun/all_to_all | solution.py:220
  273.2 0.8 branch_1_fun.32
  274.0 8.5 %all-to-all-done.6 = bf16[8,24,1024]{2,1,0:T(8,128)(2,1)} async-done(((bf16[8,24,1024]{2,1,0:T(8,128)(2,1)}), bf16[8,24,1024]{2,1,0:T(8,128)(2,1)}, u32[]{:S(2)}, u32[]{:S(2)}) %all-to-all-start.6) | async-done | bytes 393248 | tf_op jit(solution)/shard_map/cond/branch_1_fun/all_to_all | solution.py:220
  282.6 1.0 select_select_fusion.2
  283.6 17.8 %collective-permute-start.10 = (bf16[24,3072]{1,0:T(8,128)(2,1)S(1)}, bf16[24,3072]{1,0:T(8,128)(2,1)S(1)}, u32[]{:S(2)}, u32[]{:S(2)}) collective-permute-start(bf16[24,3072]{1,0:T(8,128)(2,1)S(1)} %select_select_fusion.2), channel_id=1, source_target_pairs={{0,8},{1,9},{2,10},{3,11},{4,12},{5,13},{6,14},{7,15},{8,0},{9,1},... | collective-permute-start | bytes 442376 | tf_op jit(solution)/shard_map/ppermute | solution.py:213
  301.3 1.3 reshape.65
  303.1 0.8 broadcast_in_dim_reshape.3
  (82 shorter events, 5.7 us)
Async XLA Ops:
  0.6 2.6 copy-start
  1.5 3.2 %collective-permute-start = (f32[4,3072]{1,0:T(4,128)S(1)}, f32[4,3072]{1,0:T(4,128)S(1)}, u32[]{:S(2)}, u32[]{:S(2)}) collective-permute-start(f32[4,3072]{1,0:T(4,128)S(1)} %select_maximum_fusion.params_ref), channel_id=1, source_target_pairs={{0,8},{1,9},{2,10},{3,11},{4,12},{5,13},{6,14},{7,15},{8,0},{9,1},... | collective-permute-start | bytes 147464 | tf_op jit(solution)/shard_map/ppermute | solution.py:213
  2.0 2.8 copy-start.1
  2.0 3.3 %copy-start.23 = (f32[1,3072]{1,0:T(1,128)S(1)}, f32[1,3072]{1,0:T(1,128)}, u32[]{:S(2)}) copy-start(f32[1,3072]{1,0:T(1,128)} %param.37) | copy-start | bytes 36868
  2.0 3.3 %copy-start.24 = (f32[1,2,128]{2,1,0:T(2,128)S(1)}, f32[1,2,128]{2,1,0:T(2,128)}, u32[]{:S(2)}) copy-start(f32[1,2,128]{2,1,0:T(2,128)} %param.38) | copy-start | bytes 3076
  3.2 1.4 copy-start.3
  4.7 0.6 copy-start.22
  4.7 79.2 %collective-permute-start.2 = (bf16[3,3072,256]{2,1,0:T(8,128)(2,1)}, bf16[3,3072,256]{2,1,0:T(8,128)(2,1)}, u32[]{:S(2)}, u32[]{:S(2)}) collective-permute-start(bf16[3,3072,256]{2,1,0:T(8,128)(2,1)} %bitcast.40), channel_id=1, source_target_pairs={{0,8},{1,9},{2,10},{3,11},{4,12},{5,13},{6,14},{7,15},{8,0},{9,1},... | collective-permute-start | bytes 14155784 | tf_op jit(solution)/shard_map/ppermute | solution.py:213
  4.8 79.1 %collective-permute-start.3 = (bf16[1,256,3072]{2,1,0:T(8,128)(2,1)S(1)}, bf16[1,256,3072]{2,1,0:T(8,128)(2,1)}, u32[]{:S(2)}, u32[]{:S(2)}) collective-permute-start(bf16[1,256,3072]{2,1,0:T(8,128)(2,1)S(1)} %copy-done.1), channel_id=1, source_target_pairs={{0,8},{1,9},{2,10},{3,11},{4,12},{5,13},{6,14},{7,15},{8,0},{9,1},... | collective-permute-start | bytes 4718600 | tf_op jit(solution)/shard_map/ppermute | solution.py:213
  6.2 1.2 copy-start.2
  7.4 37.6 %all-to-all-start.2 = ((bf16[8,24,3584]{2,1,0:T(8,128)(2,1)}), bf16[8,24,3584]{2,1,0:T(8,128)(2,1)S(1)}, u32[]{:S(2)}, u32[]{:S(2)}) async-start(bf16[8,24,3584]{2,1,0:T(8,128)(2,1)} %copy-done.2), calls=%async_computation.2 | async-start | bytes 2752512 | tf_op jit(solution)/shard_map/cond/branch_1_fun/all_to_all | solution.py:220
  51.3 1.5 copy-start.9
  51.3 1.5 collective-permute-start.1
  52.8 0.7 copy-start.21
  53.5 30.4 %copy-start.4 = (bf16[24,3072]{1,0:T(8,128)(2,1)S(1)}, bf16[24,3072]{1,0:T(8,128)(2,1)}, u32[]{:S(2)}) copy-start(bf16[24,3072]{1,0:T(8,128)(2,1)} %copy-done.3) | copy-start | bytes 442372
  85.5 59.7 %copy-start.5 = (bf16[24,3072]{1,0:T(8,128)(2,1)}, bf16[24,3072]{1,0:T(8,128)(2,1)S(1)}, u32[]{:S(2)}) copy-start(bf16[24,3072]{1,0:T(8,128)(2,1)S(1)} %get-tuple-element.341) | copy-start | bytes 442372
  85.5 30.6 %all-to-all-start.7 = ((bf16[8,24,3072]{2,1,0:T(8,128)(2,1)}), bf16[8,24,3072]{2,1,0:T(8,128)(2,1)S(1)}, u32[]{:S(2)}, u32[]{:S(2)}) async-start(bf16[8,24,3072]{2,1,0:T(8,128)(2,1)} %get-tuple-element.335), calls=%async_computation.7 | async-start | bytes 2359296 | tf_op jit(solution)/shard_map/all_to_all | solution.py:220
  89.8 26.3 %collective-permute-start.4 = (bf16[192,512]{1,0:T(8,128)(2,1)}, bf16[192,512]{1,0:T(8,128)(2,1)}, u32[]{:S(2)}, u32[]{:S(2)}) collective-permute-start(bf16[192,512]{1,0:T(8,128)(2,1)} %get-tuple-element.337), channel_id=1, source_target_pairs={{0,8},{1,9},{2,10},{3,11},{4,12},{5,13},{6,14},{7,15},{8,0},{9,1},... | collective-permute-start | bytes 589832 | tf_op jit(solution)/shard_map/ppermute | solution.py:213
  123.4 21.9 %all-to-all-start.8 = ((bf16[8,24,3072]{2,1,0:T(8,128)(2,1)}), bf16[8,24,3072]{2,1,0:T(8,128)(2,1)S(1)}, u32[]{:S(2)}, u32[]{:S(2)}) async-start(bf16[8,24,3072]{2,1,0:T(8,128)(2,1)} %get-tuple-element.339), calls=%async_computation.8 | async-start | bytes 2359296 | tf_op jit(solution)/shard_map/all_to_all | solution.py:220
  127.4 22.2 %collective-permute-start.5 = (bf16[2,192,256]{2,1,0:T(8,128)(2,1)}, bf16[2,192,256]{2,1,0:T(8,128)(2,1)}, u32[]{:S(2)}, u32[]{:S(2)}) collective-permute-start(bf16[2,192,256]{2,1,0:T(8,128)(2,1)} %get-tuple-element.340), channel_id=1, source_target_pairs={{0,8},{1,9},{2,10},{3,11},{4,12},{5,13},{6,14},{7,15},{8,0},{9,1},... | collective-permute-start | bytes 589832 | tf_op jit(solution)/shard_map/ppermute | solution.py:213
  145.4 6.8 %copy-start.14 = (bf16[24,3072]{1,0:T(8,128)(2,1)}, bf16[24,3072]{1,0:T(8,128)(2,1)S(1)}, u32[]{:S(2)}) copy-start(bf16[24,3072]{1,0:T(8,128)(2,1)S(1)} %get-tuple-element.404) | copy-start | bytes 442372
  145.4 6.8 %collective-permute-start.6 = (bf16[24,3072]{1,0:T(8,128)(2,1)S(1)}, bf16[24,3072]{1,0:T(8,128)(2,1)S(1)}, u32[]{:S(2)}, u32[]{:S(2)}) collective-permute-start(bf16[24,3072]{1,0:T(8,128)(2,1)S(1)} %get-tuple-element.404), channel_id=1, source_target_pairs={{0,16},{1,17},{2,18},{3,19},{4,20},{5,21},{6,22},{7,23}} | collective-permute-start | bytes 442376 | tf_op jit(solution)/shard_map/ppermute | solution.py:217
  152.2 0.7 copy-start.15
  154.4 1.3 copy-start.12
  154.4 1.3 collective-permute-start.7
  162.3 3.7 %copy-start.10 = (bf16[2,192,256]{2,1,0:T(8,128)(2,1)}, bf16[2,192,256]{2,1,0:T(8,128)(2,1)S(1)}, u32[]{:S(2)}) copy-start(bf16[2,192,256]{2,1,0:T(8,128)(2,1)S(1)} %get-tuple-element.344) | copy-start | bytes 589828
  162.3 31.5 %copy-start.16 = (bf16[24,3072]{1,0:T(8,128)(2,1)S(1)}, bf16[24,3072]{1,0:T(8,128)(2,1)}, u32[]{:S(2)}) copy-start(bf16[24,3072]{1,0:T(8,128)(2,1)} %copy-done.15) | copy-start | bytes 442372
  162.3 31.5 %all-to-all-start.9 = ((bf16[8,24,3072]{2,1,0:T(8,128)(2,1)}), bf16[8,24,3072]{2,1,0:T(8,128)(2,1)S(1)}, u32[]{:S(2)}, u32[]{:S(2)}) async-start(bf16[8,24,3072]{2,1,0:T(8,128)(2,1)} %get-tuple-element.343), calls=%async_computation.9 | async-start | bytes 2359296 | tf_op jit(solution)/shard_map/all_to_all | solution.py:220
  166.1 27.8 %collective-permute-start.8 = (bf16[2,192,256]{2,1,0:T(8,128)(2,1)S(1)}, bf16[2,192,256]{2,1,0:T(8,128)(2,1)}, u32[]{:S(2)}, u32[]{:S(2)}) collective-permute-start(bf16[2,192,256]{2,1,0:T(8,128)(2,1)S(1)} %get-tuple-element.344), channel_id=1, source_target_pairs={{0,8},{1,9},{2,10},{3,11},{4,12},{5,13},{6,14},{7,15},{8,0},{9,1},... | collective-permute-start | bytes 589832 | tf_op jit(solution)/shard_map/ppermute | solution.py:213
  196.2 33.8 %copy-start.19 = (bf16[2,192,256]{2,1,0:T(8,128)(2,1)}, bf16[2,192,256]{2,1,0:T(8,128)(2,1)S(1)}, u32[]{:S(2)}) copy-start(bf16[2,192,256]{2,1,0:T(8,128)(2,1)S(1)} %get-tuple-element.347) | copy-start | bytes 589828
  237.2 0.7 copy-start.17
  237.3 5.0 %copy-start.20 = (bf16[2,192,256]{2,1,0:T(8,128)(2,1)S(1)}, bf16[2,192,256]{2,1,0:T(8,128)(2,1)}, u32[]{:S(2)}) copy-start(bf16[2,192,256]{2,1,0:T(8,128)(2,1)} %get-tuple-element.349) | copy-start | bytes 589828
  237.9 30.4 %all-to-all-start.11 = ((bf16[8,24,3072]{2,1,0:T(8,128)(2,1)}), bf16[8,24,3072]{2,1,0:T(8,128)(2,1)S(1)}, u32[]{:S(2)}, u32[]{:S(2)}) async-start(bf16[8,24,3072]{2,1,0:T(8,128)(2,1)} %get-tuple-element.348), calls=%async_computation.11 | async-start | bytes 2359296 | tf_op jit(solution)/shard_map/all_to_all | solution.py:220
  242.3 1.5 collective-permute-start.9
  243.8 0.7 copy-start.11
  268.3 4.9 %copy-start.8 = (bf16[24,3072]{1,0:T(8,128)(2,1)S(1)}, bf16[24,3072]{1,0:T(8,128)(2,1)}, u32[]{:S(2)}) copy-start(bf16[24,3072]{1,0:T(8,128)(2,1)} %get-tuple-element.292.x_ref) | copy-start | bytes 442372 | tf_op jit(solution)/shard_map/cond
  269.1 13.5 %all-to-all-start.6 = ((bf16[8,24,1024]{2,1,0:T(8,128)(2,1)}), bf16[8,24,1024]{2,1,0:T(8,128)(2,1)}, u32[]{:S(2)}, u32[]{:S(2)}) async-start(bf16[8,24,1024]{2,1,0:T(8,128)(2,1)} %bitcast.17), calls=%async_computation.6 | async-start | bytes 786432 | tf_op jit(solution)/shard_map/cond/branch_1_fun/all_to_all | solution.py:220
  283.6 20.4 %collective-permute-start.10 = (bf16[24,3072]{1,0:T(8,128)(2,1)S(1)}, bf16[24,3072]{1,0:T(8,128)(2,1)S(1)}, u32[]{:S(2)}, u32[]{:S(2)}) collective-permute-start(bf16[24,3072]{1,0:T(8,128)(2,1)S(1)} %select_select_fusion.2), channel_id=1, source_target_pairs={{0,8},{1,9},{2,10},{3,11},{4,12},{5,13},{6,14},{7,15},{8,0},{9,1},... | collective-permute-start | bytes 442376 | tf_op jit(solution)/shard_map/ppermute | solution.py:213
  301.3 2.6 copy-start.6
  301.3 2.6 copy-start.7
  301.3 2.6 copy-start.13

commit v8 on v4

--- a/solution.py
+++ b/solution.py
@@ -15,11 +15,15 @@
 
 
 def normalise(values, params_ref):
+    return normalise_by(values, params_ref[0:1, :], params_ref[1:2, :])
+
+
+def normalise_by(values, shift_row, scale_row):
     centered = values - jnp.mean(values, axis=-1, keepdims=True)
     spread = jnp.mean(centered * centered, axis=-1, keepdims=True)
-    return (
-        centered * lax.rsqrt(spread + 1e-06) * (1.0 + params_ref[1:2, :]) + params_ref[0:1, :]
-    ).astype(jnp.bfloat16)
+    return (centered * lax.rsqrt(spread + 1e-06) * (1.0 + scale_row) + shift_row).astype(
+        jnp.bfloat16
+    )
 
 
 def spread_block(block, buffer, out_ref, sems):
@@ -40,14 +44,21 @@
         copy.wait()
 
 
-def pack_kernel(params_ref, x_ref, cache_ref, out_ref, buffer, sems, sides, sem):
+def pack_kernel(shift_ref, scale_ref, hidden_ref, stale_ref, out_ref, buffer, sems, sides, sem, cache, cache_sem):
+    fetch = pltpu.make_async_copy(stale_ref.at[0, 1], cache, cache_sem)
+    fetch.start()
     count, _, total = sides.shape
-    width = x_ref.shape[1]
+    width = hidden_ref.shape[2]
     channels = total // 2
-    block = normalise(x_ref[...].astype(jnp.float32), params_ref)
+    early = lax.rem(lax.axis_index("pipe"), 2) == 0
+    x = jnp.where(
+        early, hidden_ref[0].astype(jnp.float32), hidden_ref[1].astype(jnp.float32)
+    )
+    block = normalise_by(x, shift_ref[...], scale_ref[...])
     copies = spread_block(block, buffer, out_ref, sems)
+    fetch.wait()
     for kind in range(2):
-        rows = cache_ref[:, kind, :]
+        rows = cache[:, kind, :]
         for shard in range(count):
             sides[shard, :, kind * channels : (kind + 1) * channels] = rows[
                 :, shard * channels : (shard + 1) * channels
@@ -185,6 +196,42 @@
         copy.wait()
 
 
+def place_cache(caches, out_ref, offset):
+    channels = (caches.shape[2] - offset) // 4
+    for patch in range(2):
+        for shard in range(caches.shape[0]):
+            begin = offset + 2 * patch * channels
+            sides = [
+                caches[shard, :, begin + kind * channels : begin + (kind + 1) * channels].astype(
+                    jnp.float32
+                )
+                for kind in range(2)
+            ]
+            out_ref[patch, :, :, shard * channels : (shard + 1) * channels] = jnp.stack(
+                sides, axis=1
+            ).astype(jnp.bfloat16)
+
+
+def place_kernel(caches_ref, out_ref):
+    place_cache(caches_ref, out_ref, 0)
+
+
+def last_kernel(params_ref, x_ref, parts_ref, out_ref, cache_ref):
+    width = x_ref.shape[1]
+    update = jnp.sum(parts_ref[:, :, :width].astype(jnp.float32), axis=0)
+    out_ref[...] = (x_ref[...].astype(jnp.float32) + params_ref[2:3, :] * update).astype(
+        jnp.bfloat16
+    )
+    place_cache(parts_ref, cache_ref, width)
+
+
+def pair_kernel(mine_ref, theirs_ref, out_ref):
+    mine, theirs = mine_ref[...], theirs_ref[...]
+    early = lax.rem(lax.axis_index("pipe"), 2) == 0
+    out_ref[0] = jnp.where(early, mine, theirs)
+    out_ref[1] = jnp.where(early, theirs, mine)
+
+
 def finish_kernel(params_ref, next_ref, x_ref, parts_ref, out_ref, *rest):
     width = x_ref.shape[1]
     update = jnp.sum(parts_ref[:, :, :width].astype(jnp.float32), axis=0)
@@ -242,12 +289,13 @@
     spreading = [pltpu.VMEM((rows, width), jnp.bfloat16), pltpu.SemaphoreType.DMA((seq,))]
     packed = pl.pallas_call(
         pack_kernel, out_shape=bf16(seq, rows, width + 2 * channels),
-        in_specs=[VMEM] * 3, out_specs=HBM,
+        in_specs=[VMEM] * 3 + [ANY], out_specs=HBM,
         scratch_shapes=spreading + [
             pltpu.VMEM((seq, rows, 2 * channels), jnp.bfloat16), pltpu.SemaphoreType.DMA,
+            pltpu.VMEM(stale_cache.shape[2:], jnp.bfloat16), pltpu.SemaphoreType.DMA,
         ],
         compiler_params=params_of(16),
-    )(own_params, x, stale_cache[0, 1])
+    )(mod_shift, mod_scale, hidden, stale_cache)
 
     other_params = swap(own_params)
     own_in, own_out, other_params, packed = lax.optimization_barrier(
@@ -392,18 +440,28 @@
         ]
     )
 
+    cache_shape = bf16(2, rows, 2, seq * channels)
+
     def last_early():
         result = finish(early_x, received, last % 2, 0)[0]
         packed = pl.pallas_call(
             cache_kernel, out_shape=bf16(tokens, 4 * channels),
             in_specs=[VMEM] * 2, out_specs=VMEM, compiler_params=params_of(16),
         )(first_cache, second_cache)
-        return result, across(apart(packed))
+        cache = pl.pallas_call(
+            place_kernel, out_shape=cache_shape, in_specs=[VMEM], out_specs=VMEM,
+            compiler_params=params_of(16),
+        )(across(apart(packed)))
+        return result, cache
 
     def last_late():
         parts, _ = block(received, got, last % 2, (first_cache, second_cache))
-        parts = across(parts)
-        return finish(late_x, parts, last % 2, 0)[0], parts[:, :, width:]
+        return tuple(
+            pl.pallas_call(
+                last_kernel, out_shape=(block_shape, cache_shape),
+                in_specs=[VMEM] * 3, out_specs=(VMEM,) * 2, compiler_params=params_of(16),
+            )(params[last % 2], late_x, across(parts))
+        )
 
     x, cache = either(last_early, last_late)
     blocks_out[last, 0] = blocks_out[last, 1] = x
@@ -415,9 +473,10 @@
             [jnp.where(early, blocks_out[2 * m + 1, 0], blocks_out[2 * m, 1]) for m in range(planes)]
         )
     )
-    block_output = jnp.stack([jnp.where(early, mine, theirs), jnp.where(early, theirs, mine)])
-    cache = cache.reshape(seq, rows, 2, 2, channels)
-    cache = jnp.transpose(cache, (2, 1, 3, 0, 4)).reshape(2, rows, 2, seq * channels)
+    block_output = pl.pallas_call(
+        pair_kernel, out_shape=bf16(2, rows, width), in_specs=[VMEM] * 2, out_specs=VMEM,
+        compiler_params=params_of(16),
+    )(mine, theirs)
     return block_output[None], cache[None]
 
 

time: 288 us -> 295 us (1.024)
  Pallas kernels: 40.1 us -> 46.4 us
    unnamed x34 -> x36, local copies, waits for them, and re-layouts: 2.03 us -> 5.43 us
  transfers between devices with their start and end apart: 18 -> 18, of which waited for: 9 -> 10; matrix products, arithmetic and copies ran while one was open for 2% -> 2% of each run, Pallas kernels for 1% -> 2%
where the time goes in v8:
time: 295 us; the launch traced here: 294 us
  waiting for transfers between devices  138 us (47%)
  starting transfers between devices  62.4 us (21%)
  Pallas kernels  46.4 us (16%)
  blocking collectives  33.2 us (11%)
  local copies, waits for them, and re-layouts  8.65 us (3%)
  other arithmetic  4.06 us (1%)
    all_to_all x7, waiting for transfers between devices, across(): lax.all_to_all(blocks, 'seq', split_axis=0, concat_axis=0, tiled=True)  132 us
    all_to_all x7, starting transfers between devices, across(): lax.all_to_all(blocks, 'seq', split_axis=0, concat_axis=0, tiled=True)  34.5 us
    all_to_all x1, blocking collectives, across(): lax.all_to_all(blocks, 'seq', split_axis=0, concat_axis=0, tiled=True)  33.2 us
    pallas_call x4, Pallas kernels, block(): pl.pallas_call(functools.partial(block_kernel, turn, head_size, planes),...  28.7 us
    ppermute x9, starting transfers between devices, swap(): return lax.ppermute(value, AXES, pairs)  23.2 us
    pallas_call x4, Pallas kernels, finish(): pl.pallas_call(finish_kernel, out_shape=shapes, in_specs=[VMEM] * 4, out_...  10.8 us
  transfers between devices with their start and end apart: 18, of which 10 were waited for; matrix products, arithmetic and copies ran while one was open for 2% of the time, Pallas kernels for 2%

profile of v8, /device:TPU:0, one launch (start us, length us, event | category | flops | bytes accessed | tf_op | source)
XLA Modules:
  0.0 293.6 jit_solution(5872554594017310695)
XLA Ops:
  2.0 1.0 copy-done
  2.9 1.0 copy-done.2
  5.4 1.9 shard_map.95
  8.6 34.5 %conditional.12 = (bf16[8,24,3584]{2,1,0:T(8,128)(2,1)}, bf16[192,512]{1,0:T(8,128)(2,1)}, bf16[192,3584]{1,0:T(8,128)(2,1)}) conditional(s32[]{:T(128)} %convert_element_type.6, bf16[8,24,3584]{2,1,0:T(8,128)(2,1)} %shard_map.95, bf16[8,24,3584]{2,1,0:T(8,128)(2,1)} %shard_map.95), branch_computations={%region_0.1_spmd, %region_1.2_spmd} | conditional | bytes 6881336 | solution.py:353
  8.6 7.0 %all-to-all-start.1 = ((bf16[8,24,3584]{2,1,0:T(8,128)(2,1)}), bf16[8,24,3584]{2,1,0:T(8,128)(2,1)}, u32[]{:S(2)}, u32[]{:S(2)}) async-start(bf16[8,24,3584]{2,1,0:T(8,128)(2,1)} %param.1), calls=%async_computation.1 | async-start | bytes 2752512 | tf_op jit(solution)/shard_map/cond/branch_1_fun/all_to_all | solution.py:279
  15.7 25.0 %all-to-all-done.1 = bf16[8,24,3584]{2,1,0:T(8,128)(2,1)} async-done(((bf16[8,24,3584]{2,1,0:T(8,128)(2,1)}), bf16[8,24,3584]{2,1,0:T(8,128)(2,1)}, u32[]{:S(2)}, u32[]{:S(2)}) %all-to-all-start.1) | async-done | bytes 1376288 | tf_op jit(solution)/shard_map/cond/branch_1_fun/all_to_all | solution.py:279
  40.6 2.5 copy.15
  43.2 7.3 %conditional.13 = (bf16[8,24,3072]{2,1,0:T(8,128)(2,1)}, bf16[2,192,256]{2,1,0:T(8,128)(2,1)}) conditional(s32[]{:T(128)} %convert_element_type.6, (f32[4,3072]{1,0:T(4,128)S(1)}, bf16[24,3072]{1,0:T(8,128)(2,1)S(1)}) %tuple.187, (bf16[8,24,3584]{2,1,0:T(8,128)(2,1)}, f32[2,128]{1,0:T(2,128)S(1)}, bf16[3,3072,256]{2,1,0:T(8,128)(2,1)}, ...), branch_computations={%region_2.3_spmd, %region_3.4_spmd} | conditional | bytes 16 | solution.py:353
  43.2 7.3 %branch_1_fun.19 = (bf16[192,3072]{1,0:T(8,128)(2,1)}, bf16[2,192,256]{2,1,0:T(8,128)(2,1)}) custom-call(f32[2,128]{1,0:T(2,128)S(1)} %get-tuple-element.222.gain_ref, bf16[3,3072,256]{2,1,0:T(8,128)(2,1)} %get-tuple-element.223.own_in, bf16[3,3072,256]{2,1,0:T(8,128)(2,1)} %get-tuple-element.224.other_in, ...), custom_call_target="tpu_custom_call" | custom-call | tf_op jit(solution)/shard_map/cond/branch_1_fun/pallas_call | solution.py:322
  50.5 6.6 %all-to-all-start.5 = ((bf16[8,24,3072]{2,1,0:T(8,128)(2,1)}), bf16[8,24,3072]{2,1,0:T(8,128)(2,1)}, u32[]{:S(2)}, u32[]{:S(2)}) async-start(bf16[8,24,3072]{2,1,0:T(8,128)(2,1)} %get-tuple-element.376), calls=%async_computation.5 | async-start | bytes 2359296 | tf_op jit(solution)/shard_map/all_to_all | solution.py:279
  57.1 17.9 %all-to-all-done.5 = bf16[8,24,3072]{2,1,0:T(8,128)(2,1)} async-done(((bf16[8,24,3072]{2,1,0:T(8,128)(2,1)}), bf16[8,24,3072]{2,1,0:T(8,128)(2,1)}, u32[]{:S(2)}, u32[]{:S(2)}) %all-to-all-start.5) | async-done | bytes 1179680 | tf_op jit(solution)/shard_map/all_to_all | solution.py:279
  75.1 3.6 %conditional.14 = (bf16[8,24,3072]{2,1,0:T(8,128)(2,1)}, bf16[2,192,256]{2,1,0:T(8,128)(2,1)}, bf16[24,3072]{1,0:T(8,128)(2,1)}) conditional(s32[]{:T(128)} %convert_element_type.6, (bf16[8,24,3072]{2,1,0:T(8,128)(2,1)}, f32[2,128]{1,0:T(2,128)S(1)}, bf16[3,3072,256]{2,1,0:T(8,128)(2,1)}, bf16[3,3072,256]{2,1,0:T(8,128)(2,1)}, ...), branch_computations={%region_4.5_spmd, %region_5.6_spmd} | conditional | bytes 24 | solution.py:353
  75.1 3.6 %branch_1_fun.20 = (bf16[24,3072]{1,0:T(8,128)(2,1)}, bf16[8,24,3072]{2,1,0:T(8,128)(2,1)}) custom-call(f32[4,3072]{1,0:T(4,128)S(1)} %get-tuple-element.240.params_ref, f32[4,3072]{1,0:T(4,128)S(1)} %get-tuple-element.241.next_ref, bf16[24,3072]{1,0:T(8,128)(2,1)S(1)} %get-tuple-element.242.x_ref, bf16[8,24,3072]{2,1,0:T(8,128)(2,1)} %get-tuple-element.243.parts_ref), custom_call_target="tpu_custom_call" | custom-call | tf_op jit(solution)/shard_map/cond/branch_1_fun/pallas_call | solution.py:346
  78.6 4.3 %all-to-all-start.6 = ((bf16[8,24,3072]{2,1,0:T(8,128)(2,1)}), bf16[8,24,3072]{2,1,0:T(8,128)(2,1)}, u32[]{:S(2)}, u32[]{:S(2)}) async-start(bf16[8,24,3072]{2,1,0:T(8,128)(2,1)} %get-tuple-element.378), calls=%async_computation.6 | async-start | bytes 2359296 | tf_op jit(solution)/shard_map/all_to_all | solution.py:279
  83.0 18.5 %all-to-all-done.6 = bf16[8,24,3072]{2,1,0:T(8,128)(2,1)} async-done(((bf16[8,24,3072]{2,1,0:T(8,128)(2,1)}), bf16[8,24,3072]{2,1,0:T(8,128)(2,1)}, u32[]{:S(2)}, u32[]{:S(2)}) %all-to-all-start.6) | async-done | bytes 1179680 | tf_op jit(solution)/shard_map/all_to_all | solution.py:279
  101.6 7.4 %conditional.15 = (bf16[8,24,3072]{2,1,0:T(8,128)(2,1)}, bf16[2,192,256]{2,1,0:T(8,128)(2,1)}, bf16[24,3072]{1,0:T(8,128)(2,1)}) conditional(s32[]{:T(128)} %convert_element_type.6, (f32[4,3072]{1,0:T(4,128)S(1)}, f32[4,3072]{1,0:T(4,128)S(1)}, bf16[24,3072]{1,0:T(8,128)(2,1)S(1)}, bf16[8,24,3072]{2,1,0:T(8,128)(2,1)}, ...), branch_computations={%region_6.7_spmd, %region_7.8_spmd} | conditional | bytes 24 | solution.py:353
  101.6 7.4 %branch_1_fun.22 = (bf16[192,3072]{1,0:T(8,128)(2,1)}, bf16[2,192,256]{2,1,0:T(8,128)(2,1)}) custom-call(f32[2,128]{1,0:T(2,128)S(1)} %get-tuple-element.253.gain_ref, bf16[3,3072,256]{2,1,0:T(8,128)(2,1)} %get-tuple-element.254.own_in, bf16[3,3072,256]{2,1,0:T(8,128)(2,1)} %get-tuple-element.255.other_in, ...), custom_call_target="tpu_custom_call" | custom-call | tf_op jit(solution)/shard_map/cond/branch_1_fun/pallas_call | solution.py:322
  109.0 4.4 %all-to-all-start.7 = ((bf16[8,24,3072]{2,1,0:T(8,128)(2,1)}), bf16[8,24,3072]{2,1,0:T(8,128)(2,1)}, u32[]{:S(2)}, u32[]{:S(2)}) async-start(bf16[8,24,3072]{2,1,0:T(8,128)(2,1)} %get-tuple-element.382), calls=%async_computation.7 | async-start | bytes 2359296 | tf_op jit(solution)/shard_map/all_to_all | solution.py:279
  113.4 17.8 %all-to-all-done.7 = bf16[8,24,3072]{2,1,0:T(8,128)(2,1)} async-done(((bf16[8,24,3072]{2,1,0:T(8,128)(2,1)}), bf16[8,24,3072]{2,1,0:T(8,128)(2,1)}, u32[]{:S(2)}, u32[]{:S(2)}) %all-to-all-start.7) | async-done | bytes 1179680 | tf_op jit(solution)/shard_map/all_to_all | solution.py:279
  131.3 2.1 conditional.16
  131.3 2.1 branch_1_fun.24
  133.4 3.4 %collective-permute-start.6 = (bf16[24,3072]{1,0:T(8,128)(2,1)}, bf16[24,3072]{1,0:T(8,128)(2,1)S(1)}, u32[]{:S(2)}, u32[]{:S(2)}) collective-permute-start(bf16[24,3072]{1,0:T(8,128)(2,1)} %get-tuple-element.454), channel_id=1, source_target_pairs={{0,16},{1,17},{2,18},{3,19},{4,20},{5,21},{6,22},{7,23}} | collective-permute-start | bytes 442376 | tf_op jit(solution)/shard_map/ppermute | solution.py:276
  136.9 2.9 %collective-permute-done.6 = bf16[24,3072]{1,0:T(8,128)(2,1)S(1)} collective-permute-done((bf16[24,3072]{1,0:T(8,128)(2,1)}, bf16[24,3072]{1,0:T(8,128)(2,1)S(1)}, u32[]{:S(2)}, u32[]{:S(2)}) %collective-permute-start.6) | collective-permute-done | bytes 147488 | tf_op jit(solution)/shard_map/ppermute | solution.py:276
  140.5 1.9 conditional.17
  140.5 1.9 branch_1_fun.26
  142.4 1.3 collective-permute-start.7
  143.8 6.7 %conditional.20 = (bf16[8,24,3072]{2,1,0:T(8,128)(2,1)}, bf16[2,192,256]{2,1,0:T(8,128)(2,1)S(1)}) conditional(s32[]{:T(128)} %convert_element_type.6, (f32[4,3072]{1,0:T(4,128)S(1)}, bf16[24,3072]{1,0:T(8,128)(2,1)}) %tuple.128, (bf16[8,24,3072]{2,1,0:T(8,128)(2,1)}, f32[2,128]{1,0:T(2,128)S(1)}, bf16[3,3072,256]{2,1,0:T(8,128)(2,1)}, ...), branch_computations={%region_16.17_spmd, %region_17.18_spmd} | conditional | bytes 16 | solution.py:353
  143.8 6.7 %branch_1_fun.28 = (bf16[192,3072]{1,0:T(8,128)(2,1)}, bf16[2,192,256]{2,1,0:T(8,128)(2,1)S(1)}) custom-call(f32[2,128]{1,0:T(2,128)S(1)} %get-tuple-element.283.gain_ref, bf16[3,3072,256]{2,1,0:T(8,128)(2,1)} %get-tuple-element.284.own_in, bf16[3,3072,256]{2,1,0:T(8,128)(2,1)} %get-tuple-element.285.other_in, ...), custom_call_target="tpu_custom_call" | custom-call | tf_op jit(solution)/shard_map/cond/branch_1_fun/pallas_call | solution.py:322
  150.5 4.3 %all-to-all-start.8 = ((bf16[8,24,3072]{2,1,0:T(8,128)(2,1)}), bf16[8,24,3072]{2,1,0:T(8,128)(2,1)}, u32[]{:S(2)}, u32[]{:S(2)}) async-start(bf16[8,24,3072]{2,1,0:T(8,128)(2,1)} %get-tuple-element.386), calls=%async_computation.8 | async-start | bytes 2359296 | tf_op jit(solution)/shard_map/all_to_all | solution.py:279
  154.8 4.8 %collective-permute-start.8 = (bf16[2,192,256]{2,1,0:T(8,128)(2,1)S(1)}, bf16[2,192,256]{2,1,0:T(8,128)(2,1)}, u32[]{:S(2)}, u32[]{:S(2)}) collective-permute-start(bf16[2,192,256]{2,1,0:T(8,128)(2,1)S(1)} %get-tuple-element.387), channel_id=1, source_target_pairs={{0,8},{1,9},{2,10},{3,11},{4,12},{5,13},{6,14},{7,15},{8,0},{9,1},... | collective-permute-start | bytes 589832 | tf_op jit(solution)/shard_map/ppermute | solution.py:272
  159.5 23.1 %all-to-all-done.8 = bf16[8,24,3072]{2,1,0:T(8,128)(2,1)} async-done(((bf16[8,24,3072]{2,1,0:T(8,128)(2,1)}), bf16[8,24,3072]{2,1,0:T(8,128)(2,1)}, u32[]{:S(2)}, u32[]{:S(2)}) %all-to-all-start.8) | async-done | bytes 1179680 | tf_op jit(solution)/shard_map/all_to_all | solution.py:279
  182.6 3.7 %conditional.21 = (bf16[8,24,3072]{2,1,0:T(8,128)(2,1)}, bf16[2,192,256]{2,1,0:T(8,128)(2,1)}, bf16[24,3072]{1,0:T(8,128)(2,1)}) conditional(s32[]{:T(128)} %convert_element_type.6, (bf16[8,24,3072]{2,1,0:T(8,128)(2,1)}, f32[2,128]{1,0:T(2,128)S(1)}, bf16[3,3072,256]{2,1,0:T(8,128)(2,1)}, bf16[3,3072,256]{2,1,0:T(8,128)(2,1)}, ...), branch_computations={%region_18.19_spmd, %region_19.20_spmd} | conditional | bytes 24 | solution.py:353
  182.6 3.6 %branch_1_fun.29 = (bf16[24,3072]{1,0:T(8,128)(2,1)}, bf16[8,24,3072]{2,1,0:T(8,128)(2,1)}) custom-call(f32[4,3072]{1,0:T(4,128)S(1)} %get-tuple-element.301.params_ref, f32[4,3072]{1,0:T(4,128)S(1)} %get-tuple-element.302.next_ref, bf16[24,3072]{1,0:T(8,128)(2,1)} %get-tuple-element.303.x_ref, bf16[8,24,3072]{2,1,0:T(8,128)(2,1)} %get-tuple-element.304.parts_ref), custom_call_target="tpu_custom_call" | custom-call | tf_op jit(solution)/shard_map/cond/branch_1_fun/pallas_call | solution.py:346
  186.3 33.2 %all_to_all.52 = bf16[8,24,3072]{2,1,0:T(8,128)(2,1)S(1)} all-to-all(bf16[8,24,3072]{2,1,0:T(8,128)(2,1)} %get-tuple-element.389), channel_id=1, replica_groups=mesh['pipe'=4,'seq'=8] {'seq'}, dimensions={0} | all-to-all | bytes 2359296 | tf_op jit(solution)/shard_map/all_to_all | solution.py:279
  219.5 7.3 %conditional.22 = (bf16[8,24,3072]{2,1,0:T(8,128)(2,1)}, bf16[2,192,256]{2,1,0:T(8,128)(2,1)}, bf16[24,3072]{1,0:T(8,128)(2,1)S(1)}) conditional(s32[]{:T(128)} %convert_element_type.6, (f32[4,3072]{1,0:T(4,128)S(1)}, f32[4,3072]{1,0:T(4,128)S(1)}, bf16[24,3072]{1,0:T(8,128)(2,1)}, bf16[8,24,3072]{2,1,0:T(8,128)(2,1)S(1)}, ...), branch_computations={%region_20.21_spmd, %region_21.22_spmd} | conditional | bytes 24 | solution.py:353
  219.5 7.3 %branch_1_fun.31 = (bf16[192,3072]{1,0:T(8,128)(2,1)}, bf16[2,192,256]{2,1,0:T(8,128)(2,1)}) custom-call(f32[2,128]{1,0:T(2,128)S(1)} %get-tuple-element.314.gain_ref, bf16[3,3072,256]{2,1,0:T(8,128)(2,1)} %get-tuple-element.315.own_in, bf16[3,3072,256]{2,1,0:T(8,128)(2,1)} %get-tuple-element.316.other_in, ...), custom_call_target="tpu_custom_call" | custom-call | tf_op jit(solution)/shard_map/cond/branch_1_fun/pallas_call | solution.py:322
  227.5 4.4 %all-to-all-start.10 = ((bf16[8,24,3072]{2,1,0:T(8,128)(2,1)}), bf16[8,24,3072]{2,1,0:T(8,128)(2,1)}, u32[]{:S(2)}, u32[]{:S(2)}) async-start(bf16[8,24,3072]{2,1,0:T(8,128)(2,1)} %get-tuple-element.391), calls=%async_computation.10 | async-start | bytes 2359296 | tf_op jit(solution)/shard_map/all_to_all | solution.py:279
  231.9 1.6 collective-permute-done.9
  234.2 2.0 select_select_fusion
  236.2 22.1 %all-to-all-done.10 = bf16[8,24,3072]{2,1,0:T(8,128)(2,1)} async-done(((bf16[8,24,3072]{2,1,0:T(8,128)(2,1)}), bf16[8,24,3072]{2,1,0:T(8,128)(2,1)}, u32[]{:S(2)}, u32[]{:S(2)}) %all-to-all-start.10) | async-done | bytes 1179680 | tf_op jit(solution)/shard_map/all_to_all | solution.py:279
  258.3 15.1 %conditional.23 = ((bf16[24,3072]{1,0:T(8,128)(2,1)S(1)}, bf16[2,24,2,2048]{3,2,1,0:T(2,128)(2,1)S(1)})) conditional(s32[]{:T(128)} %convert_element_type.6, (bf16[8,24,3072]{2,1,0:T(8,128)(2,1)}, f32[2,128]{1,0:T(2,128)S(1)}, bf16[3,3072,256]{2,1,0:T(8,128)(2,1)}, bf16[3,3072,256]{2,1,0:T(8,128)(2,1)}, bf16[1,256,3072]{2,1,0:T(8,128)(2,1)S(1)}, ...), branch_computations={%region_22.23_spmd, %region_23.24_spmd} | conditional | bytes 3735588 | solution.py:353
  258.3 1.8 branch_1_fun.34
  260.1 3.5 %all-to-all-start.4 = ((bf16[8,24,1024]{2,1,0:T(8,128)(2,1)}), bf16[8,24,1024]{2,1,0:T(8,128)(2,1)S(1)}, u32[]{:S(2)}, u32[]{:S(2)}) async-start(bf16[8,24,1024]{2,1,0:T(8,128)(2,1)} %bitcast.19), calls=%async_computation.4 | async-start | bytes 786432 | tf_op jit(solution)/shard_map/cond/branch_1_fun/all_to_all | solution.py:279
  263.5 1.5 branch_1_fun.33
  265.0 7.7 %all-to-all-done.4.caches_ref = bf16[8,24,1024]{2,1,0:T(8,128)(2,1)S(1)} async-done(((bf16[8,24,1024]{2,1,0:T(8,128)(2,1)}), bf16[8,24,1024]{2,1,0:T(8,128)(2,1)S(1)}, u32[]{:S(2)}, u32[]{:S(2)}) %all-to-all-start.4) | async-done | bytes 393248 | tf_op jit(solution)/shard_map/cond/branch_1_fun/all_to_all | solution.py:279
  273.4 1.3 select_select_fusion.2
  274.6 17.2 %collective-permute-start.10 = (bf16[24,3072]{1,0:T(8,128)(2,1)S(1)}, bf16[24,3072]{1,0:T(8,128)(2,1)S(1)}, u32[]{:S(2)}, u32[]{:S(2)}) collective-permute-start(bf16[24,3072]{1,0:T(8,128)(2,1)S(1)} %get-tuple-element.404), channel_id=1, source_target_pairs={{0,8},{1,9},{2,10},{3,11},{4,12},{5,13},{6,14},{7,15},{8,0},{9,1},... | collective-permute-start | bytes 442376 | tf_op jit(solution)/shard_map/ppermute | solution.py:272
  291.8 1.0 collective-permute-done.10.theirs_ref
  (68 shorter events, 7.7 us)
Async XLA Ops:
  1.4 5.8 %collective-permute-start = (f32[4,3072]{1,0:T(4,128)S(1)}, f32[4,3072]{1,0:T(4,128)S(1)}, u32[]{:S(2)}, u32[]{:S(2)}) collective-permute-start(f32[4,3072]{1,0:T(4,128)S(1)} %select_maximum_fusion), channel_id=1, source_target_pairs={{0,8},{1,9},{2,10},{3,11},{4,12},{5,13},{6,14},{7,15},{8,0},{9,1},... | collective-permute-start | bytes 147464 | tf_op jit(solution)/shard_map/ppermute | solution.py:272
  2.0 1.0 copy-start
  2.9 1.0 copy-start.2
  3.9 0.7 copy-start.3
  4.6 0.7 copy-start.5
  5.3 2.1 copy-start.7
  5.3 2.5 copy-start.1
  5.3 3.2 %copy-start.4 = (f32[1,3072]{1,0:T(1,128)S(1)}, f32[1,3072]{1,0:T(1,128)}, u32[]{:S(2)}) copy-start(f32[1,3072]{1,0:T(1,128)} %scale_ref.1) | copy-start | bytes 36868
  5.3 3.2 %copy-start.6 = (f32[1,3072]{1,0:T(1,128)S(1)}, f32[1,3072]{1,0:T(1,128)}, u32[]{:S(2)}) copy-start(f32[1,3072]{1,0:T(1,128)} %shift_ref.1) | copy-start | bytes 36868
  5.3 3.2 %copy-start.17 = (f32[1,3072]{1,0:T(1,128)S(1)}, f32[1,3072]{1,0:T(1,128)}, u32[]{:S(2)}) copy-start(f32[1,3072]{1,0:T(1,128)} %param.35) | copy-start | bytes 36868
  5.3 3.2 %copy-start.18 = (f32[1,2,128]{2,1,0:T(2,128)S(1)}, f32[1,2,128]{2,1,0:T(2,128)}, u32[]{:S(2)}) copy-start(f32[1,2,128]{2,1,0:T(2,128)} %param.36) | copy-start | bytes 3076
  7.3 35.9 %collective-permute-start.1 = (bf16[3,3072,256]{2,1,0:T(8,128)(2,1)}, bf16[3,3072,256]{2,1,0:T(8,128)(2,1)}, u32[]{:S(2)}, u32[]{:S(2)}) collective-permute-start(bf16[3,3072,256]{2,1,0:T(8,128)(2,1)} %bitcast.31), channel_id=1, source_target_pairs={{0,8},{1,9},{2,10},{3,11},{4,12},{5,13},{6,14},{7,15},{8,0},{9,1},... | collective-permute-start | bytes 14155784 | tf_op jit(solution)/shard_map/ppermute | solution.py:272
  7.4 35.8 %collective-permute-start.2 = (bf16[1,256,3072]{2,1,0:T(8,128)(2,1)S(1)}, bf16[1,256,3072]{2,1,0:T(8,128)(2,1)S(1)}, u32[]{:S(2)}, u32[]{:S(2)}) collective-permute-start(bf16[1,256,3072]{2,1,0:T(8,128)(2,1)S(1)} %copy-done.7), channel_id=1, source_target_pairs={{0,8},{1,9},{2,10},{3,11},{4,12},{5,13},{6,14},{7,15},{8,0},{9,1},... | collective-permute-start | bytes 4718600 | tf_op jit(solution)/shard_map/ppermute | solution.py:272
  8.6 34.6 %copy-start.8 = (bf16[24,3072]{1,0:T(8,128)(2,1)S(1)}, bf16[24,3072]{1,0:T(8,128)(2,1)}, u32[]{:S(2)}) copy-start(bf16[24,3072]{1,0:T(8,128)(2,1)} %dynamic-slice_bitcast_fusion) | copy-start | bytes 442372
  8.6 32.0 %all-to-all-start.1 = ((bf16[8,24,3584]{2,1,0:T(8,128)(2,1)}), bf16[8,24,3584]{2,1,0:T(8,128)(2,1)}, u32[]{:S(2)}, u32[]{:S(2)}) async-start(bf16[8,24,3584]{2,1,0:T(8,128)(2,1)} %param.1), calls=%async_computation.1 | async-start | bytes 2752512 | tf_op jit(solution)/shard_map/cond/branch_1_fun/all_to_all | solution.py:279
  50.5 24.6 %all-to-all-start.5 = ((bf16[8,24,3072]{2,1,0:T(8,128)(2,1)}), bf16[8,24,3072]{2,1,0:T(8,128)(2,1)}, u32[]{:S(2)}, u32[]{:S(2)}) async-start(bf16[8,24,3072]{2,1,0:T(8,128)(2,1)} %get-tuple-element.376), calls=%async_computation.5 | async-start | bytes 2359296 | tf_op jit(solution)/shard_map/all_to_all | solution.py:279
  57.1 18.0 %collective-permute-start.3 = (bf16[2,192,256]{2,1,0:T(8,128)(2,1)}, bf16[2,192,256]{2,1,0:T(8,128)(2,1)}, u32[]{:S(2)}, u32[]{:S(2)}) collective-permute-start(bf16[2,192,256]{2,1,0:T(8,128)(2,1)} %get-tuple-element.377), channel_id=1, source_target_pairs={{0,8},{1,9},{2,10},{3,11},{4,12},{5,13},{6,14},{7,15},{8,0},{9,1},... | collective-permute-start | bytes 589832 | tf_op jit(solution)/shard_map/ppermute | solution.py:272
  78.6 22.9 %all-to-all-start.6 = ((bf16[8,24,3072]{2,1,0:T(8,128)(2,1)}), bf16[8,24,3072]{2,1,0:T(8,128)(2,1)}, u32[]{:S(2)}, u32[]{:S(2)}) async-start(bf16[8,24,3072]{2,1,0:T(8,128)(2,1)} %get-tuple-element.378), calls=%async_computation.6 | async-start | bytes 2359296 | tf_op jit(solution)/shard_map/all_to_all | solution.py:279
  82.9 18.6 %collective-permute-start.4 = (bf16[192,512]{1,0:T(8,128)(2,1)}, bf16[192,512]{1,0:T(8,128)(2,1)}, u32[]{:S(2)}, u32[]{:S(2)}) collective-permute-start(bf16[192,512]{1,0:T(8,128)(2,1)} %get-tuple-element.380), channel_id=1, source_target_pairs={{0,8},{1,9},{2,10},{3,11},{4,12},{5,13},{6,14},{7,15},{8,0},{9,1},... | collective-permute-start | bytes 589832 | tf_op jit(solution)/shard_map/ppermute | solution.py:272
  109.0 22.3 %copy-start.9 = (bf16[24,3072]{1,0:T(8,128)(2,1)S(1)}, bf16[24,3072]{1,0:T(8,128)(2,1)}, u32[]{:S(2)}) copy-start(bf16[24,3072]{1,0:T(8,128)(2,1)} %get-tuple-element.384) | copy-start | bytes 442372
  109.0 22.3 %all-to-all-start.7 = ((bf16[8,24,3072]{2,1,0:T(8,128)(2,1)}), bf16[8,24,3072]{2,1,0:T(8,128)(2,1)}, u32[]{:S(2)}, u32[]{:S(2)}) async-start(bf16[8,24,3072]{2,1,0:T(8,128)(2,1)} %get-tuple-element.382), calls=%async_computation.7 | async-start | bytes 2359296 | tf_op jit(solution)/shard_map/all_to_all | solution.py:279
  113.4 23.5 %collective-permute-start.5 = (bf16[2,192,256]{2,1,0:T(8,128)(2,1)}, bf16[2,192,256]{2,1,0:T(8,128)(2,1)}, u32[]{:S(2)}, u32[]{:S(2)}) collective-permute-start(bf16[2,192,256]{2,1,0:T(8,128)(2,1)} %get-tuple-element.383), channel_id=1, source_target_pairs={{0,8},{1,9},{2,10},{3,11},{4,12},{5,13},{6,14},{7,15},{8,0},{9,1},... | collective-permute-start | bytes 589832 | tf_op jit(solution)/shard_map/ppermute | solution.py:272
  133.4 6.4 %collective-permute-start.6 = (bf16[24,3072]{1,0:T(8,128)(2,1)}, bf16[24,3072]{1,0:T(8,128)(2,1)S(1)}, u32[]{:S(2)}, u32[]{:S(2)}) collective-permute-start(bf16[24,3072]{1,0:T(8,128)(2,1)} %get-tuple-element.454), channel_id=1, source_target_pairs={{0,16},{1,17},{2,18},{3,19},{4,20},{5,21},{6,22},{7,23}} | collective-permute-start | bytes 442376 | tf_op jit(solution)/shard_map/ppermute | solution.py:276
  139.8 0.7 copy-start.16
  142.4 1.4 copy-start.15
  142.4 1.3 collective-permute-start.7
  150.5 4.3 %copy-start.12 = (bf16[2,192,256]{2,1,0:T(8,128)(2,1)}, bf16[2,192,256]{2,1,0:T(8,128)(2,1)S(1)}, u32[]{:S(2)}) copy-start(bf16[2,192,256]{2,1,0:T(8,128)(2,1)S(1)} %get-tuple-element.387) | copy-start | bytes 589828
  150.5 32.1 %all-to-all-start.8 = ((bf16[8,24,3072]{2,1,0:T(8,128)(2,1)}), bf16[8,24,3072]{2,1,0:T(8,128)(2,1)}, u32[]{:S(2)}, u32[]{:S(2)}) async-start(bf16[8,24,3072]{2,1,0:T(8,128)(2,1)} %get-tuple-element.386), calls=%async_computation.8 | async-start | bytes 2359296 | tf_op jit(solution)/shard_map/all_to_all | solution.py:279
  154.8 27.9 %collective-permute-start.8 = (bf16[2,192,256]{2,1,0:T(8,128)(2,1)S(1)}, bf16[2,192,256]{2,1,0:T(8,128)(2,1)}, u32[]{:S(2)}, u32[]{:S(2)}) collective-permute-start(bf16[2,192,256]{2,1,0:T(8,128)(2,1)S(1)} %get-tuple-element.387), channel_id=1, source_target_pairs={{0,8},{1,9},{2,10},{3,11},{4,12},{5,13},{6,14},{7,15},{8,0},{9,1},... | collective-permute-start | bytes 589832 | tf_op jit(solution)/shard_map/ppermute | solution.py:272
  226.8 0.7 copy-start.13
  227.5 30.8 %all-to-all-start.10 = ((bf16[8,24,3072]{2,1,0:T(8,128)(2,1)}), bf16[8,24,3072]{2,1,0:T(8,128)(2,1)}, u32[]{:S(2)}, u32[]{:S(2)}) async-start(bf16[8,24,3072]{2,1,0:T(8,128)(2,1)} %get-tuple-element.391), calls=%async_computation.10 | async-start | bytes 2359296 | tf_op jit(solution)/shard_map/all_to_all | solution.py:279
  231.9 1.7 collective-permute-start.9
  233.5 0.7 copy-start.11
  258.3 5.2 %copy-start.10 = (bf16[24,3072]{1,0:T(8,128)(2,1)S(1)}, bf16[24,3072]{1,0:T(8,128)(2,1)}, u32[]{:S(2)}) copy-start(bf16[24,3072]{1,0:T(8,128)(2,1)} %get-tuple-element.337.x_ref) | copy-start | bytes 442372 | tf_op jit(solution)/shard_map/cond
  260.1 12.7 %all-to-all-start.4 = ((bf16[8,24,1024]{2,1,0:T(8,128)(2,1)}), bf16[8,24,1024]{2,1,0:T(8,128)(2,1)S(1)}, u32[]{:S(2)}, u32[]{:S(2)}) async-start(bf16[8,24,1024]{2,1,0:T(8,128)(2,1)} %bitcast.19), calls=%async_computation.4 | async-start | bytes 786432 | tf_op jit(solution)/shard_map/cond/branch_1_fun/all_to_all | solution.py:279
  273.4 20.2 %copy-start.19 = (bf16[2,24,2,2048]{3,2,1,0:T(2,128)(2,1)}, bf16[2,24,2,2048]{3,2,1,0:T(2,128)(2,1)S(1)}, u32[]{:S(2)}) copy-start(bf16[2,24,2,2048]{3,2,1,0:T(2,128)(2,1)S(1)} %get-tuple-element.401) | copy-start | bytes 1179652
  274.6 18.2 %collective-permute-start.10 = (bf16[24,3072]{1,0:T(8,128)(2,1)S(1)}, bf16[24,3072]{1,0:T(8,128)(2,1)S(1)}, u32[]{:S(2)}, u32[]{:S(2)}) collective-permute-start(bf16[24,3072]{1,0:T(8,128)(2,1)S(1)} %get-tuple-element.404), channel_id=1, source_target_pairs={{0,8},{1,9},{2,10},{3,11},{4,12},{5,13},{6,14},{7,15},{8,0},{9,1},... | collective-permute-start | bytes 442376 | tf_op jit(solution)/shard_map/ppermute | solution.py:272

commit v9 on v8

--- a/solution.py
+++ b/solution.py
@@ -15,15 +15,11 @@
 
 
 def normalise(values, params_ref):
-    return normalise_by(values, params_ref[0:1, :], params_ref[1:2, :])
-
-
-def normalise_by(values, shift_row, scale_row):
     centered = values - jnp.mean(values, axis=-1, keepdims=True)
     spread = jnp.mean(centered * centered, axis=-1, keepdims=True)
-    return (centered * lax.rsqrt(spread + 1e-06) * (1.0 + scale_row) + shift_row).astype(
-        jnp.bfloat16
-    )
+    return (
+        centered * lax.rsqrt(spread + 1e-06) * (1.0 + params_ref[1:2, :]) + params_ref[0:1, :]
+    ).astype(jnp.bfloat16)
 
 
 def spread_block(block, buffer, out_ref, sems):
@@ -44,21 +40,14 @@
         copy.wait()
 
 
-def pack_kernel(shift_ref, scale_ref, hidden_ref, stale_ref, out_ref, buffer, sems, sides, sem, cache, cache_sem):
-    fetch = pltpu.make_async_copy(stale_ref.at[0, 1], cache, cache_sem)
-    fetch.start()
+def pack_kernel(params_ref, x_ref, cache_ref, out_ref, buffer, sems, sides, sem):
     count, _, total = sides.shape
-    width = hidden_ref.shape[2]
+    width = x_ref.shape[1]
     channels = total // 2
-    early = lax.rem(lax.axis_index("pipe"), 2) == 0
-    x = jnp.where(
-        early, hidden_ref[0].astype(jnp.float32), hidden_ref[1].astype(jnp.float32)
-    )
-    block = normalise_by(x, shift_ref[...], scale_ref[...])
+    block = normalise(x_ref[...].astype(jnp.float32), params_ref)
     copies = spread_block(block, buffer, out_ref, sems)
-    fetch.wait()
     for kind in range(2):
-        rows = cache[:, kind, :]
+        rows = cache_ref[:, kind, :]
         for shard in range(count):
             sides[shard, :, kind * channels : (kind + 1) * channels] = rows[
                 :, shard * channels : (shard + 1) * channels
@@ -289,13 +278,12 @@
     spreading = [pltpu.VMEM((rows, width), jnp.bfloat16), pltpu.SemaphoreType.DMA((seq,))]
     packed = pl.pallas_call(
         pack_kernel, out_shape=bf16(seq, rows, width + 2 * channels),
-        in_specs=[VMEM] * 3 + [ANY], out_specs=HBM,
+        in_specs=[VMEM] * 3, out_specs=HBM,
         scratch_shapes=spreading + [
             pltpu.VMEM((seq, rows, 2 * channels), jnp.bfloat16), pltpu.SemaphoreType.DMA,
-            pltpu.VMEM(stale_cache.shape[2:], jnp.bfloat16), pltpu.SemaphoreType.DMA,
         ],
         compiler_params=params_of(16),
-    )(mod_shift, mod_scale, hidden, stale_cache)
+    )(own_params, x, stale_cache[0, 1])
 
     other_params = swap(own_params)
     own_in, own_out, other_params, packed = lax.optimization_barrier(
@@ -401,7 +389,8 @@
             if crossing:
                 return norm(early_x, 1 - turn), blank(pair_shape)[0], blank(block_shape)[0]
             result, normed = finish(early_x, received, turn, 1)
-            return normed, blank(pair_shape)[0], result
+            kept = sources[layer, 0] if layer == sections - 2 else blank(pair_shape)[0]
+            return normed, kept, result
 
         def late_scatter():
             parts, fresh = block(received, got, turn)
@@ -417,6 +406,17 @@
         if not crossing:
             early_x = blocks_out[layer, 0] = result
         sources[layer, 1] = late_pair
+        if layer == sections - 2:
+            lowered = lax.ppermute(
+                late_pair,
+                AXES,
+                [(place(r, s), place((r - 2) % sections, s)) for r in range(sections) for s in range(seq)],
+            )
+            lowered = lax.cond(
+                plane == planes - 2,
+                lambda: across(apart(jnp.concatenate([lowered[0], lowered[1]], axis=1))),
+                lambda: blank(bf16(seq, rows, 2 * channels))[0],
+            )
         if crossing:
             active = pipe == jnp.where(early, 2 * level + 2, 2 * level + 1)
             received = lax.cond(active, across, lambda _: blank(blocks_shape)[0], payload)
@@ -430,6 +430,22 @@
         return chosen
 
     last = sections - 1
+    lowered, received = lax.optimization_barrier((lowered, received))
+    crossed = lax.ppermute(
+        lowered,
+        AXES,
+        [
+            (place(r, s), place(r ^ (r // 2 == planes - 2), s))
+            for r in range(sections)
+            for s in range(seq)
+        ],
+    )
+    partner = {2 * planes - 4: 2 * planes - 2, 2 * planes - 2: 2 * planes - 4}
+    returned = lax.ppermute(
+        jnp.concatenate([lowered, crossed], axis=2),
+        AXES,
+        [(place(r, s), place(partner.get(r, r), s)) for r in range(sections) for s in range(seq)],
+    )
     first_cache = by_plane(
         [jnp.where(early, sources[2 * m, 0], sources[2 * m + 1, 2]) for m in range(planes)]
     )
@@ -442,25 +458,35 @@
 
     cache_shape = bf16(2, rows, 2, seq * channels)
 
-    def last_early():
-        result = finish(early_x, received, last % 2, 0)[0]
+    def laid_out(caches):
+        return pl.pallas_call(
+            place_kernel, out_shape=cache_shape, in_specs=[VMEM], out_specs=VMEM,
+            compiler_params=params_of(16),
+        )(caches)
+
+    def packed_cache():
         packed = pl.pallas_call(
             cache_kernel, out_shape=bf16(tokens, 4 * channels),
             in_specs=[VMEM] * 2, out_specs=VMEM, compiler_params=params_of(16),
         )(first_cache, second_cache)
-        cache = pl.pallas_call(
-            place_kernel, out_shape=cache_shape, in_specs=[VMEM], out_specs=VMEM,
-            compiler_params=params_of(16),
-        )(across(apart(packed)))
-        return result, cache
+        return laid_out(across(apart(packed)))
+
+    def last_early():
+        result = finish(early_x, received, last % 2, 0)[0]
+        return result, lax.cond(plane == planes - 1, lambda: laid_out(returned), packed_cache)
 
     def last_late():
-        parts, _ = block(received, got, last % 2, (first_cache, second_cache))
         return tuple(
             pl.pallas_call(
                 last_kernel, out_shape=(block_shape, cache_shape),
                 in_specs=[VMEM] * 3, out_specs=(VMEM,) * 2, compiler_params=params_of(16),
-            )(params[last % 2], late_x, across(parts))
+            )(
+                params[last % 2],
+                late_x,
+                across(
+                    block(received, got, last % 2, (first_cache, second_cache))[0]
+                ),
+            )
         )
 
     x, cache = either(last_early, last_late)

time: 295 us -> 316 us (1.071)
  blocking collectives: 33.2 us -> 75.4 us
  waiting for transfers between devices: 138 us -> 117 us
  starting transfers between devices: 62.4 us -> 68.5 us
  local copies, waits for them, and re-layouts: 8.65 us -> 4.67 us
    all_to_all x1 -> x4, blocking collectives: 33.2 us -> 75.4 us  [across(): lax.all_to_all(blocks, 'seq', split_axis=0, concat_axis=0, tiled=True)]
    all_to_all x7 -> x5, waiting for transfers between devices: 132 us -> 100 us  [across(): lax.all_to_all(blocks, 'seq', split_axis=0, concat_axis=0, tiled=True)]
    ppermute x0 -> x3, starting transfers between devices: none -> 17 us  [the longest x1 13.2 us: body(): lax.ppermute(late_pair, AXES, [(place(r, s), place((r - 2) % sections, s)...]
    ppermute x0 -> x3, waiting for transfers between devices: none -> 10.7 us  [the longest x1 6.03 us: body(): lax.ppermute(jnp.concatenate([lowered, crossed], axis=2), AXES, [(place(r...]
    all_to_all x7 -> x5, starting transfers between devices: 34.5 us -> 25.9 us  [across(): lax.all_to_all(blocks, 'seq', split_axis=0, concat_axis=0, tiled=True)]
    unnamed x36 -> x34, local copies, waits for them, and re-layouts: 5.43 us -> 1.42 us
  transfers between devices with their start and end apart: 18 -> 19, of which waited for: 10 -> 11; matrix products, arithmetic and copies ran while one was open for 2% -> 1% of each run, Pallas kernels for 2% -> 1%
where the time goes in v9:
time: 316 us; the launch traced here: 314 us
  waiting for transfers between devices  117 us (37%)
  blocking collectives  75.4 us (24%)
  starting transfers between devices  68.5 us (22%)
  Pallas kernels  43.7 us (14%)
  local copies, waits for them, and re-layouts  4.67 us (1%)
  other arithmetic  4.19 us (1%)
    all_to_all x5, waiting for transfers between devices, across(): lax.all_to_all(blocks, 'seq', split_axis=0, concat_axis=0, tiled=True)  100 us
    all_to_all x4, blocking collectives, across(): lax.all_to_all(blocks, 'seq', split_axis=0, concat_axis=0, tiled=True)  75.4 us
    pallas_call x4, Pallas kernels, block(): pl.pallas_call(functools.partial(block_kernel, turn, head_size, planes),...  28.4 us
    all_to_all x5, starting transfers between devices, across(): lax.all_to_all(blocks, 'seq', split_axis=0, concat_axis=0, tiled=True)  25.9 us
    ppermute x9, starting transfers between devices, swap(): return lax.ppermute(value, AXES, pairs)  20.8 us
    ppermute x1, starting transfers between devices, body(): lax.ppermute(late_pair, AXES, [(place(r, s), place((r - 2) % sections, s)...  13.2 us
    pallas_call x4, Pallas kernels, finish(): pl.pallas_call(finish_kernel, out_shape=shapes, in_specs=[VMEM] * 4, out_...  9.72 us
  transfers between devices with their start and end apart: 19, of which 11 were waited for; matrix products, arithmetic and copies ran while one was open for 1% of the time, Pallas kernels for 1%

profile of v9, /device:TPU:0, one launch (start us, length us, event | category | flops | bytes accessed | tf_op | source)
XLA Modules:
  0.0 314.4 jit_solution(4042238688691743223)
XLA Ops:
  3.3 1.5 shard_map.95
  5.5 33.2 %conditional.14 = (bf16[8,24,3584]{2,1,0:T(8,128)(2,1)}, bf16[192,512]{1,0:T(8,128)(2,1)}, bf16[192,3584]{1,0:T(8,128)(2,1)S(1)}) conditional(s32[]{:T(128)} %convert_element_type.10, bf16[8,24,3584]{2,1,0:T(8,128)(2,1)} %shard_map.95, bf16[8,24,3584]{2,1,0:T(8,128)(2,1)} %shard_map.95), branch_computations={%region_0.1_spmd, %region_1.2_spmd} | conditional | bytes 6881336 | solution.py:341
  5.5 6.9 %all-to-all-start.1 = ((bf16[8,24,3584]{2,1,0:T(8,128)(2,1)}), bf16[8,24,3584]{2,1,0:T(8,128)(2,1)}, u32[]{:S(2)}, u32[]{:S(2)}) async-start(bf16[8,24,3584]{2,1,0:T(8,128)(2,1)} %param.1), calls=%async_computation.1 | async-start | bytes 2752512 | tf_op jit(solution)/shard_map/cond/branch_1_fun/all_to_all | solution.py:268
  12.4 25.0 %all-to-all-done.1 = bf16[8,24,3584]{2,1,0:T(8,128)(2,1)} async-done(((bf16[8,24,3584]{2,1,0:T(8,128)(2,1)}), bf16[8,24,3584]{2,1,0:T(8,128)(2,1)}, u32[]{:S(2)}, u32[]{:S(2)}) %all-to-all-start.1) | async-done | bytes 1376288 | tf_op jit(solution)/shard_map/cond/branch_1_fun/all_to_all | solution.py:268
  37.3 1.3 copy.17
  38.7 7.2 %conditional.15 = (bf16[8,24,3072]{2,1,0:T(8,128)(2,1)}, bf16[2,192,256]{2,1,0:T(8,128)(2,1)}) conditional(s32[]{:T(128)} %convert_element_type.10, (f32[4,3072]{1,0:T(4,128)S(1)}, bf16[24,3072]{1,0:T(8,128)(2,1)S(1)}) %tuple.123, (bf16[8,24,3584]{2,1,0:T(8,128)(2,1)}, f32[2,128]{1,0:T(2,128)S(1)}, bf16[3,3072,256]{2,1,0:T(8,128)(2,1)}, ...), branch_computations={%region_2.3_spmd, %region_3.4_spmd} | conditional | bytes 16 | solution.py:341
  38.7 7.2 %branch_1_fun.17 = (bf16[192,3072]{1,0:T(8,128)(2,1)}, bf16[2,192,256]{2,1,0:T(8,128)(2,1)}) custom-call(f32[2,128]{1,0:T(2,128)S(1)} %get-tuple-element.234.gain_ref, bf16[3,3072,256]{2,1,0:T(8,128)(2,1)} %get-tuple-element.235.own_in, bf16[3,3072,256]{2,1,0:T(8,128)(2,1)} %get-tuple-element.236.other_in, ...), custom_call_target="tpu_custom_call" | custom-call | tf_op jit(solution)/shard_map/cond/branch_1_fun/pallas_call | solution.py:310
  45.9 6.6 %all-to-all-start.6 = ((bf16[8,24,3072]{2,1,0:T(8,128)(2,1)}), bf16[8,24,3072]{2,1,0:T(8,128)(2,1)}, u32[]{:S(2)}, u32[]{:S(2)}) async-start(bf16[8,24,3072]{2,1,0:T(8,128)(2,1)} %get-tuple-element.397), calls=%async_computation.6 | async-start | bytes 2359296 | tf_op jit(solution)/shard_map/all_to_all | solution.py:268
  52.6 1.8 collective-permute-done.3
  54.3 16.2 %all-to-all-done.6 = bf16[8,24,3072]{2,1,0:T(8,128)(2,1)} async-done(((bf16[8,24,3072]{2,1,0:T(8,128)(2,1)}), bf16[8,24,3072]{2,1,0:T(8,128)(2,1)}, u32[]{:S(2)}, u32[]{:S(2)}) %all-to-all-start.6) | async-done | bytes 1179680 | tf_op jit(solution)/shard_map/all_to_all | solution.py:268
  70.5 3.5 %conditional.16 = (bf16[8,24,3072]{2,1,0:T(8,128)(2,1)}, bf16[2,192,256]{2,1,0:T(8,128)(2,1)}, bf16[24,3072]{1,0:T(8,128)(2,1)}) conditional(s32[]{:T(128)} %convert_element_type.10, (bf16[8,24,3072]{2,1,0:T(8,128)(2,1)}, f32[2,128]{1,0:T(2,128)S(1)}, bf16[3,3072,256]{2,1,0:T(8,128)(2,1)}, bf16[3,3072,256]{2,1,0:T(8,128)(2,1)}, ...), branch_computations={%region_4.5_spmd, %region_5.6_spmd} | conditional | bytes 24 | solution.py:341
  70.5 3.5 %branch_1_fun.18 = (bf16[24,3072]{1,0:T(8,128)(2,1)}, bf16[8,24,3072]{2,1,0:T(8,128)(2,1)}) custom-call(f32[4,3072]{1,0:T(4,128)S(1)} %get-tuple-element.252.params_ref, f32[4,3072]{1,0:T(4,128)S(1)} %get-tuple-element.253.next_ref, bf16[24,3072]{1,0:T(8,128)(2,1)S(1)} %get-tuple-element.254.x_ref, bf16[8,24,3072]{2,1,0:T(8,128)(2,1)} %get-tuple-element.255.parts_ref), custom_call_target="tpu_custom_call" | custom-call | tf_op jit(solution)/shard_map/cond/branch_1_fun/pallas_call | solution.py:334
  74.1 4.3 %all-to-all-start.7 = ((bf16[8,24,3072]{2,1,0:T(8,128)(2,1)}), bf16[8,24,3072]{2,1,0:T(8,128)(2,1)}, u32[]{:S(2)}, u32[]{:S(2)}) async-start(bf16[8,24,3072]{2,1,0:T(8,128)(2,1)} %get-tuple-element.399), calls=%async_computation.7 | async-start | bytes 2359296 | tf_op jit(solution)/shard_map/all_to_all | solution.py:268
  78.4 18.5 %all-to-all-done.7 = bf16[8,24,3072]{2,1,0:T(8,128)(2,1)} async-done(((bf16[8,24,3072]{2,1,0:T(8,128)(2,1)}), bf16[8,24,3072]{2,1,0:T(8,128)(2,1)}, u32[]{:S(2)}, u32[]{:S(2)}) %all-to-all-start.7) | async-done | bytes 1179680 | tf_op jit(solution)/shard_map/all_to_all | solution.py:268
  97.0 7.3 %conditional.17 = (bf16[8,24,3072]{2,1,0:T(8,128)(2,1)}, bf16[2,192,256]{2,1,0:T(8,128)(2,1)}, bf16[24,3072]{1,0:T(8,128)(2,1)}) conditional(s32[]{:T(128)} %convert_element_type.10, (f32[4,3072]{1,0:T(4,128)S(1)}, f32[4,3072]{1,0:T(4,128)S(1)}, bf16[24,3072]{1,0:T(8,128)(2,1)S(1)}, bf16[8,24,3072]{2,1,0:T(8,128)(2,1)}, ...), branch_computations={%region_6.7_spmd, %region_7.8_spmd} | conditional | bytes 24 | solution.py:341
  97.0 7.3 %branch_1_fun.20 = (bf16[192,3072]{1,0:T(8,128)(2,1)}, bf16[2,192,256]{2,1,0:T(8,128)(2,1)}) custom-call(f32[2,128]{1,0:T(2,128)S(1)} %get-tuple-element.265.gain_ref, bf16[3,3072,256]{2,1,0:T(8,128)(2,1)} %get-tuple-element.266.own_in, bf16[3,3072,256]{2,1,0:T(8,128)(2,1)} %get-tuple-element.267.other_in, ...), custom_call_target="tpu_custom_call" | custom-call | tf_op jit(solution)/shard_map/cond/branch_1_fun/pallas_call | solution.py:310
  104.3 4.4 %all-to-all-start.8 = ((bf16[8,24,3072]{2,1,0:T(8,128)(2,1)}), bf16[8,24,3072]{2,1,0:T(8,128)(2,1)}, u32[]{:S(2)}, u32[]{:S(2)}) async-start(bf16[8,24,3072]{2,1,0:T(8,128)(2,1)} %get-tuple-element.403), calls=%async_computation.8 | async-start | bytes 2359296 | tf_op jit(solution)/shard_map/all_to_all | solution.py:268
  108.8 17.9 %all-to-all-done.8 = bf16[8,24,3072]{2,1,0:T(8,128)(2,1)} async-done(((bf16[8,24,3072]{2,1,0:T(8,128)(2,1)}), bf16[8,24,3072]{2,1,0:T(8,128)(2,1)}, u32[]{:S(2)}, u32[]{:S(2)}) %all-to-all-start.8) | async-done | bytes 1179680 | tf_op jit(solution)/shard_map/all_to_all | solution.py:268
  126.7 2.1 conditional.18
  126.7 2.1 branch_1_fun.22
  128.8 3.4 %collective-permute-start.6 = (bf16[24,3072]{1,0:T(8,128)(2,1)}, bf16[24,3072]{1,0:T(8,128)(2,1)S(1)}, u32[]{:S(2)}, u32[]{:S(2)}) collective-permute-start(bf16[24,3072]{1,0:T(8,128)(2,1)} %get-tuple-element.475), channel_id=1, source_target_pairs={{0,16},{1,17},{2,18},{3,19},{4,20},{5,21},{6,22},{7,23}} | collective-permute-start | bytes 442376 | tf_op jit(solution)/shard_map/ppermute | solution.py:265
  132.3 2.9 collective-permute-done.6
  135.9 1.9 conditional.19
  135.9 1.9 branch_1_fun.24
  139.1 6.6 %conditional.22 = (bf16[8,24,3072]{2,1,0:T(8,128)(2,1)}, bf16[2,192,256]{2,1,0:T(8,128)(2,1)S(1)}) conditional(s32[]{:T(128)} %convert_element_type.10, (f32[4,3072]{1,0:T(4,128)S(1)}, bf16[24,3072]{1,0:T(8,128)(2,1)}) %tuple.136, (bf16[8,24,3072]{2,1,0:T(8,128)(2,1)}, f32[2,128]{1,0:T(2,128)S(1)}, bf16[3,3072,256]{2,1,0:T(8,128)(2,1)}, ...), branch_computations={%region_16.17_spmd, %region_17.18_spmd} | conditional | bytes 16 | solution.py:341
  139.1 6.6 %branch_1_fun.26 = (bf16[192,3072]{1,0:T(8,128)(2,1)}, bf16[2,192,256]{2,1,0:T(8,128)(2,1)S(1)}) custom-call(f32[2,128]{1,0:T(2,128)S(1)} %get-tuple-element.295.gain_ref, bf16[3,3072,256]{2,1,0:T(8,128)(2,1)} %get-tuple-element.296.own_in, bf16[3,3072,256]{2,1,0:T(8,128)(2,1)} %get-tuple-element.297.other_in, ...), custom_call_target="tpu_custom_call" | custom-call | tf_op jit(solution)/shard_map/cond/branch_1_fun/pallas_call | solution.py:310
  145.8 3.7 %all-to-all-start.9 = ((bf16[8,24,3072]{2,1,0:T(8,128)(2,1)}), bf16[8,24,3072]{2,1,0:T(8,128)(2,1)S(1)}, u32[]{:S(2)}, u32[]{:S(2)}) async-start(bf16[8,24,3072]{2,1,0:T(8,128)(2,1)} %get-tuple-element.407), calls=%async_computation.9 | async-start | bytes 2359296 | tf_op jit(solution)/shard_map/all_to_all | solution.py:268
  149.5 4.9 %collective-permute-start.8 = (bf16[2,192,256]{2,1,0:T(8,128)(2,1)S(1)}, bf16[2,192,256]{2,1,0:T(8,128)(2,1)}, u32[]{:S(2)}, u32[]{:S(2)}) collective-permute-start(bf16[2,192,256]{2,1,0:T(8,128)(2,1)S(1)} %get-tuple-element.408), channel_id=1, source_target_pairs={{0,8},{1,9},{2,10},{3,11},{4,12},{5,13},{6,14},{7,15},{8,0},{9,1},... | collective-permute-start | bytes 589832 | tf_op jit(solution)/shard_map/ppermute | solution.py:261
  154.4 22.9 %all-to-all-done.9 = bf16[8,24,3072]{2,1,0:T(8,128)(2,1)S(1)} async-done(((bf16[8,24,3072]{2,1,0:T(8,128)(2,1)}), bf16[8,24,3072]{2,1,0:T(8,128)(2,1)S(1)}, u32[]{:S(2)}, u32[]{:S(2)}) %all-to-all-start.9) | async-done | bytes 1179680 | tf_op jit(solution)/shard_map/all_to_all | solution.py:268
  177.3 3.1 conditional.23
  177.3 2.3 branch_1_fun.27
  180.3 13.2 %collective-permute-start.9 = (bf16[2,192,256]{2,1,0:T(8,128)(2,1)}, bf16[2,192,256]{2,1,0:T(8,128)(2,1)S(1)}, u32[]{:S(2)}, u32[]{:S(2)}) collective-permute-start(bf16[2,192,256]{2,1,0:T(8,128)(2,1)} %get-tuple-element.410), channel_id=1, source_target_pairs={{0,16},{1,17},{2,18},{3,19},{4,20},{5,21},{6,22},{7,23},{8,24},{9,... | collective-permute-start | bytes 589832 | tf_op jit(solution)/shard_map/ppermute | solution.py:410
  193.5 3.9 %collective-permute-done.9 = bf16[2,192,256]{2,1,0:T(8,128)(2,1)S(1)} collective-permute-done((bf16[2,192,256]{2,1,0:T(8,128)(2,1)}, bf16[2,192,256]{2,1,0:T(8,128)(2,1)S(1)}, u32[]{:S(2)}, u32[]{:S(2)}) %collective-permute-start.9) | collective-permute-done | bytes 196640 | tf_op jit(solution)/shard_map/ppermute | solution.py:410
  197.4 10.8 %conditional.24 = (bf16[8,24,512]{2,1,0:T(8,128)(2,1)S(1)}) conditional(s32[]{:T(128)} %convert_element_type.12, () %tuple.140, bf16[2,192,256]{2,1,0:T(8,128)(2,1)S(1)} %collective-permute-done.9), branch_computations={%region_20.21_spmd, %region_21.22_spmd} | conditional | flops 393216 | bytes 1179656 | solution.py:415
  197.4 10.8 %all_to_all.55 = bf16[8,24,512]{2,1,0:T(8,128)(2,1)S(1)} all-to-all(bf16[8,24,512]{2,1,0:T(8,128)(2,1)S(1)} %pad_maximum_fusion), channel_id=1, replica_groups=mesh['pipe'=4,'seq'=8] {'seq'}, dimensions={0} | all-to-all | bytes 393216 | tf_op jit(solution)/shard_map/cond/branch_1_fun/all_to_all | solution.py:268
  208.2 25.0 %all_to_all.58 = bf16[8,24,3072]{2,1,0:T(8,128)(2,1)S(1)} all-to-all(bf16[8,24,3072]{2,1,0:T(8,128)(2,1)S(1)} %copy-done.4), channel_id=1, replica_groups=mesh['pipe'=4,'seq'=8] {'seq'}, dimensions={0} | all-to-all | bytes 2359296 | tf_op jit(solution)/shard_map/all_to_all | solution.py:268
  233.2 7.3 %conditional.25 = (bf16[8,24,3072]{2,1,0:T(8,128)(2,1)}, bf16[2,192,256]{2,1,0:T(8,128)(2,1)}, bf16[24,3072]{1,0:T(8,128)(2,1)S(1)}) conditional(s32[]{:T(128)} %convert_element_type.10, (f32[4,3072]{1,0:T(4,128)S(1)}, f32[4,3072]{1,0:T(4,128)S(1)}, bf16[24,3072]{1,0:T(8,128)(2,1)}, bf16[8,24,3072]{2,1,0:T(8,128)(2,1)S(1)}, ...), branch_computations={%region_22.23_spmd, %region_23.24_spmd} | conditional | bytes 24 | solution.py:341
  233.2 7.3 %branch_1_fun.28 = (bf16[192,3072]{1,0:T(8,128)(2,1)}, bf16[2,192,256]{2,1,0:T(8,128)(2,1)}) custom-call(f32[2,128]{1,0:T(2,128)S(1)} %get-tuple-element.327.gain_ref, bf16[3,3072,256]{2,1,0:T(8,128)(2,1)} %get-tuple-element.328.own_in, bf16[3,3072,256]{2,1,0:T(8,128)(2,1)} %get-tuple-element.329.other_in, ...), custom_call_target="tpu_custom_call" | custom-call | tf_op jit(solution)/shard_map/cond/branch_1_fun/pallas_call | solution.py:310
  240.5 24.9 %all_to_all.59 = bf16[8,24,3072]{2,1,0:T(8,128)(2,1)S(1)} all-to-all(bf16[8,24,3072]{2,1,0:T(8,128)(2,1)} %get-tuple-element.412), channel_id=1, replica_groups=mesh['pipe'=4,'seq'=8] {'seq'}, dimensions={0} | all-to-all | bytes 2359296 | tf_op jit(solution)/shard_map/all_to_all | solution.py:268
  265.4 1.9 collective-permute-start.11
  269.5 1.9 collective-permute-start.12
  273.5 6.0 %collective-permute-done.12 = bf16[8,24,1024]{2,1,0:T(8,128)(2,1)} collective-permute-done((bf16[8,24,1024]{2,1,0:T(8,128)(2,1)}, bf16[8,24,1024]{2,1,0:T(8,128)(2,1)}, u32[]{:S(2)}, u32[]{:S(2)}) %collective-permute-start.12) | collective-permute-done | bytes 393248 | tf_op jit(solution)/shard_map/ppermute | solution.py:444
  279.5 17.9 %conditional.26 = (bf16[24,3072]{1,0:T(8,128)(2,1)}, bf16[1,2,24,2,2048]{4,3,2,1,0:T(2,128)(2,1)}) conditional(s32[]{:T(128)} %convert_element_type.10, (bf16[8,24,3072]{2,1,0:T(8,128)(2,1)S(1)}, f32[2,128]{1,0:T(2,128)S(1)}, bf16[3,3072,256]{2,1,0:T(8,128)(2,1)}, bf16[3,3072,256]{2,1,0:T(8,128)(2,1)}, bf16[1,256,3072]{2,1,0:T(8,128)(2,1)S(1)}, ...), branch_computations={%region_24.25_spmd, %region_25.28_spmd} | conditional | flops 2 | bytes 3735596 | solution.py:341
  279.5 1.8 branch_1_fun.31
  281.2 16.1 %conditional = (bf16[1,2,24,2,2048]{4,3,2,1,0:T(2,128)(2,1)}) conditional(s32[]{:T(128)} %convert_element_type.2, (bf16[2,192,256]{2,1,0:T(8,128)(2,1)S(1)}, bf16[2,192,256]{2,1,0:T(8,128)(2,1)S(1)}) %tuple.94, bf16[8,24,1024]{2,1,0:T(8,128)(2,1)} %get-tuple-element.359), branch_computations={%region_26.26_spmd, %region_27.27_spmd} | conditional | bytes 786440 | solution.py:476
  281.3 14.7 %all_to_all.57.caches_ref = bf16[8,24,1024]{2,1,0:T(8,128)(2,1)S(1)} all-to-all(bf16[8,24,1024]{2,1,0:T(8,128)(2,1)S(1)} %bitcast.37), channel_id=1, replica_groups=mesh['pipe'=4,'seq'=8] {'seq'}, dimensions={0} | all-to-all | bytes 786432 | tf_op jit(solution)/shard_map/cond/branch_1_fun/cond/branch_0_fun/all_to_all | solution.py:268
  296.0 1.4 branch_0_fun.39
  298.6 14.1 %collective-permute-start.13 = (bf16[24,3072]{1,0:T(8,128)(2,1)S(1)}, bf16[24,3072]{1,0:T(8,128)(2,1)S(1)}, u32[]{:S(2)}, u32[]{:S(2)}) collective-permute-start(bf16[24,3072]{1,0:T(8,128)(2,1)S(1)} %get-tuple-element.424), channel_id=1, source_target_pairs={{0,8},{1,9},{2,10},{3,11},{4,12},{5,13},{6,14},{7,15},{8,0},{9,1},... | collective-permute-start | bytes 442376 | tf_op jit(solution)/shard_map/ppermute | solution.py:261
  (75 shorter events, 13.3 us)
Async XLA Ops:
  0.6 2.6 copy-start
  1.5 3.3 %collective-permute-start = (f32[4,3072]{1,0:T(4,128)S(1)}, f32[4,3072]{1,0:T(4,128)S(1)}, u32[]{:S(2)}, u32[]{:S(2)}) collective-permute-start(f32[4,3072]{1,0:T(4,128)S(1)} %select_maximum_fusion.params_ref), channel_id=1, source_target_pairs={{0,8},{1,9},{2,10},{3,11},{4,12},{5,13},{6,14},{7,15},{8,0},{9,1},... | collective-permute-start | bytes 147464 | tf_op jit(solution)/shard_map/ppermute | solution.py:261
  2.0 2.9 copy-start.1
  2.0 3.4 %copy-start.14 = (f32[1,3072]{1,0:T(1,128)S(1)}, f32[1,3072]{1,0:T(1,128)}, u32[]{:S(2)}) copy-start(f32[1,3072]{1,0:T(1,128)} %param.39) | copy-start | bytes 36868
  2.0 3.4 %copy-start.15 = (f32[1,3072]{1,0:T(1,128)S(1)}, f32[1,3072]{1,0:T(1,128)}, u32[]{:S(2)}) copy-start(f32[1,3072]{1,0:T(1,128)} %param.38) | copy-start | bytes 36868
  2.0 3.4 %copy-start.16 = (f32[1,3072]{1,0:T(1,128)S(1)}, f32[1,3072]{1,0:T(1,128)}, u32[]{:S(2)}) copy-start(f32[1,3072]{1,0:T(1,128)} %param.37) | copy-start | bytes 36868
  2.0 3.4 %copy-start.17 = (f32[1,2,128]{2,1,0:T(2,128)S(1)}, f32[1,2,128]{2,1,0:T(2,128)}, u32[]{:S(2)}) copy-start(f32[1,2,128]{2,1,0:T(2,128)} %param.40) | copy-start | bytes 3076
  4.8 33.9 %collective-permute-start.1 = (bf16[3,3072,256]{2,1,0:T(8,128)(2,1)}, bf16[3,3072,256]{2,1,0:T(8,128)(2,1)}, u32[]{:S(2)}, u32[]{:S(2)}) collective-permute-start(bf16[3,3072,256]{2,1,0:T(8,128)(2,1)} %bitcast.38), channel_id=1, source_target_pairs={{0,8},{1,9},{2,10},{3,11},{4,12},{5,13},{6,14},{7,15},{8,0},{9,1},... | collective-permute-start | bytes 14155784 | tf_op jit(solution)/shard_map/ppermute | solution.py:261
  4.9 33.8 %collective-permute-start.2 = (bf16[1,256,3072]{2,1,0:T(8,128)(2,1)S(1)}, bf16[1,256,3072]{2,1,0:T(8,128)(2,1)}, u32[]{:S(2)}, u32[]{:S(2)}) collective-permute-start(bf16[1,256,3072]{2,1,0:T(8,128)(2,1)S(1)} %copy-done.1), channel_id=1, source_target_pairs={{0,8},{1,9},{2,10},{3,11},{4,12},{5,13},{6,14},{7,15},{8,0},{9,1},... | collective-permute-start | bytes 4718600 | tf_op jit(solution)/shard_map/ppermute | solution.py:261
  5.5 31.9 %all-to-all-start.1 = ((bf16[8,24,3584]{2,1,0:T(8,128)(2,1)}), bf16[8,24,3584]{2,1,0:T(8,128)(2,1)}, u32[]{:S(2)}, u32[]{:S(2)}) async-start(bf16[8,24,3584]{2,1,0:T(8,128)(2,1)} %param.1), calls=%async_computation.1 | async-start | bytes 2752512 | tf_op jit(solution)/shard_map/cond/branch_1_fun/all_to_all | solution.py:268
  45.9 24.6 %all-to-all-start.6 = ((bf16[8,24,3072]{2,1,0:T(8,128)(2,1)}), bf16[8,24,3072]{2,1,0:T(8,128)(2,1)}, u32[]{:S(2)}, u32[]{:S(2)}) async-start(bf16[8,24,3072]{2,1,0:T(8,128)(2,1)} %get-tuple-element.397), calls=%async_computation.6 | async-start | bytes 2359296 | tf_op jit(solution)/shard_map/all_to_all | solution.py:268
  52.6 1.8 collective-permute-start.3
  74.1 22.9 %all-to-all-start.7 = ((bf16[8,24,3072]{2,1,0:T(8,128)(2,1)}), bf16[8,24,3072]{2,1,0:T(8,128)(2,1)}, u32[]{:S(2)}, u32[]{:S(2)}) async-start(bf16[8,24,3072]{2,1,0:T(8,128)(2,1)} %get-tuple-element.399), calls=%async_computation.7 | async-start | bytes 2359296 | tf_op jit(solution)/shard_map/all_to_all | solution.py:268
  78.3 18.6 %collective-permute-start.4 = (bf16[192,512]{1,0:T(8,128)(2,1)}, bf16[192,512]{1,0:T(8,128)(2,1)}, u32[]{:S(2)}, u32[]{:S(2)}) collective-permute-start(bf16[192,512]{1,0:T(8,128)(2,1)} %get-tuple-element.401), channel_id=1, source_target_pairs={{0,8},{1,9},{2,10},{3,11},{4,12},{5,13},{6,14},{7,15},{8,0},{9,1},... | collective-permute-start | bytes 589832 | tf_op jit(solution)/shard_map/ppermute | solution.py:261
  104.3 22.4 %copy-start.3 = (bf16[24,3072]{1,0:T(8,128)(2,1)S(1)}, bf16[24,3072]{1,0:T(8,128)(2,1)}, u32[]{:S(2)}) copy-start(bf16[24,3072]{1,0:T(8,128)(2,1)} %get-tuple-element.405) | copy-start | bytes 442372
  104.3 22.4 %all-to-all-start.8 = ((bf16[8,24,3072]{2,1,0:T(8,128)(2,1)}), bf16[8,24,3072]{2,1,0:T(8,128)(2,1)}, u32[]{:S(2)}, u32[]{:S(2)}) async-start(bf16[8,24,3072]{2,1,0:T(8,128)(2,1)} %get-tuple-element.403), calls=%async_computation.8 | async-start | bytes 2359296 | tf_op jit(solution)/shard_map/all_to_all | solution.py:268
  108.7 23.5 %collective-permute-start.5 = (bf16[2,192,256]{2,1,0:T(8,128)(2,1)}, bf16[2,192,256]{2,1,0:T(8,128)(2,1)}, u32[]{:S(2)}, u32[]{:S(2)}) collective-permute-start(bf16[2,192,256]{2,1,0:T(8,128)(2,1)} %get-tuple-element.404), channel_id=1, source_target_pairs={{0,8},{1,9},{2,10},{3,11},{4,12},{5,13},{6,14},{7,15},{8,0},{9,1},... | collective-permute-start | bytes 589832 | tf_op jit(solution)/shard_map/ppermute | solution.py:261
  128.8 6.4 %collective-permute-start.6 = (bf16[24,3072]{1,0:T(8,128)(2,1)}, bf16[24,3072]{1,0:T(8,128)(2,1)S(1)}, u32[]{:S(2)}, u32[]{:S(2)}) collective-permute-start(bf16[24,3072]{1,0:T(8,128)(2,1)} %get-tuple-element.475), channel_id=1, source_target_pairs={{0,16},{1,17},{2,18},{3,19},{4,20},{5,21},{6,22},{7,23}} | collective-permute-start | bytes 442376 | tf_op jit(solution)/shard_map/ppermute | solution.py:265
  135.2 0.7 copy-start.12
  137.8 1.3 copy-start.11
  137.8 1.3 collective-permute-start.7
  145.7 31.5 %copy-start.2 = (bf16[2,192,256]{2,1,0:T(8,128)(2,1)}, bf16[2,192,256]{2,1,0:T(8,128)(2,1)S(1)}, u32[]{:S(2)}) copy-start(bf16[2,192,256]{2,1,0:T(8,128)(2,1)S(1)} %get-tuple-element.408) | copy-start | bytes 589828
  145.7 31.5 %copy-start.13 = (bf16[24,3072]{1,0:T(8,128)(2,1)S(1)}, bf16[24,3072]{1,0:T(8,128)(2,1)}, u32[]{:S(2)}) copy-start(bf16[24,3072]{1,0:T(8,128)(2,1)} %copy-done.12) | copy-start | bytes 442372
  145.8 31.5 %all-to-all-start.9 = ((bf16[8,24,3072]{2,1,0:T(8,128)(2,1)}), bf16[8,24,3072]{2,1,0:T(8,128)(2,1)S(1)}, u32[]{:S(2)}, u32[]{:S(2)}) async-start(bf16[8,24,3072]{2,1,0:T(8,128)(2,1)} %get-tuple-element.407), calls=%async_computation.9 | async-start | bytes 2359296 | tf_op jit(solution)/shard_map/all_to_all | solution.py:268
  149.5 27.8 %collective-permute-start.8 = (bf16[2,192,256]{2,1,0:T(8,128)(2,1)S(1)}, bf16[2,192,256]{2,1,0:T(8,128)(2,1)}, u32[]{:S(2)}, u32[]{:S(2)}) collective-permute-start(bf16[2,192,256]{2,1,0:T(8,128)(2,1)S(1)} %get-tuple-element.408), channel_id=1, source_target_pairs={{0,8},{1,9},{2,10},{3,11},{4,12},{5,13},{6,14},{7,15},{8,0},{9,1},... | collective-permute-start | bytes 589832 | tf_op jit(solution)/shard_map/ppermute | solution.py:261
  180.3 27.9 %copy-start.4 = (bf16[8,24,3072]{2,1,0:T(8,128)(2,1)S(1)}, bf16[8,24,3072]{2,1,0:T(8,128)(2,1)}, u32[]{:S(2)}) copy-start(bf16[8,24,3072]{2,1,0:T(8,128)(2,1)} %get-tuple-element.411) | copy-start | bytes 3538948
  180.3 17.1 %collective-permute-start.9 = (bf16[2,192,256]{2,1,0:T(8,128)(2,1)}, bf16[2,192,256]{2,1,0:T(8,128)(2,1)S(1)}, u32[]{:S(2)}, u32[]{:S(2)}) collective-permute-start(bf16[2,192,256]{2,1,0:T(8,128)(2,1)} %get-tuple-element.410), channel_id=1, source_target_pairs={{0,16},{1,17},{2,18},{3,19},{4,20},{5,21},{6,22},{7,23},{8,24},{9,... | collective-permute-start | bytes 589832 | tf_op jit(solution)/shard_map/ppermute | solution.py:410
  208.2 25.0 %copy-start.7 = (bf16[8,24,512]{2,1,0:T(8,128)(2,1)}, bf16[8,24,512]{2,1,0:T(8,128)(2,1)S(1)}, u32[]{:S(2)}) copy-start(bf16[8,24,512]{2,1,0:T(8,128)(2,1)S(1)} %get-tuple-element.478) | copy-start | bytes 589828
  240.5 24.9 %copy-start.9 = (bf16[24,3072]{1,0:T(8,128)(2,1)}, bf16[24,3072]{1,0:T(8,128)(2,1)S(1)}, u32[]{:S(2)}) copy-start(bf16[24,3072]{1,0:T(8,128)(2,1)S(1)} %get-tuple-element.416) | copy-start | bytes 442372
  240.5 24.9 %copy-start.8 = (bf16[8,24,512]{2,1,0:T(8,128)(2,1)S(1)}, bf16[8,24,512]{2,1,0:T(8,128)(2,1)}, u32[]{:S(2)}) copy-start(bf16[8,24,512]{2,1,0:T(8,128)(2,1)} %copy-done.7) | copy-start | bytes 589828
  265.4 3.3 %collective-permute-start.11 = (bf16[8,24,512]{2,1,0:T(8,128)(2,1)S(1)}, bf16[8,24,512]{2,1,0:T(8,128)(2,1)S(1)}, u32[]{:S(2)}, u32[]{:S(2)}) collective-permute-start(bf16[8,24,512]{2,1,0:T(8,128)(2,1)S(1)} %copy-done.8), channel_id=1, source_target_pairs={{0,8},{1,9},{2,10},{3,11},{4,12},{5,13},{6,14},{7,15},{8,0},{9,1},... | collective-permute-start | bytes 589832 | tf_op jit(solution)/shard_map/ppermute | solution.py:434
  267.3 4.1 %collective-permute-start.10 = (bf16[2,192,256]{2,1,0:T(8,128)(2,1)}, bf16[2,192,256]{2,1,0:T(8,128)(2,1)S(1)}, u32[]{:S(2)}, u32[]{:S(2)}) collective-permute-start(bf16[2,192,256]{2,1,0:T(8,128)(2,1)} %get-tuple-element.414), channel_id=1, source_target_pairs={{0,8},{1,9},{2,10},{3,11},{4,12},{5,13},{6,14},{7,15},{8,0},{9,1},... | collective-permute-start | bytes 589832 | tf_op jit(solution)/shard_map/ppermute | solution.py:261
  269.5 10.0 %collective-permute-start.12 = (bf16[8,24,1024]{2,1,0:T(8,128)(2,1)}, bf16[8,24,1024]{2,1,0:T(8,128)(2,1)}, u32[]{:S(2)}, u32[]{:S(2)}) collective-permute-start(bf16[8,24,1024]{2,1,0:T(8,128)(2,1)} %pad_maximum_fusion.1), channel_id=1, source_target_pairs={{0,16},{1,17},{2,18},{3,19},{4,20},{5,21},{6,22},{7,23},{8,8},{9,9... | collective-permute-start | bytes 1179656 | tf_op jit(solution)/shard_map/ppermute | solution.py:444
  271.4 0.7 copy-start.5
  272.1 7.3 %copy-start.6 = (bf16[2,192,256]{2,1,0:T(8,128)(2,1)S(1)}, bf16[2,192,256]{2,1,0:T(8,128)(2,1)}, u32[]{:S(2)}) copy-start(bf16[2,192,256]{2,1,0:T(8,128)(2,1)} %copy-done.5) | copy-start | bytes 589828
  298.6 15.1 %collective-permute-start.13 = (bf16[24,3072]{1,0:T(8,128)(2,1)S(1)}, bf16[24,3072]{1,0:T(8,128)(2,1)S(1)}, u32[]{:S(2)}, u32[]{:S(2)}) collective-permute-start(bf16[24,3072]{1,0:T(8,128)(2,1)S(1)} %get-tuple-element.424), channel_id=1, source_target_pairs={{0,8},{1,9},{2,10},{3,11},{4,12},{5,13},{6,14},{7,15},{8,0},{9,1},... | collective-permute-start | bytes 442376 | tf_op jit(solution)/shard_map/ppermute | solution.py:261

commit v10 on v8

--- a/solution.py
+++ b/solution.py
@@ -15,15 +15,11 @@
 
 
 def normalise(values, params_ref):
-    return normalise_by(values, params_ref[0:1, :], params_ref[1:2, :])
-
-
-def normalise_by(values, shift_row, scale_row):
     centered = values - jnp.mean(values, axis=-1, keepdims=True)
     spread = jnp.mean(centered * centered, axis=-1, keepdims=True)
-    return (centered * lax.rsqrt(spread + 1e-06) * (1.0 + scale_row) + shift_row).astype(
-        jnp.bfloat16
-    )
+    return (
+        centered * lax.rsqrt(spread + 1e-06) * (1.0 + params_ref[1:2, :]) + params_ref[0:1, :]
+    ).astype(jnp.bfloat16)
 
 
 def spread_block(block, buffer, out_ref, sems):
@@ -44,21 +40,14 @@
         copy.wait()
 
 
-def pack_kernel(shift_ref, scale_ref, hidden_ref, stale_ref, out_ref, buffer, sems, sides, sem, cache, cache_sem):
-    fetch = pltpu.make_async_copy(stale_ref.at[0, 1], cache, cache_sem)
-    fetch.start()
+def pack_kernel(params_ref, x_ref, cache_ref, out_ref, buffer, sems, sides, sem):
     count, _, total = sides.shape
-    width = hidden_ref.shape[2]
+    width = x_ref.shape[1]
     channels = total // 2
-    early = lax.rem(lax.axis_index("pipe"), 2) == 0
-    x = jnp.where(
-        early, hidden_ref[0].astype(jnp.float32), hidden_ref[1].astype(jnp.float32)
-    )
-    block = normalise_by(x, shift_ref[...], scale_ref[...])
+    block = normalise(x_ref[...].astype(jnp.float32), params_ref)
     copies = spread_block(block, buffer, out_ref, sems)
-    fetch.wait()
     for kind in range(2):
-        rows = cache[:, kind, :]
+        rows = cache_ref[:, kind, :]
         for shard in range(count):
             sides[shard, :, kind * channels : (kind + 1) * channels] = rows[
                 :, shard * channels : (shard + 1) * channels
@@ -289,13 +278,12 @@
     spreading = [pltpu.VMEM((rows, width), jnp.bfloat16), pltpu.SemaphoreType.DMA((seq,))]
     packed = pl.pallas_call(
         pack_kernel, out_shape=bf16(seq, rows, width + 2 * channels),
-        in_specs=[VMEM] * 3 + [ANY], out_specs=HBM,
+        in_specs=[VMEM] * 3, out_specs=HBM,
         scratch_shapes=spreading + [
             pltpu.VMEM((seq, rows, 2 * channels), jnp.bfloat16), pltpu.SemaphoreType.DMA,
-            pltpu.VMEM(stale_cache.shape[2:], jnp.bfloat16), pltpu.SemaphoreType.DMA,
         ],
         compiler_params=params_of(16),
-    )(mod_shift, mod_scale, hidden, stale_cache)
+    )(own_params, x, stale_cache[0, 1])
 
     other_params = swap(own_params)
     own_in, own_out, other_params, packed = lax.optimization_barrier(

time: 295 us -> 286 us (0.969)
  Pallas kernels: 46.4 us -> 41.5 us
  local copies, waits for them, and re-layouts: 8.65 us -> 4.58 us
    unnamed x36 -> x30, local copies, waits for them, and re-layouts: 5.43 us -> 2.03 us
  transfers between devices with their start and end apart: 18 -> 18, of which waited for: 10 -> 10; matrix products, arithmetic and copies ran while one was open for 2% -> 1% of each run, Pallas kernels for 2% -> 1%
where the time goes in v10:
time: 286 us; the launch traced here: 285 us
  waiting for transfers between devices  140 us (49%)
  starting transfers between devices  62.2 us (22%)
  Pallas kernels  41.5 us (15%)
  blocking collectives  32.7 us (11%)
  local copies, waits for them, and re-layouts  4.58 us (2%)
  other arithmetic  3.43 us (1%)
    all_to_all x7, waiting for transfers between devices, across(): lax.all_to_all(blocks, 'seq', split_axis=0, concat_axis=0, tiled=True)  135 us
    all_to_all x7, starting transfers between devices, across(): lax.all_to_all(blocks, 'seq', split_axis=0, concat_axis=0, tiled=True)  33.8 us
    all_to_all x1, blocking collectives, across(): lax.all_to_all(blocks, 'seq', split_axis=0, concat_axis=0, tiled=True)  32.7 us
    pallas_call x4, Pallas kernels, block(): pl.pallas_call(functools.partial(block_kernel, turn, head_size, planes),...  27.8 us
    ppermute x9, starting transfers between devices, swap(): return lax.ppermute(value, AXES, pairs)  23.7 us
    pallas_call x4, Pallas kernels, finish(): pl.pallas_call(finish_kernel, out_shape=shapes, in_specs=[VMEM] * 4, out_...  8.17 us
  transfers between devices with their start and end apart: 18, of which 10 were waited for; matrix products, arithmetic and copies ran while one was open for 1% of the time, Pallas kernels for 1%

profile of v10, /device:TPU:0, one launch (start us, length us, event | category | flops | bytes accessed | tf_op | source)
XLA Modules:
  0.0 285.5 jit_solution(7696733015658320712)
XLA Ops:
  0.6 0.8 select_maximum_fusion.params_ref
  2.0 1.2 slice_bitcast_fusion.cache_ref
  3.3 1.5 shard_map.95
  5.5 33.2 %conditional.12 = (bf16[8,24,3584]{2,1,0:T(8,128)(2,1)}, bf16[192,512]{1,0:T(8,128)(2,1)}, bf16[192,3584]{1,0:T(8,128)(2,1)S(1)}) conditional(s32[]{:T(128)} %convert_element_type.6, bf16[8,24,3584]{2,1,0:T(8,128)(2,1)} %shard_map.95, bf16[8,24,3584]{2,1,0:T(8,128)(2,1)} %shard_map.95), branch_computations={%region_0.1_spmd, %region_1.2_spmd} | conditional | bytes 6881336 | solution.py:341
  5.5 6.9 %all-to-all-start.1 = ((bf16[8,24,3584]{2,1,0:T(8,128)(2,1)}), bf16[8,24,3584]{2,1,0:T(8,128)(2,1)}, u32[]{:S(2)}, u32[]{:S(2)}) async-start(bf16[8,24,3584]{2,1,0:T(8,128)(2,1)} %param.1), calls=%async_computation.1 | async-start | bytes 2752512 | tf_op jit(solution)/shard_map/cond/branch_1_fun/all_to_all | solution.py:268
  12.4 25.0 %all-to-all-done.1 = bf16[8,24,3584]{2,1,0:T(8,128)(2,1)} async-done(((bf16[8,24,3584]{2,1,0:T(8,128)(2,1)}), bf16[8,24,3584]{2,1,0:T(8,128)(2,1)}, u32[]{:S(2)}, u32[]{:S(2)}) %all-to-all-start.1) | async-done | bytes 1376288 | tf_op jit(solution)/shard_map/cond/branch_1_fun/all_to_all | solution.py:268
  37.4 1.3 copy.15
  38.7 7.2 %conditional.13 = (bf16[8,24,3072]{2,1,0:T(8,128)(2,1)}, bf16[2,192,256]{2,1,0:T(8,128)(2,1)}) conditional(s32[]{:T(128)} %convert_element_type.6, (f32[4,3072]{1,0:T(4,128)S(1)}, bf16[24,3072]{1,0:T(8,128)(2,1)S(1)}) %tuple.115, (bf16[8,24,3584]{2,1,0:T(8,128)(2,1)}, f32[2,128]{1,0:T(2,128)S(1)}, bf16[3,3072,256]{2,1,0:T(8,128)(2,1)}, ...), branch_computations={%region_2.3_spmd, %region_3.4_spmd} | conditional | bytes 16 | solution.py:341
  38.7 7.2 %branch_1_fun.19 = (bf16[192,3072]{1,0:T(8,128)(2,1)}, bf16[2,192,256]{2,1,0:T(8,128)(2,1)}) custom-call(f32[2,128]{1,0:T(2,128)S(1)} %get-tuple-element.222.gain_ref, bf16[3,3072,256]{2,1,0:T(8,128)(2,1)} %get-tuple-element.223.own_in, bf16[3,3072,256]{2,1,0:T(8,128)(2,1)} %get-tuple-element.224.other_in, ...), custom_call_target="tpu_custom_call" | custom-call | tf_op jit(solution)/shard_map/cond/branch_1_fun/pallas_call | solution.py:310
  46.0 6.6 %all-to-all-start.5 = ((bf16[8,24,3072]{2,1,0:T(8,128)(2,1)}), bf16[8,24,3072]{2,1,0:T(8,128)(2,1)}, u32[]{:S(2)}, u32[]{:S(2)}) async-start(bf16[8,24,3072]{2,1,0:T(8,128)(2,1)} %get-tuple-element.376), calls=%async_computation.5 | async-start | bytes 2359296 | tf_op jit(solution)/shard_map/all_to_all | solution.py:268
  52.6 17.9 %all-to-all-done.5 = bf16[8,24,3072]{2,1,0:T(8,128)(2,1)} async-done(((bf16[8,24,3072]{2,1,0:T(8,128)(2,1)}), bf16[8,24,3072]{2,1,0:T(8,128)(2,1)}, u32[]{:S(2)}, u32[]{:S(2)}) %all-to-all-start.5) | async-done | bytes 1179680 | tf_op jit(solution)/shard_map/all_to_all | solution.py:268
  70.5 3.6 %conditional.14 = (bf16[8,24,3072]{2,1,0:T(8,128)(2,1)}, bf16[2,192,256]{2,1,0:T(8,128)(2,1)}, bf16[24,3072]{1,0:T(8,128)(2,1)}) conditional(s32[]{:T(128)} %convert_element_type.6, (bf16[8,24,3072]{2,1,0:T(8,128)(2,1)}, f32[2,128]{1,0:T(2,128)S(1)}, bf16[3,3072,256]{2,1,0:T(8,128)(2,1)}, bf16[3,3072,256]{2,1,0:T(8,128)(2,1)}, ...), branch_computations={%region_4.5_spmd, %region_5.6_spmd} | conditional | bytes 24 | solution.py:341
  70.5 3.5 %branch_1_fun.20 = (bf16[24,3072]{1,0:T(8,128)(2,1)}, bf16[8,24,3072]{2,1,0:T(8,128)(2,1)}) custom-call(f32[4,3072]{1,0:T(4,128)S(1)} %get-tuple-element.240.params_ref, f32[4,3072]{1,0:T(4,128)S(1)} %get-tuple-element.241.next_ref, bf16[24,3072]{1,0:T(8,128)(2,1)S(1)} %get-tuple-element.242.x_ref, bf16[8,24,3072]{2,1,0:T(8,128)(2,1)} %get-tuple-element.243.parts_ref), custom_call_target="tpu_custom_call" | custom-call | tf_op jit(solution)/shard_map/cond/branch_1_fun/pallas_call | solution.py:334
  74.1 4.3 %all-to-all-start.6 = ((bf16[8,24,3072]{2,1,0:T(8,128)(2,1)}), bf16[8,24,3072]{2,1,0:T(8,128)(2,1)}, u32[]{:S(2)}, u32[]{:S(2)}) async-start(bf16[8,24,3072]{2,1,0:T(8,128)(2,1)} %get-tuple-element.378), calls=%async_computation.6 | async-start | bytes 2359296 | tf_op jit(solution)/shard_map/all_to_all | solution.py:268
  78.5 18.5 %all-to-all-done.6 = bf16[8,24,3072]{2,1,0:T(8,128)(2,1)} async-done(((bf16[8,24,3072]{2,1,0:T(8,128)(2,1)}), bf16[8,24,3072]{2,1,0:T(8,128)(2,1)}, u32[]{:S(2)}, u32[]{:S(2)}) %all-to-all-start.6) | async-done | bytes 1179680 | tf_op jit(solution)/shard_map/all_to_all | solution.py:268
  96.9 7.3 %conditional.15 = (bf16[8,24,3072]{2,1,0:T(8,128)(2,1)}, bf16[2,192,256]{2,1,0:T(8,128)(2,1)}, bf16[24,3072]{1,0:T(8,128)(2,1)}) conditional(s32[]{:T(128)} %convert_element_type.6, (f32[4,3072]{1,0:T(4,128)S(1)}, f32[4,3072]{1,0:T(4,128)S(1)}, bf16[24,3072]{1,0:T(8,128)(2,1)S(1)}, bf16[8,24,3072]{2,1,0:T(8,128)(2,1)}, ...), branch_computations={%region_6.7_spmd, %region_7.8_spmd} | conditional | bytes 24 | solution.py:341
  96.9 7.3 %branch_1_fun.22 = (bf16[192,3072]{1,0:T(8,128)(2,1)}, bf16[2,192,256]{2,1,0:T(8,128)(2,1)}) custom-call(f32[2,128]{1,0:T(2,128)S(1)} %get-tuple-element.253.gain_ref, bf16[3,3072,256]{2,1,0:T(8,128)(2,1)} %get-tuple-element.254.own_in, bf16[3,3072,256]{2,1,0:T(8,128)(2,1)} %get-tuple-element.255.other_in, ...), custom_call_target="tpu_custom_call" | custom-call | tf_op jit(solution)/shard_map/cond/branch_1_fun/pallas_call | solution.py:310
  104.3 4.4 %all-to-all-start.7 = ((bf16[8,24,3072]{2,1,0:T(8,128)(2,1)}), bf16[8,24,3072]{2,1,0:T(8,128)(2,1)}, u32[]{:S(2)}, u32[]{:S(2)}) async-start(bf16[8,24,3072]{2,1,0:T(8,128)(2,1)} %get-tuple-element.382), calls=%async_computation.7 | async-start | bytes 2359296 | tf_op jit(solution)/shard_map/all_to_all | solution.py:268
  108.8 18.0 %all-to-all-done.7 = bf16[8,24,3072]{2,1,0:T(8,128)(2,1)} async-done(((bf16[8,24,3072]{2,1,0:T(8,128)(2,1)}), bf16[8,24,3072]{2,1,0:T(8,128)(2,1)}, u32[]{:S(2)}, u32[]{:S(2)}) %all-to-all-start.7) | async-done | bytes 1179680 | tf_op jit(solution)/shard_map/all_to_all | solution.py:268
  126.7 2.1 conditional.16
  126.7 2.1 branch_1_fun.24
  128.8 3.4 %collective-permute-start.6 = (bf16[24,3072]{1,0:T(8,128)(2,1)}, bf16[24,3072]{1,0:T(8,128)(2,1)S(1)}, u32[]{:S(2)}, u32[]{:S(2)}) collective-permute-start(bf16[24,3072]{1,0:T(8,128)(2,1)} %get-tuple-element.454), channel_id=1, source_target_pairs={{0,16},{1,17},{2,18},{3,19},{4,20},{5,21},{6,22},{7,23}} | collective-permute-start | bytes 442376 | tf_op jit(solution)/shard_map/ppermute | solution.py:265
  132.3 2.9 %collective-permute-done.6 = bf16[24,3072]{1,0:T(8,128)(2,1)S(1)} collective-permute-done((bf16[24,3072]{1,0:T(8,128)(2,1)}, bf16[24,3072]{1,0:T(8,128)(2,1)S(1)}, u32[]{:S(2)}, u32[]{:S(2)}) %collective-permute-start.6) | collective-permute-done | bytes 147488 | tf_op jit(solution)/shard_map/ppermute | solution.py:265
  135.9 1.9 conditional.17
  135.9 1.9 branch_1_fun.26
  137.8 1.4 collective-permute-start.7
  139.2 6.6 %conditional.20 = (bf16[8,24,3072]{2,1,0:T(8,128)(2,1)}, bf16[2,192,256]{2,1,0:T(8,128)(2,1)S(1)}) conditional(s32[]{:T(128)} %convert_element_type.6, (f32[4,3072]{1,0:T(4,128)S(1)}, bf16[24,3072]{1,0:T(8,128)(2,1)}) %tuple.128, (bf16[8,24,3072]{2,1,0:T(8,128)(2,1)}, f32[2,128]{1,0:T(2,128)S(1)}, bf16[3,3072,256]{2,1,0:T(8,128)(2,1)}, ...), branch_computations={%region_16.17_spmd, %region_17.18_spmd} | conditional | bytes 16 | solution.py:341
  139.2 6.6 %branch_1_fun.28 = (bf16[192,3072]{1,0:T(8,128)(2,1)}, bf16[2,192,256]{2,1,0:T(8,128)(2,1)S(1)}) custom-call(f32[2,128]{1,0:T(2,128)S(1)} %get-tuple-element.283.gain_ref, bf16[3,3072,256]{2,1,0:T(8,128)(2,1)} %get-tuple-element.284.own_in, bf16[3,3072,256]{2,1,0:T(8,128)(2,1)} %get-tuple-element.285.other_in, ...), custom_call_target="tpu_custom_call" | custom-call | tf_op jit(solution)/shard_map/cond/branch_1_fun/pallas_call | solution.py:310
  145.8 3.7 %all-to-all-start.8 = ((bf16[8,24,3072]{2,1,0:T(8,128)(2,1)}), bf16[8,24,3072]{2,1,0:T(8,128)(2,1)S(1)}, u32[]{:S(2)}, u32[]{:S(2)}) async-start(bf16[8,24,3072]{2,1,0:T(8,128)(2,1)} %get-tuple-element.386), calls=%async_computation.8 | async-start | bytes 2359296 | tf_op jit(solution)/shard_map/all_to_all | solution.py:268
  149.5 4.9 %collective-permute-start.8 = (bf16[2,192,256]{2,1,0:T(8,128)(2,1)S(1)}, bf16[2,192,256]{2,1,0:T(8,128)(2,1)}, u32[]{:S(2)}, u32[]{:S(2)}) collective-permute-start(bf16[2,192,256]{2,1,0:T(8,128)(2,1)S(1)} %get-tuple-element.387), channel_id=1, source_target_pairs={{0,8},{1,9},{2,10},{3,11},{4,12},{5,13},{6,14},{7,15},{8,0},{9,1},... | collective-permute-start | bytes 589832 | tf_op jit(solution)/shard_map/ppermute | solution.py:261
  154.4 22.9 %all-to-all-done.8 = bf16[8,24,3072]{2,1,0:T(8,128)(2,1)S(1)} async-done(((bf16[8,24,3072]{2,1,0:T(8,128)(2,1)}), bf16[8,24,3072]{2,1,0:T(8,128)(2,1)S(1)}, u32[]{:S(2)}, u32[]{:S(2)}) %all-to-all-start.8) | async-done | bytes 1179680 | tf_op jit(solution)/shard_map/all_to_all | solution.py:268
  177.3 2.3 conditional.21
  177.3 2.3 branch_1_fun.29
  179.7 32.7 %all_to_all.52 = bf16[8,24,3072]{2,1,0:T(8,128)(2,1)S(1)} all-to-all(bf16[8,24,3072]{2,1,0:T(8,128)(2,1)} %get-tuple-element.389), channel_id=1, replica_groups=mesh['pipe'=4,'seq'=8] {'seq'}, dimensions={0} | all-to-all | bytes 2359296 | tf_op jit(solution)/shard_map/all_to_all | solution.py:268
  212.4 6.7 %conditional.22 = (bf16[8,24,3072]{2,1,0:T(8,128)(2,1)}, bf16[2,192,256]{2,1,0:T(8,128)(2,1)S(1)}, bf16[24,3072]{1,0:T(8,128)(2,1)S(1)}) conditional(s32[]{:T(128)} %convert_element_type.6, (f32[4,3072]{1,0:T(4,128)S(1)}, f32[4,3072]{1,0:T(4,128)S(1)}, bf16[24,3072]{1,0:T(8,128)(2,1)}, bf16[8,24,3072]{2,1,0:T(8,128)(2,1)S(1)}, ...), branch_computations={%region_20.21_spmd, %region_21.22_spmd} | conditional | bytes 24 | solution.py:341
  212.4 6.6 %branch_1_fun.31 = (bf16[192,3072]{1,0:T(8,128)(2,1)}, bf16[2,192,256]{2,1,0:T(8,128)(2,1)S(1)}) custom-call(f32[2,128]{1,0:T(2,128)S(1)} %get-tuple-element.314.gain_ref, bf16[3,3072,256]{2,1,0:T(8,128)(2,1)} %get-tuple-element.315.own_in, bf16[3,3072,256]{2,1,0:T(8,128)(2,1)} %get-tuple-element.316.other_in, ...), custom_call_target="tpu_custom_call" | custom-call | tf_op jit(solution)/shard_map/cond/branch_1_fun/pallas_call | solution.py:310
  219.7 4.5 %all-to-all-start.10 = ((bf16[8,24,3072]{2,1,0:T(8,128)(2,1)}), bf16[8,24,3072]{2,1,0:T(8,128)(2,1)S(1)}, u32[]{:S(2)}, u32[]{:S(2)}) async-start(bf16[8,24,3072]{2,1,0:T(8,128)(2,1)} %get-tuple-element.391), calls=%async_computation.10 | async-start | bytes 2359296 | tf_op jit(solution)/shard_map/all_to_all | solution.py:268
  224.3 1.4 collective-permute-done.9
  226.4 1.3 select_select_fusion
  227.7 23.2 %all-to-all-done.10 = bf16[8,24,3072]{2,1,0:T(8,128)(2,1)S(1)} async-done(((bf16[8,24,3072]{2,1,0:T(8,128)(2,1)}), bf16[8,24,3072]{2,1,0:T(8,128)(2,1)S(1)}, u32[]{:S(2)}, u32[]{:S(2)}) %all-to-all-start.10) | async-done | bytes 1179680 | tf_op jit(solution)/shard_map/all_to_all | solution.py:268
  250.8 14.1 %conditional.23 = ((bf16[24,3072]{1,0:T(8,128)(2,1)S(1)}, bf16[2,24,2,2048]{3,2,1,0:T(2,128)(2,1)S(1)})) conditional(s32[]{:T(128)} %convert_element_type.6, (bf16[8,24,3072]{2,1,0:T(8,128)(2,1)S(1)}, f32[2,128]{1,0:T(2,128)S(1)}, bf16[3,3072,256]{2,1,0:T(8,128)(2,1)}, bf16[3,3072,256]{2,1,0:T(8,128)(2,1)}, bf16[1,256,3072]{2,1,0:T(8,128)(2,1)S(1)}, ...), branch_computations={%region_22.23_spmd, %region_23.24_spmd} | conditional | bytes 3735588 | solution.py:341
  250.8 0.8 branch_1_fun.34
  251.6 3.5 %all-to-all-start.4 = ((bf16[8,24,1024]{2,1,0:T(8,128)(2,1)}), bf16[8,24,1024]{2,1,0:T(8,128)(2,1)S(1)}, u32[]{:S(2)}, u32[]{:S(2)}) async-start(bf16[8,24,1024]{2,1,0:T(8,128)(2,1)} %bitcast.19), calls=%async_computation.4 | async-start | bytes 786432 | tf_op jit(solution)/shard_map/cond/branch_1_fun/all_to_all | solution.py:268
  255.3 9.1 %all-to-all-done.4.caches_ref = bf16[8,24,1024]{2,1,0:T(8,128)(2,1)S(1)} async-done(((bf16[8,24,1024]{2,1,0:T(8,128)(2,1)}), bf16[8,24,1024]{2,1,0:T(8,128)(2,1)S(1)}, u32[]{:S(2)}, u32[]{:S(2)}) %all-to-all-start.4) | async-done | bytes 393248 | tf_op jit(solution)/shard_map/cond/branch_1_fun/all_to_all | solution.py:268
  265.0 1.3 select_select_fusion.2
  266.3 17.5 %collective-permute-start.10 = (bf16[24,3072]{1,0:T(8,128)(2,1)S(1)}, bf16[24,3072]{1,0:T(8,128)(2,1)S(1)}, u32[]{:S(2)}, u32[]{:S(2)}) collective-permute-start(bf16[24,3072]{1,0:T(8,128)(2,1)S(1)} %get-tuple-element.404), channel_id=1, source_target_pairs={{0,8},{1,9},{2,10},{3,11},{4,12},{5,13},{6,14},{7,15},{8,0},{9,1},... | collective-permute-start | bytes 442376 | tf_op jit(solution)/shard_map/ppermute | solution.py:261
  283.7 1.0 collective-permute-done.10.theirs_ref
  284.7 0.7 shard_map.96
  (63 shorter events, 4.3 us)
Async XLA Ops:
  0.6 2.6 copy-start
  1.5 3.3 %collective-permute-start = (f32[4,3072]{1,0:T(4,128)S(1)}, f32[4,3072]{1,0:T(4,128)S(1)}, u32[]{:S(2)}, u32[]{:S(2)}) collective-permute-start(f32[4,3072]{1,0:T(4,128)S(1)} %select_maximum_fusion.params_ref), channel_id=1, source_target_pairs={{0,8},{1,9},{2,10},{3,11},{4,12},{5,13},{6,14},{7,15},{8,0},{9,1},... | collective-permute-start | bytes 147464 | tf_op jit(solution)/shard_map/ppermute | solution.py:261
  2.0 2.9 %copy-start.1 = (bf16[1,256,3072]{2,1,0:T(8,128)(2,1)S(1)}, bf16[1,256,3072]{2,1,0:T(8,128)(2,1)}, u32[]{:S(2)}) copy-start(bf16[1,256,3072]{2,1,0:T(8,128)(2,1)} %param.38) | copy-start | bytes 4718596
  2.0 3.4 %copy-start.12 = (f32[1,3072]{1,0:T(1,128)S(1)}, f32[1,3072]{1,0:T(1,128)}, u32[]{:S(2)}) copy-start(f32[1,3072]{1,0:T(1,128)} %param.35) | copy-start | bytes 36868
  2.0 3.4 %copy-start.13 = (f32[1,3072]{1,0:T(1,128)S(1)}, f32[1,3072]{1,0:T(1,128)}, u32[]{:S(2)}) copy-start(f32[1,3072]{1,0:T(1,128)} %param.34) | copy-start | bytes 36868
  2.0 3.4 %copy-start.14 = (f32[1,3072]{1,0:T(1,128)S(1)}, f32[1,3072]{1,0:T(1,128)}, u32[]{:S(2)}) copy-start(f32[1,3072]{1,0:T(1,128)} %param.33) | copy-start | bytes 36868
  2.0 3.4 %copy-start.15 = (f32[1,2,128]{2,1,0:T(2,128)S(1)}, f32[1,2,128]{2,1,0:T(2,128)}, u32[]{:S(2)}) copy-start(f32[1,2,128]{2,1,0:T(2,128)} %param.36) | copy-start | bytes 3076
  4.8 33.9 %collective-permute-start.1 = (bf16[3,3072,256]{2,1,0:T(8,128)(2,1)}, bf16[3,3072,256]{2,1,0:T(8,128)(2,1)}, u32[]{:S(2)}, u32[]{:S(2)}) collective-permute-start(bf16[3,3072,256]{2,1,0:T(8,128)(2,1)} %bitcast.33), channel_id=1, source_target_pairs={{0,8},{1,9},{2,10},{3,11},{4,12},{5,13},{6,14},{7,15},{8,0},{9,1},... | collective-permute-start | bytes 14155784 | tf_op jit(solution)/shard_map/ppermute | solution.py:261
  4.9 33.8 %collective-permute-start.2 = (bf16[1,256,3072]{2,1,0:T(8,128)(2,1)S(1)}, bf16[1,256,3072]{2,1,0:T(8,128)(2,1)}, u32[]{:S(2)}, u32[]{:S(2)}) collective-permute-start(bf16[1,256,3072]{2,1,0:T(8,128)(2,1)S(1)} %copy-done.1), channel_id=1, source_target_pairs={{0,8},{1,9},{2,10},{3,11},{4,12},{5,13},{6,14},{7,15},{8,0},{9,1},... | collective-permute-start | bytes 4718600 | tf_op jit(solution)/shard_map/ppermute | solution.py:261
  5.5 31.9 %all-to-all-start.1 = ((bf16[8,24,3584]{2,1,0:T(8,128)(2,1)}), bf16[8,24,3584]{2,1,0:T(8,128)(2,1)}, u32[]{:S(2)}, u32[]{:S(2)}) async-start(bf16[8,24,3584]{2,1,0:T(8,128)(2,1)} %param.1), calls=%async_computation.1 | async-start | bytes 2752512 | tf_op jit(solution)/shard_map/cond/branch_1_fun/all_to_all | solution.py:268
  46.0 24.6 %all-to-all-start.5 = ((bf16[8,24,3072]{2,1,0:T(8,128)(2,1)}), bf16[8,24,3072]{2,1,0:T(8,128)(2,1)}, u32[]{:S(2)}, u32[]{:S(2)}) async-start(bf16[8,24,3072]{2,1,0:T(8,128)(2,1)} %get-tuple-element.376), calls=%async_computation.5 | async-start | bytes 2359296 | tf_op jit(solution)/shard_map/all_to_all | solution.py:268
  52.6 18.0 %collective-permute-start.3 = (bf16[2,192,256]{2,1,0:T(8,128)(2,1)}, bf16[2,192,256]{2,1,0:T(8,128)(2,1)}, u32[]{:S(2)}, u32[]{:S(2)}) collective-permute-start(bf16[2,192,256]{2,1,0:T(8,128)(2,1)} %get-tuple-element.377), channel_id=1, source_target_pairs={{0,8},{1,9},{2,10},{3,11},{4,12},{5,13},{6,14},{7,15},{8,0},{9,1},... | collective-permute-start | bytes 589832 | tf_op jit(solution)/shard_map/ppermute | solution.py:261
  74.1 22.8 %all-to-all-start.6 = ((bf16[8,24,3072]{2,1,0:T(8,128)(2,1)}), bf16[8,24,3072]{2,1,0:T(8,128)(2,1)}, u32[]{:S(2)}, u32[]{:S(2)}) async-start(bf16[8,24,3072]{2,1,0:T(8,128)(2,1)} %get-tuple-element.378), calls=%async_computation.6 | async-start | bytes 2359296 | tf_op jit(solution)/shard_map/all_to_all | solution.py:268
  78.4 18.6 %collective-permute-start.4 = (bf16[192,512]{1,0:T(8,128)(2,1)}, bf16[192,512]{1,0:T(8,128)(2,1)}, u32[]{:S(2)}, u32[]{:S(2)}) collective-permute-start(bf16[192,512]{1,0:T(8,128)(2,1)} %get-tuple-element.380), channel_id=1, source_target_pairs={{0,8},{1,9},{2,10},{3,11},{4,12},{5,13},{6,14},{7,15},{8,0},{9,1},... | collective-permute-start | bytes 589832 | tf_op jit(solution)/shard_map/ppermute | solution.py:261
  104.3 22.4 %copy-start.2 = (bf16[24,3072]{1,0:T(8,128)(2,1)S(1)}, bf16[24,3072]{1,0:T(8,128)(2,1)}, u32[]{:S(2)}) copy-start(bf16[24,3072]{1,0:T(8,128)(2,1)} %get-tuple-element.384) | copy-start | bytes 442372
  104.3 22.4 %all-to-all-start.7 = ((bf16[8,24,3072]{2,1,0:T(8,128)(2,1)}), bf16[8,24,3072]{2,1,0:T(8,128)(2,1)}, u32[]{:S(2)}, u32[]{:S(2)}) async-start(bf16[8,24,3072]{2,1,0:T(8,128)(2,1)} %get-tuple-element.382), calls=%async_computation.7 | async-start | bytes 2359296 | tf_op jit(solution)/shard_map/all_to_all | solution.py:268
  108.7 23.6 %collective-permute-start.5 = (bf16[2,192,256]{2,1,0:T(8,128)(2,1)}, bf16[2,192,256]{2,1,0:T(8,128)(2,1)}, u32[]{:S(2)}, u32[]{:S(2)}) collective-permute-start(bf16[2,192,256]{2,1,0:T(8,128)(2,1)} %get-tuple-element.383), channel_id=1, source_target_pairs={{0,8},{1,9},{2,10},{3,11},{4,12},{5,13},{6,14},{7,15},{8,0},{9,1},... | collective-permute-start | bytes 589832 | tf_op jit(solution)/shard_map/ppermute | solution.py:261
  128.8 6.4 %collective-permute-start.6 = (bf16[24,3072]{1,0:T(8,128)(2,1)}, bf16[24,3072]{1,0:T(8,128)(2,1)S(1)}, u32[]{:S(2)}, u32[]{:S(2)}) collective-permute-start(bf16[24,3072]{1,0:T(8,128)(2,1)} %get-tuple-element.454), channel_id=1, source_target_pairs={{0,16},{1,17},{2,18},{3,19},{4,20},{5,21},{6,22},{7,23}} | collective-permute-start | bytes 442376 | tf_op jit(solution)/shard_map/ppermute | solution.py:265
  135.2 0.7 copy-start.9
  137.8 1.4 copy-start.8
  137.8 1.4 collective-permute-start.7
  145.8 3.7 %copy-start.5 = (bf16[2,192,256]{2,1,0:T(8,128)(2,1)}, bf16[2,192,256]{2,1,0:T(8,128)(2,1)S(1)}, u32[]{:S(2)}) copy-start(bf16[2,192,256]{2,1,0:T(8,128)(2,1)S(1)} %get-tuple-element.387) | copy-start | bytes 589828
  145.8 31.5 %copy-start.10 = (bf16[24,3072]{1,0:T(8,128)(2,1)S(1)}, bf16[24,3072]{1,0:T(8,128)(2,1)}, u32[]{:S(2)}) copy-start(bf16[24,3072]{1,0:T(8,128)(2,1)} %copy-done.9) | copy-start | bytes 442372
  145.8 31.5 %all-to-all-start.8 = ((bf16[8,24,3072]{2,1,0:T(8,128)(2,1)}), bf16[8,24,3072]{2,1,0:T(8,128)(2,1)S(1)}, u32[]{:S(2)}, u32[]{:S(2)}) async-start(bf16[8,24,3072]{2,1,0:T(8,128)(2,1)} %get-tuple-element.386), calls=%async_computation.8 | async-start | bytes 2359296 | tf_op jit(solution)/shard_map/all_to_all | solution.py:268
  149.5 27.8 %collective-permute-start.8 = (bf16[2,192,256]{2,1,0:T(8,128)(2,1)S(1)}, bf16[2,192,256]{2,1,0:T(8,128)(2,1)}, u32[]{:S(2)}, u32[]{:S(2)}) collective-permute-start(bf16[2,192,256]{2,1,0:T(8,128)(2,1)S(1)} %get-tuple-element.387), channel_id=1, source_target_pairs={{0,8},{1,9},{2,10},{3,11},{4,12},{5,13},{6,14},{7,15},{8,0},{9,1},... | collective-permute-start | bytes 589832 | tf_op jit(solution)/shard_map/ppermute | solution.py:261
  219.1 0.7 copy-start.6
  219.1 5.1 %copy-start.11 = (bf16[2,192,256]{2,1,0:T(8,128)(2,1)}, bf16[2,192,256]{2,1,0:T(8,128)(2,1)S(1)}, u32[]{:S(2)}) copy-start(bf16[2,192,256]{2,1,0:T(8,128)(2,1)S(1)} %get-tuple-element.392) | copy-start | bytes 589828
  219.7 31.1 %all-to-all-start.10 = ((bf16[8,24,3072]{2,1,0:T(8,128)(2,1)}), bf16[8,24,3072]{2,1,0:T(8,128)(2,1)S(1)}, u32[]{:S(2)}, u32[]{:S(2)}) async-start(bf16[8,24,3072]{2,1,0:T(8,128)(2,1)} %get-tuple-element.391), calls=%async_computation.10 | async-start | bytes 2359296 | tf_op jit(solution)/shard_map/all_to_all | solution.py:268
  224.2 1.5 collective-permute-start.9
  225.7 0.7 copy-start.4
  250.8 4.3 %copy-start.3 = (bf16[24,3072]{1,0:T(8,128)(2,1)S(1)}, bf16[24,3072]{1,0:T(8,128)(2,1)}, u32[]{:S(2)}) copy-start(bf16[24,3072]{1,0:T(8,128)(2,1)} %get-tuple-element.337.x_ref) | copy-start | bytes 442372 | tf_op jit(solution)/shard_map/cond
  251.6 12.7 %all-to-all-start.4 = ((bf16[8,24,1024]{2,1,0:T(8,128)(2,1)}), bf16[8,24,1024]{2,1,0:T(8,128)(2,1)S(1)}, u32[]{:S(2)}, u32[]{:S(2)}) async-start(bf16[8,24,1024]{2,1,0:T(8,128)(2,1)} %bitcast.19), calls=%async_computation.4 | async-start | bytes 786432 | tf_op jit(solution)/shard_map/cond/branch_1_fun/all_to_all | solution.py:268
  265.0 20.5 %copy-start.16 = (bf16[2,24,2,2048]{3,2,1,0:T(2,128)(2,1)}, bf16[2,24,2,2048]{3,2,1,0:T(2,128)(2,1)S(1)}, u32[]{:S(2)}) copy-start(bf16[2,24,2,2048]{3,2,1,0:T(2,128)(2,1)S(1)} %get-tuple-element.401) | copy-start | bytes 1179652
  266.3 18.5 %collective-permute-start.10 = (bf16[24,3072]{1,0:T(8,128)(2,1)S(1)}, bf16[24,3072]{1,0:T(8,128)(2,1)S(1)}, u32[]{:S(2)}, u32[]{:S(2)}) collective-permute-start(bf16[24,3072]{1,0:T(8,128)(2,1)S(1)} %get-tuple-element.404), channel_id=1, source_target_pairs={{0,8},{1,9},{2,10},{3,11},{4,12},{5,13},{6,14},{7,15},{8,0},{9,1},... | collective-permute-start | bytes 442376 | tf_op jit(solution)/shard_map/ppermute | solution.py:261

commit v11 on v10

--- a/solution.py
+++ b/solution.py
@@ -98,7 +98,7 @@
 
 
 def block_kernel(
-    turn, head_size, planes, gain_ref, own_in, other_in, own_out, other_out, blocks_ref, far_ref, *refs
+    head_size, planes, gain_ref, in_ref, out_weights_ref, blocks_ref, far_ref, *refs
 ):
     caches, refs = refs[:-11], refs[-11:]
     out_ref, kv_ref, blocks, far, w_in, w_out, parts, q_ref, in_sems, sems, part_sems = refs
@@ -106,17 +106,6 @@
     channels = w_out.shape[0]
     pieces = in_sems.shape[1]
     depth = width // pieces
-    mine = lax.rem(lax.axis_index("pipe"), 2) == turn
-
-    def weight_copies(source_in, source_out):
-        for part in (1, 2, 0):
-            for piece in range(pieces):
-                cut = pl.ds(piece * depth, depth)
-                pltpu.make_async_copy(
-                    source_in.at[part, cut], w_in.at[part, cut], in_sems.at[part, piece]
-                ).start()
-        pltpu.make_async_copy(source_out.at[0], w_out, sems.at[1]).start()
-
     fetch = pltpu.make_async_copy(blocks_ref.at[:, :width], blocks, sems.at[0])
     fetch.start()
     if len(far.shape) == 3:
@@ -126,21 +115,20 @@
         fetch_far = pltpu.make_async_copy(far_ref.at[:, begin:], far, sems.at[2])
     fetch_far.start()
 
-    @pl.when(mine)
-    def _():
-        weight_copies(own_in, own_out)
-
-    @pl.when(jnp.logical_not(mine))
-    def _():
-        weight_copies(other_in, other_out)
-
+    for part in (1, 2, 0):
+        for piece in range(pieces):
+            cut = pl.ds(piece * depth, depth)
+            pltpu.make_async_copy(
+                in_ref.at[part, cut], w_in.at[part, cut], in_sems.at[part, piece]
+            ).start()
+    pltpu.make_async_copy(out_weights_ref.at[0], w_out, sems.at[1]).start()
     fetch.wait()
     tokens = blocks[...]
     for part in (1, 2, 0):
         for piece in range(pieces):
             cut = pl.ds(piece * depth, depth)
             pltpu.make_async_copy(
-                own_in.at[part, cut], w_in.at[part, cut], in_sems.at[part, piece]
+                in_ref.at[part, cut], w_in.at[part, cut], in_sems.at[part, piece]
             ).wait()
         projected = jnp.dot(tokens, w_in[part], preferred_element_type=jnp.float32)
         if part == 2:
@@ -174,7 +162,7 @@
         put_cache((first, jnp.where(last, kv_ref[...], second[...])), parts, width)
         send(width, 4 * channels, steps)
     attended = attention(head_size, q_ref, kv_ref, far)
-    pltpu.make_async_copy(own_out.at[0], w_out, sems.at[1]).wait()
+    pltpu.make_async_copy(out_weights_ref.at[0], w_out, sems.at[1]).wait()
     tile = width // steps
     for step in range(steps):
         cut = slice(step * tile, (step + 1) * tile)
@@ -291,6 +279,7 @@
     )
     other_in = swap(own_in)
     other_out = swap(own_out)
+    own, other = (own_in, own_out), (other_in, other_out)
     params = [jnp.where(core == turn, own_params, other_params) for turn in range(2)]
     gain_rows = [p[3, : 2 * head_size].reshape(2, head_size) for p in params]
     blocks_shape = bf16(seq, rows, width)
@@ -304,13 +293,13 @@
     flat = lambda blocks: blocks.reshape(tokens, blocks.shape[2])
     apart = lambda values: values.reshape(seq, rows, values.shape[1])
 
-    def block(blocks, far, turn, caches=()):
+    def block(blocks, far, turn, weights, caches=()):
         total = width + 2 * channels * len(caches)
         side = (2, tokens, channels) if far.ndim == 3 else (tokens, 2 * channels)
         out, pair = pl.pallas_call(
-            functools.partial(block_kernel, turn, head_size, planes),
+            functools.partial(block_kernel, head_size, planes),
             out_shape=(bf16(tokens, total), bf16(2, tokens, channels)),
-            in_specs=[VMEM] + [HBM] * 4 + [ANY] * 2 + [VMEM] * len(caches),
+            in_specs=[VMEM] + [HBM] * 2 + [ANY] * 2 + [VMEM] * len(caches),
             out_specs=(HBM, VMEM),
             scratch_shapes=[
                 pltpu.VMEM((tokens, width), jnp.bfloat16),
@@ -325,7 +314,7 @@
             ],
             compiler_params=params_of(32),
         )(
-            gain_rows[turn], own_in, other_in, own_out, other_out, flat(blocks), far, *caches
+            gain_rows[turn], *weights, flat(blocks), far, *caches
         )
         return apart(out), pair
 
@@ -340,15 +329,21 @@
     early = core == 0
     either = lambda on_early, on_late: lax.cond(early, on_early, on_late)
 
+    pair_shape, block_shape = bf16(2, tokens, channels), bf16(rows, width)
+    side_shape = bf16(tokens, 2 * channels)
+
     def first_early():
-        return across(packed), blank(bf16(tokens, 2 * channels))[0]
+        received = across(packed)
+        side = flat(received)
+        parts, fresh = block(received, side, 0, own)
+        kept = lax.cond(plane == 0, lambda: blank(side_shape)[0], lambda: side[:, width:])
+        return parts, fresh, kept
 
     def first_late():
-        return blank(bf16(*packed.shape))[0], flat(across(packed[:, :, width:]))
-
-    received, stale = either(first_early, first_late)
-    stales = [flat(received), swap(stale)]
-    pair_shape, block_shape = bf16(2, tokens, channels), bf16(rows, width)
+        side = flat(across(packed[:, :, width:]))
+        later, side = lax.optimization_barrier((x, side))
+        return norm(later, 0), blank(pair_shape)[0], side
+
     late_pair = None
     early_x, late_x = x, x
     blocks_out, sources = {}, {}
@@ -357,7 +352,7 @@
         crossing = layer > 0 and turn == 0
 
         def early_scatter():
-            parts, fresh = block(received, stales[turn], turn)
+            parts, fresh = block(received, stales[turn], turn, other if turn else own)
             return parts, fresh, blank(block_shape)[0]
 
         def late_gather():
@@ -373,7 +368,11 @@
             )
             blocks_out[layer - 1, 1] = late_x
             late_x = upward(late_x, level - 1, 1)
-        payload, pair, result = either(early_scatter, late_gather)
+        if layer == 0:
+            payload, pair, side = either(first_early, first_late)
+            stales = [side, swap(side)]
+        else:
+            payload, pair, result = either(early_scatter, late_gather)
         if turn:
             late_x = blocks_out[layer - 1, 1] = result
         sources[layer, 0] = pair
@@ -392,7 +391,7 @@
             return normed, blank(pair_shape)[0], result
 
         def late_scatter():
-            parts, fresh = block(received, got, turn)
+            parts, fresh = block(received, got, turn, own if turn else other)
             return parts, fresh, blank(block_shape)[0]
 
         if crossing:
@@ -443,7 +442,7 @@
         return result, cache
 
     def last_late():
-        parts, _ = block(received, got, last % 2, (first_cache, second_cache))
+        parts, _ = block(received, got, last % 2, own if last % 2 else other, (first_cache, second_cache))
         return tuple(
             pl.pallas_call(
                 last_kernel, out_shape=(block_shape, cache_shape),

time: 286 us -> 299 us (1.045)
  the two profiles are of different devices: /device:TPU:0 before, /device:TPU:5 now
where the time goes in v11:
time: 299 us; the launch traced here: 298 us
  waiting for transfers between devices  103 us (34%)
  starting transfers between devices  86.1 us (29%)
  blocking collectives  59.2 us (20%)
  Pallas kernels  40.6 us (14%)
  local copies, waits for them, and re-layouts  4.15 us (1%)
  other arithmetic  3.49 us (1%)
    all_to_all x6, waiting for transfers between devices, across(): lax.all_to_all(blocks, 'seq', split_axis=0, concat_axis=0, tiled=True)  75.6 us
    all_to_all x2, blocking collectives, across(): lax.all_to_all(blocks, 'seq', split_axis=0, concat_axis=0, tiled=True)  59.2 us
    ppermute x9, starting transfers between devices, swap(): return lax.ppermute(value, AXES, pairs)  54.5 us
    all_to_all x6, starting transfers between devices, across(): lax.all_to_all(blocks, 'seq', split_axis=0, concat_axis=0, tiled=True)  29.6 us
    pallas_call x4, Pallas kernels, block(): pl.pallas_call(functools.partial(block_kernel, head_size, planes), out_sh...  27.7 us
    ppermute x2, waiting for transfers between devices, upward(): lax.ppermute(value, AXES, [(place(row, s), place(row + 2, s)) for s in ra...  21.7 us
    pallas_call x3, Pallas kernels, finish(): pl.pallas_call(finish_kernel, out_shape=shapes, in_specs=[VMEM] * 4, out_...  6.03 us
  transfers between devices with their start and end apart: 17, of which 9 were waited for; matrix products, arithmetic and copies ran while one was open for 1% of the time, Pallas kernels for 1%

profile of v11, /device:TPU:5, one launch (start us, length us, event | category | flops | bytes accessed | tf_op | source)
XLA Modules:
  0.0 298.2 jit_solution(7044555584313555300)
XLA Ops:
  0.6 0.8 select_maximum_fusion.params_ref
  2.2 1.1 slice_bitcast_fusion.cache_ref
  3.4 1.5 shard_map.95
  5.2 16.5 %conditional.12 = (bf16[8,24,3072]{2,1,0:T(8,128)(2,1)}, bf16[2,192,256]{2,1,0:T(8,128)(2,1)S(1)}, bf16[192,512]{1,0:T(8,128)(2,1)}) conditional(s32[]{:T(128)} %convert_element_type.9, (bf16[8,24,3584]{2,1,0:T(8,128)(2,1)}, bf16[24,3072]{1,0:T(8,128)(2,1)S(1)}, f32[4,3072]{1,0:T(4,128)S(1)}) %tuple.112, (bf16[8,24,3584]{2,1,0:T(8,128)(2,1)}, ...), branch_computations={%region_0.1_spmd, %region_1.4_spmd} | conditional | flops 2 | bytes 4522062 | solution.py:330
  5.2 1.6 slice.10
  6.8 5.5 %all-to-all-start = ((bf16[8,24,512]{2,1,0:T(8,128)(2,1)}), bf16[8,24,512]{2,1,0:T(8,128)(2,1)}, u32[]{:S(2)}, u32[]{:S(2)}) async-start(bf16[8,24,512]{2,1,0:T(8,128)(2,1)} %slice.10), calls=%async_computation | async-start | bytes 393216 | tf_op jit(solution)/shard_map/cond/branch_0_fun/all_to_all | solution.py:256
  12.3 8.0 %all-to-all-done = bf16[8,24,512]{2,1,0:T(8,128)(2,1)} async-done(((bf16[8,24,512]{2,1,0:T(8,128)(2,1)}), bf16[8,24,512]{2,1,0:T(8,128)(2,1)}, u32[]{:S(2)}, u32[]{:S(2)}) %all-to-all-start) | async-done | bytes 196640 | tf_op jit(solution)/shard_map/cond/branch_0_fun/all_to_all | solution.py:256
  20.3 1.4 branch_0_fun.16
  21.7 5.5 %all-to-all-start.5 = ((bf16[8,24,3072]{2,1,0:T(8,128)(2,1)}), bf16[8,24,3072]{2,1,0:T(8,128)(2,1)S(1)}, u32[]{:S(2)}, u32[]{:S(2)}) async-start(bf16[8,24,3072]{2,1,0:T(8,128)(2,1)} %get-tuple-element.330), calls=%async_computation.5 | async-start | bytes 2359296 | tf_op jit(solution)/shard_map/all_to_all | solution.py:256
  27.2 24.7 %collective-permute-start.2 = (bf16[1,256,3072]{2,1,0:T(8,128)(2,1)S(1)}, bf16[1,256,3072]{2,1,0:T(8,128)(2,1)}, u32[]{:S(2)}, u32[]{:S(2)}) collective-permute-start(bf16[1,256,3072]{2,1,0:T(8,128)(2,1)S(1)} %copy-done.1), channel_id=1, source_target_pairs={{0,8},{1,9},{2,10},{3,11},{4,12},{5,13},{6,14},{7,15},{8,0},{9,1},... | collective-permute-start | bytes 4718600 | tf_op jit(solution)/shard_map/ppermute | solution.py:249
  51.9 3.4 %collective-permute-done.3 = bf16[2,192,256]{2,1,0:T(8,128)(2,1)} collective-permute-done((bf16[2,192,256]{2,1,0:T(8,128)(2,1)S(1)}, bf16[2,192,256]{2,1,0:T(8,128)(2,1)}, u32[]{:S(2)}, u32[]{:S(2)}) %collective-permute-start.3) | collective-permute-done | bytes 196640 | tf_op jit(solution)/shard_map/ppermute | solution.py:249
  55.3 7.2 %conditional.13 = (bf16[8,24,3072]{2,1,0:T(8,128)(2,1)}, bf16[2,192,256]{2,1,0:T(8,128)(2,1)}, bf16[24,3072]{1,0:T(8,128)(2,1)S(1)}) conditional(s32[]{:T(128)} %convert_element_type.9, (bf16[8,24,3072]{2,1,0:T(8,128)(2,1)S(1)}, f32[2,128]{1,0:T(2,128)S(1)}, bf16[3,3072,256]{2,1,0:T(8,128)(2,1)}, bf16[1,256,3072]{2,1,0:T(8,128)(2,1)}, ...), branch_computations={%region_4.5_spmd, %region_5.6_spmd} | conditional | bytes 24 | solution.py:330
  55.3 7.2 %branch_0_fun.18 = (bf16[192,3072]{1,0:T(8,128)(2,1)}, bf16[2,192,256]{2,1,0:T(8,128)(2,1)}) custom-call(f32[2,128]{1,0:T(2,128)S(1)} %get-tuple-element.203.gain_ref, bf16[3,3072,256]{2,1,0:T(8,128)(2,1)} %get-tuple-element.204.in_ref, bf16[1,256,3072]{2,1,0:T(8,128)(2,1)} %get-tuple-element.205.out_weights_ref, bf16[192,3072]{1,0:T(8,128)(2,1)S(1)} %bitcast.38, ...), custom_call_target="tpu_custom_call" | custom-call | tf_op jit(solution)/shard_map/cond/branch_0_fun/pallas_call | solution.py:299
  62.5 5.7 %all-to-all-start.6 = ((bf16[8,24,3072]{2,1,0:T(8,128)(2,1)}), bf16[8,24,3072]{2,1,0:T(8,128)(2,1)S(1)}, u32[]{:S(2)}, u32[]{:S(2)}) async-start(bf16[8,24,3072]{2,1,0:T(8,128)(2,1)} %get-tuple-element.332), calls=%async_computation.6 | async-start | bytes 2359296 | tf_op jit(solution)/shard_map/all_to_all | solution.py:256
  68.3 6.8 %collective-permute-start.4 = (bf16[192,512]{1,0:T(8,128)(2,1)}, bf16[192,512]{1,0:T(8,128)(2,1)}, u32[]{:S(2)}, u32[]{:S(2)}) collective-permute-start(bf16[192,512]{1,0:T(8,128)(2,1)} %get-tuple-element.334), channel_id=1, source_target_pairs={{0,8},{1,9},{2,10},{3,11},{4,12},{5,13},{6,14},{7,15},{8,0},{9,1},... | collective-permute-start | bytes 589832 | tf_op jit(solution)/shard_map/ppermute | solution.py:249
  75.1 18.0 %all-to-all-done.6 = bf16[8,24,3072]{2,1,0:T(8,128)(2,1)S(1)} async-done(((bf16[8,24,3072]{2,1,0:T(8,128)(2,1)}), bf16[8,24,3072]{2,1,0:T(8,128)(2,1)S(1)}, u32[]{:S(2)}, u32[]{:S(2)}) %all-to-all-start.6) | async-done | bytes 1179680 | tf_op jit(solution)/shard_map/all_to_all | solution.py:256
  93.1 2.4 conditional.14
  93.1 2.4 branch_0_fun.20
  95.5 5.2 %all-to-all-start.7 = ((bf16[8,24,3072]{2,1,0:T(8,128)(2,1)}), bf16[8,24,3072]{2,1,0:T(8,128)(2,1)S(1)}, u32[]{:S(2)}, u32[]{:S(2)}) async-start(bf16[8,24,3072]{2,1,0:T(8,128)(2,1)} %get-tuple-element.336), calls=%async_computation.7 | async-start | bytes 2359296 | tf_op jit(solution)/shard_map/all_to_all | solution.py:256
  100.7 8.1 %collective-permute-start.5 = (bf16[2,192,256]{2,1,0:T(8,128)(2,1)}, bf16[2,192,256]{2,1,0:T(8,128)(2,1)}, u32[]{:S(2)}, u32[]{:S(2)}) collective-permute-start(bf16[2,192,256]{2,1,0:T(8,128)(2,1)} %get-tuple-element.337), channel_id=1, source_target_pairs={{0,8},{1,9},{2,10},{3,11},{4,12},{5,13},{6,14},{7,15},{8,0},{9,1},... | collective-permute-start | bytes 589832 | tf_op jit(solution)/shard_map/ppermute | solution.py:249
  108.9 16.7 %all-to-all-done.7 = bf16[8,24,3072]{2,1,0:T(8,128)(2,1)S(1)} async-done(((bf16[8,24,3072]{2,1,0:T(8,128)(2,1)}), bf16[8,24,3072]{2,1,0:T(8,128)(2,1)S(1)}, u32[]{:S(2)}, u32[]{:S(2)}) %all-to-all-start.7) | async-done | bytes 1179680 | tf_op jit(solution)/shard_map/all_to_all | solution.py:256
  126.3 7.2 %conditional.16 = (bf16[2,192,256]{2,1,0:T(8,128)(2,1)}, bf16[8,24,3072]{2,1,0:T(8,128)(2,1)S(1)}) conditional(s32[]{:T(128)} %convert_element_type.9, (bf16[8,24,3072]{2,1,0:T(8,128)(2,1)S(1)}, f32[2,128]{1,0:T(2,128)S(1)}, bf16[3,3072,256]{2,1,0:T(8,128)(2,1)}, bf16[1,256,3072]{2,1,0:T(8,128)(2,1)S(1)}, ...), branch_computations={%region_10.11_spmd, %region_11.12_spmd} | conditional | bytes 16 | solution.py:330
  126.5 7.0 %branch_0_fun.22 = (bf16[192,3072]{1,0:T(8,128)(2,1)S(1)}, bf16[2,192,256]{2,1,0:T(8,128)(2,1)}) custom-call(f32[2,128]{1,0:T(2,128)S(1)} %get-tuple-element.234.gain_ref, bf16[3,3072,256]{2,1,0:T(8,128)(2,1)} %get-tuple-element.235.in_ref, bf16[1,256,3072]{2,1,0:T(8,128)(2,1)S(1)} %get-tuple-element.236.out_weights_ref, bf16[192,3072]{1,0:T(8,128)(2,1)S(1)} %bitcast.37, ...), custom_call_target="tpu_custom_call" | custom-call | tf_op jit(solution)/shard_map/cond/branch_0_fun/pallas_call | solution.py:299
  133.5 1.1 conditional.18
  133.5 1.1 branch_0_fun.24
  134.7 1.3 collective-permute-start.7
  136.0 21.7 %collective-permute-done.7 = bf16[24,3072]{1,0:T(8,128)(2,1)} collective-permute-done((bf16[24,3072]{1,0:T(8,128)(2,1)S(1)}, bf16[24,3072]{1,0:T(8,128)(2,1)}, u32[]{:S(2)}, u32[]{:S(2)}) %collective-permute-start.7) | collective-permute-done | bytes 147488 | tf_op jit(solution)/shard_map/ppermute | solution.py:253
  157.7 2.4 conditional.19
  157.7 2.4 branch_0_fun.25
  160.1 3.6 %all-to-all-start.8 = ((bf16[8,24,3072]{2,1,0:T(8,128)(2,1)}), bf16[8,24,3072]{2,1,0:T(8,128)(2,1)S(1)}, u32[]{:S(2)}, u32[]{:S(2)}) async-start(bf16[8,24,3072]{2,1,0:T(8,128)(2,1)} %get-tuple-element.340), calls=%async_computation.8 | async-start | bytes 2359296 | tf_op jit(solution)/shard_map/all_to_all | solution.py:256
  163.7 8.4 %collective-permute-start.8 = (bf16[2,192,256]{2,1,0:T(8,128)(2,1)S(1)}, bf16[2,192,256]{2,1,0:T(8,128)(2,1)}, u32[]{:S(2)}, u32[]{:S(2)}) collective-permute-start(bf16[2,192,256]{2,1,0:T(8,128)(2,1)S(1)} %get-tuple-element.341), channel_id=1, source_target_pairs={{0,8},{1,9},{2,10},{3,11},{4,12},{5,13},{6,14},{7,15},{8,0},{9,1},... | collective-permute-start | bytes 589832 | tf_op jit(solution)/shard_map/ppermute | solution.py:249
  172.1 16.3 %all-to-all-done.8 = bf16[8,24,3072]{2,1,0:T(8,128)(2,1)S(1)} async-done(((bf16[8,24,3072]{2,1,0:T(8,128)(2,1)}), bf16[8,24,3072]{2,1,0:T(8,128)(2,1)S(1)}, u32[]{:S(2)}, u32[]{:S(2)}) %all-to-all-start.8) | async-done | bytes 1179680 | tf_op jit(solution)/shard_map/all_to_all | solution.py:256
  188.4 6.5 %conditional.20 = (bf16[8,24,3072]{2,1,0:T(8,128)(2,1)}, bf16[2,192,256]{2,1,0:T(8,128)(2,1)S(1)}, bf16[24,3072]{1,0:T(8,128)(2,1)}) conditional(s32[]{:T(128)} %convert_element_type.9, (bf16[8,24,3072]{2,1,0:T(8,128)(2,1)S(1)}, f32[2,128]{1,0:T(2,128)S(1)}, bf16[3,3072,256]{2,1,0:T(8,128)(2,1)}, bf16[1,256,3072]{2,1,0:T(8,128)(2,1)}, ...), branch_computations={%region_18.19_spmd, %region_19.20_spmd} | conditional | bytes 24 | solution.py:330
  188.4 6.5 %branch_0_fun.27 = (bf16[192,3072]{1,0:T(8,128)(2,1)}, bf16[2,192,256]{2,1,0:T(8,128)(2,1)S(1)}) custom-call(f32[2,128]{1,0:T(2,128)S(1)} %get-tuple-element.256.gain_ref, bf16[3,3072,256]{2,1,0:T(8,128)(2,1)} %get-tuple-element.257.in_ref, bf16[1,256,3072]{2,1,0:T(8,128)(2,1)} %get-tuple-element.258.out_weights_ref, bf16[192,3072]{1,0:T(8,128)(2,1)S(1)} %bitcast.39, ...), custom_call_target="tpu_custom_call" | custom-call | tf_op jit(solution)/shard_map/cond/branch_0_fun/pallas_call | solution.py:299
  194.9 32.3 %all_to_all.52 = bf16[8,24,3072]{2,1,0:T(8,128)(2,1)S(1)} all-to-all(bf16[8,24,3072]{2,1,0:T(8,128)(2,1)} %get-tuple-element.343), channel_id=1, replica_groups=mesh['pipe'=4,'seq'=8] {'seq'}, dimensions={0} | all-to-all | bytes 2359296 | tf_op jit(solution)/shard_map/all_to_all | solution.py:256
  227.2 2.8 conditional.21
  227.2 2.6 branch_0_fun.29
  230.7 4.1 %all-to-all-start.10 = ((bf16[8,24,3072]{2,1,0:T(8,128)(2,1)}), bf16[8,24,3072]{2,1,0:T(8,128)(2,1)S(1)}, u32[]{:S(2)}, u32[]{:S(2)}) async-start(bf16[8,24,3072]{2,1,0:T(8,128)(2,1)} %get-tuple-element.345), calls=%async_computation.10 | async-start | bytes 2359296 | tf_op jit(solution)/shard_map/all_to_all | solution.py:256
  234.8 5.5 %collective-permute-start.9 = (bf16[2,192,256]{2,1,0:T(8,128)(2,1)S(1)}, bf16[2,192,256]{2,1,0:T(8,128)(2,1)S(1)}, u32[]{:S(2)}, u32[]{:S(2)}) collective-permute-start(bf16[2,192,256]{2,1,0:T(8,128)(2,1)S(1)} %copy-done.12), channel_id=1, source_target_pairs={{0,8},{1,9},{2,10},{3,11},{4,12},{5,13},{6,14},{7,15},{8,0},{9,1},... | collective-permute-start | bytes 589832 | tf_op jit(solution)/shard_map/ppermute | solution.py:249
  240.3 1.1 collective-permute-done.9
  242.1 1.3 select_select_fusion
  243.3 16.5 %all-to-all-done.10 = bf16[8,24,3072]{2,1,0:T(8,128)(2,1)S(1)} async-done(((bf16[8,24,3072]{2,1,0:T(8,128)(2,1)}), bf16[8,24,3072]{2,1,0:T(8,128)(2,1)S(1)}, u32[]{:S(2)}, u32[]{:S(2)}) %all-to-all-start.10) | async-done | bytes 1179680 | tf_op jit(solution)/shard_map/all_to_all | solution.py:256
  259.9 34.8 %conditional.22 = ((bf16[24,3072]{1,0:T(8,128)(2,1)}, bf16[2,24,2,2048]{3,2,1,0:T(2,128)(2,1)S(1)})) conditional(s32[]{:T(128)} %convert_element_type.9, (bf16[8,24,3072]{2,1,0:T(8,128)(2,1)S(1)}, f32[2,128]{1,0:T(2,128)S(1)}, bf16[3,3072,256]{2,1,0:T(8,128)(2,1)}, bf16[1,256,3072]{2,1,0:T(8,128)(2,1)S(1)}, bf16[2,192,256]{2,1,0:T(8,128)(2,1)}, ...), branch_computations={%region_22.23_spmd, %region_23.24_spmd} | conditional | bytes 3735588 | solution.py:330
  259.9 7.1 %branch_0_fun.30 = (bf16[192,4096]{1,0:T(8,128)(2,1)S(1)}, bf16[2,192,256]{2,1,0:T(8,128)(2,1)}) custom-call(f32[2,128]{1,0:T(2,128)S(1)} %get-tuple-element.285.gain_ref, bf16[3,3072,256]{2,1,0:T(8,128)(2,1)} %get-tuple-element.286.in_ref, bf16[1,256,3072]{2,1,0:T(8,128)(2,1)S(1)} %get-tuple-element.287.out_weights_ref, bf16[192,3072]{1,0:T(8,128)(2,1)S(1)} %bitcast.36, ...), custom_call_target="tpu_custom_call" | custom-call | tf_op jit(solution)/shard_map/cond/branch_0_fun/pallas_call | solution.py:299
  267.0 26.9 %all_to_all.51.parts_ref = bf16[8,24,4096]{2,1,0:T(8,128)(2,1)S(1)} all-to-all(bf16[8,24,4096]{2,1,0:T(8,128)(2,1)S(1)} %bitcast.30), channel_id=1, replica_groups=mesh['pipe'=4,'seq'=8] {'seq'}, dimensions={0} | all-to-all | bytes 3145728 | tf_op jit(solution)/shard_map/cond/branch_0_fun/all_to_all | solution.py:256
  293.9 0.8 branch_0_fun.31
  294.7 1.3 select_select_fusion.2
  296.1 1.4 collective-permute-done.10.theirs_ref
  (60 shorter events, 3.9 us)
Async XLA Ops:
  0.6 2.8 copy-start
  1.5 3.4 %collective-permute-start = (f32[4,3072]{1,0:T(4,128)S(1)}, f32[4,3072]{1,0:T(4,128)S(1)}, u32[]{:S(2)}, u32[]{:S(2)}) collective-permute-start(f32[4,3072]{1,0:T(4,128)S(1)} %select_maximum_fusion.params_ref), channel_id=1, source_target_pairs={{0,8},{1,9},{2,10},{3,11},{4,12},{5,13},{6,14},{7,15},{8,0},{9,1},... | collective-permute-start | bytes 147464 | tf_op jit(solution)/shard_map/ppermute | solution.py:249
  2.2 2.8 copy-start.13
  2.2 2.8 copy-start.14
  2.2 2.8 copy-start.15
  2.2 2.8 copy-start.16
  3.4 1.8 copy-start.1
  4.9 50.4 %collective-permute-start.1 = (bf16[3,3072,256]{2,1,0:T(8,128)(2,1)}, bf16[3,3072,256]{2,1,0:T(8,128)(2,1)}, u32[]{:S(2)}, u32[]{:S(2)}) collective-permute-start(bf16[3,3072,256]{2,1,0:T(8,128)(2,1)} %bitcast.31), channel_id=1, source_target_pairs={{0,8},{1,9},{2,10},{3,11},{4,12},{5,13},{6,14},{7,15},{8,0},{9,1},... | collective-permute-start | bytes 14155784 | tf_op jit(solution)/shard_map/ppermute | solution.py:249
  6.8 13.5 %all-to-all-start = ((bf16[8,24,512]{2,1,0:T(8,128)(2,1)}), bf16[8,24,512]{2,1,0:T(8,128)(2,1)}, u32[]{:S(2)}, u32[]{:S(2)}) async-start(bf16[8,24,512]{2,1,0:T(8,128)(2,1)} %slice.10), calls=%async_computation | async-start | bytes 393216 | tf_op jit(solution)/shard_map/cond/branch_0_fun/all_to_all | solution.py:256
  21.7 30.2 %copy-start.4 = (bf16[2,192,256]{2,1,0:T(8,128)(2,1)}, bf16[2,192,256]{2,1,0:T(8,128)(2,1)S(1)}, u32[]{:S(2)}) copy-start(bf16[2,192,256]{2,1,0:T(8,128)(2,1)S(1)} %get-tuple-element.331) | copy-start | bytes 589828
  21.7 30.3 %all-to-all-start.5 = ((bf16[8,24,3072]{2,1,0:T(8,128)(2,1)}), bf16[8,24,3072]{2,1,0:T(8,128)(2,1)S(1)}, u32[]{:S(2)}, u32[]{:S(2)}) async-start(bf16[8,24,3072]{2,1,0:T(8,128)(2,1)} %get-tuple-element.330), calls=%async_computation.5 | async-start | bytes 2359296 | tf_op jit(solution)/shard_map/all_to_all | solution.py:256
  27.2 28.1 %collective-permute-start.2 = (bf16[1,256,3072]{2,1,0:T(8,128)(2,1)S(1)}, bf16[1,256,3072]{2,1,0:T(8,128)(2,1)}, u32[]{:S(2)}, u32[]{:S(2)}) collective-permute-start(bf16[1,256,3072]{2,1,0:T(8,128)(2,1)S(1)} %copy-done.1), channel_id=1, source_target_pairs={{0,8},{1,9},{2,10},{3,11},{4,12},{5,13},{6,14},{7,15},{8,0},{9,1},... | collective-permute-start | bytes 4718600 | tf_op jit(solution)/shard_map/ppermute | solution.py:249
  51.9 3.4 %collective-permute-start.3 = (bf16[2,192,256]{2,1,0:T(8,128)(2,1)S(1)}, bf16[2,192,256]{2,1,0:T(8,128)(2,1)}, u32[]{:S(2)}, u32[]{:S(2)}) collective-permute-start(bf16[2,192,256]{2,1,0:T(8,128)(2,1)S(1)} %get-tuple-element.331), channel_id=1, source_target_pairs={{0,8},{1,9},{2,10},{3,11},{4,12},{5,13},{6,14},{7,15},{8,0},{9,1},... | collective-permute-start | bytes 589832 | tf_op jit(solution)/shard_map/ppermute | solution.py:249
  62.5 63.1 %copy-start.2 = (bf16[24,3072]{1,0:T(8,128)(2,1)}, bf16[24,3072]{1,0:T(8,128)(2,1)S(1)}, u32[]{:S(2)}) copy-start(bf16[24,3072]{1,0:T(8,128)(2,1)S(1)} %get-tuple-element.338) | copy-start | bytes 442372
  62.5 30.6 %all-to-all-start.6 = ((bf16[8,24,3072]{2,1,0:T(8,128)(2,1)}), bf16[8,24,3072]{2,1,0:T(8,128)(2,1)S(1)}, u32[]{:S(2)}, u32[]{:S(2)}) async-start(bf16[8,24,3072]{2,1,0:T(8,128)(2,1)} %get-tuple-element.332), calls=%async_computation.6 | async-start | bytes 2359296 | tf_op jit(solution)/shard_map/all_to_all | solution.py:256
  68.3 24.9 %collective-permute-start.4 = (bf16[192,512]{1,0:T(8,128)(2,1)}, bf16[192,512]{1,0:T(8,128)(2,1)}, u32[]{:S(2)}, u32[]{:S(2)}) collective-permute-start(bf16[192,512]{1,0:T(8,128)(2,1)} %get-tuple-element.334), channel_id=1, source_target_pairs={{0,8},{1,9},{2,10},{3,11},{4,12},{5,13},{6,14},{7,15},{8,0},{9,1},... | collective-permute-start | bytes 589832 | tf_op jit(solution)/shard_map/ppermute | solution.py:249
  95.5 30.1 %all-to-all-start.7 = ((bf16[8,24,3072]{2,1,0:T(8,128)(2,1)}), bf16[8,24,3072]{2,1,0:T(8,128)(2,1)S(1)}, u32[]{:S(2)}, u32[]{:S(2)}) async-start(bf16[8,24,3072]{2,1,0:T(8,128)(2,1)} %get-tuple-element.336), calls=%async_computation.7 | async-start | bytes 2359296 | tf_op jit(solution)/shard_map/all_to_all | solution.py:256
  100.7 25.6 %collective-permute-start.5 = (bf16[2,192,256]{2,1,0:T(8,128)(2,1)}, bf16[2,192,256]{2,1,0:T(8,128)(2,1)}, u32[]{:S(2)}, u32[]{:S(2)}) collective-permute-start(bf16[2,192,256]{2,1,0:T(8,128)(2,1)} %get-tuple-element.337), channel_id=1, source_target_pairs={{0,8},{1,9},{2,10},{3,11},{4,12},{5,13},{6,14},{7,15},{8,0},{9,1},... | collective-permute-start | bytes 589832 | tf_op jit(solution)/shard_map/ppermute | solution.py:249
  125.6 0.7 copy-start.10
  125.6 0.7 collective-permute-start.6
  134.6 23.0 %copy-start.9 = (bf16[24,3072]{1,0:T(8,128)(2,1)}, bf16[24,3072]{1,0:T(8,128)(2,1)S(1)}, u32[]{:S(2)}) copy-start(bf16[24,3072]{1,0:T(8,128)(2,1)S(1)} %get-tuple-element.407) | copy-start | bytes 442372
  134.7 23.0 %collective-permute-start.7 = (bf16[24,3072]{1,0:T(8,128)(2,1)S(1)}, bf16[24,3072]{1,0:T(8,128)(2,1)}, u32[]{:S(2)}, u32[]{:S(2)}) collective-permute-start(bf16[24,3072]{1,0:T(8,128)(2,1)S(1)} %get-tuple-element.407), channel_id=1, source_target_pairs={{8,24},{9,25},{10,26},{11,27},{12,28},{13,29},{14,30},{15,31}} | collective-permute-start | bytes 442376 | tf_op jit(solution)/shard_map/ppermute | solution.py:253
  160.1 3.6 %copy-start.5 = (bf16[2,192,256]{2,1,0:T(8,128)(2,1)}, bf16[2,192,256]{2,1,0:T(8,128)(2,1)S(1)}, u32[]{:S(2)}) copy-start(bf16[2,192,256]{2,1,0:T(8,128)(2,1)S(1)} %get-tuple-element.341) | copy-start | bytes 589828
  160.1 28.3 %all-to-all-start.8 = ((bf16[8,24,3072]{2,1,0:T(8,128)(2,1)}), bf16[8,24,3072]{2,1,0:T(8,128)(2,1)S(1)}, u32[]{:S(2)}, u32[]{:S(2)}) async-start(bf16[8,24,3072]{2,1,0:T(8,128)(2,1)} %get-tuple-element.340), calls=%async_computation.8 | async-start | bytes 2359296 | tf_op jit(solution)/shard_map/all_to_all | solution.py:256
  163.7 24.7 %collective-permute-start.8 = (bf16[2,192,256]{2,1,0:T(8,128)(2,1)S(1)}, bf16[2,192,256]{2,1,0:T(8,128)(2,1)}, u32[]{:S(2)}, u32[]{:S(2)}) collective-permute-start(bf16[2,192,256]{2,1,0:T(8,128)(2,1)S(1)} %get-tuple-element.341), channel_id=1, source_target_pairs={{0,8},{1,9},{2,10},{3,11},{4,12},{5,13},{6,14},{7,15},{8,0},{9,1},... | collective-permute-start | bytes 589832 | tf_op jit(solution)/shard_map/ppermute | solution.py:249
  194.9 32.3 %copy-start.11 = (bf16[2,192,256]{2,1,0:T(8,128)(2,1)}, bf16[2,192,256]{2,1,0:T(8,128)(2,1)S(1)}, u32[]{:S(2)}) copy-start(bf16[2,192,256]{2,1,0:T(8,128)(2,1)S(1)} %get-tuple-element.344) | copy-start | bytes 589828
  230.1 0.7 copy-start.7
  230.1 4.7 %copy-start.12 = (bf16[2,192,256]{2,1,0:T(8,128)(2,1)S(1)}, bf16[2,192,256]{2,1,0:T(8,128)(2,1)}, u32[]{:S(2)}) copy-start(bf16[2,192,256]{2,1,0:T(8,128)(2,1)} %get-tuple-element.346) | copy-start | bytes 589828
  230.7 29.2 %all-to-all-start.10 = ((bf16[8,24,3072]{2,1,0:T(8,128)(2,1)}), bf16[8,24,3072]{2,1,0:T(8,128)(2,1)S(1)}, u32[]{:S(2)}, u32[]{:S(2)}) async-start(bf16[8,24,3072]{2,1,0:T(8,128)(2,1)} %get-tuple-element.345), calls=%async_computation.10 | async-start | bytes 2359296 | tf_op jit(solution)/shard_map/all_to_all | solution.py:256
  234.8 6.6 %collective-permute-start.9 = (bf16[2,192,256]{2,1,0:T(8,128)(2,1)S(1)}, bf16[2,192,256]{2,1,0:T(8,128)(2,1)S(1)}, u32[]{:S(2)}, u32[]{:S(2)}) collective-permute-start(bf16[2,192,256]{2,1,0:T(8,128)(2,1)S(1)} %copy-done.12), channel_id=1, source_target_pairs={{0,8},{1,9},{2,10},{3,11},{4,12},{5,13},{6,14},{7,15},{8,0},{9,1},... | collective-permute-start | bytes 589832 | tf_op jit(solution)/shard_map/ppermute | solution.py:249
  241.4 0.7 copy-start.6
  267.0 26.9 %copy-start.8 = (bf16[24,3072]{1,0:T(8,128)(2,1)S(1)}, bf16[24,3072]{1,0:T(8,128)(2,1)}, u32[]{:S(2)}) copy-start(bf16[24,3072]{1,0:T(8,128)(2,1)} %get-tuple-element.284.x_ref) | copy-start | bytes 442372 | tf_op jit(solution)/shard_map/cond
  294.7 3.5 %copy-start.17 = (bf16[2,24,2,2048]{3,2,1,0:T(2,128)(2,1)}, bf16[2,24,2,2048]{3,2,1,0:T(2,128)(2,1)S(1)}, u32[]{:S(2)}) copy-start(bf16[2,24,2,2048]{3,2,1,0:T(2,128)(2,1)S(1)} %get-tuple-element.355) | copy-start | bytes 1179652
  296.0 1.4 collective-permute-start.10

commit v12 on v10

--- a/solution.py
+++ b/solution.py
@@ -388,8 +388,8 @@
         def early_gather():
             if crossing:
                 return norm(early_x, 1 - turn), blank(pair_shape)[0], blank(block_shape)[0]
-            result, normed = finish(early_x, received, turn, 1)
-            return normed, blank(pair_shape)[0], result
+            result = finish(early_x, received, turn, 0)[0]
+            return norm(result, 1 - turn), blank(pair_shape)[0], result
 
         def late_scatter():
             parts, fresh = block(received, got, turn)

time: 286 us -> 290 us (1.014)
  Pallas kernels: 41.5 us -> 48.4 us
  starting transfers between devices: 62.2 us -> 59 us
    pallas_call x1 -> x3, Pallas kernels: 1.87 us -> 7.5 us  [norm(): pl.pallas_call(norm_kernel, out_shape=blocks_shape, in_specs=[VMEM] * 2,...]
    ppermute x9, starting transfers between devices: 23.7 us -> 19.9 us  [swap(): return lax.ppermute(value, AXES, pairs)]
  transfers between devices with their start and end apart: 18 -> 18, of which waited for: 10 -> 10; matrix products, arithmetic and copies ran while one was open for 1% -> 2% of each run, Pallas kernels for 1% -> 2%
where the time goes in v12:
time: 290 us; the launch traced here: 289 us
  waiting for transfers between devices  141 us (49%)
  starting transfers between devices  59 us (20%)
  Pallas kernels  48.4 us (17%)
  blocking collectives  32.4 us (11%)
  other arithmetic  4.03 us (1%)
  local copies, waits for them, and re-layouts  3.94 us (1%)
    all_to_all x7, waiting for transfers between devices, across(): lax.all_to_all(blocks, 'seq', split_axis=0, concat_axis=0, tiled=True)  136 us
    all_to_all x7, starting transfers between devices, across(): lax.all_to_all(blocks, 'seq', split_axis=0, concat_axis=0, tiled=True)  33.6 us
    all_to_all x1, blocking collectives, across(): lax.all_to_all(blocks, 'seq', split_axis=0, concat_axis=0, tiled=True)  32.4 us
    pallas_call x4, Pallas kernels, block(): pl.pallas_call(functools.partial(block_kernel, turn, head_size, planes),...  29.2 us
    ppermute x9, starting transfers between devices, swap(): return lax.ppermute(value, AXES, pairs)  19.9 us
    pallas_call x3, Pallas kernels, norm(): pl.pallas_call(norm_kernel, out_shape=blocks_shape, in_specs=[VMEM] * 2,...  7.5 us
    pallas_call x4, Pallas kernels, finish(): pl.pallas_call(finish_kernel, out_shape=shapes, in_specs=[VMEM] * 4, out_...  7.07 us
  transfers between devices with their start and end apart: 18, of which 10 were waited for; matrix products, arithmetic and copies ran while one was open for 2% of the time, Pallas kernels for 2%

profile of v12, /device:TPU:0, one launch (start us, length us, event | category | flops | bytes accessed | tf_op | source)
XLA Modules:
  0.0 289.5 jit_solution(846570708626263190)
XLA Ops:
  2.0 1.2 slice_bitcast_fusion.cache_ref
  3.3 1.5 shard_map.95
  5.5 33.2 %conditional.12 = (bf16[8,24,3584]{2,1,0:T(8,128)(2,1)}, bf16[192,512]{1,0:T(8,128)(2,1)}, bf16[192,3584]{1,0:T(8,128)(2,1)S(1)}) conditional(s32[]{:T(128)} %convert_element_type.6, bf16[8,24,3584]{2,1,0:T(8,128)(2,1)} %shard_map.95, bf16[8,24,3584]{2,1,0:T(8,128)(2,1)} %shard_map.95), branch_computations={%region_0.1_spmd, %region_1.2_spmd} | conditional | bytes 6881336 | solution.py:341
  5.5 6.9 %all-to-all-start.1 = ((bf16[8,24,3584]{2,1,0:T(8,128)(2,1)}), bf16[8,24,3584]{2,1,0:T(8,128)(2,1)}, u32[]{:S(2)}, u32[]{:S(2)}) async-start(bf16[8,24,3584]{2,1,0:T(8,128)(2,1)} %param.1), calls=%async_computation.1 | async-start | bytes 2752512 | tf_op jit(solution)/shard_map/cond/branch_1_fun/all_to_all | solution.py:268
  12.4 25.0 %all-to-all-done.1 = bf16[8,24,3584]{2,1,0:T(8,128)(2,1)} async-done(((bf16[8,24,3584]{2,1,0:T(8,128)(2,1)}), bf16[8,24,3584]{2,1,0:T(8,128)(2,1)}, u32[]{:S(2)}, u32[]{:S(2)}) %all-to-all-start.1) | async-done | bytes 1376288 | tf_op jit(solution)/shard_map/cond/branch_1_fun/all_to_all | solution.py:268
  37.4 1.3 copy.15
  38.7 7.2 %conditional.13 = (bf16[8,24,3072]{2,1,0:T(8,128)(2,1)}, bf16[2,192,256]{2,1,0:T(8,128)(2,1)}) conditional(s32[]{:T(128)} %convert_element_type.6, (f32[4,3072]{1,0:T(4,128)S(1)}, bf16[24,3072]{1,0:T(8,128)(2,1)S(1)}) %tuple.115, (bf16[8,24,3584]{2,1,0:T(8,128)(2,1)}, f32[2,128]{1,0:T(2,128)S(1)}, bf16[3,3072,256]{2,1,0:T(8,128)(2,1)}, ...), branch_computations={%region_2.3_spmd, %region_3.4_spmd} | conditional | bytes 16 | solution.py:341
  38.7 7.2 %branch_1_fun.21 = (bf16[192,3072]{1,0:T(8,128)(2,1)}, bf16[2,192,256]{2,1,0:T(8,128)(2,1)}) custom-call(f32[2,128]{1,0:T(2,128)S(1)} %get-tuple-element.222.gain_ref, bf16[3,3072,256]{2,1,0:T(8,128)(2,1)} %get-tuple-element.223.own_in, bf16[3,3072,256]{2,1,0:T(8,128)(2,1)} %get-tuple-element.224.other_in, ...), custom_call_target="tpu_custom_call" | custom-call | tf_op jit(solution)/shard_map/cond/branch_1_fun/pallas_call | solution.py:310
  45.9 6.6 %all-to-all-start.5 = ((bf16[8,24,3072]{2,1,0:T(8,128)(2,1)}), bf16[8,24,3072]{2,1,0:T(8,128)(2,1)}, u32[]{:S(2)}, u32[]{:S(2)}) async-start(bf16[8,24,3072]{2,1,0:T(8,128)(2,1)} %get-tuple-element.372), calls=%async_computation.5 | async-start | bytes 2359296 | tf_op jit(solution)/shard_map/all_to_all | solution.py:268
  52.6 17.9 %all-to-all-done.5 = bf16[8,24,3072]{2,1,0:T(8,128)(2,1)} async-done(((bf16[8,24,3072]{2,1,0:T(8,128)(2,1)}), bf16[8,24,3072]{2,1,0:T(8,128)(2,1)}, u32[]{:S(2)}, u32[]{:S(2)}) %all-to-all-start.5) | async-done | bytes 1179680 | tf_op jit(solution)/shard_map/all_to_all | solution.py:268
  70.5 4.5 %conditional.14 = (bf16[8,24,3072]{2,1,0:T(8,128)(2,1)}, bf16[2,192,256]{2,1,0:T(8,128)(2,1)}, bf16[24,3072]{1,0:T(8,128)(2,1)}) conditional(s32[]{:T(128)} %convert_element_type.6, (bf16[8,24,3072]{2,1,0:T(8,128)(2,1)}, f32[2,128]{1,0:T(2,128)S(1)}, bf16[3,3072,256]{2,1,0:T(8,128)(2,1)}, bf16[3,3072,256]{2,1,0:T(8,128)(2,1)}, ...), branch_computations={%region_4.5_spmd, %region_5.6_spmd} | conditional | bytes 24 | solution.py:341
  70.5 2.1 branch_1_fun.22.x_ref
  72.6 2.4 branch_1_fun.23
  75.0 4.3 %all-to-all-start.6 = ((bf16[8,24,3072]{2,1,0:T(8,128)(2,1)}), bf16[8,24,3072]{2,1,0:T(8,128)(2,1)}, u32[]{:S(2)}, u32[]{:S(2)}) async-start(bf16[8,24,3072]{2,1,0:T(8,128)(2,1)} %get-tuple-element.374), calls=%async_computation.6 | async-start | bytes 2359296 | tf_op jit(solution)/shard_map/all_to_all | solution.py:268
  79.4 18.2 %all-to-all-done.6 = bf16[8,24,3072]{2,1,0:T(8,128)(2,1)} async-done(((bf16[8,24,3072]{2,1,0:T(8,128)(2,1)}), bf16[8,24,3072]{2,1,0:T(8,128)(2,1)}, u32[]{:S(2)}, u32[]{:S(2)}) %all-to-all-start.6) | async-done | bytes 1179680 | tf_op jit(solution)/shard_map/all_to_all | solution.py:268
  97.6 7.4 %conditional.15 = (bf16[8,24,3072]{2,1,0:T(8,128)(2,1)}, bf16[2,192,256]{2,1,0:T(8,128)(2,1)}, bf16[24,3072]{1,0:T(8,128)(2,1)}) conditional(s32[]{:T(128)} %convert_element_type.6, (f32[4,3072]{1,0:T(4,128)S(1)}, f32[4,3072]{1,0:T(4,128)S(1)}, bf16[24,3072]{1,0:T(8,128)(2,1)S(1)}, bf16[8,24,3072]{2,1,0:T(8,128)(2,1)}, ...), branch_computations={%region_6.7_spmd, %region_7.8_spmd} | conditional | bytes 24 | solution.py:341
  97.6 7.4 %branch_1_fun.25 = (bf16[192,3072]{1,0:T(8,128)(2,1)}, bf16[2,192,256]{2,1,0:T(8,128)(2,1)}) custom-call(f32[2,128]{1,0:T(2,128)S(1)} %get-tuple-element.251.gain_ref, bf16[3,3072,256]{2,1,0:T(8,128)(2,1)} %get-tuple-element.252.own_in, bf16[3,3072,256]{2,1,0:T(8,128)(2,1)} %get-tuple-element.253.other_in, ...), custom_call_target="tpu_custom_call" | custom-call | tf_op jit(solution)/shard_map/cond/branch_1_fun/pallas_call | solution.py:310
  105.0 4.4 %all-to-all-start.7 = ((bf16[8,24,3072]{2,1,0:T(8,128)(2,1)}), bf16[8,24,3072]{2,1,0:T(8,128)(2,1)}, u32[]{:S(2)}, u32[]{:S(2)}) async-start(bf16[8,24,3072]{2,1,0:T(8,128)(2,1)} %get-tuple-element.378), calls=%async_computation.7 | async-start | bytes 2359296 | tf_op jit(solution)/shard_map/all_to_all | solution.py:268
  109.4 17.8 %all-to-all-done.7 = bf16[8,24,3072]{2,1,0:T(8,128)(2,1)} async-done(((bf16[8,24,3072]{2,1,0:T(8,128)(2,1)}), bf16[8,24,3072]{2,1,0:T(8,128)(2,1)}, u32[]{:S(2)}, u32[]{:S(2)}) %all-to-all-start.7) | async-done | bytes 1179680 | tf_op jit(solution)/shard_map/all_to_all | solution.py:268
  127.2 2.1 conditional.16
  127.2 2.1 branch_1_fun.27
  129.3 4.1 %collective-permute-start.6 = (bf16[24,3072]{1,0:T(8,128)(2,1)}, bf16[24,3072]{1,0:T(8,128)(2,1)}, u32[]{:S(2)}, u32[]{:S(2)}) collective-permute-start(bf16[24,3072]{1,0:T(8,128)(2,1)} %get-tuple-element.450), channel_id=1, source_target_pairs={{0,16},{1,17},{2,18},{3,19},{4,20},{5,21},{6,22},{7,23}} | collective-permute-start | bytes 442376 | tf_op jit(solution)/shard_map/ppermute | solution.py:265
  133.4 2.3 collective-permute-done.6
  135.7 2.8 conditional.17
  135.7 2.8 branch_1_fun.29
  138.6 1.3 collective-permute-start.7
  139.9 7.3 %conditional.20 = (bf16[8,24,3072]{2,1,0:T(8,128)(2,1)}, bf16[2,192,256]{2,1,0:T(8,128)(2,1)}) conditional(s32[]{:T(128)} %convert_element_type.6, (f32[4,3072]{1,0:T(4,128)S(1)}, bf16[24,3072]{1,0:T(8,128)(2,1)}) %tuple.128, (bf16[8,24,3072]{2,1,0:T(8,128)(2,1)}, f32[2,128]{1,0:T(2,128)S(1)}, bf16[3,3072,256]{2,1,0:T(8,128)(2,1)}, ...), branch_computations={%region_16.17_spmd, %region_17.18_spmd} | conditional | bytes 16 | solution.py:341
  139.9 7.3 %branch_1_fun.31 = (bf16[192,3072]{1,0:T(8,128)(2,1)}, bf16[2,192,256]{2,1,0:T(8,128)(2,1)}) custom-call(f32[2,128]{1,0:T(2,128)S(1)} %get-tuple-element.281.gain_ref, bf16[3,3072,256]{2,1,0:T(8,128)(2,1)} %get-tuple-element.282.own_in, bf16[3,3072,256]{2,1,0:T(8,128)(2,1)} %get-tuple-element.283.other_in, ...), custom_call_target="tpu_custom_call" | custom-call | tf_op jit(solution)/shard_map/cond/branch_1_fun/pallas_call | solution.py:310
  147.2 3.6 %all-to-all-start.8 = ((bf16[8,24,3072]{2,1,0:T(8,128)(2,1)}), bf16[8,24,3072]{2,1,0:T(8,128)(2,1)S(1)}, u32[]{:S(2)}, u32[]{:S(2)}) async-start(bf16[8,24,3072]{2,1,0:T(8,128)(2,1)} %get-tuple-element.382), calls=%async_computation.8 | async-start | bytes 2359296 | tf_op jit(solution)/shard_map/all_to_all | solution.py:268
  150.8 1.9 collective-permute-start.8
  152.7 27.6 %all-to-all-done.8 = bf16[8,24,3072]{2,1,0:T(8,128)(2,1)S(1)} async-done(((bf16[8,24,3072]{2,1,0:T(8,128)(2,1)}), bf16[8,24,3072]{2,1,0:T(8,128)(2,1)S(1)}, u32[]{:S(2)}, u32[]{:S(2)}) %all-to-all-start.8) | async-done | bytes 1179680 | tf_op jit(solution)/shard_map/all_to_all | solution.py:268
  180.3 4.1 %conditional.21 = (bf16[8,24,3072]{2,1,0:T(8,128)(2,1)}, bf16[2,192,256]{2,1,0:T(8,128)(2,1)S(1)}, bf16[24,3072]{1,0:T(8,128)(2,1)}) conditional(s32[]{:T(128)} %convert_element_type.6, (bf16[8,24,3072]{2,1,0:T(8,128)(2,1)S(1)}, f32[2,128]{1,0:T(2,128)S(1)}, bf16[3,3072,256]{2,1,0:T(8,128)(2,1)}, bf16[3,3072,256]{2,1,0:T(8,128)(2,1)}, ...), branch_computations={%region_18.19_spmd, %region_19.20_spmd} | conditional | bytes 786484 | solution.py:341
  180.3 1.7 branch_1_fun.32.x_ref
  182.1 2.4 branch_1_fun.33
  184.4 32.4 %all_to_all.52 = bf16[8,24,3072]{2,1,0:T(8,128)(2,1)S(1)} all-to-all(bf16[8,24,3072]{2,1,0:T(8,128)(2,1)} %get-tuple-element.385), channel_id=1, replica_groups=mesh['pipe'=4,'seq'=8] {'seq'}, dimensions={0} | all-to-all | bytes 2359296 | tf_op jit(solution)/shard_map/all_to_all | solution.py:268
  216.8 7.3 %conditional.22 = (bf16[8,24,3072]{2,1,0:T(8,128)(2,1)}, bf16[2,192,256]{2,1,0:T(8,128)(2,1)}, bf16[24,3072]{1,0:T(8,128)(2,1)S(1)}) conditional(s32[]{:T(128)} %convert_element_type.6, (f32[4,3072]{1,0:T(4,128)S(1)}, f32[4,3072]{1,0:T(4,128)S(1)}, bf16[24,3072]{1,0:T(8,128)(2,1)}, bf16[8,24,3072]{2,1,0:T(8,128)(2,1)S(1)}, ...), branch_computations={%region_20.21_spmd, %region_21.22_spmd} | conditional | bytes 24 | solution.py:341
  216.8 7.3 %branch_1_fun.35 = (bf16[192,3072]{1,0:T(8,128)(2,1)}, bf16[2,192,256]{2,1,0:T(8,128)(2,1)}) custom-call(f32[2,128]{1,0:T(2,128)S(1)} %get-tuple-element.310.gain_ref, bf16[3,3072,256]{2,1,0:T(8,128)(2,1)} %get-tuple-element.311.own_in, bf16[3,3072,256]{2,1,0:T(8,128)(2,1)} %get-tuple-element.312.other_in, ...), custom_call_target="tpu_custom_call" | custom-call | tf_op jit(solution)/shard_map/cond/branch_1_fun/pallas_call | solution.py:310
  224.8 4.4 %all-to-all-start.10 = ((bf16[8,24,3072]{2,1,0:T(8,128)(2,1)}), bf16[8,24,3072]{2,1,0:T(8,128)(2,1)S(1)}, u32[]{:S(2)}, u32[]{:S(2)}) async-start(bf16[8,24,3072]{2,1,0:T(8,128)(2,1)} %get-tuple-element.387), calls=%async_computation.10 | async-start | bytes 2359296 | tf_op jit(solution)/shard_map/all_to_all | solution.py:268
  229.3 1.6 collective-permute-done.9
  231.6 2.0 select_select_fusion
  233.5 21.0 %all-to-all-done.10 = bf16[8,24,3072]{2,1,0:T(8,128)(2,1)S(1)} async-done(((bf16[8,24,3072]{2,1,0:T(8,128)(2,1)}), bf16[8,24,3072]{2,1,0:T(8,128)(2,1)S(1)}, u32[]{:S(2)}, u32[]{:S(2)}) %all-to-all-start.10) | async-done | bytes 1179680 | tf_op jit(solution)/shard_map/all_to_all | solution.py:268
  254.6 15.1 %conditional.23 = ((bf16[24,3072]{1,0:T(8,128)(2,1)S(1)}, bf16[2,24,2,2048]{3,2,1,0:T(2,128)(2,1)S(1)})) conditional(s32[]{:T(128)} %convert_element_type.6, (bf16[8,24,3072]{2,1,0:T(8,128)(2,1)S(1)}, f32[2,128]{1,0:T(2,128)S(1)}, bf16[3,3072,256]{2,1,0:T(8,128)(2,1)}, bf16[3,3072,256]{2,1,0:T(8,128)(2,1)}, bf16[1,256,3072]{2,1,0:T(8,128)(2,1)S(1)}, ...), branch_computations={%region_22.23_spmd, %region_23.24_spmd} | conditional | bytes 3735588 | solution.py:341
  254.6 1.7 branch_1_fun.38
  256.3 3.5 %all-to-all-start.4 = ((bf16[8,24,1024]{2,1,0:T(8,128)(2,1)}), bf16[8,24,1024]{2,1,0:T(8,128)(2,1)S(1)}, u32[]{:S(2)}, u32[]{:S(2)}) async-start(bf16[8,24,1024]{2,1,0:T(8,128)(2,1)} %bitcast.19), calls=%async_computation.4 | async-start | bytes 786432 | tf_op jit(solution)/shard_map/cond/branch_1_fun/all_to_all | solution.py:268
  259.7 1.1 branch_1_fun.37
  260.8 8.2 %all-to-all-done.4.caches_ref = bf16[8,24,1024]{2,1,0:T(8,128)(2,1)S(1)} async-done(((bf16[8,24,1024]{2,1,0:T(8,128)(2,1)}), bf16[8,24,1024]{2,1,0:T(8,128)(2,1)S(1)}, u32[]{:S(2)}, u32[]{:S(2)}) %all-to-all-start.4) | async-done | bytes 393248 | tf_op jit(solution)/shard_map/cond/branch_1_fun/all_to_all | solution.py:268
  269.7 1.2 select_select_fusion.2
  270.9 16.8 %collective-permute-start.10 = (bf16[24,3072]{1,0:T(8,128)(2,1)S(1)}, bf16[24,3072]{1,0:T(8,128)(2,1)S(1)}, u32[]{:S(2)}, u32[]{:S(2)}) collective-permute-start(bf16[24,3072]{1,0:T(8,128)(2,1)S(1)} %get-tuple-element.400), channel_id=1, source_target_pairs={{0,8},{1,9},{2,10},{3,11},{4,12},{5,13},{6,14},{7,15},{8,0},{9,1},... | collective-permute-start | bytes 442376 | tf_op jit(solution)/shard_map/ppermute | solution.py:261
  (55 shorter events, 6.0 us)
Async XLA Ops:
  0.6 2.6 copy-start
  1.5 3.3 %collective-permute-start = (f32[4,3072]{1,0:T(4,128)S(1)}, f32[4,3072]{1,0:T(4,128)S(1)}, u32[]{:S(2)}, u32[]{:S(2)}) collective-permute-start(f32[4,3072]{1,0:T(4,128)S(1)} %select_maximum_fusion.params_ref), channel_id=1, source_target_pairs={{0,8},{1,9},{2,10},{3,11},{4,12},{5,13},{6,14},{7,15},{8,0},{9,1},... | collective-permute-start | bytes 147464 | tf_op jit(solution)/shard_map/ppermute | solution.py:261
  2.0 2.9 %copy-start.1 = (bf16[1,256,3072]{2,1,0:T(8,128)(2,1)S(1)}, bf16[1,256,3072]{2,1,0:T(8,128)(2,1)}, u32[]{:S(2)}) copy-start(bf16[1,256,3072]{2,1,0:T(8,128)(2,1)} %param.38) | copy-start | bytes 4718596
  2.0 3.4 %copy-start.8 = (f32[1,3072]{1,0:T(1,128)S(1)}, f32[1,3072]{1,0:T(1,128)}, u32[]{:S(2)}) copy-start(f32[1,3072]{1,0:T(1,128)} %param.35) | copy-start | bytes 36868
  2.0 3.4 %copy-start.9 = (f32[1,3072]{1,0:T(1,128)S(1)}, f32[1,3072]{1,0:T(1,128)}, u32[]{:S(2)}) copy-start(f32[1,3072]{1,0:T(1,128)} %param.34) | copy-start | bytes 36868
  2.0 3.4 %copy-start.10 = (f32[1,3072]{1,0:T(1,128)S(1)}, f32[1,3072]{1,0:T(1,128)}, u32[]{:S(2)}) copy-start(f32[1,3072]{1,0:T(1,128)} %param.33) | copy-start | bytes 36868
  2.0 3.4 %copy-start.11 = (f32[1,2,128]{2,1,0:T(2,128)S(1)}, f32[1,2,128]{2,1,0:T(2,128)}, u32[]{:S(2)}) copy-start(f32[1,2,128]{2,1,0:T(2,128)} %param.36) | copy-start | bytes 3076
  4.8 33.9 %collective-permute-start.1 = (bf16[3,3072,256]{2,1,0:T(8,128)(2,1)}, bf16[3,3072,256]{2,1,0:T(8,128)(2,1)}, u32[]{:S(2)}, u32[]{:S(2)}) collective-permute-start(bf16[3,3072,256]{2,1,0:T(8,128)(2,1)} %bitcast.33), channel_id=1, source_target_pairs={{0,8},{1,9},{2,10},{3,11},{4,12},{5,13},{6,14},{7,15},{8,0},{9,1},... | collective-permute-start | bytes 14155784 | tf_op jit(solution)/shard_map/ppermute | solution.py:261
  4.9 33.8 %collective-permute-start.2 = (bf16[1,256,3072]{2,1,0:T(8,128)(2,1)S(1)}, bf16[1,256,3072]{2,1,0:T(8,128)(2,1)}, u32[]{:S(2)}, u32[]{:S(2)}) collective-permute-start(bf16[1,256,3072]{2,1,0:T(8,128)(2,1)S(1)} %copy-done.1), channel_id=1, source_target_pairs={{0,8},{1,9},{2,10},{3,11},{4,12},{5,13},{6,14},{7,15},{8,0},{9,1},... | collective-permute-start | bytes 4718600 | tf_op jit(solution)/shard_map/ppermute | solution.py:261
  5.5 31.9 %all-to-all-start.1 = ((bf16[8,24,3584]{2,1,0:T(8,128)(2,1)}), bf16[8,24,3584]{2,1,0:T(8,128)(2,1)}, u32[]{:S(2)}, u32[]{:S(2)}) async-start(bf16[8,24,3584]{2,1,0:T(8,128)(2,1)} %param.1), calls=%async_computation.1 | async-start | bytes 2752512 | tf_op jit(solution)/shard_map/cond/branch_1_fun/all_to_all | solution.py:268
  45.9 24.6 %all-to-all-start.5 = ((bf16[8,24,3072]{2,1,0:T(8,128)(2,1)}), bf16[8,24,3072]{2,1,0:T(8,128)(2,1)}, u32[]{:S(2)}, u32[]{:S(2)}) async-start(bf16[8,24,3072]{2,1,0:T(8,128)(2,1)} %get-tuple-element.372), calls=%async_computation.5 | async-start | bytes 2359296 | tf_op jit(solution)/shard_map/all_to_all | solution.py:268
  52.6 18.0 %collective-permute-start.3 = (bf16[2,192,256]{2,1,0:T(8,128)(2,1)}, bf16[2,192,256]{2,1,0:T(8,128)(2,1)}, u32[]{:S(2)}, u32[]{:S(2)}) collective-permute-start(bf16[2,192,256]{2,1,0:T(8,128)(2,1)} %get-tuple-element.373), channel_id=1, source_target_pairs={{0,8},{1,9},{2,10},{3,11},{4,12},{5,13},{6,14},{7,15},{8,0},{9,1},... | collective-permute-start | bytes 589832 | tf_op jit(solution)/shard_map/ppermute | solution.py:261
  75.0 22.6 %all-to-all-start.6 = ((bf16[8,24,3072]{2,1,0:T(8,128)(2,1)}), bf16[8,24,3072]{2,1,0:T(8,128)(2,1)}, u32[]{:S(2)}, u32[]{:S(2)}) async-start(bf16[8,24,3072]{2,1,0:T(8,128)(2,1)} %get-tuple-element.374), calls=%async_computation.6 | async-start | bytes 2359296 | tf_op jit(solution)/shard_map/all_to_all | solution.py:268
  79.3 18.3 %collective-permute-start.4 = (bf16[192,512]{1,0:T(8,128)(2,1)}, bf16[192,512]{1,0:T(8,128)(2,1)}, u32[]{:S(2)}, u32[]{:S(2)}) collective-permute-start(bf16[192,512]{1,0:T(8,128)(2,1)} %get-tuple-element.376), channel_id=1, source_target_pairs={{0,8},{1,9},{2,10},{3,11},{4,12},{5,13},{6,14},{7,15},{8,0},{9,1},... | collective-permute-start | bytes 589832 | tf_op jit(solution)/shard_map/ppermute | solution.py:261
  105.0 22.2 %copy-start.2 = (bf16[24,3072]{1,0:T(8,128)(2,1)S(1)}, bf16[24,3072]{1,0:T(8,128)(2,1)}, u32[]{:S(2)}) copy-start(bf16[24,3072]{1,0:T(8,128)(2,1)} %get-tuple-element.380) | copy-start | bytes 442372
  105.0 22.2 %all-to-all-start.7 = ((bf16[8,24,3072]{2,1,0:T(8,128)(2,1)}), bf16[8,24,3072]{2,1,0:T(8,128)(2,1)}, u32[]{:S(2)}, u32[]{:S(2)}) async-start(bf16[8,24,3072]{2,1,0:T(8,128)(2,1)} %get-tuple-element.378), calls=%async_computation.7 | async-start | bytes 2359296 | tf_op jit(solution)/shard_map/all_to_all | solution.py:268
  109.4 24.0 %collective-permute-start.5 = (bf16[2,192,256]{2,1,0:T(8,128)(2,1)}, bf16[2,192,256]{2,1,0:T(8,128)(2,1)}, u32[]{:S(2)}, u32[]{:S(2)}) collective-permute-start(bf16[2,192,256]{2,1,0:T(8,128)(2,1)} %get-tuple-element.379), channel_id=1, source_target_pairs={{0,8},{1,9},{2,10},{3,11},{4,12},{5,13},{6,14},{7,15},{8,0},{9,1},... | collective-permute-start | bytes 589832 | tf_op jit(solution)/shard_map/ppermute | solution.py:261
  129.3 6.4 %collective-permute-start.6 = (bf16[24,3072]{1,0:T(8,128)(2,1)}, bf16[24,3072]{1,0:T(8,128)(2,1)}, u32[]{:S(2)}, u32[]{:S(2)}) collective-permute-start(bf16[24,3072]{1,0:T(8,128)(2,1)} %get-tuple-element.450), channel_id=1, source_target_pairs={{0,16},{1,17},{2,18},{3,19},{4,20},{5,21},{6,22},{7,23}} | collective-permute-start | bytes 442376 | tf_op jit(solution)/shard_map/ppermute | solution.py:265
  138.6 1.3 collective-permute-start.7
  147.2 33.1 %all-to-all-start.8 = ((bf16[8,24,3072]{2,1,0:T(8,128)(2,1)}), bf16[8,24,3072]{2,1,0:T(8,128)(2,1)S(1)}, u32[]{:S(2)}, u32[]{:S(2)}) async-start(bf16[8,24,3072]{2,1,0:T(8,128)(2,1)} %get-tuple-element.382), calls=%async_computation.8 | async-start | bytes 2359296 | tf_op jit(solution)/shard_map/all_to_all | solution.py:268
  150.8 29.5 %collective-permute-start.8 = (bf16[2,192,256]{2,1,0:T(8,128)(2,1)}, bf16[2,192,256]{2,1,0:T(8,128)(2,1)S(1)}, u32[]{:S(2)}, u32[]{:S(2)}) collective-permute-start(bf16[2,192,256]{2,1,0:T(8,128)(2,1)} %get-tuple-element.383), channel_id=1, source_target_pairs={{0,8},{1,9},{2,10},{3,11},{4,12},{5,13},{6,14},{7,15},{8,0},{9,1},... | collective-permute-start | bytes 589832 | tf_op jit(solution)/shard_map/ppermute | solution.py:261
  184.4 32.4 %copy-start.6 = (bf16[2,192,256]{2,1,0:T(8,128)(2,1)}, bf16[2,192,256]{2,1,0:T(8,128)(2,1)S(1)}, u32[]{:S(2)}) copy-start(bf16[2,192,256]{2,1,0:T(8,128)(2,1)S(1)} %get-tuple-element.386) | copy-start | bytes 589828
  224.2 0.7 copy-start.4
  224.8 29.7 %all-to-all-start.10 = ((bf16[8,24,3072]{2,1,0:T(8,128)(2,1)}), bf16[8,24,3072]{2,1,0:T(8,128)(2,1)S(1)}, u32[]{:S(2)}, u32[]{:S(2)}) async-start(bf16[8,24,3072]{2,1,0:T(8,128)(2,1)} %get-tuple-element.387), calls=%async_computation.10 | async-start | bytes 2359296 | tf_op jit(solution)/shard_map/all_to_all | solution.py:268
  229.2 1.7 collective-permute-start.9
  230.9 0.7 copy-start.3
  256.3 12.8 %all-to-all-start.4 = ((bf16[8,24,1024]{2,1,0:T(8,128)(2,1)}), bf16[8,24,1024]{2,1,0:T(8,128)(2,1)S(1)}, u32[]{:S(2)}, u32[]{:S(2)}) async-start(bf16[8,24,1024]{2,1,0:T(8,128)(2,1)} %bitcast.19), calls=%async_computation.4 | async-start | bytes 786432 | tf_op jit(solution)/shard_map/cond/branch_1_fun/all_to_all | solution.py:268
  269.7 19.8 %copy-start.12 = (bf16[2,24,2,2048]{3,2,1,0:T(2,128)(2,1)}, bf16[2,24,2,2048]{3,2,1,0:T(2,128)(2,1)S(1)}, u32[]{:S(2)}) copy-start(bf16[2,24,2,2048]{3,2,1,0:T(2,128)(2,1)S(1)} %get-tuple-element.397) | copy-start | bytes 1179652
  270.9 17.8 %collective-permute-start.10 = (bf16[24,3072]{1,0:T(8,128)(2,1)S(1)}, bf16[24,3072]{1,0:T(8,128)(2,1)S(1)}, u32[]{:S(2)}, u32[]{:S(2)}) collective-permute-start(bf16[24,3072]{1,0:T(8,128)(2,1)S(1)} %get-tuple-element.400), channel_id=1, source_target_pairs={{0,8},{1,9},{2,10},{3,11},{4,12},{5,13},{6,14},{7,15},{8,0},{9,1},... | collective-permute-start | bytes 442376 | tf_op jit(solution)/shard_map/ppermute | solution.py:261

commit v13 on v10

--- a/solution.py
+++ b/solution.py
@@ -388,6 +388,9 @@
         def early_gather():
             if crossing:
                 return norm(early_x, 1 - turn), blank(pair_shape)[0], blank(block_shape)[0]
+            if level:
+                result = finish(early_x, received, turn, 0)[0]
+                return norm(result, 1 - turn), blank(pair_shape)[0], result
             result, normed = finish(early_x, received, turn, 1)
             return normed, blank(pair_shape)[0], result
 

time: 286 us -> 287 us (level)
  transfers between devices with their start and end apart: 18 -> 18, of which waited for: 10 -> 10; matrix products, arithmetic and copies ran while one was open for 1% -> 1% of each run, Pallas kernels for 1% -> 2%
where the time goes in v13:
time: 287 us; the launch traced here: 286 us
  waiting for transfers between devices  139 us (48%)
  starting transfers between devices  61.8 us (22%)
  Pallas kernels  43.3 us (15%)
  blocking collectives  33.1 us (12%)
  local copies, waits for them, and re-layouts  4.58 us (2%)
  other arithmetic  3.43 us (1%)
    all_to_all x7, waiting for transfers between devices, across(): lax.all_to_all(blocks, 'seq', split_axis=0, concat_axis=0, tiled=True)  133 us
    all_to_all x7, starting transfers between devices, across(): lax.all_to_all(blocks, 'seq', split_axis=0, concat_axis=0, tiled=True)  33.6 us
    all_to_all x1, blocking collectives, across(): lax.all_to_all(blocks, 'seq', split_axis=0, concat_axis=0, tiled=True)  33.1 us
    pallas_call x4, Pallas kernels, block(): pl.pallas_call(functools.partial(block_kernel, turn, head_size, planes),...  27.8 us
    ppermute x9, starting transfers between devices, swap(): return lax.ppermute(value, AXES, pairs)  23.4 us
    pallas_call x4, Pallas kernels, finish(): pl.pallas_call(finish_kernel, out_shape=shapes, in_specs=[VMEM] * 4, out_...  7.59 us
  transfers between devices with their start and end apart: 18, of which 10 were waited for; matrix products, arithmetic and copies ran while one was open for 1% of the time, Pallas kernels for 2%

profile of v13, /device:TPU:0, one launch (start us, length us, event | category | flops | bytes accessed | tf_op | source)
XLA Modules:
  0.0 285.9 jit_solution(1383257938863868604)
XLA Ops:
  0.6 0.8 select_maximum_fusion.params_ref
  2.0 1.2 slice_bitcast_fusion.cache_ref
  3.3 1.5 shard_map.95
  5.5 33.2 %conditional.12 = (bf16[8,24,3584]{2,1,0:T(8,128)(2,1)}, bf16[192,512]{1,0:T(8,128)(2,1)}, bf16[192,3584]{1,0:T(8,128)(2,1)S(1)}) conditional(s32[]{:T(128)} %convert_element_type.6, bf16[8,24,3584]{2,1,0:T(8,128)(2,1)} %shard_map.95, bf16[8,24,3584]{2,1,0:T(8,128)(2,1)} %shard_map.95), branch_computations={%region_0.1_spmd, %region_1.2_spmd} | conditional | bytes 6881336 | solution.py:341
  5.5 6.9 %all-to-all-start.1 = ((bf16[8,24,3584]{2,1,0:T(8,128)(2,1)}), bf16[8,24,3584]{2,1,0:T(8,128)(2,1)}, u32[]{:S(2)}, u32[]{:S(2)}) async-start(bf16[8,24,3584]{2,1,0:T(8,128)(2,1)} %param.1), calls=%async_computation.1 | async-start | bytes 2752512 | tf_op jit(solution)/shard_map/cond/branch_1_fun/all_to_all | solution.py:268
  12.4 25.0 %all-to-all-done.1 = bf16[8,24,3584]{2,1,0:T(8,128)(2,1)} async-done(((bf16[8,24,3584]{2,1,0:T(8,128)(2,1)}), bf16[8,24,3584]{2,1,0:T(8,128)(2,1)}, u32[]{:S(2)}, u32[]{:S(2)}) %all-to-all-start.1) | async-done | bytes 1376288 | tf_op jit(solution)/shard_map/cond/branch_1_fun/all_to_all | solution.py:268
  37.4 1.3 copy.15
  38.7 7.3 %conditional.13 = (bf16[8,24,3072]{2,1,0:T(8,128)(2,1)}, bf16[2,192,256]{2,1,0:T(8,128)(2,1)}) conditional(s32[]{:T(128)} %convert_element_type.6, (f32[4,3072]{1,0:T(4,128)S(1)}, bf16[24,3072]{1,0:T(8,128)(2,1)S(1)}) %tuple.115, (bf16[8,24,3584]{2,1,0:T(8,128)(2,1)}, f32[2,128]{1,0:T(2,128)S(1)}, bf16[3,3072,256]{2,1,0:T(8,128)(2,1)}, ...), branch_computations={%region_2.3_spmd, %region_3.4_spmd} | conditional | bytes 16 | solution.py:341
  38.7 7.3 %branch_1_fun.20 = (bf16[192,3072]{1,0:T(8,128)(2,1)}, bf16[2,192,256]{2,1,0:T(8,128)(2,1)}) custom-call(f32[2,128]{1,0:T(2,128)S(1)} %get-tuple-element.222.gain_ref, bf16[3,3072,256]{2,1,0:T(8,128)(2,1)} %get-tuple-element.223.own_in, bf16[3,3072,256]{2,1,0:T(8,128)(2,1)} %get-tuple-element.224.other_in, ...), custom_call_target="tpu_custom_call" | custom-call | tf_op jit(solution)/shard_map/cond/branch_1_fun/pallas_call | solution.py:310
  46.0 6.6 %all-to-all-start.5 = ((bf16[8,24,3072]{2,1,0:T(8,128)(2,1)}), bf16[8,24,3072]{2,1,0:T(8,128)(2,1)}, u32[]{:S(2)}, u32[]{:S(2)}) async-start(bf16[8,24,3072]{2,1,0:T(8,128)(2,1)} %get-tuple-element.374), calls=%async_computation.5 | async-start | bytes 2359296 | tf_op jit(solution)/shard_map/all_to_all | solution.py:268
  52.6 18.0 %all-to-all-done.5 = bf16[8,24,3072]{2,1,0:T(8,128)(2,1)} async-done(((bf16[8,24,3072]{2,1,0:T(8,128)(2,1)}), bf16[8,24,3072]{2,1,0:T(8,128)(2,1)}, u32[]{:S(2)}, u32[]{:S(2)}) %all-to-all-start.5) | async-done | bytes 1179680 | tf_op jit(solution)/shard_map/all_to_all | solution.py:268
  70.6 3.6 %conditional.14 = (bf16[8,24,3072]{2,1,0:T(8,128)(2,1)}, bf16[2,192,256]{2,1,0:T(8,128)(2,1)}, bf16[24,3072]{1,0:T(8,128)(2,1)}) conditional(s32[]{:T(128)} %convert_element_type.6, (bf16[8,24,3072]{2,1,0:T(8,128)(2,1)}, f32[2,128]{1,0:T(2,128)S(1)}, bf16[3,3072,256]{2,1,0:T(8,128)(2,1)}, bf16[3,3072,256]{2,1,0:T(8,128)(2,1)}, ...), branch_computations={%region_4.5_spmd, %region_5.6_spmd} | conditional | bytes 24 | solution.py:341
  70.6 3.6 %branch_1_fun.21 = (bf16[24,3072]{1,0:T(8,128)(2,1)}, bf16[8,24,3072]{2,1,0:T(8,128)(2,1)}) custom-call(f32[4,3072]{1,0:T(4,128)S(1)} %get-tuple-element.240.params_ref, f32[4,3072]{1,0:T(4,128)S(1)} %get-tuple-element.241.next_ref, bf16[24,3072]{1,0:T(8,128)(2,1)S(1)} %get-tuple-element.242.x_ref, bf16[8,24,3072]{2,1,0:T(8,128)(2,1)} %get-tuple-element.243.parts_ref), custom_call_target="tpu_custom_call" | custom-call | tf_op jit(solution)/shard_map/cond/branch_1_fun/pallas_call | solution.py:334
  74.2 4.2 %all-to-all-start.6 = ((bf16[8,24,3072]{2,1,0:T(8,128)(2,1)}), bf16[8,24,3072]{2,1,0:T(8,128)(2,1)}, u32[]{:S(2)}, u32[]{:S(2)}) async-start(bf16[8,24,3072]{2,1,0:T(8,128)(2,1)} %get-tuple-element.376), calls=%async_computation.6 | async-start | bytes 2359296 | tf_op jit(solution)/shard_map/all_to_all | solution.py:268
  78.5 18.4 %all-to-all-done.6 = bf16[8,24,3072]{2,1,0:T(8,128)(2,1)} async-done(((bf16[8,24,3072]{2,1,0:T(8,128)(2,1)}), bf16[8,24,3072]{2,1,0:T(8,128)(2,1)}, u32[]{:S(2)}, u32[]{:S(2)}) %all-to-all-start.6) | async-done | bytes 1179680 | tf_op jit(solution)/shard_map/all_to_all | solution.py:268
  96.9 7.3 %conditional.15 = (bf16[8,24,3072]{2,1,0:T(8,128)(2,1)}, bf16[2,192,256]{2,1,0:T(8,128)(2,1)}, bf16[24,3072]{1,0:T(8,128)(2,1)}) conditional(s32[]{:T(128)} %convert_element_type.6, (f32[4,3072]{1,0:T(4,128)S(1)}, f32[4,3072]{1,0:T(4,128)S(1)}, bf16[24,3072]{1,0:T(8,128)(2,1)S(1)}, bf16[8,24,3072]{2,1,0:T(8,128)(2,1)}, ...), branch_computations={%region_6.7_spmd, %region_7.8_spmd} | conditional | bytes 24 | solution.py:341
  96.9 7.3 %branch_1_fun.23 = (bf16[192,3072]{1,0:T(8,128)(2,1)}, bf16[2,192,256]{2,1,0:T(8,128)(2,1)}) custom-call(f32[2,128]{1,0:T(2,128)S(1)} %get-tuple-element.253.gain_ref, bf16[3,3072,256]{2,1,0:T(8,128)(2,1)} %get-tuple-element.254.own_in, bf16[3,3072,256]{2,1,0:T(8,128)(2,1)} %get-tuple-element.255.other_in, ...), custom_call_target="tpu_custom_call" | custom-call | tf_op jit(solution)/shard_map/cond/branch_1_fun/pallas_call | solution.py:310
  104.3 4.4 %all-to-all-start.7 = ((bf16[8,24,3072]{2,1,0:T(8,128)(2,1)}), bf16[8,24,3072]{2,1,0:T(8,128)(2,1)}, u32[]{:S(2)}, u32[]{:S(2)}) async-start(bf16[8,24,3072]{2,1,0:T(8,128)(2,1)} %get-tuple-element.380), calls=%async_computation.7 | async-start | bytes 2359296 | tf_op jit(solution)/shard_map/all_to_all | solution.py:268
  108.8 18.0 %all-to-all-done.7 = bf16[8,24,3072]{2,1,0:T(8,128)(2,1)} async-done(((bf16[8,24,3072]{2,1,0:T(8,128)(2,1)}), bf16[8,24,3072]{2,1,0:T(8,128)(2,1)}, u32[]{:S(2)}, u32[]{:S(2)}) %all-to-all-start.7) | async-done | bytes 1179680 | tf_op jit(solution)/shard_map/all_to_all | solution.py:268
  126.7 2.1 conditional.16
  126.8 2.1 branch_1_fun.25
  128.9 3.4 %collective-permute-start.6 = (bf16[24,3072]{1,0:T(8,128)(2,1)}, bf16[24,3072]{1,0:T(8,128)(2,1)S(1)}, u32[]{:S(2)}, u32[]{:S(2)}) collective-permute-start(bf16[24,3072]{1,0:T(8,128)(2,1)} %get-tuple-element.452), channel_id=1, source_target_pairs={{0,16},{1,17},{2,18},{3,19},{4,20},{5,21},{6,22},{7,23}} | collective-permute-start | bytes 442376 | tf_op jit(solution)/shard_map/ppermute | solution.py:265
  132.3 2.9 %collective-permute-done.6 = bf16[24,3072]{1,0:T(8,128)(2,1)S(1)} collective-permute-done((bf16[24,3072]{1,0:T(8,128)(2,1)}, bf16[24,3072]{1,0:T(8,128)(2,1)S(1)}, u32[]{:S(2)}, u32[]{:S(2)}) %collective-permute-start.6) | collective-permute-done | bytes 147488 | tf_op jit(solution)/shard_map/ppermute | solution.py:265
  135.9 1.9 conditional.17
  135.9 1.9 branch_1_fun.27
  137.9 1.3 collective-permute-start.7
  139.2 6.6 %conditional.20 = (bf16[8,24,3072]{2,1,0:T(8,128)(2,1)}, bf16[2,192,256]{2,1,0:T(8,128)(2,1)S(1)}) conditional(s32[]{:T(128)} %convert_element_type.6, (f32[4,3072]{1,0:T(4,128)S(1)}, bf16[24,3072]{1,0:T(8,128)(2,1)}) %tuple.128, (bf16[8,24,3072]{2,1,0:T(8,128)(2,1)}, f32[2,128]{1,0:T(2,128)S(1)}, bf16[3,3072,256]{2,1,0:T(8,128)(2,1)}, ...), branch_computations={%region_16.17_spmd, %region_17.18_spmd} | conditional | bytes 16 | solution.py:341
  139.2 6.6 %branch_1_fun.29 = (bf16[192,3072]{1,0:T(8,128)(2,1)}, bf16[2,192,256]{2,1,0:T(8,128)(2,1)S(1)}) custom-call(f32[2,128]{1,0:T(2,128)S(1)} %get-tuple-element.283.gain_ref, bf16[3,3072,256]{2,1,0:T(8,128)(2,1)} %get-tuple-element.284.own_in, bf16[3,3072,256]{2,1,0:T(8,128)(2,1)} %get-tuple-element.285.other_in, ...), custom_call_target="tpu_custom_call" | custom-call | tf_op jit(solution)/shard_map/cond/branch_1_fun/pallas_call | solution.py:310
  145.8 3.7 %all-to-all-start.8 = ((bf16[8,24,3072]{2,1,0:T(8,128)(2,1)}), bf16[8,24,3072]{2,1,0:T(8,128)(2,1)S(1)}, u32[]{:S(2)}, u32[]{:S(2)}) async-start(bf16[8,24,3072]{2,1,0:T(8,128)(2,1)} %get-tuple-element.384), calls=%async_computation.8 | async-start | bytes 2359296 | tf_op jit(solution)/shard_map/all_to_all | solution.py:268
  149.5 5.0 %collective-permute-start.8 = (bf16[2,192,256]{2,1,0:T(8,128)(2,1)S(1)}, bf16[2,192,256]{2,1,0:T(8,128)(2,1)}, u32[]{:S(2)}, u32[]{:S(2)}) collective-permute-start(bf16[2,192,256]{2,1,0:T(8,128)(2,1)S(1)} %get-tuple-element.385), channel_id=1, source_target_pairs={{0,8},{1,9},{2,10},{3,11},{4,12},{5,13},{6,14},{7,15},{8,0},{9,1},... | collective-permute-start | bytes 589832 | tf_op jit(solution)/shard_map/ppermute | solution.py:261
  154.5 22.8 %all-to-all-done.8 = bf16[8,24,3072]{2,1,0:T(8,128)(2,1)S(1)} async-done(((bf16[8,24,3072]{2,1,0:T(8,128)(2,1)}), bf16[8,24,3072]{2,1,0:T(8,128)(2,1)S(1)}, u32[]{:S(2)}, u32[]{:S(2)}) %all-to-all-start.8) | async-done | bytes 1179680 | tf_op jit(solution)/shard_map/all_to_all | solution.py:268
  177.3 3.2 %conditional.21 = (bf16[8,24,3072]{2,1,0:T(8,128)(2,1)}, bf16[2,192,256]{2,1,0:T(8,128)(2,1)S(1)}, bf16[24,3072]{1,0:T(8,128)(2,1)}) conditional(s32[]{:T(128)} %convert_element_type.6, (bf16[8,24,3072]{2,1,0:T(8,128)(2,1)S(1)}, f32[2,128]{1,0:T(2,128)S(1)}, bf16[3,3072,256]{2,1,0:T(8,128)(2,1)}, bf16[3,3072,256]{2,1,0:T(8,128)(2,1)}, ...), branch_computations={%region_18.19_spmd, %region_19.20_spmd} | conditional | bytes 24 | solution.py:341
  177.3 0.8 branch_1_fun.30.x_ref
  178.2 2.4 branch_1_fun.31
  180.5 33.1 %all_to_all.52 = bf16[8,24,3072]{2,1,0:T(8,128)(2,1)S(1)} all-to-all(bf16[8,24,3072]{2,1,0:T(8,128)(2,1)} %get-tuple-element.387), channel_id=1, replica_groups=mesh['pipe'=4,'seq'=8] {'seq'}, dimensions={0} | all-to-all | bytes 2359296 | tf_op jit(solution)/shard_map/all_to_all | solution.py:268
  213.6 6.6 %conditional.22 = (bf16[8,24,3072]{2,1,0:T(8,128)(2,1)}, bf16[2,192,256]{2,1,0:T(8,128)(2,1)S(1)}, bf16[24,3072]{1,0:T(8,128)(2,1)S(1)}) conditional(s32[]{:T(128)} %convert_element_type.6, (f32[4,3072]{1,0:T(4,128)S(1)}, f32[4,3072]{1,0:T(4,128)S(1)}, bf16[24,3072]{1,0:T(8,128)(2,1)}, bf16[8,24,3072]{2,1,0:T(8,128)(2,1)S(1)}, ...), branch_computations={%region_20.21_spmd, %region_21.22_spmd} | conditional | bytes 24 | solution.py:341
  213.6 6.6 %branch_1_fun.33 = (bf16[192,3072]{1,0:T(8,128)(2,1)}, bf16[2,192,256]{2,1,0:T(8,128)(2,1)S(1)}) custom-call(f32[2,128]{1,0:T(2,128)S(1)} %get-tuple-element.312.gain_ref, bf16[3,3072,256]{2,1,0:T(8,128)(2,1)} %get-tuple-element.313.own_in, bf16[3,3072,256]{2,1,0:T(8,128)(2,1)} %get-tuple-element.314.other_in, ...), custom_call_target="tpu_custom_call" | custom-call | tf_op jit(solution)/shard_map/cond/branch_1_fun/pallas_call | solution.py:310
  220.9 4.3 %all-to-all-start.10 = ((bf16[8,24,3072]{2,1,0:T(8,128)(2,1)}), bf16[8,24,3072]{2,1,0:T(8,128)(2,1)S(1)}, u32[]{:S(2)}, u32[]{:S(2)}) async-start(bf16[8,24,3072]{2,1,0:T(8,128)(2,1)} %get-tuple-element.389), calls=%async_computation.10 | async-start | bytes 2359296 | tf_op jit(solution)/shard_map/all_to_all | solution.py:268
  225.3 1.4 collective-permute-done.9
  227.4 1.3 select_select_fusion
  228.7 22.9 %all-to-all-done.10 = bf16[8,24,3072]{2,1,0:T(8,128)(2,1)S(1)} async-done(((bf16[8,24,3072]{2,1,0:T(8,128)(2,1)}), bf16[8,24,3072]{2,1,0:T(8,128)(2,1)S(1)}, u32[]{:S(2)}, u32[]{:S(2)}) %all-to-all-start.10) | async-done | bytes 1179680 | tf_op jit(solution)/shard_map/all_to_all | solution.py:268
  251.6 14.1 %conditional.23 = ((bf16[24,3072]{1,0:T(8,128)(2,1)S(1)}, bf16[2,24,2,2048]{3,2,1,0:T(2,128)(2,1)S(1)})) conditional(s32[]{:T(128)} %convert_element_type.6, (bf16[8,24,3072]{2,1,0:T(8,128)(2,1)S(1)}, f32[2,128]{1,0:T(2,128)S(1)}, bf16[3,3072,256]{2,1,0:T(8,128)(2,1)}, bf16[3,3072,256]{2,1,0:T(8,128)(2,1)}, bf16[1,256,3072]{2,1,0:T(8,128)(2,1)S(1)}, ...), branch_computations={%region_22.23_spmd, %region_23.24_spmd} | conditional | bytes 3735588 | solution.py:341
  252.4 3.5 %all-to-all-start.4 = ((bf16[8,24,1024]{2,1,0:T(8,128)(2,1)}), bf16[8,24,1024]{2,1,0:T(8,128)(2,1)S(1)}, u32[]{:S(2)}, u32[]{:S(2)}) async-start(bf16[8,24,1024]{2,1,0:T(8,128)(2,1)} %bitcast.19), calls=%async_computation.4 | async-start | bytes 786432 | tf_op jit(solution)/shard_map/cond/branch_1_fun/all_to_all | solution.py:268
  255.9 1.1 branch_1_fun.35
  257.0 8.1 %all-to-all-done.4.caches_ref = bf16[8,24,1024]{2,1,0:T(8,128)(2,1)S(1)} async-done(((bf16[8,24,1024]{2,1,0:T(8,128)(2,1)}), bf16[8,24,1024]{2,1,0:T(8,128)(2,1)S(1)}, u32[]{:S(2)}, u32[]{:S(2)}) %all-to-all-start.4) | async-done | bytes 393248 | tf_op jit(solution)/shard_map/cond/branch_1_fun/all_to_all | solution.py:268
  265.7 1.3 select_select_fusion.2
  267.0 17.2 %collective-permute-start.10 = (bf16[24,3072]{1,0:T(8,128)(2,1)S(1)}, bf16[24,3072]{1,0:T(8,128)(2,1)S(1)}, u32[]{:S(2)}, u32[]{:S(2)}) collective-permute-start(bf16[24,3072]{1,0:T(8,128)(2,1)S(1)} %get-tuple-element.402), channel_id=1, source_target_pairs={{0,8},{1,9},{2,10},{3,11},{4,12},{5,13},{6,14},{7,15},{8,0},{9,1},... | collective-permute-start | bytes 442376 | tf_op jit(solution)/shard_map/ppermute | solution.py:261
  284.2 1.0 collective-permute-done.10.theirs_ref
  (62 shorter events, 5.7 us)
Async XLA Ops:
  0.6 2.6 copy-start
  1.5 3.3 %collective-permute-start = (f32[4,3072]{1,0:T(4,128)S(1)}, f32[4,3072]{1,0:T(4,128)S(1)}, u32[]{:S(2)}, u32[]{:S(2)}) collective-permute-start(f32[4,3072]{1,0:T(4,128)S(1)} %select_maximum_fusion.params_ref), channel_id=1, source_target_pairs={{0,8},{1,9},{2,10},{3,11},{4,12},{5,13},{6,14},{7,15},{8,0},{9,1},... | collective-permute-start | bytes 147464 | tf_op jit(solution)/shard_map/ppermute | solution.py:261
  2.0 2.9 %copy-start.1 = (bf16[1,256,3072]{2,1,0:T(8,128)(2,1)S(1)}, bf16[1,256,3072]{2,1,0:T(8,128)(2,1)}, u32[]{:S(2)}) copy-start(bf16[1,256,3072]{2,1,0:T(8,128)(2,1)} %param.38) | copy-start | bytes 4718596
  2.0 3.4 %copy-start.11 = (f32[1,3072]{1,0:T(1,128)S(1)}, f32[1,3072]{1,0:T(1,128)}, u32[]{:S(2)}) copy-start(f32[1,3072]{1,0:T(1,128)} %param.35) | copy-start | bytes 36868
  2.0 3.4 %copy-start.12 = (f32[1,3072]{1,0:T(1,128)S(1)}, f32[1,3072]{1,0:T(1,128)}, u32[]{:S(2)}) copy-start(f32[1,3072]{1,0:T(1,128)} %param.34) | copy-start | bytes 36868
  2.0 3.4 %copy-start.13 = (f32[1,3072]{1,0:T(1,128)S(1)}, f32[1,3072]{1,0:T(1,128)}, u32[]{:S(2)}) copy-start(f32[1,3072]{1,0:T(1,128)} %param.33) | copy-start | bytes 36868
  2.0 3.4 %copy-start.14 = (f32[1,2,128]{2,1,0:T(2,128)S(1)}, f32[1,2,128]{2,1,0:T(2,128)}, u32[]{:S(2)}) copy-start(f32[1,2,128]{2,1,0:T(2,128)} %param.36) | copy-start | bytes 3076
  4.8 33.9 %collective-permute-start.1 = (bf16[3,3072,256]{2,1,0:T(8,128)(2,1)}, bf16[3,3072,256]{2,1,0:T(8,128)(2,1)}, u32[]{:S(2)}, u32[]{:S(2)}) collective-permute-start(bf16[3,3072,256]{2,1,0:T(8,128)(2,1)} %bitcast.33), channel_id=1, source_target_pairs={{0,8},{1,9},{2,10},{3,11},{4,12},{5,13},{6,14},{7,15},{8,0},{9,1},... | collective-permute-start | bytes 14155784 | tf_op jit(solution)/shard_map/ppermute | solution.py:261
  4.9 33.8 %collective-permute-start.2 = (bf16[1,256,3072]{2,1,0:T(8,128)(2,1)S(1)}, bf16[1,256,3072]{2,1,0:T(8,128)(2,1)}, u32[]{:S(2)}, u32[]{:S(2)}) collective-permute-start(bf16[1,256,3072]{2,1,0:T(8,128)(2,1)S(1)} %copy-done.1), channel_id=1, source_target_pairs={{0,8},{1,9},{2,10},{3,11},{4,12},{5,13},{6,14},{7,15},{8,0},{9,1},... | collective-permute-start | bytes 4718600 | tf_op jit(solution)/shard_map/ppermute | solution.py:261
  5.5 31.9 %all-to-all-start.1 = ((bf16[8,24,3584]{2,1,0:T(8,128)(2,1)}), bf16[8,24,3584]{2,1,0:T(8,128)(2,1)}, u32[]{:S(2)}, u32[]{:S(2)}) async-start(bf16[8,24,3584]{2,1,0:T(8,128)(2,1)} %param.1), calls=%async_computation.1 | async-start | bytes 2752512 | tf_op jit(solution)/shard_map/cond/branch_1_fun/all_to_all | solution.py:268
  46.0 24.6 %all-to-all-start.5 = ((bf16[8,24,3072]{2,1,0:T(8,128)(2,1)}), bf16[8,24,3072]{2,1,0:T(8,128)(2,1)}, u32[]{:S(2)}, u32[]{:S(2)}) async-start(bf16[8,24,3072]{2,1,0:T(8,128)(2,1)} %get-tuple-element.374), calls=%async_computation.5 | async-start | bytes 2359296 | tf_op jit(solution)/shard_map/all_to_all | solution.py:268
  52.6 18.0 %collective-permute-start.3 = (bf16[2,192,256]{2,1,0:T(8,128)(2,1)}, bf16[2,192,256]{2,1,0:T(8,128)(2,1)}, u32[]{:S(2)}, u32[]{:S(2)}) collective-permute-start(bf16[2,192,256]{2,1,0:T(8,128)(2,1)} %get-tuple-element.375), channel_id=1, source_target_pairs={{0,8},{1,9},{2,10},{3,11},{4,12},{5,13},{6,14},{7,15},{8,0},{9,1},... | collective-permute-start | bytes 589832 | tf_op jit(solution)/shard_map/ppermute | solution.py:261
  74.2 22.8 %all-to-all-start.6 = ((bf16[8,24,3072]{2,1,0:T(8,128)(2,1)}), bf16[8,24,3072]{2,1,0:T(8,128)(2,1)}, u32[]{:S(2)}, u32[]{:S(2)}) async-start(bf16[8,24,3072]{2,1,0:T(8,128)(2,1)} %get-tuple-element.376), calls=%async_computation.6 | async-start | bytes 2359296 | tf_op jit(solution)/shard_map/all_to_all | solution.py:268
  78.4 18.5 %collective-permute-start.4 = (bf16[192,512]{1,0:T(8,128)(2,1)}, bf16[192,512]{1,0:T(8,128)(2,1)}, u32[]{:S(2)}, u32[]{:S(2)}) collective-permute-start(bf16[192,512]{1,0:T(8,128)(2,1)} %get-tuple-element.378), channel_id=1, source_target_pairs={{0,8},{1,9},{2,10},{3,11},{4,12},{5,13},{6,14},{7,15},{8,0},{9,1},... | collective-permute-start | bytes 589832 | tf_op jit(solution)/shard_map/ppermute | solution.py:261
  104.3 22.5 %copy-start.2 = (bf16[24,3072]{1,0:T(8,128)(2,1)S(1)}, bf16[24,3072]{1,0:T(8,128)(2,1)}, u32[]{:S(2)}) copy-start(bf16[24,3072]{1,0:T(8,128)(2,1)} %get-tuple-element.382) | copy-start | bytes 442372
  104.3 22.5 %all-to-all-start.7 = ((bf16[8,24,3072]{2,1,0:T(8,128)(2,1)}), bf16[8,24,3072]{2,1,0:T(8,128)(2,1)}, u32[]{:S(2)}, u32[]{:S(2)}) async-start(bf16[8,24,3072]{2,1,0:T(8,128)(2,1)} %get-tuple-element.380), calls=%async_computation.7 | async-start | bytes 2359296 | tf_op jit(solution)/shard_map/all_to_all | solution.py:268
  108.7 23.6 %collective-permute-start.5 = (bf16[2,192,256]{2,1,0:T(8,128)(2,1)}, bf16[2,192,256]{2,1,0:T(8,128)(2,1)}, u32[]{:S(2)}, u32[]{:S(2)}) collective-permute-start(bf16[2,192,256]{2,1,0:T(8,128)(2,1)} %get-tuple-element.381), channel_id=1, source_target_pairs={{0,8},{1,9},{2,10},{3,11},{4,12},{5,13},{6,14},{7,15},{8,0},{9,1},... | collective-permute-start | bytes 589832 | tf_op jit(solution)/shard_map/ppermute | solution.py:261
  128.9 6.4 %collective-permute-start.6 = (bf16[24,3072]{1,0:T(8,128)(2,1)}, bf16[24,3072]{1,0:T(8,128)(2,1)S(1)}, u32[]{:S(2)}, u32[]{:S(2)}) collective-permute-start(bf16[24,3072]{1,0:T(8,128)(2,1)} %get-tuple-element.452), channel_id=1, source_target_pairs={{0,16},{1,17},{2,18},{3,19},{4,20},{5,21},{6,22},{7,23}} | collective-permute-start | bytes 442376 | tf_op jit(solution)/shard_map/ppermute | solution.py:265
  135.2 0.7 copy-start.8
  137.8 1.4 copy-start.7
  137.9 1.3 collective-permute-start.7
  145.8 3.7 %copy-start.4 = (bf16[2,192,256]{2,1,0:T(8,128)(2,1)}, bf16[2,192,256]{2,1,0:T(8,128)(2,1)S(1)}, u32[]{:S(2)}) copy-start(bf16[2,192,256]{2,1,0:T(8,128)(2,1)S(1)} %get-tuple-element.385) | copy-start | bytes 589828
  145.8 31.5 %copy-start.9 = (bf16[24,3072]{1,0:T(8,128)(2,1)S(1)}, bf16[24,3072]{1,0:T(8,128)(2,1)}, u32[]{:S(2)}) copy-start(bf16[24,3072]{1,0:T(8,128)(2,1)} %copy-done.8) | copy-start | bytes 442372
  145.8 31.5 %all-to-all-start.8 = ((bf16[8,24,3072]{2,1,0:T(8,128)(2,1)}), bf16[8,24,3072]{2,1,0:T(8,128)(2,1)S(1)}, u32[]{:S(2)}, u32[]{:S(2)}) async-start(bf16[8,24,3072]{2,1,0:T(8,128)(2,1)} %get-tuple-element.384), calls=%async_computation.8 | async-start | bytes 2359296 | tf_op jit(solution)/shard_map/all_to_all | solution.py:268
  149.5 27.8 %collective-permute-start.8 = (bf16[2,192,256]{2,1,0:T(8,128)(2,1)S(1)}, bf16[2,192,256]{2,1,0:T(8,128)(2,1)}, u32[]{:S(2)}, u32[]{:S(2)}) collective-permute-start(bf16[2,192,256]{2,1,0:T(8,128)(2,1)S(1)} %get-tuple-element.385), channel_id=1, source_target_pairs={{0,8},{1,9},{2,10},{3,11},{4,12},{5,13},{6,14},{7,15},{8,0},{9,1},... | collective-permute-start | bytes 589832 | tf_op jit(solution)/shard_map/ppermute | solution.py:261
  220.3 0.7 copy-start.5
  220.3 4.9 %copy-start.10 = (bf16[2,192,256]{2,1,0:T(8,128)(2,1)}, bf16[2,192,256]{2,1,0:T(8,128)(2,1)S(1)}, u32[]{:S(2)}) copy-start(bf16[2,192,256]{2,1,0:T(8,128)(2,1)S(1)} %get-tuple-element.390) | copy-start | bytes 589828
  220.9 30.7 %all-to-all-start.10 = ((bf16[8,24,3072]{2,1,0:T(8,128)(2,1)}), bf16[8,24,3072]{2,1,0:T(8,128)(2,1)S(1)}, u32[]{:S(2)}, u32[]{:S(2)}) async-start(bf16[8,24,3072]{2,1,0:T(8,128)(2,1)} %get-tuple-element.389), calls=%async_computation.10 | async-start | bytes 2359296 | tf_op jit(solution)/shard_map/all_to_all | solution.py:268
  225.2 1.5 collective-permute-start.9
  226.7 0.7 copy-start.3
  252.4 12.7 %all-to-all-start.4 = ((bf16[8,24,1024]{2,1,0:T(8,128)(2,1)}), bf16[8,24,1024]{2,1,0:T(8,128)(2,1)S(1)}, u32[]{:S(2)}, u32[]{:S(2)}) async-start(bf16[8,24,1024]{2,1,0:T(8,128)(2,1)} %bitcast.19), calls=%async_computation.4 | async-start | bytes 786432 | tf_op jit(solution)/shard_map/cond/branch_1_fun/all_to_all | solution.py:268
  265.7 20.2 %copy-start.15 = (bf16[2,24,2,2048]{3,2,1,0:T(2,128)(2,1)}, bf16[2,24,2,2048]{3,2,1,0:T(2,128)(2,1)S(1)}, u32[]{:S(2)}) copy-start(bf16[2,24,2,2048]{3,2,1,0:T(2,128)(2,1)S(1)} %get-tuple-element.399) | copy-start | bytes 1179652
  267.0 18.2 %collective-permute-start.10 = (bf16[24,3072]{1,0:T(8,128)(2,1)S(1)}, bf16[24,3072]{1,0:T(8,128)(2,1)S(1)}, u32[]{:S(2)}, u32[]{:S(2)}) collective-permute-start(bf16[24,3072]{1,0:T(8,128)(2,1)S(1)} %get-tuple-element.402), channel_id=1, source_target_pairs={{0,8},{1,9},{2,10},{3,11},{4,12},{5,13},{6,14},{7,15},{8,0},{9,1},... | collective-permute-start | bytes 442376 | tf_op jit(solution)/shard_map/ppermute | solution.py:261

commit v14 on v13

--- a/solution.py
+++ b/solution.py
@@ -433,25 +433,31 @@
 
     cache_shape = bf16(2, rows, 2, seq * channels)
 
-    def last_early():
-        result = finish(early_x, received, last % 2, 0)[0]
+    def cache_alone():
         packed = pl.pallas_call(
             cache_kernel, out_shape=bf16(tokens, 4 * channels),
             in_specs=[VMEM] * 2, out_specs=VMEM, compiler_params=params_of(16),
         )(first_cache, second_cache)
-        cache = pl.pallas_call(
+        return pl.pallas_call(
             place_kernel, out_shape=cache_shape, in_specs=[VMEM], out_specs=VMEM,
             compiler_params=params_of(16),
         )(across(apart(packed)))
-        return result, cache
-
-    def last_late():
+
+    def last_block():
         parts, _ = block(received, got, last % 2, (first_cache, second_cache))
         return tuple(
             pl.pallas_call(
                 last_kernel, out_shape=(block_shape, cache_shape),
                 in_specs=[VMEM] * 3, out_specs=(VMEM,) * 2, compiler_params=params_of(16),
             )(params[last % 2], late_x, across(parts))
+        )
+
+    def last_early():
+        return finish(early_x, received, last % 2, 0)[0], cache_alone()
+
+    def last_late():
+        return lax.cond(
+            plane == planes - 1, last_block, lambda: (blank(block_shape)[0], cache_alone())
         )
 
     x, cache = either(last_early, last_late)

time: 287 us -> 274 us (0.955)
  starting transfers between devices: 61.8 us -> 44.6 us
    ppermute x9, starting transfers between devices: 23.4 us -> 6.27 us  [swap(): return lax.ppermute(value, AXES, pairs)]
  transfers between devices with their start and end apart: 18 -> 18, of which waited for: 10 -> 11; matrix products, arithmetic and copies ran while one was open for 1% -> 1% of each run, Pallas kernels for 2% -> 2%
where the time goes in v14:
time: 274 us; the launch traced here: 272 us
  waiting for transfers between devices  141 us (51%)
  starting transfers between devices  44.6 us (16%)
  Pallas kernels  44.6 us (16%)
  blocking collectives  33.2 us (12%)
  local copies, waits for them, and re-layouts  4.58 us (2%)
  other arithmetic  3.35 us (1%)
    all_to_all x7, waiting for transfers between devices, across(): lax.all_to_all(blocks, 'seq', split_axis=0, concat_axis=0, tiled=True)  133 us
    all_to_all x7, starting transfers between devices, across(): lax.all_to_all(blocks, 'seq', split_axis=0, concat_axis=0, tiled=True)  33.6 us
    all_to_all x1, blocking collectives, across(): lax.all_to_all(blocks, 'seq', split_axis=0, concat_axis=0, tiled=True)  33.2 us
    pallas_call x4, Pallas kernels, block(): pl.pallas_call(functools.partial(block_kernel, turn, head_size, planes),...  27.8 us
    pallas_call x4, Pallas kernels, finish(): pl.pallas_call(finish_kernel, out_shape=shapes, in_specs=[VMEM] * 4, out_...  8.21 us
    ppermute x9, starting transfers between devices, swap(): return lax.ppermute(value, AXES, pairs)  6.27 us
  transfers between devices with their start and end apart: 18, of which 11 were waited for; matrix products, arithmetic and copies ran while one was open for 1% of the time, Pallas kernels for 2%

profile of v14, /device:TPU:0, one launch (start us, length us, event | category | flops | bytes accessed | tf_op | source)
XLA Modules:
  0.0 272.0 jit_solution(1999450611864516370)
XLA Ops:
  0.6 0.8 select_maximum_fusion.params_ref
  2.0 1.2 slice_bitcast_fusion.cache_ref
  3.3 1.5 shard_map.95
  5.5 33.2 %conditional.13 = (bf16[8,24,3584]{2,1,0:T(8,128)(2,1)}, bf16[192,512]{1,0:T(8,128)(2,1)}, bf16[192,3584]{1,0:T(8,128)(2,1)S(1)}) conditional(s32[]{:T(128)} %convert_element_type.8, bf16[8,24,3584]{2,1,0:T(8,128)(2,1)} %shard_map.95, bf16[8,24,3584]{2,1,0:T(8,128)(2,1)} %shard_map.95), branch_computations={%region_0.1_spmd, %region_1.2_spmd} | conditional | bytes 6881336 | solution.py:341
  5.5 6.9 %all-to-all-start.1 = ((bf16[8,24,3584]{2,1,0:T(8,128)(2,1)}), bf16[8,24,3584]{2,1,0:T(8,128)(2,1)}, u32[]{:S(2)}, u32[]{:S(2)}) async-start(bf16[8,24,3584]{2,1,0:T(8,128)(2,1)} %param.1), calls=%async_computation.1 | async-start | bytes 2752512 | tf_op jit(solution)/shard_map/cond/branch_1_fun/all_to_all | solution.py:268
  12.4 25.0 %all-to-all-done.1 = bf16[8,24,3584]{2,1,0:T(8,128)(2,1)} async-done(((bf16[8,24,3584]{2,1,0:T(8,128)(2,1)}), bf16[8,24,3584]{2,1,0:T(8,128)(2,1)}, u32[]{:S(2)}, u32[]{:S(2)}) %all-to-all-start.1) | async-done | bytes 1376288 | tf_op jit(solution)/shard_map/cond/branch_1_fun/all_to_all | solution.py:268
  37.4 1.3 copy.19
  38.7 7.2 %conditional.14 = (bf16[8,24,3072]{2,1,0:T(8,128)(2,1)}, bf16[2,192,256]{2,1,0:T(8,128)(2,1)}) conditional(s32[]{:T(128)} %convert_element_type.8, (f32[4,3072]{1,0:T(4,128)S(1)}, bf16[24,3072]{1,0:T(8,128)(2,1)S(1)}) %tuple.117, (bf16[8,24,3584]{2,1,0:T(8,128)(2,1)}, f32[2,128]{1,0:T(2,128)S(1)}, bf16[3,3072,256]{2,1,0:T(8,128)(2,1)}, ...), branch_computations={%region_2.3_spmd, %region_3.4_spmd} | conditional | bytes 16 | solution.py:341
  38.7 7.2 %branch_1_fun.22 = (bf16[192,3072]{1,0:T(8,128)(2,1)}, bf16[2,192,256]{2,1,0:T(8,128)(2,1)}) custom-call(f32[2,128]{1,0:T(2,128)S(1)} %get-tuple-element.246.gain_ref, bf16[3,3072,256]{2,1,0:T(8,128)(2,1)} %get-tuple-element.247.own_in, bf16[3,3072,256]{2,1,0:T(8,128)(2,1)} %get-tuple-element.248.other_in, ...), custom_call_target="tpu_custom_call" | custom-call | tf_op jit(solution)/shard_map/cond/branch_1_fun/pallas_call | solution.py:310
  46.0 6.6 %all-to-all-start.6 = ((bf16[8,24,3072]{2,1,0:T(8,128)(2,1)}), bf16[8,24,3072]{2,1,0:T(8,128)(2,1)}, u32[]{:S(2)}, u32[]{:S(2)}) async-start(bf16[8,24,3072]{2,1,0:T(8,128)(2,1)} %get-tuple-element.414), calls=%async_computation.6 | async-start | bytes 2359296 | tf_op jit(solution)/shard_map/all_to_all | solution.py:268
  52.6 1.8 collective-permute-done.3
  54.4 16.2 %all-to-all-done.6 = bf16[8,24,3072]{2,1,0:T(8,128)(2,1)} async-done(((bf16[8,24,3072]{2,1,0:T(8,128)(2,1)}), bf16[8,24,3072]{2,1,0:T(8,128)(2,1)}, u32[]{:S(2)}, u32[]{:S(2)}) %all-to-all-start.6) | async-done | bytes 1179680 | tf_op jit(solution)/shard_map/all_to_all | solution.py:268
  70.5 3.5 %conditional.15 = (bf16[8,24,3072]{2,1,0:T(8,128)(2,1)}, bf16[2,192,256]{2,1,0:T(8,128)(2,1)}, bf16[24,3072]{1,0:T(8,128)(2,1)}) conditional(s32[]{:T(128)} %convert_element_type.8, (bf16[8,24,3072]{2,1,0:T(8,128)(2,1)}, f32[2,128]{1,0:T(2,128)S(1)}, bf16[3,3072,256]{2,1,0:T(8,128)(2,1)}, bf16[3,3072,256]{2,1,0:T(8,128)(2,1)}, ...), branch_computations={%region_4.5_spmd, %region_5.6_spmd} | conditional | bytes 24 | solution.py:341
  70.5 3.5 %branch_1_fun.23 = (bf16[24,3072]{1,0:T(8,128)(2,1)}, bf16[8,24,3072]{2,1,0:T(8,128)(2,1)}) custom-call(f32[4,3072]{1,0:T(4,128)S(1)} %get-tuple-element.264.params_ref, f32[4,3072]{1,0:T(4,128)S(1)} %get-tuple-element.265.next_ref, bf16[24,3072]{1,0:T(8,128)(2,1)S(1)} %get-tuple-element.266.x_ref, bf16[8,24,3072]{2,1,0:T(8,128)(2,1)} %get-tuple-element.267.parts_ref), custom_call_target="tpu_custom_call" | custom-call | tf_op jit(solution)/shard_map/cond/branch_1_fun/pallas_call | solution.py:334
  74.1 4.3 %all-to-all-start.7 = ((bf16[8,24,3072]{2,1,0:T(8,128)(2,1)}), bf16[8,24,3072]{2,1,0:T(8,128)(2,1)}, u32[]{:S(2)}, u32[]{:S(2)}) async-start(bf16[8,24,3072]{2,1,0:T(8,128)(2,1)} %get-tuple-element.416), calls=%async_computation.7 | async-start | bytes 2359296 | tf_op jit(solution)/shard_map/all_to_all | solution.py:268
  78.4 18.5 %all-to-all-done.7 = bf16[8,24,3072]{2,1,0:T(8,128)(2,1)} async-done(((bf16[8,24,3072]{2,1,0:T(8,128)(2,1)}), bf16[8,24,3072]{2,1,0:T(8,128)(2,1)}, u32[]{:S(2)}, u32[]{:S(2)}) %all-to-all-start.7) | async-done | bytes 1179680 | tf_op jit(solution)/shard_map/all_to_all | solution.py:268
  97.0 7.3 %conditional.16 = (bf16[8,24,3072]{2,1,0:T(8,128)(2,1)}, bf16[2,192,256]{2,1,0:T(8,128)(2,1)}, bf16[24,3072]{1,0:T(8,128)(2,1)}) conditional(s32[]{:T(128)} %convert_element_type.8, (f32[4,3072]{1,0:T(4,128)S(1)}, f32[4,3072]{1,0:T(4,128)S(1)}, bf16[24,3072]{1,0:T(8,128)(2,1)S(1)}, bf16[8,24,3072]{2,1,0:T(8,128)(2,1)}, ...), branch_computations={%region_6.7_spmd, %region_7.8_spmd} | conditional | bytes 24 | solution.py:341
  97.0 7.3 %branch_1_fun.25 = (bf16[192,3072]{1,0:T(8,128)(2,1)}, bf16[2,192,256]{2,1,0:T(8,128)(2,1)}) custom-call(f32[2,128]{1,0:T(2,128)S(1)} %get-tuple-element.277.gain_ref, bf16[3,3072,256]{2,1,0:T(8,128)(2,1)} %get-tuple-element.278.own_in, bf16[3,3072,256]{2,1,0:T(8,128)(2,1)} %get-tuple-element.279.other_in, ...), custom_call_target="tpu_custom_call" | custom-call | tf_op jit(solution)/shard_map/cond/branch_1_fun/pallas_call | solution.py:310
  104.3 4.4 %all-to-all-start.8 = ((bf16[8,24,3072]{2,1,0:T(8,128)(2,1)}), bf16[8,24,3072]{2,1,0:T(8,128)(2,1)}, u32[]{:S(2)}, u32[]{:S(2)}) async-start(bf16[8,24,3072]{2,1,0:T(8,128)(2,1)} %get-tuple-element.420), calls=%async_computation.8 | async-start | bytes 2359296 | tf_op jit(solution)/shard_map/all_to_all | solution.py:268
  108.8 17.9 %all-to-all-done.8 = bf16[8,24,3072]{2,1,0:T(8,128)(2,1)} async-done(((bf16[8,24,3072]{2,1,0:T(8,128)(2,1)}), bf16[8,24,3072]{2,1,0:T(8,128)(2,1)}, u32[]{:S(2)}, u32[]{:S(2)}) %all-to-all-start.8) | async-done | bytes 1179680 | tf_op jit(solution)/shard_map/all_to_all | solution.py:268
  126.8 2.1 conditional.17
  126.8 2.1 branch_1_fun.27
  128.9 3.4 %collective-permute-start.6 = (bf16[24,3072]{1,0:T(8,128)(2,1)}, bf16[24,3072]{1,0:T(8,128)(2,1)S(1)}, u32[]{:S(2)}, u32[]{:S(2)}) collective-permute-start(bf16[24,3072]{1,0:T(8,128)(2,1)} %get-tuple-element.491), channel_id=1, source_target_pairs={{0,16},{1,17},{2,18},{3,19},{4,20},{5,21},{6,22},{7,23}} | collective-permute-start | bytes 442376 | tf_op jit(solution)/shard_map/ppermute | solution.py:265
  132.3 2.9 %collective-permute-done.6 = bf16[24,3072]{1,0:T(8,128)(2,1)S(1)} collective-permute-done((bf16[24,3072]{1,0:T(8,128)(2,1)}, bf16[24,3072]{1,0:T(8,128)(2,1)S(1)}, u32[]{:S(2)}, u32[]{:S(2)}) %collective-permute-start.6) | collective-permute-done | bytes 147488 | tf_op jit(solution)/shard_map/ppermute | solution.py:265
  135.9 1.9 conditional.18
  135.9 1.9 branch_1_fun.29
  137.9 1.3 collective-permute-start.7
  139.2 6.6 %conditional.21 = (bf16[8,24,3072]{2,1,0:T(8,128)(2,1)}, bf16[2,192,256]{2,1,0:T(8,128)(2,1)S(1)}) conditional(s32[]{:T(128)} %convert_element_type.8, (f32[4,3072]{1,0:T(4,128)S(1)}, bf16[24,3072]{1,0:T(8,128)(2,1)}) %tuple.130, (bf16[8,24,3072]{2,1,0:T(8,128)(2,1)}, f32[2,128]{1,0:T(2,128)S(1)}, bf16[3,3072,256]{2,1,0:T(8,128)(2,1)}, ...), branch_computations={%region_16.17_spmd, %region_17.18_spmd} | conditional | bytes 16 | solution.py:341
  139.2 6.6 %branch_1_fun.31 = (bf16[192,3072]{1,0:T(8,128)(2,1)}, bf16[2,192,256]{2,1,0:T(8,128)(2,1)S(1)}) custom-call(f32[2,128]{1,0:T(2,128)S(1)} %get-tuple-element.307.gain_ref, bf16[3,3072,256]{2,1,0:T(8,128)(2,1)} %get-tuple-element.308.own_in, bf16[3,3072,256]{2,1,0:T(8,128)(2,1)} %get-tuple-element.309.other_in, ...), custom_call_target="tpu_custom_call" | custom-call | tf_op jit(solution)/shard_map/cond/branch_1_fun/pallas_call | solution.py:310
  145.8 3.7 %all-to-all-start.9 = ((bf16[8,24,3072]{2,1,0:T(8,128)(2,1)}), bf16[8,24,3072]{2,1,0:T(8,128)(2,1)S(1)}, u32[]{:S(2)}, u32[]{:S(2)}) async-start(bf16[8,24,3072]{2,1,0:T(8,128)(2,1)} %get-tuple-element.424), calls=%async_computation.9 | async-start | bytes 2359296 | tf_op jit(solution)/shard_map/all_to_all | solution.py:268
  149.5 4.9 %collective-permute-start.8 = (bf16[2,192,256]{2,1,0:T(8,128)(2,1)S(1)}, bf16[2,192,256]{2,1,0:T(8,128)(2,1)}, u32[]{:S(2)}, u32[]{:S(2)}) collective-permute-start(bf16[2,192,256]{2,1,0:T(8,128)(2,1)S(1)} %get-tuple-element.425), channel_id=1, source_target_pairs={{0,8},{1,9},{2,10},{3,11},{4,12},{5,13},{6,14},{7,15},{8,0},{9,1},... | collective-permute-start | bytes 589832 | tf_op jit(solution)/shard_map/ppermute | solution.py:261
  154.4 22.9 %all-to-all-done.9 = bf16[8,24,3072]{2,1,0:T(8,128)(2,1)S(1)} async-done(((bf16[8,24,3072]{2,1,0:T(8,128)(2,1)}), bf16[8,24,3072]{2,1,0:T(8,128)(2,1)S(1)}, u32[]{:S(2)}, u32[]{:S(2)}) %all-to-all-start.9) | async-done | bytes 1179680 | tf_op jit(solution)/shard_map/all_to_all | solution.py:268
  177.3 3.2 %conditional.22 = (bf16[8,24,3072]{2,1,0:T(8,128)(2,1)}, bf16[2,192,256]{2,1,0:T(8,128)(2,1)S(1)}, bf16[24,3072]{1,0:T(8,128)(2,1)}) conditional(s32[]{:T(128)} %convert_element_type.8, (bf16[8,24,3072]{2,1,0:T(8,128)(2,1)S(1)}, f32[2,128]{1,0:T(2,128)S(1)}, bf16[3,3072,256]{2,1,0:T(8,128)(2,1)}, bf16[3,3072,256]{2,1,0:T(8,128)(2,1)}, ...), branch_computations={%region_18.19_spmd, %region_19.20_spmd} | conditional | bytes 24 | solution.py:341
  178.2 2.4 branch_1_fun.33
  180.5 33.2 %all_to_all.56 = bf16[8,24,3072]{2,1,0:T(8,128)(2,1)S(1)} all-to-all(bf16[8,24,3072]{2,1,0:T(8,128)(2,1)} %get-tuple-element.427), channel_id=1, replica_groups=mesh['pipe'=4,'seq'=8] {'seq'}, dimensions={0} | all-to-all | bytes 2359296 | tf_op jit(solution)/shard_map/all_to_all | solution.py:268
  213.7 6.6 %conditional.23 = (bf16[8,24,3072]{2,1,0:T(8,128)(2,1)}, bf16[2,192,256]{2,1,0:T(8,128)(2,1)S(1)}, bf16[24,3072]{1,0:T(8,128)(2,1)S(1)}) conditional(s32[]{:T(128)} %convert_element_type.8, (f32[4,3072]{1,0:T(4,128)S(1)}, f32[4,3072]{1,0:T(4,128)S(1)}, bf16[24,3072]{1,0:T(8,128)(2,1)}, bf16[8,24,3072]{2,1,0:T(8,128)(2,1)S(1)}, ...), branch_computations={%region_20.21_spmd, %region_21.22_spmd} | conditional | bytes 24 | solution.py:341
  213.7 6.6 %branch_1_fun.35 = (bf16[192,3072]{1,0:T(8,128)(2,1)}, bf16[2,192,256]{2,1,0:T(8,128)(2,1)S(1)}) custom-call(f32[2,128]{1,0:T(2,128)S(1)} %get-tuple-element.336.gain_ref, bf16[3,3072,256]{2,1,0:T(8,128)(2,1)} %get-tuple-element.337.own_in, bf16[3,3072,256]{2,1,0:T(8,128)(2,1)} %get-tuple-element.338.other_in, ...), custom_call_target="tpu_custom_call" | custom-call | tf_op jit(solution)/shard_map/cond/branch_1_fun/pallas_call | solution.py:310
  221.0 4.3 %all-to-all-start.11 = ((bf16[8,24,3072]{2,1,0:T(8,128)(2,1)}), bf16[8,24,3072]{2,1,0:T(8,128)(2,1)S(1)}, u32[]{:S(2)}, u32[]{:S(2)}) async-start(bf16[8,24,3072]{2,1,0:T(8,128)(2,1)} %get-tuple-element.431), calls=%async_computation.11 | async-start | bytes 2359296 | tf_op jit(solution)/shard_map/all_to_all | solution.py:268
  225.4 1.4 collective-permute-done.9
  227.5 1.3 select_select_fusion
  228.8 22.9 %all-to-all-done.11 = bf16[8,24,3072]{2,1,0:T(8,128)(2,1)S(1)} async-done(((bf16[8,24,3072]{2,1,0:T(8,128)(2,1)}), bf16[8,24,3072]{2,1,0:T(8,128)(2,1)S(1)}, u32[]{:S(2)}, u32[]{:S(2)}) %all-to-all-start.11) | async-done | bytes 1179680 | tf_op jit(solution)/shard_map/all_to_all | solution.py:268
  251.7 16.9 %conditional.24 = ((bf16[24,3072]{1,0:T(8,128)(2,1)}, bf16[1,2,24,2,2048]{4,3,2,1,0:T(2,128)(2,1)})) conditional(s32[]{:T(128)} %convert_element_type.8, (s32[]{:T(128)}, bf16[2,192,256]{2,1,0:T(8,128)(2,1)S(1)}, bf16[2,192,256]{2,1,0:T(8,128)(2,1)S(1)}, bf16[8,24,3072]{2,1,0:T(8,128)(2,1)S(1)}, f32[2,128]{1,0:T(2,128)S(1)}, ...), branch_computations={%region_22.25_spmd, %region_25.26_spmd} | conditional | flops 2 | bytes 3735722 | solution.py:341
  252.5 3.5 %all-to-all-start.5 = ((bf16[8,24,1024]{2,1,0:T(8,128)(2,1)}), bf16[8,24,1024]{2,1,0:T(8,128)(2,1)S(1)}, u32[]{:S(2)}, u32[]{:S(2)}) async-start(bf16[8,24,1024]{2,1,0:T(8,128)(2,1)} %bitcast.22), calls=%async_computation.5 | async-start | bytes 786432 | tf_op jit(solution)/shard_map/cond/branch_1_fun/all_to_all | solution.py:268
  255.9 1.8 branch_1_fun.39
  257.7 9.6 %all-to-all-done.5.caches_ref = bf16[8,24,1024]{2,1,0:T(8,128)(2,1)S(1)} async-done(((bf16[8,24,1024]{2,1,0:T(8,128)(2,1)}), bf16[8,24,1024]{2,1,0:T(8,128)(2,1)S(1)}, u32[]{:S(2)}, u32[]{:S(2)}) %all-to-all-start.5) | async-done | bytes 393248 | tf_op jit(solution)/shard_map/cond/branch_1_fun/all_to_all | solution.py:268
  267.3 1.4 branch_1_fun.41
  268.6 1.2 select_select_fusion.2
  269.9 1.4 collective-permute-done.10.theirs_ref
  (60 shorter events, 5.9 us)
Async XLA Ops:
  0.6 2.6 copy-start
  1.5 3.3 %collective-permute-start = (f32[4,3072]{1,0:T(4,128)S(1)}, f32[4,3072]{1,0:T(4,128)S(1)}, u32[]{:S(2)}, u32[]{:S(2)}) collective-permute-start(f32[4,3072]{1,0:T(4,128)S(1)} %select_maximum_fusion.params_ref), channel_id=1, source_target_pairs={{0,8},{1,9},{2,10},{3,11},{4,12},{5,13},{6,14},{7,15},{8,0},{9,1},... | collective-permute-start | bytes 147464 | tf_op jit(solution)/shard_map/ppermute | solution.py:261
  2.0 2.9 %copy-start.1 = (bf16[1,256,3072]{2,1,0:T(8,128)(2,1)S(1)}, bf16[1,256,3072]{2,1,0:T(8,128)(2,1)}, u32[]{:S(2)}) copy-start(bf16[1,256,3072]{2,1,0:T(8,128)(2,1)} %param.40) | copy-start | bytes 4718596
  2.0 3.4 %copy-start.11 = (f32[1,3072]{1,0:T(1,128)S(1)}, f32[1,3072]{1,0:T(1,128)}, u32[]{:S(2)}) copy-start(f32[1,3072]{1,0:T(1,128)} %param.37) | copy-start | bytes 36868
  2.0 3.4 %copy-start.12 = (f32[1,3072]{1,0:T(1,128)S(1)}, f32[1,3072]{1,0:T(1,128)}, u32[]{:S(2)}) copy-start(f32[1,3072]{1,0:T(1,128)} %param.36) | copy-start | bytes 36868
  2.0 3.4 %copy-start.13 = (f32[1,3072]{1,0:T(1,128)S(1)}, f32[1,3072]{1,0:T(1,128)}, u32[]{:S(2)}) copy-start(f32[1,3072]{1,0:T(1,128)} %param.35) | copy-start | bytes 36868
  2.0 3.4 %copy-start.14 = (f32[1,2,128]{2,1,0:T(2,128)S(1)}, f32[1,2,128]{2,1,0:T(2,128)}, u32[]{:S(2)}) copy-start(f32[1,2,128]{2,1,0:T(2,128)} %param.38) | copy-start | bytes 3076
  4.8 33.9 %collective-permute-start.1 = (bf16[3,3072,256]{2,1,0:T(8,128)(2,1)}, bf16[3,3072,256]{2,1,0:T(8,128)(2,1)}, u32[]{:S(2)}, u32[]{:S(2)}) collective-permute-start(bf16[3,3072,256]{2,1,0:T(8,128)(2,1)} %bitcast.36), channel_id=1, source_target_pairs={{0,8},{1,9},{2,10},{3,11},{4,12},{5,13},{6,14},{7,15},{8,0},{9,1},... | collective-permute-start | bytes 14155784 | tf_op jit(solution)/shard_map/ppermute | solution.py:261
  4.9 33.8 %collective-permute-start.2 = (bf16[1,256,3072]{2,1,0:T(8,128)(2,1)S(1)}, bf16[1,256,3072]{2,1,0:T(8,128)(2,1)}, u32[]{:S(2)}, u32[]{:S(2)}) collective-permute-start(bf16[1,256,3072]{2,1,0:T(8,128)(2,1)S(1)} %copy-done.1), channel_id=1, source_target_pairs={{0,8},{1,9},{2,10},{3,11},{4,12},{5,13},{6,14},{7,15},{8,0},{9,1},... | collective-permute-start | bytes 4718600 | tf_op jit(solution)/shard_map/ppermute | solution.py:261
  5.5 31.9 %all-to-all-start.1 = ((bf16[8,24,3584]{2,1,0:T(8,128)(2,1)}), bf16[8,24,3584]{2,1,0:T(8,128)(2,1)}, u32[]{:S(2)}, u32[]{:S(2)}) async-start(bf16[8,24,3584]{2,1,0:T(8,128)(2,1)} %param.1), calls=%async_computation.1 | async-start | bytes 2752512 | tf_op jit(solution)/shard_map/cond/branch_1_fun/all_to_all | solution.py:268
  46.0 24.6 %all-to-all-start.6 = ((bf16[8,24,3072]{2,1,0:T(8,128)(2,1)}), bf16[8,24,3072]{2,1,0:T(8,128)(2,1)}, u32[]{:S(2)}, u32[]{:S(2)}) async-start(bf16[8,24,3072]{2,1,0:T(8,128)(2,1)} %get-tuple-element.414), calls=%async_computation.6 | async-start | bytes 2359296 | tf_op jit(solution)/shard_map/all_to_all | solution.py:268
  52.6 1.8 collective-permute-start.3
  74.1 22.9 %all-to-all-start.7 = ((bf16[8,24,3072]{2,1,0:T(8,128)(2,1)}), bf16[8,24,3072]{2,1,0:T(8,128)(2,1)}, u32[]{:S(2)}, u32[]{:S(2)}) async-start(bf16[8,24,3072]{2,1,0:T(8,128)(2,1)} %get-tuple-element.416), calls=%async_computation.7 | async-start | bytes 2359296 | tf_op jit(solution)/shard_map/all_to_all | solution.py:268
  78.3 18.6 %collective-permute-start.4 = (bf16[192,512]{1,0:T(8,128)(2,1)}, bf16[192,512]{1,0:T(8,128)(2,1)}, u32[]{:S(2)}, u32[]{:S(2)}) collective-permute-start(bf16[192,512]{1,0:T(8,128)(2,1)} %get-tuple-element.418), channel_id=1, source_target_pairs={{0,8},{1,9},{2,10},{3,11},{4,12},{5,13},{6,14},{7,15},{8,0},{9,1},... | collective-permute-start | bytes 589832 | tf_op jit(solution)/shard_map/ppermute | solution.py:261
  104.3 22.4 %copy-start.2 = (bf16[24,3072]{1,0:T(8,128)(2,1)S(1)}, bf16[24,3072]{1,0:T(8,128)(2,1)}, u32[]{:S(2)}) copy-start(bf16[24,3072]{1,0:T(8,128)(2,1)} %get-tuple-element.422) | copy-start | bytes 442372
  104.3 22.4 %all-to-all-start.8 = ((bf16[8,24,3072]{2,1,0:T(8,128)(2,1)}), bf16[8,24,3072]{2,1,0:T(8,128)(2,1)}, u32[]{:S(2)}, u32[]{:S(2)}) async-start(bf16[8,24,3072]{2,1,0:T(8,128)(2,1)} %get-tuple-element.420), calls=%async_computation.8 | async-start | bytes 2359296 | tf_op jit(solution)/shard_map/all_to_all | solution.py:268
  108.7 23.6 %collective-permute-start.5 = (bf16[2,192,256]{2,1,0:T(8,128)(2,1)}, bf16[2,192,256]{2,1,0:T(8,128)(2,1)}, u32[]{:S(2)}, u32[]{:S(2)}) collective-permute-start(bf16[2,192,256]{2,1,0:T(8,128)(2,1)} %get-tuple-element.421), channel_id=1, source_target_pairs={{0,8},{1,9},{2,10},{3,11},{4,12},{5,13},{6,14},{7,15},{8,0},{9,1},... | collective-permute-start | bytes 589832 | tf_op jit(solution)/shard_map/ppermute | solution.py:261
  128.9 6.4 %collective-permute-start.6 = (bf16[24,3072]{1,0:T(8,128)(2,1)}, bf16[24,3072]{1,0:T(8,128)(2,1)S(1)}, u32[]{:S(2)}, u32[]{:S(2)}) collective-permute-start(bf16[24,3072]{1,0:T(8,128)(2,1)} %get-tuple-element.491), channel_id=1, source_target_pairs={{0,16},{1,17},{2,18},{3,19},{4,20},{5,21},{6,22},{7,23}} | collective-permute-start | bytes 442376 | tf_op jit(solution)/shard_map/ppermute | solution.py:265
  135.3 0.7 copy-start.8
  137.9 1.3 copy-start.7
  137.9 1.3 collective-permute-start.7
  145.8 3.7 %copy-start.4 = (bf16[2,192,256]{2,1,0:T(8,128)(2,1)}, bf16[2,192,256]{2,1,0:T(8,128)(2,1)S(1)}, u32[]{:S(2)}) copy-start(bf16[2,192,256]{2,1,0:T(8,128)(2,1)S(1)} %get-tuple-element.425) | copy-start | bytes 589828
  145.8 31.5 %copy-start.9 = (bf16[24,3072]{1,0:T(8,128)(2,1)S(1)}, bf16[24,3072]{1,0:T(8,128)(2,1)}, u32[]{:S(2)}) copy-start(bf16[24,3072]{1,0:T(8,128)(2,1)} %copy-done.8) | copy-start | bytes 442372
  145.8 31.5 %all-to-all-start.9 = ((bf16[8,24,3072]{2,1,0:T(8,128)(2,1)}), bf16[8,24,3072]{2,1,0:T(8,128)(2,1)S(1)}, u32[]{:S(2)}, u32[]{:S(2)}) async-start(bf16[8,24,3072]{2,1,0:T(8,128)(2,1)} %get-tuple-element.424), calls=%async_computation.9 | async-start | bytes 2359296 | tf_op jit(solution)/shard_map/all_to_all | solution.py:268
  149.5 27.8 %collective-permute-start.8 = (bf16[2,192,256]{2,1,0:T(8,128)(2,1)S(1)}, bf16[2,192,256]{2,1,0:T(8,128)(2,1)}, u32[]{:S(2)}, u32[]{:S(2)}) collective-permute-start(bf16[2,192,256]{2,1,0:T(8,128)(2,1)S(1)} %get-tuple-element.425), channel_id=1, source_target_pairs={{0,8},{1,9},{2,10},{3,11},{4,12},{5,13},{6,14},{7,15},{8,0},{9,1},... | collective-permute-start | bytes 589832 | tf_op jit(solution)/shard_map/ppermute | solution.py:261
  220.3 0.7 copy-start.5
  220.3 5.0 %copy-start.10 = (bf16[2,192,256]{2,1,0:T(8,128)(2,1)}, bf16[2,192,256]{2,1,0:T(8,128)(2,1)S(1)}, u32[]{:S(2)}) copy-start(bf16[2,192,256]{2,1,0:T(8,128)(2,1)S(1)} %get-tuple-element.429) | copy-start | bytes 589828
  221.0 30.7 %all-to-all-start.11 = ((bf16[8,24,3072]{2,1,0:T(8,128)(2,1)}), bf16[8,24,3072]{2,1,0:T(8,128)(2,1)S(1)}, u32[]{:S(2)}, u32[]{:S(2)}) async-start(bf16[8,24,3072]{2,1,0:T(8,128)(2,1)} %get-tuple-element.431), calls=%async_computation.11 | async-start | bytes 2359296 | tf_op jit(solution)/shard_map/all_to_all | solution.py:268
  225.3 1.5 collective-permute-start.9
  226.8 0.7 copy-start.3
  252.5 14.8 %all-to-all-start.5 = ((bf16[8,24,1024]{2,1,0:T(8,128)(2,1)}), bf16[8,24,1024]{2,1,0:T(8,128)(2,1)S(1)}, u32[]{:S(2)}, u32[]{:S(2)}) async-start(bf16[8,24,1024]{2,1,0:T(8,128)(2,1)} %bitcast.22), calls=%async_computation.5 | async-start | bytes 786432 | tf_op jit(solution)/shard_map/cond/branch_1_fun/all_to_all | solution.py:268
  269.8 1.4 collective-permute-start.10

commit v15 on v14

--- a/solution.py
+++ b/solution.py
@@ -452,24 +452,26 @@
             )(params[last % 2], late_x, across(parts))
         )
 
+    rest = range(planes - 1)
+    below = lambda at, side: by_plane(
+        [blocks_out[2 * m + at, side] for m in rest] + [blocks_out[0, 0]]
+    )
+    first_done = by_plane([blocks_out[2 * m, 0] for m in range(planes)])
+    first_sent = by_plane([blocks_out[2 * m, 1] for m in range(planes)])
+    second_done, second_sent = below(1, 1), below(1, 0)
+
     def last_early():
-        return finish(early_x, received, last % 2, 0)[0], cache_alone()
+        result = finish(early_x, received, last % 2, 0)[0]
+        return first_done, jnp.where(plane == planes - 1, result, second_sent), cache_alone()
 
     def last_late():
-        return lax.cond(
-            plane == planes - 1, last_block, lambda: (blank(block_shape)[0], cache_alone())
+        result, cache = lax.cond(
+            plane == planes - 1, last_block, lambda: (second_done, cache_alone())
         )
-
-    x, cache = either(last_early, last_late)
-    blocks_out[last, 0] = blocks_out[last, 1] = x
-    mine = by_plane(
-        [jnp.where(early, blocks_out[2 * m, 0], blocks_out[2 * m + 1, 1]) for m in range(planes)]
-    )
-    theirs = swap(
-        by_plane(
-            [jnp.where(early, blocks_out[2 * m + 1, 0], blocks_out[2 * m, 1]) for m in range(planes)]
-        )
-    )
+        return result, first_sent, cache
+
+    mine, theirs, cache = either(last_early, last_late)
+    theirs = swap(theirs)
     block_output = pl.pallas_call(
         pair_kernel, out_shape=bf16(2, rows, width), in_specs=[VMEM] * 2, out_specs=VMEM,
         compiler_params=params_of(16),

time: 274 us -> 275 us (level)
  transfers between devices with their start and end apart: 18 -> 18, of which waited for: 11 -> 10; matrix products, arithmetic and copies ran while one was open for 1% -> 2% of each run, Pallas kernels for 2% -> 2%
where the time goes in v15:
time: 275 us; the launch traced here: 273 us
  waiting for transfers between devices  139 us (51%)
  Pallas kernels  45.6 us (17%)
  starting transfers between devices  44.8 us (16%)
  blocking collectives  33.2 us (12%)
  other arithmetic  4.88 us (2%)
  local copies, waits for them, and re-layouts  4.61 us (2%)
    all_to_all x7, waiting for transfers between devices, across(): lax.all_to_all(blocks, 'seq', split_axis=0, concat_axis=0, tiled=True)  133 us
    all_to_all x7, starting transfers between devices, across(): lax.all_to_all(blocks, 'seq', split_axis=0, concat_axis=0, tiled=True)  33.7 us
    all_to_all x1, blocking collectives, across(): lax.all_to_all(blocks, 'seq', split_axis=0, concat_axis=0, tiled=True)  33.2 us
    pallas_call x4, Pallas kernels, block(): pl.pallas_call(functools.partial(block_kernel, turn, head_size, planes),...  27.8 us
    pallas_call x4, Pallas kernels, finish(): pl.pallas_call(finish_kernel, out_shape=shapes, in_specs=[VMEM] * 4, out_...  8.21 us
    ppermute x9, starting transfers between devices, swap(): return lax.ppermute(value, AXES, pairs)  6.25 us
  transfers between devices with their start and end apart: 18, of which 10 were waited for; matrix products, arithmetic and copies ran while one was open for 2% of the time, Pallas kernels for 2%

profile of v15, /device:TPU:0, one launch (start us, length us, event | category | flops | bytes accessed | tf_op | source)
XLA Modules:
  0.0 272.8 jit_solution(2631888735611064782)
XLA Ops:
  2.0 1.2 slice_bitcast_fusion.cache_ref
  3.3 1.5 shard_map.95
  5.5 33.2 %conditional.13 = (bf16[8,24,3584]{2,1,0:T(8,128)(2,1)}, bf16[192,512]{1,0:T(8,128)(2,1)}, bf16[192,3584]{1,0:T(8,128)(2,1)S(1)}) conditional(s32[]{:T(128)} %convert_element_type.8, bf16[8,24,3584]{2,1,0:T(8,128)(2,1)} %shard_map.95, bf16[8,24,3584]{2,1,0:T(8,128)(2,1)} %shard_map.95), branch_computations={%region_0.1_spmd, %region_1.2_spmd} | conditional | bytes 6881336 | solution.py:341
  5.5 6.9 %all-to-all-start.1 = ((bf16[8,24,3584]{2,1,0:T(8,128)(2,1)}), bf16[8,24,3584]{2,1,0:T(8,128)(2,1)}, u32[]{:S(2)}, u32[]{:S(2)}) async-start(bf16[8,24,3584]{2,1,0:T(8,128)(2,1)} %param.1), calls=%async_computation.1 | async-start | bytes 2752512 | tf_op jit(solution)/shard_map/cond/branch_1_fun/all_to_all | solution.py:268
  12.4 25.0 %all-to-all-done.1 = bf16[8,24,3584]{2,1,0:T(8,128)(2,1)} async-done(((bf16[8,24,3584]{2,1,0:T(8,128)(2,1)}), bf16[8,24,3584]{2,1,0:T(8,128)(2,1)}, u32[]{:S(2)}, u32[]{:S(2)}) %all-to-all-start.1) | async-done | bytes 1376288 | tf_op jit(solution)/shard_map/cond/branch_1_fun/all_to_all | solution.py:268
  37.3 1.3 copy.19
  38.7 7.3 %conditional.14 = (bf16[8,24,3072]{2,1,0:T(8,128)(2,1)}, bf16[2,192,256]{2,1,0:T(8,128)(2,1)}) conditional(s32[]{:T(128)} %convert_element_type.8, (f32[4,3072]{1,0:T(4,128)S(1)}, bf16[24,3072]{1,0:T(8,128)(2,1)S(1)}) %tuple.118, (bf16[8,24,3584]{2,1,0:T(8,128)(2,1)}, f32[2,128]{1,0:T(2,128)S(1)}, bf16[3,3072,256]{2,1,0:T(8,128)(2,1)}, ...), branch_computations={%region_2.3_spmd, %region_3.4_spmd} | conditional | bytes 16 | solution.py:341
  38.7 7.3 %branch_1_fun.22 = (bf16[192,3072]{1,0:T(8,128)(2,1)}, bf16[2,192,256]{2,1,0:T(8,128)(2,1)}) custom-call(f32[2,128]{1,0:T(2,128)S(1)} %get-tuple-element.280.gain_ref, bf16[3,3072,256]{2,1,0:T(8,128)(2,1)} %get-tuple-element.281.own_in, bf16[3,3072,256]{2,1,0:T(8,128)(2,1)} %get-tuple-element.282.other_in, ...), custom_call_target="tpu_custom_call" | custom-call | tf_op jit(solution)/shard_map/cond/branch_1_fun/pallas_call | solution.py:310
  45.9 6.6 %all-to-all-start.6 = ((bf16[8,24,3072]{2,1,0:T(8,128)(2,1)}), bf16[8,24,3072]{2,1,0:T(8,128)(2,1)}, u32[]{:S(2)}, u32[]{:S(2)}) async-start(bf16[8,24,3072]{2,1,0:T(8,128)(2,1)} %get-tuple-element.462), calls=%async_computation.6 | async-start | bytes 2359296 | tf_op jit(solution)/shard_map/all_to_all | solution.py:268
  52.6 17.9 %all-to-all-done.6 = bf16[8,24,3072]{2,1,0:T(8,128)(2,1)} async-done(((bf16[8,24,3072]{2,1,0:T(8,128)(2,1)}), bf16[8,24,3072]{2,1,0:T(8,128)(2,1)}, u32[]{:S(2)}, u32[]{:S(2)}) %all-to-all-start.6) | async-done | bytes 1179680 | tf_op jit(solution)/shard_map/all_to_all | solution.py:268
  70.5 3.5 %conditional.15 = (bf16[8,24,3072]{2,1,0:T(8,128)(2,1)}, bf16[2,192,256]{2,1,0:T(8,128)(2,1)}, bf16[24,3072]{1,0:T(8,128)(2,1)}) conditional(s32[]{:T(128)} %convert_element_type.8, (bf16[8,24,3072]{2,1,0:T(8,128)(2,1)}, f32[2,128]{1,0:T(2,128)S(1)}, bf16[3,3072,256]{2,1,0:T(8,128)(2,1)}, bf16[3,3072,256]{2,1,0:T(8,128)(2,1)}, ...), branch_computations={%region_4.5_spmd, %region_5.6_spmd} | conditional | bytes 24 | solution.py:341
  70.5 3.5 %branch_1_fun.23 = (bf16[24,3072]{1,0:T(8,128)(2,1)}, bf16[8,24,3072]{2,1,0:T(8,128)(2,1)}) custom-call(f32[4,3072]{1,0:T(4,128)S(1)} %get-tuple-element.298.params_ref, f32[4,3072]{1,0:T(4,128)S(1)} %get-tuple-element.299.next_ref, bf16[24,3072]{1,0:T(8,128)(2,1)S(1)} %get-tuple-element.300.x_ref, bf16[8,24,3072]{2,1,0:T(8,128)(2,1)} %get-tuple-element.301.parts_ref), custom_call_target="tpu_custom_call" | custom-call | tf_op jit(solution)/shard_map/cond/branch_1_fun/pallas_call | solution.py:334
  74.1 4.2 %all-to-all-start.7 = ((bf16[8,24,3072]{2,1,0:T(8,128)(2,1)}), bf16[8,24,3072]{2,1,0:T(8,128)(2,1)}, u32[]{:S(2)}, u32[]{:S(2)}) async-start(bf16[8,24,3072]{2,1,0:T(8,128)(2,1)} %get-tuple-element.465), calls=%async_computation.7 | async-start | bytes 2359296 | tf_op jit(solution)/shard_map/all_to_all | solution.py:268
  78.4 18.5 %all-to-all-done.7 = bf16[8,24,3072]{2,1,0:T(8,128)(2,1)} async-done(((bf16[8,24,3072]{2,1,0:T(8,128)(2,1)}), bf16[8,24,3072]{2,1,0:T(8,128)(2,1)}, u32[]{:S(2)}, u32[]{:S(2)}) %all-to-all-start.7) | async-done | bytes 1179680 | tf_op jit(solution)/shard_map/all_to_all | solution.py:268
  97.0 7.3 %conditional.16 = (bf16[8,24,3072]{2,1,0:T(8,128)(2,1)}, bf16[2,192,256]{2,1,0:T(8,128)(2,1)}, bf16[24,3072]{1,0:T(8,128)(2,1)}) conditional(s32[]{:T(128)} %convert_element_type.8, (f32[4,3072]{1,0:T(4,128)S(1)}, f32[4,3072]{1,0:T(4,128)S(1)}, bf16[24,3072]{1,0:T(8,128)(2,1)S(1)}, bf16[8,24,3072]{2,1,0:T(8,128)(2,1)}, ...), branch_computations={%region_6.7_spmd, %region_7.8_spmd} | conditional | bytes 24 | solution.py:341
  97.0 7.3 %branch_1_fun.25 = (bf16[192,3072]{1,0:T(8,128)(2,1)}, bf16[2,192,256]{2,1,0:T(8,128)(2,1)}) custom-call(f32[2,128]{1,0:T(2,128)S(1)} %get-tuple-element.311.gain_ref, bf16[3,3072,256]{2,1,0:T(8,128)(2,1)} %get-tuple-element.312.own_in, bf16[3,3072,256]{2,1,0:T(8,128)(2,1)} %get-tuple-element.313.other_in, ...), custom_call_target="tpu_custom_call" | custom-call | tf_op jit(solution)/shard_map/cond/branch_1_fun/pallas_call | solution.py:310
  104.3 4.4 %all-to-all-start.8 = ((bf16[8,24,3072]{2,1,0:T(8,128)(2,1)}), bf16[8,24,3072]{2,1,0:T(8,128)(2,1)}, u32[]{:S(2)}, u32[]{:S(2)}) async-start(bf16[8,24,3072]{2,1,0:T(8,128)(2,1)} %get-tuple-element.469), calls=%async_computation.8 | async-start | bytes 2359296 | tf_op jit(solution)/shard_map/all_to_all | solution.py:268
  108.8 17.9 %all-to-all-done.8 = bf16[8,24,3072]{2,1,0:T(8,128)(2,1)} async-done(((bf16[8,24,3072]{2,1,0:T(8,128)(2,1)}), bf16[8,24,3072]{2,1,0:T(8,128)(2,1)}, u32[]{:S(2)}, u32[]{:S(2)}) %all-to-all-start.8) | async-done | bytes 1179680 | tf_op jit(solution)/shard_map/all_to_all | solution.py:268
  126.7 2.1 conditional.17
  126.7 2.1 branch_1_fun.27
  128.8 3.4 %collective-permute-start.6 = (bf16[24,3072]{1,0:T(8,128)(2,1)}, bf16[24,3072]{1,0:T(8,128)(2,1)S(1)}, u32[]{:S(2)}, u32[]{:S(2)}) collective-permute-start(bf16[24,3072]{1,0:T(8,128)(2,1)} %get-tuple-element.549), channel_id=1, source_target_pairs={{0,16},{1,17},{2,18},{3,19},{4,20},{5,21},{6,22},{7,23}} | collective-permute-start | bytes 442376 | tf_op jit(solution)/shard_map/ppermute | solution.py:265
  132.3 2.9 %collective-permute-done.6 = bf16[24,3072]{1,0:T(8,128)(2,1)S(1)} collective-permute-done((bf16[24,3072]{1,0:T(8,128)(2,1)}, bf16[24,3072]{1,0:T(8,128)(2,1)S(1)}, u32[]{:S(2)}, u32[]{:S(2)}) %collective-permute-start.6) | collective-permute-done | bytes 147488 | tf_op jit(solution)/shard_map/ppermute | solution.py:265
  135.9 1.9 conditional.18
  135.9 1.9 branch_1_fun.29
  137.8 1.3 collective-permute-start.7
  139.2 6.6 %conditional.21 = (bf16[8,24,3072]{2,1,0:T(8,128)(2,1)}, bf16[2,192,256]{2,1,0:T(8,128)(2,1)S(1)}) conditional(s32[]{:T(128)} %convert_element_type.8, (f32[4,3072]{1,0:T(4,128)S(1)}, bf16[24,3072]{1,0:T(8,128)(2,1)}) %tuple.131, (bf16[8,24,3072]{2,1,0:T(8,128)(2,1)}, f32[2,128]{1,0:T(2,128)S(1)}, bf16[3,3072,256]{2,1,0:T(8,128)(2,1)}, ...), branch_computations={%region_16.17_spmd, %region_17.18_spmd} | conditional | bytes 16 | solution.py:341
  139.2 6.6 %branch_1_fun.31 = (bf16[192,3072]{1,0:T(8,128)(2,1)}, bf16[2,192,256]{2,1,0:T(8,128)(2,1)S(1)}) custom-call(f32[2,128]{1,0:T(2,128)S(1)} %get-tuple-element.341.gain_ref, bf16[3,3072,256]{2,1,0:T(8,128)(2,1)} %get-tuple-element.342.own_in, bf16[3,3072,256]{2,1,0:T(8,128)(2,1)} %get-tuple-element.343.other_in, ...), custom_call_target="tpu_custom_call" | custom-call | tf_op jit(solution)/shard_map/cond/branch_1_fun/pallas_call | solution.py:310
  145.8 3.7 %all-to-all-start.9 = ((bf16[8,24,3072]{2,1,0:T(8,128)(2,1)}), bf16[8,24,3072]{2,1,0:T(8,128)(2,1)S(1)}, u32[]{:S(2)}, u32[]{:S(2)}) async-start(bf16[8,24,3072]{2,1,0:T(8,128)(2,1)} %get-tuple-element.473), calls=%async_computation.9 | async-start | bytes 2359296 | tf_op jit(solution)/shard_map/all_to_all | solution.py:268
  149.5 4.9 %collective-permute-start.8 = (bf16[2,192,256]{2,1,0:T(8,128)(2,1)S(1)}, bf16[2,192,256]{2,1,0:T(8,128)(2,1)}, u32[]{:S(2)}, u32[]{:S(2)}) collective-permute-start(bf16[2,192,256]{2,1,0:T(8,128)(2,1)S(1)} %get-tuple-element.472), channel_id=1, source_target_pairs={{0,8},{1,9},{2,10},{3,11},{4,12},{5,13},{6,14},{7,15},{8,0},{9,1},... | collective-permute-start | bytes 589832 | tf_op jit(solution)/shard_map/ppermute | solution.py:261
  154.4 22.9 %all-to-all-done.9 = bf16[8,24,3072]{2,1,0:T(8,128)(2,1)S(1)} async-done(((bf16[8,24,3072]{2,1,0:T(8,128)(2,1)}), bf16[8,24,3072]{2,1,0:T(8,128)(2,1)S(1)}, u32[]{:S(2)}, u32[]{:S(2)}) %all-to-all-start.9) | async-done | bytes 1179680 | tf_op jit(solution)/shard_map/all_to_all | solution.py:268
  177.3 3.2 %conditional.22 = (bf16[8,24,3072]{2,1,0:T(8,128)(2,1)}, bf16[2,192,256]{2,1,0:T(8,128)(2,1)S(1)}, bf16[24,3072]{1,0:T(8,128)(2,1)}) conditional(s32[]{:T(128)} %convert_element_type.8, (bf16[8,24,3072]{2,1,0:T(8,128)(2,1)S(1)}, f32[2,128]{1,0:T(2,128)S(1)}, bf16[3,3072,256]{2,1,0:T(8,128)(2,1)}, bf16[3,3072,256]{2,1,0:T(8,128)(2,1)}, ...), branch_computations={%region_18.19_spmd, %region_19.20_spmd} | conditional | bytes 24 | solution.py:341
  178.2 2.4 branch_1_fun.33
  180.5 33.2 %all_to_all.56 = bf16[8,24,3072]{2,1,0:T(8,128)(2,1)S(1)} all-to-all(bf16[8,24,3072]{2,1,0:T(8,128)(2,1)} %get-tuple-element.474), channel_id=1, replica_groups=mesh['pipe'=4,'seq'=8] {'seq'}, dimensions={0} | all-to-all | bytes 2359296 | tf_op jit(solution)/shard_map/all_to_all | solution.py:268
  213.7 6.6 %conditional.23 = (bf16[8,24,3072]{2,1,0:T(8,128)(2,1)}, bf16[2,192,256]{2,1,0:T(8,128)(2,1)S(1)}, bf16[24,3072]{1,0:T(8,128)(2,1)S(1)}) conditional(s32[]{:T(128)} %convert_element_type.8, (f32[4,3072]{1,0:T(4,128)S(1)}, f32[4,3072]{1,0:T(4,128)S(1)}, bf16[24,3072]{1,0:T(8,128)(2,1)}, bf16[8,24,3072]{2,1,0:T(8,128)(2,1)S(1)}, ...), branch_computations={%region_20.21_spmd, %region_21.22_spmd} | conditional | bytes 24 | solution.py:341
  213.7 6.6 %branch_1_fun.35 = (bf16[192,3072]{1,0:T(8,128)(2,1)}, bf16[2,192,256]{2,1,0:T(8,128)(2,1)S(1)}) custom-call(f32[2,128]{1,0:T(2,128)S(1)} %get-tuple-element.370.gain_ref, bf16[3,3072,256]{2,1,0:T(8,128)(2,1)} %get-tuple-element.371.own_in, bf16[3,3072,256]{2,1,0:T(8,128)(2,1)} %get-tuple-element.372.other_in, ...), custom_call_target="tpu_custom_call" | custom-call | tf_op jit(solution)/shard_map/cond/branch_1_fun/pallas_call | solution.py:310
  221.0 4.3 %all-to-all-start.11 = ((bf16[8,24,3072]{2,1,0:T(8,128)(2,1)}), bf16[8,24,3072]{2,1,0:T(8,128)(2,1)S(1)}, u32[]{:S(2)}, u32[]{:S(2)}) async-start(bf16[8,24,3072]{2,1,0:T(8,128)(2,1)} %get-tuple-element.478), calls=%async_computation.11 | async-start | bytes 2359296 | tf_op jit(solution)/shard_map/all_to_all | solution.py:268
  225.4 1.4 collective-permute-done.9
  227.5 1.3 select_select_fusion
  228.8 22.9 %all-to-all-done.11 = bf16[8,24,3072]{2,1,0:T(8,128)(2,1)S(1)} async-done(((bf16[8,24,3072]{2,1,0:T(8,128)(2,1)}), bf16[8,24,3072]{2,1,0:T(8,128)(2,1)S(1)}, u32[]{:S(2)}, u32[]{:S(2)}) %all-to-all-start.11) | async-done | bytes 1179680 | tf_op jit(solution)/shard_map/all_to_all | solution.py:268
  251.7 17.0 %conditional.24 = (bf16[24,3072]{1,0:T(8,128)(2,1)}, bf16[2,24,2,2048]{3,2,1,0:T(2,128)(2,1)}, pred[24,3072]{1,0:T(8,128)(4,1)S(1)}, bf16[24,3072]{1,0:T(8,128)(2,1)}, bf16[24,3072]{1,0:T(8,128)(2,1)}) conditional(s32[]{:T(128)} %convert_element_type.8, (s32[]{:T(128)}, pred[]{:T(512)}, bf16[24,3072]{1,0:T(8,128)(2,1)}, ...), branch_computations={%region_22.25_spmd, %region_25.26_spmd} | conditional | flops 147457 | bytes 3809499 | solution.py:341
  252.5 3.6 %all-to-all-start.5 = ((bf16[8,24,1024]{2,1,0:T(8,128)(2,1)}), bf16[8,24,1024]{2,1,0:T(8,128)(2,1)S(1)}, u32[]{:S(2)}, u32[]{:S(2)}) async-start(bf16[8,24,1024]{2,1,0:T(8,128)(2,1)} %bitcast.20), calls=%async_computation.5 | async-start | bytes 786432 | tf_op jit(solution)/shard_map/cond/branch_1_fun/all_to_all | solution.py:268
  256.1 1.8 branch_1_fun.41
  257.8 1.7 broadcast_select_fusion.1
  259.5 7.8 %all-to-all-done.5.caches_ref = bf16[8,24,1024]{2,1,0:T(8,128)(2,1)S(1)} async-done(((bf16[8,24,1024]{2,1,0:T(8,128)(2,1)}), bf16[8,24,1024]{2,1,0:T(8,128)(2,1)S(1)}, u32[]{:S(2)}, u32[]{:S(2)}) %all-to-all-start.5) | async-done | bytes 393248 | tf_op jit(solution)/shard_map/cond/branch_1_fun/all_to_all | solution.py:268
  267.3 1.4 branch_1_fun.40
  268.7 1.0 select_n.109
  269.8 1.4 collective-permute-done.10.theirs_ref
  271.1 1.7 shard_map.96
  (64 shorter events, 6.1 us)
Async XLA Ops:
  0.6 2.6 copy-start
  1.5 3.3 %collective-permute-start = (f32[4,3072]{1,0:T(4,128)S(1)}, f32[4,3072]{1,0:T(4,128)S(1)}, u32[]{:S(2)}, u32[]{:S(2)}) collective-permute-start(f32[4,3072]{1,0:T(4,128)S(1)} %select_maximum_fusion.params_ref), channel_id=1, source_target_pairs={{0,8},{1,9},{2,10},{3,11},{4,12},{5,13},{6,14},{7,15},{8,0},{9,1},... | collective-permute-start | bytes 147464 | tf_op jit(solution)/shard_map/ppermute | solution.py:261
  2.0 2.9 %copy-start.1 = (bf16[1,256,3072]{2,1,0:T(8,128)(2,1)S(1)}, bf16[1,256,3072]{2,1,0:T(8,128)(2,1)}, u32[]{:S(2)}) copy-start(bf16[1,256,3072]{2,1,0:T(8,128)(2,1)} %param.40) | copy-start | bytes 4718596
  2.0 3.4 %copy-start.14 = (f32[1,3072]{1,0:T(1,128)S(1)}, f32[1,3072]{1,0:T(1,128)}, u32[]{:S(2)}) copy-start(f32[1,3072]{1,0:T(1,128)} %param.37) | copy-start | bytes 36868
  2.0 3.4 %copy-start.15 = (f32[1,3072]{1,0:T(1,128)S(1)}, f32[1,3072]{1,0:T(1,128)}, u32[]{:S(2)}) copy-start(f32[1,3072]{1,0:T(1,128)} %param.36) | copy-start | bytes 36868
  2.0 3.4 %copy-start.16 = (f32[1,3072]{1,0:T(1,128)S(1)}, f32[1,3072]{1,0:T(1,128)}, u32[]{:S(2)}) copy-start(f32[1,3072]{1,0:T(1,128)} %param.35) | copy-start | bytes 36868
  2.0 3.4 %copy-start.17 = (f32[1,2,128]{2,1,0:T(2,128)S(1)}, f32[1,2,128]{2,1,0:T(2,128)}, u32[]{:S(2)}) copy-start(f32[1,2,128]{2,1,0:T(2,128)} %param.38) | copy-start | bytes 3076
  4.8 33.9 %collective-permute-start.1 = (bf16[3,3072,256]{2,1,0:T(8,128)(2,1)}, bf16[3,3072,256]{2,1,0:T(8,128)(2,1)}, u32[]{:S(2)}, u32[]{:S(2)}) collective-permute-start(bf16[3,3072,256]{2,1,0:T(8,128)(2,1)} %bitcast.34), channel_id=1, source_target_pairs={{0,8},{1,9},{2,10},{3,11},{4,12},{5,13},{6,14},{7,15},{8,0},{9,1},... | collective-permute-start | bytes 14155784 | tf_op jit(solution)/shard_map/ppermute | solution.py:261
  4.9 33.8 %collective-permute-start.2 = (bf16[1,256,3072]{2,1,0:T(8,128)(2,1)S(1)}, bf16[1,256,3072]{2,1,0:T(8,128)(2,1)}, u32[]{:S(2)}, u32[]{:S(2)}) collective-permute-start(bf16[1,256,3072]{2,1,0:T(8,128)(2,1)S(1)} %copy-done.1), channel_id=1, source_target_pairs={{0,8},{1,9},{2,10},{3,11},{4,12},{5,13},{6,14},{7,15},{8,0},{9,1},... | collective-permute-start | bytes 4718600 | tf_op jit(solution)/shard_map/ppermute | solution.py:261
  5.5 31.9 %all-to-all-start.1 = ((bf16[8,24,3584]{2,1,0:T(8,128)(2,1)}), bf16[8,24,3584]{2,1,0:T(8,128)(2,1)}, u32[]{:S(2)}, u32[]{:S(2)}) async-start(bf16[8,24,3584]{2,1,0:T(8,128)(2,1)} %param.1), calls=%async_computation.1 | async-start | bytes 2752512 | tf_op jit(solution)/shard_map/cond/branch_1_fun/all_to_all | solution.py:268
  45.9 24.6 %all-to-all-start.6 = ((bf16[8,24,3072]{2,1,0:T(8,128)(2,1)}), bf16[8,24,3072]{2,1,0:T(8,128)(2,1)}, u32[]{:S(2)}, u32[]{:S(2)}) async-start(bf16[8,24,3072]{2,1,0:T(8,128)(2,1)} %get-tuple-element.462), calls=%async_computation.6 | async-start | bytes 2359296 | tf_op jit(solution)/shard_map/all_to_all | solution.py:268
  52.6 18.0 %collective-permute-start.3 = (bf16[2,192,256]{2,1,0:T(8,128)(2,1)}, bf16[2,192,256]{2,1,0:T(8,128)(2,1)}, u32[]{:S(2)}, u32[]{:S(2)}) collective-permute-start(bf16[2,192,256]{2,1,0:T(8,128)(2,1)} %get-tuple-element.463), channel_id=1, source_target_pairs={{0,8},{1,9},{2,10},{3,11},{4,12},{5,13},{6,14},{7,15},{8,0},{9,1},... | collective-permute-start | bytes 589832 | tf_op jit(solution)/shard_map/ppermute | solution.py:261
  74.1 22.9 %all-to-all-start.7 = ((bf16[8,24,3072]{2,1,0:T(8,128)(2,1)}), bf16[8,24,3072]{2,1,0:T(8,128)(2,1)}, u32[]{:S(2)}, u32[]{:S(2)}) async-start(bf16[8,24,3072]{2,1,0:T(8,128)(2,1)} %get-tuple-element.465), calls=%async_computation.7 | async-start | bytes 2359296 | tf_op jit(solution)/shard_map/all_to_all | solution.py:268
  78.3 18.6 %collective-permute-start.4 = (bf16[192,512]{1,0:T(8,128)(2,1)}, bf16[192,512]{1,0:T(8,128)(2,1)}, u32[]{:S(2)}, u32[]{:S(2)}) collective-permute-start(bf16[192,512]{1,0:T(8,128)(2,1)} %get-tuple-element.467), channel_id=1, source_target_pairs={{0,8},{1,9},{2,10},{3,11},{4,12},{5,13},{6,14},{7,15},{8,0},{9,1},... | collective-permute-start | bytes 589832 | tf_op jit(solution)/shard_map/ppermute | solution.py:261
  104.3 22.4 %copy-start.2 = (bf16[24,3072]{1,0:T(8,128)(2,1)S(1)}, bf16[24,3072]{1,0:T(8,128)(2,1)}, u32[]{:S(2)}) copy-start(bf16[24,3072]{1,0:T(8,128)(2,1)} %get-tuple-element.464) | copy-start | bytes 442372
  104.3 22.4 %all-to-all-start.8 = ((bf16[8,24,3072]{2,1,0:T(8,128)(2,1)}), bf16[8,24,3072]{2,1,0:T(8,128)(2,1)}, u32[]{:S(2)}, u32[]{:S(2)}) async-start(bf16[8,24,3072]{2,1,0:T(8,128)(2,1)} %get-tuple-element.469), calls=%async_computation.8 | async-start | bytes 2359296 | tf_op jit(solution)/shard_map/all_to_all | solution.py:268
  108.7 23.6 %collective-permute-start.5 = (bf16[2,192,256]{2,1,0:T(8,128)(2,1)}, bf16[2,192,256]{2,1,0:T(8,128)(2,1)}, u32[]{:S(2)}, u32[]{:S(2)}) collective-permute-start(bf16[2,192,256]{2,1,0:T(8,128)(2,1)} %get-tuple-element.470), channel_id=1, source_target_pairs={{0,8},{1,9},{2,10},{3,11},{4,12},{5,13},{6,14},{7,15},{8,0},{9,1},... | collective-permute-start | bytes 589832 | tf_op jit(solution)/shard_map/ppermute | solution.py:261
  128.8 6.4 %collective-permute-start.6 = (bf16[24,3072]{1,0:T(8,128)(2,1)}, bf16[24,3072]{1,0:T(8,128)(2,1)S(1)}, u32[]{:S(2)}, u32[]{:S(2)}) collective-permute-start(bf16[24,3072]{1,0:T(8,128)(2,1)} %get-tuple-element.549), channel_id=1, source_target_pairs={{0,16},{1,17},{2,18},{3,19},{4,20},{5,21},{6,22},{7,23}} | collective-permute-start | bytes 442376 | tf_op jit(solution)/shard_map/ppermute | solution.py:265
  135.2 0.6 copy-start.7
  137.8 1.4 copy-start.11
  137.8 1.3 collective-permute-start.7
  145.8 3.7 %copy-start.6 = (bf16[2,192,256]{2,1,0:T(8,128)(2,1)}, bf16[2,192,256]{2,1,0:T(8,128)(2,1)S(1)}, u32[]{:S(2)}) copy-start(bf16[2,192,256]{2,1,0:T(8,128)(2,1)S(1)} %get-tuple-element.472) | copy-start | bytes 589828
  145.8 31.5 %copy-start.8 = (bf16[24,3072]{1,0:T(8,128)(2,1)S(1)}, bf16[24,3072]{1,0:T(8,128)(2,1)}, u32[]{:S(2)}) copy-start(bf16[24,3072]{1,0:T(8,128)(2,1)} %copy-done.7) | copy-start | bytes 442372
  145.8 31.5 %all-to-all-start.9 = ((bf16[8,24,3072]{2,1,0:T(8,128)(2,1)}), bf16[8,24,3072]{2,1,0:T(8,128)(2,1)S(1)}, u32[]{:S(2)}, u32[]{:S(2)}) async-start(bf16[8,24,3072]{2,1,0:T(8,128)(2,1)} %get-tuple-element.473), calls=%async_computation.9 | async-start | bytes 2359296 | tf_op jit(solution)/shard_map/all_to_all | solution.py:268
  149.5 27.8 %collective-permute-start.8 = (bf16[2,192,256]{2,1,0:T(8,128)(2,1)S(1)}, bf16[2,192,256]{2,1,0:T(8,128)(2,1)}, u32[]{:S(2)}, u32[]{:S(2)}) collective-permute-start(bf16[2,192,256]{2,1,0:T(8,128)(2,1)S(1)} %get-tuple-element.472), channel_id=1, source_target_pairs={{0,8},{1,9},{2,10},{3,11},{4,12},{5,13},{6,14},{7,15},{8,0},{9,1},... | collective-permute-start | bytes 589832 | tf_op jit(solution)/shard_map/ppermute | solution.py:261
  220.3 0.7 copy-start.9
  220.3 5.0 %copy-start.13 = (bf16[2,192,256]{2,1,0:T(8,128)(2,1)}, bf16[2,192,256]{2,1,0:T(8,128)(2,1)S(1)}, u32[]{:S(2)}) copy-start(bf16[2,192,256]{2,1,0:T(8,128)(2,1)S(1)} %get-tuple-element.476) | copy-start | bytes 589828
  221.0 30.7 %all-to-all-start.11 = ((bf16[8,24,3072]{2,1,0:T(8,128)(2,1)}), bf16[8,24,3072]{2,1,0:T(8,128)(2,1)S(1)}, u32[]{:S(2)}, u32[]{:S(2)}) async-start(bf16[8,24,3072]{2,1,0:T(8,128)(2,1)} %get-tuple-element.478), calls=%async_computation.11 | async-start | bytes 2359296 | tf_op jit(solution)/shard_map/all_to_all | solution.py:268
  225.3 1.5 collective-permute-start.9
  226.8 0.7 copy-start.5
  252.5 5.4 %copy-start.4 = (bf16[24,3072]{1,0:T(8,128)(2,1)S(1)}, bf16[24,3072]{1,0:T(8,128)(2,1)}, u32[]{:S(2)}) copy-start(bf16[24,3072]{1,0:T(8,128)(2,1)} %get-tuple-element.416) | copy-start | bytes 442372 | tf_op jit(solution)/shard_map/cond
  252.5 14.8 %all-to-all-start.5 = ((bf16[8,24,1024]{2,1,0:T(8,128)(2,1)}), bf16[8,24,1024]{2,1,0:T(8,128)(2,1)S(1)}, u32[]{:S(2)}, u32[]{:S(2)}) async-start(bf16[8,24,1024]{2,1,0:T(8,128)(2,1)} %bitcast.20), calls=%async_computation.5 | async-start | bytes 786432 | tf_op jit(solution)/shard_map/cond/branch_1_fun/all_to_all | solution.py:268
  269.7 1.4 collective-permute-start.10

commit v16 on v14

--- a/solution.py
+++ b/solution.py
@@ -319,7 +319,7 @@
                 pltpu.VMEM(own_out.shape[1:], jnp.bfloat16),
                 pltpu.VMEM((tokens, total), jnp.bfloat16),
                 pltpu.VMEM((tokens, channels), jnp.bfloat16),
-                pltpu.SemaphoreType.DMA((3, 2)),
+                pltpu.SemaphoreType.DMA((3, 4)),
                 pltpu.SemaphoreType.DMA((3,)),
                 pltpu.SemaphoreType.DMA((5,)),
             ],

time: 274 us -> 275 us (level)
  no operation moved by 1% of the time
where the time goes in v16:
time: 275 us; the launch traced here: 272 us
  waiting for transfers between devices  140 us (51%)
  Pallas kernels  44.8 us (16%)
  starting transfers between devices  44.7 us (16%)
  blocking collectives  33.1 us (12%)
  local copies, waits for them, and re-layouts  4.58 us (2%)
  other arithmetic  3.35 us (1%)
    all_to_all x7, waiting for transfers between devices, across(): lax.all_to_all(blocks, 'seq', split_axis=0, concat_axis=0, tiled=True)  133 us
    all_to_all x7, starting transfers between devices, across(): lax.all_to_all(blocks, 'seq', split_axis=0, concat_axis=0, tiled=True)  33.6 us
    all_to_all x1, blocking collectives, across(): lax.all_to_all(blocks, 'seq', split_axis=0, concat_axis=0, tiled=True)  33.1 us
    pallas_call x4, Pallas kernels, block(): pl.pallas_call(functools.partial(block_kernel, turn, head_size, planes),...  27.9 us
    pallas_call x4, Pallas kernels, finish(): pl.pallas_call(finish_kernel, out_shape=shapes, in_specs=[VMEM] * 4, out_...  8.21 us
    ppermute x9, starting transfers between devices, swap(): return lax.ppermute(value, AXES, pairs)  6.31 us
  transfers between devices with their start and end apart: 18, of which 11 were waited for; matrix products, arithmetic and copies ran while one was open for 1% of the time, Pallas kernels for 2%

profile of v16, /device:TPU:0, one launch (start us, length us, event | category | flops | bytes accessed | tf_op | source)
XLA Modules:
  0.0 272.1 jit_solution(10547024768429805391)
XLA Ops:
  0.6 0.8 select_maximum_fusion.params_ref
  2.0 1.2 slice_bitcast_fusion.cache_ref
  3.3 1.5 shard_map.95
  5.5 33.2 %conditional.13 = (bf16[8,24,3584]{2,1,0:T(8,128)(2,1)}, bf16[192,512]{1,0:T(8,128)(2,1)}, bf16[192,3584]{1,0:T(8,128)(2,1)S(1)}) conditional(s32[]{:T(128)} %convert_element_type.8, bf16[8,24,3584]{2,1,0:T(8,128)(2,1)} %shard_map.95, bf16[8,24,3584]{2,1,0:T(8,128)(2,1)} %shard_map.95), branch_computations={%region_0.1_spmd, %region_1.2_spmd} | conditional | bytes 6881336 | solution.py:341
  5.5 6.9 %all-to-all-start.1 = ((bf16[8,24,3584]{2,1,0:T(8,128)(2,1)}), bf16[8,24,3584]{2,1,0:T(8,128)(2,1)}, u32[]{:S(2)}, u32[]{:S(2)}) async-start(bf16[8,24,3584]{2,1,0:T(8,128)(2,1)} %param.1), calls=%async_computation.1 | async-start | bytes 2752512 | tf_op jit(solution)/shard_map/cond/branch_1_fun/all_to_all | solution.py:268
  12.4 25.0 %all-to-all-done.1 = bf16[8,24,3584]{2,1,0:T(8,128)(2,1)} async-done(((bf16[8,24,3584]{2,1,0:T(8,128)(2,1)}), bf16[8,24,3584]{2,1,0:T(8,128)(2,1)}, u32[]{:S(2)}, u32[]{:S(2)}) %all-to-all-start.1) | async-done | bytes 1376288 | tf_op jit(solution)/shard_map/cond/branch_1_fun/all_to_all | solution.py:268
  37.4 1.3 copy.19
  38.7 7.3 %conditional.14 = (bf16[8,24,3072]{2,1,0:T(8,128)(2,1)}, bf16[2,192,256]{2,1,0:T(8,128)(2,1)}) conditional(s32[]{:T(128)} %convert_element_type.8, (f32[4,3072]{1,0:T(4,128)S(1)}, bf16[24,3072]{1,0:T(8,128)(2,1)S(1)}) %tuple.117, (bf16[8,24,3584]{2,1,0:T(8,128)(2,1)}, f32[2,128]{1,0:T(2,128)S(1)}, bf16[3,3072,256]{2,1,0:T(8,128)(2,1)}, ...), branch_computations={%region_2.3_spmd, %region_3.4_spmd} | conditional | bytes 16 | solution.py:341
  38.7 7.3 %branch_1_fun.22 = (bf16[192,3072]{1,0:T(8,128)(2,1)}, bf16[2,192,256]{2,1,0:T(8,128)(2,1)}) custom-call(f32[2,128]{1,0:T(2,128)S(1)} %get-tuple-element.246.gain_ref, bf16[3,3072,256]{2,1,0:T(8,128)(2,1)} %get-tuple-element.247.own_in, bf16[3,3072,256]{2,1,0:T(8,128)(2,1)} %get-tuple-element.248.other_in, ...), custom_call_target="tpu_custom_call" | custom-call | tf_op jit(solution)/shard_map/cond/branch_1_fun/pallas_call | solution.py:310
  46.0 6.6 %all-to-all-start.6 = ((bf16[8,24,3072]{2,1,0:T(8,128)(2,1)}), bf16[8,24,3072]{2,1,0:T(8,128)(2,1)}, u32[]{:S(2)}, u32[]{:S(2)}) async-start(bf16[8,24,3072]{2,1,0:T(8,128)(2,1)} %get-tuple-element.414), calls=%async_computation.6 | async-start | bytes 2359296 | tf_op jit(solution)/shard_map/all_to_all | solution.py:268
  52.6 1.8 collective-permute-done.3
  54.4 16.2 %all-to-all-done.6 = bf16[8,24,3072]{2,1,0:T(8,128)(2,1)} async-done(((bf16[8,24,3072]{2,1,0:T(8,128)(2,1)}), bf16[8,24,3072]{2,1,0:T(8,128)(2,1)}, u32[]{:S(2)}, u32[]{:S(2)}) %all-to-all-start.6) | async-done | bytes 1179680 | tf_op jit(solution)/shard_map/all_to_all | solution.py:268
  70.6 3.5 %conditional.15 = (bf16[8,24,3072]{2,1,0:T(8,128)(2,1)}, bf16[2,192,256]{2,1,0:T(8,128)(2,1)}, bf16[24,3072]{1,0:T(8,128)(2,1)}) conditional(s32[]{:T(128)} %convert_element_type.8, (bf16[8,24,3072]{2,1,0:T(8,128)(2,1)}, f32[2,128]{1,0:T(2,128)S(1)}, bf16[3,3072,256]{2,1,0:T(8,128)(2,1)}, bf16[3,3072,256]{2,1,0:T(8,128)(2,1)}, ...), branch_computations={%region_4.5_spmd, %region_5.6_spmd} | conditional | bytes 24 | solution.py:341
  70.6 3.5 %branch_1_fun.23 = (bf16[24,3072]{1,0:T(8,128)(2,1)}, bf16[8,24,3072]{2,1,0:T(8,128)(2,1)}) custom-call(f32[4,3072]{1,0:T(4,128)S(1)} %get-tuple-element.264.params_ref, f32[4,3072]{1,0:T(4,128)S(1)} %get-tuple-element.265.next_ref, bf16[24,3072]{1,0:T(8,128)(2,1)S(1)} %get-tuple-element.266.x_ref, bf16[8,24,3072]{2,1,0:T(8,128)(2,1)} %get-tuple-element.267.parts_ref), custom_call_target="tpu_custom_call" | custom-call | tf_op jit(solution)/shard_map/cond/branch_1_fun/pallas_call | solution.py:334
  74.1 4.3 %all-to-all-start.7 = ((bf16[8,24,3072]{2,1,0:T(8,128)(2,1)}), bf16[8,24,3072]{2,1,0:T(8,128)(2,1)}, u32[]{:S(2)}, u32[]{:S(2)}) async-start(bf16[8,24,3072]{2,1,0:T(8,128)(2,1)} %get-tuple-element.416), calls=%async_computation.7 | async-start | bytes 2359296 | tf_op jit(solution)/shard_map/all_to_all | solution.py:268
  78.5 18.5 %all-to-all-done.7 = bf16[8,24,3072]{2,1,0:T(8,128)(2,1)} async-done(((bf16[8,24,3072]{2,1,0:T(8,128)(2,1)}), bf16[8,24,3072]{2,1,0:T(8,128)(2,1)}, u32[]{:S(2)}, u32[]{:S(2)}) %all-to-all-start.7) | async-done | bytes 1179680 | tf_op jit(solution)/shard_map/all_to_all | solution.py:268
  97.0 7.4 %conditional.16 = (bf16[8,24,3072]{2,1,0:T(8,128)(2,1)}, bf16[2,192,256]{2,1,0:T(8,128)(2,1)}, bf16[24,3072]{1,0:T(8,128)(2,1)}) conditional(s32[]{:T(128)} %convert_element_type.8, (f32[4,3072]{1,0:T(4,128)S(1)}, f32[4,3072]{1,0:T(4,128)S(1)}, bf16[24,3072]{1,0:T(8,128)(2,1)S(1)}, bf16[8,24,3072]{2,1,0:T(8,128)(2,1)}, ...), branch_computations={%region_6.7_spmd, %region_7.8_spmd} | conditional | bytes 24 | solution.py:341
  97.0 7.4 %branch_1_fun.25 = (bf16[192,3072]{1,0:T(8,128)(2,1)}, bf16[2,192,256]{2,1,0:T(8,128)(2,1)}) custom-call(f32[2,128]{1,0:T(2,128)S(1)} %get-tuple-element.277.gain_ref, bf16[3,3072,256]{2,1,0:T(8,128)(2,1)} %get-tuple-element.278.own_in, bf16[3,3072,256]{2,1,0:T(8,128)(2,1)} %get-tuple-element.279.other_in, ...), custom_call_target="tpu_custom_call" | custom-call | tf_op jit(solution)/shard_map/cond/branch_1_fun/pallas_call | solution.py:310
  104.4 4.4 %all-to-all-start.8 = ((bf16[8,24,3072]{2,1,0:T(8,128)(2,1)}), bf16[8,24,3072]{2,1,0:T(8,128)(2,1)}, u32[]{:S(2)}, u32[]{:S(2)}) async-start(bf16[8,24,3072]{2,1,0:T(8,128)(2,1)} %get-tuple-element.420), calls=%async_computation.8 | async-start | bytes 2359296 | tf_op jit(solution)/shard_map/all_to_all | solution.py:268
  108.9 18.0 %all-to-all-done.8 = bf16[8,24,3072]{2,1,0:T(8,128)(2,1)} async-done(((bf16[8,24,3072]{2,1,0:T(8,128)(2,1)}), bf16[8,24,3072]{2,1,0:T(8,128)(2,1)}, u32[]{:S(2)}, u32[]{:S(2)}) %all-to-all-start.8) | async-done | bytes 1179680 | tf_op jit(solution)/shard_map/all_to_all | solution.py:268
  126.9 2.1 conditional.17
  126.9 2.1 branch_1_fun.27
  129.0 3.4 %collective-permute-start.6 = (bf16[24,3072]{1,0:T(8,128)(2,1)}, bf16[24,3072]{1,0:T(8,128)(2,1)S(1)}, u32[]{:S(2)}, u32[]{:S(2)}) collective-permute-start(bf16[24,3072]{1,0:T(8,128)(2,1)} %get-tuple-element.491), channel_id=1, source_target_pairs={{0,16},{1,17},{2,18},{3,19},{4,20},{5,21},{6,22},{7,23}} | collective-permute-start | bytes 442376 | tf_op jit(solution)/shard_map/ppermute | solution.py:265
  132.4 2.9 %collective-permute-done.6 = bf16[24,3072]{1,0:T(8,128)(2,1)S(1)} collective-permute-done((bf16[24,3072]{1,0:T(8,128)(2,1)}, bf16[24,3072]{1,0:T(8,128)(2,1)S(1)}, u32[]{:S(2)}, u32[]{:S(2)}) %collective-permute-start.6) | collective-permute-done | bytes 147488 | tf_op jit(solution)/shard_map/ppermute | solution.py:265
  136.0 1.9 conditional.18
  136.0 1.9 branch_1_fun.29
  138.0 1.3 collective-permute-start.7
  139.3 6.6 %conditional.21 = (bf16[8,24,3072]{2,1,0:T(8,128)(2,1)}, bf16[2,192,256]{2,1,0:T(8,128)(2,1)S(1)}) conditional(s32[]{:T(128)} %convert_element_type.8, (f32[4,3072]{1,0:T(4,128)S(1)}, bf16[24,3072]{1,0:T(8,128)(2,1)}) %tuple.130, (bf16[8,24,3072]{2,1,0:T(8,128)(2,1)}, f32[2,128]{1,0:T(2,128)S(1)}, bf16[3,3072,256]{2,1,0:T(8,128)(2,1)}, ...), branch_computations={%region_16.17_spmd, %region_17.18_spmd} | conditional | bytes 16 | solution.py:341
  139.3 6.6 %branch_1_fun.31 = (bf16[192,3072]{1,0:T(8,128)(2,1)}, bf16[2,192,256]{2,1,0:T(8,128)(2,1)S(1)}) custom-call(f32[2,128]{1,0:T(2,128)S(1)} %get-tuple-element.307.gain_ref, bf16[3,3072,256]{2,1,0:T(8,128)(2,1)} %get-tuple-element.308.own_in, bf16[3,3072,256]{2,1,0:T(8,128)(2,1)} %get-tuple-element.309.other_in, ...), custom_call_target="tpu_custom_call" | custom-call | tf_op jit(solution)/shard_map/cond/branch_1_fun/pallas_call | solution.py:310
  146.0 3.7 %all-to-all-start.9 = ((bf16[8,24,3072]{2,1,0:T(8,128)(2,1)}), bf16[8,24,3072]{2,1,0:T(8,128)(2,1)S(1)}, u32[]{:S(2)}, u32[]{:S(2)}) async-start(bf16[8,24,3072]{2,1,0:T(8,128)(2,1)} %get-tuple-element.424), calls=%async_computation.9 | async-start | bytes 2359296 | tf_op jit(solution)/shard_map/all_to_all | solution.py:268
  149.7 4.9 %collective-permute-start.8 = (bf16[2,192,256]{2,1,0:T(8,128)(2,1)S(1)}, bf16[2,192,256]{2,1,0:T(8,128)(2,1)}, u32[]{:S(2)}, u32[]{:S(2)}) collective-permute-start(bf16[2,192,256]{2,1,0:T(8,128)(2,1)S(1)} %get-tuple-element.425), channel_id=1, source_target_pairs={{0,8},{1,9},{2,10},{3,11},{4,12},{5,13},{6,14},{7,15},{8,0},{9,1},... | collective-permute-start | bytes 589832 | tf_op jit(solution)/shard_map/ppermute | solution.py:261
  154.6 22.9 %all-to-all-done.9 = bf16[8,24,3072]{2,1,0:T(8,128)(2,1)S(1)} async-done(((bf16[8,24,3072]{2,1,0:T(8,128)(2,1)}), bf16[8,24,3072]{2,1,0:T(8,128)(2,1)S(1)}, u32[]{:S(2)}, u32[]{:S(2)}) %all-to-all-start.9) | async-done | bytes 1179680 | tf_op jit(solution)/shard_map/all_to_all | solution.py:268
  177.5 3.2 %conditional.22 = (bf16[8,24,3072]{2,1,0:T(8,128)(2,1)}, bf16[2,192,256]{2,1,0:T(8,128)(2,1)S(1)}, bf16[24,3072]{1,0:T(8,128)(2,1)}) conditional(s32[]{:T(128)} %convert_element_type.8, (bf16[8,24,3072]{2,1,0:T(8,128)(2,1)S(1)}, f32[2,128]{1,0:T(2,128)S(1)}, bf16[3,3072,256]{2,1,0:T(8,128)(2,1)}, bf16[3,3072,256]{2,1,0:T(8,128)(2,1)}, ...), branch_computations={%region_18.19_spmd, %region_19.20_spmd} | conditional | bytes 24 | solution.py:341
  178.3 2.4 branch_1_fun.33
  180.7 33.1 %all_to_all.56 = bf16[8,24,3072]{2,1,0:T(8,128)(2,1)S(1)} all-to-all(bf16[8,24,3072]{2,1,0:T(8,128)(2,1)} %get-tuple-element.427), channel_id=1, replica_groups=mesh['pipe'=4,'seq'=8] {'seq'}, dimensions={0} | all-to-all | bytes 2359296 | tf_op jit(solution)/shard_map/all_to_all | solution.py:268
  213.8 6.6 %conditional.23 = (bf16[8,24,3072]{2,1,0:T(8,128)(2,1)}, bf16[2,192,256]{2,1,0:T(8,128)(2,1)S(1)}, bf16[24,3072]{1,0:T(8,128)(2,1)S(1)}) conditional(s32[]{:T(128)} %convert_element_type.8, (f32[4,3072]{1,0:T(4,128)S(1)}, f32[4,3072]{1,0:T(4,128)S(1)}, bf16[24,3072]{1,0:T(8,128)(2,1)}, bf16[8,24,3072]{2,1,0:T(8,128)(2,1)S(1)}, ...), branch_computations={%region_20.21_spmd, %region_21.22_spmd} | conditional | bytes 24 | solution.py:341
  213.8 6.6 %branch_1_fun.35 = (bf16[192,3072]{1,0:T(8,128)(2,1)}, bf16[2,192,256]{2,1,0:T(8,128)(2,1)S(1)}) custom-call(f32[2,128]{1,0:T(2,128)S(1)} %get-tuple-element.336.gain_ref, bf16[3,3072,256]{2,1,0:T(8,128)(2,1)} %get-tuple-element.337.own_in, bf16[3,3072,256]{2,1,0:T(8,128)(2,1)} %get-tuple-element.338.other_in, ...), custom_call_target="tpu_custom_call" | custom-call | tf_op jit(solution)/shard_map/cond/branch_1_fun/pallas_call | solution.py:310
  221.1 4.3 %all-to-all-start.11 = ((bf16[8,24,3072]{2,1,0:T(8,128)(2,1)}), bf16[8,24,3072]{2,1,0:T(8,128)(2,1)S(1)}, u32[]{:S(2)}, u32[]{:S(2)}) async-start(bf16[8,24,3072]{2,1,0:T(8,128)(2,1)} %get-tuple-element.431), calls=%async_computation.11 | async-start | bytes 2359296 | tf_op jit(solution)/shard_map/all_to_all | solution.py:268
  225.5 1.4 collective-permute-done.9
  227.6 1.3 select_select_fusion
  228.9 22.9 %all-to-all-done.11 = bf16[8,24,3072]{2,1,0:T(8,128)(2,1)S(1)} async-done(((bf16[8,24,3072]{2,1,0:T(8,128)(2,1)}), bf16[8,24,3072]{2,1,0:T(8,128)(2,1)S(1)}, u32[]{:S(2)}, u32[]{:S(2)}) %all-to-all-start.11) | async-done | bytes 1179680 | tf_op jit(solution)/shard_map/all_to_all | solution.py:268
  251.8 16.9 %conditional.24 = ((bf16[24,3072]{1,0:T(8,128)(2,1)}, bf16[1,2,24,2,2048]{4,3,2,1,0:T(2,128)(2,1)})) conditional(s32[]{:T(128)} %convert_element_type.8, (s32[]{:T(128)}, bf16[2,192,256]{2,1,0:T(8,128)(2,1)S(1)}, bf16[2,192,256]{2,1,0:T(8,128)(2,1)S(1)}, bf16[8,24,3072]{2,1,0:T(8,128)(2,1)S(1)}, f32[2,128]{1,0:T(2,128)S(1)}, ...), branch_computations={%region_22.25_spmd, %region_25.26_spmd} | conditional | flops 2 | bytes 3735722 | solution.py:341
  252.6 3.5 %all-to-all-start.5 = ((bf16[8,24,1024]{2,1,0:T(8,128)(2,1)}), bf16[8,24,1024]{2,1,0:T(8,128)(2,1)S(1)}, u32[]{:S(2)}, u32[]{:S(2)}) async-start(bf16[8,24,1024]{2,1,0:T(8,128)(2,1)} %bitcast.22), calls=%async_computation.5 | async-start | bytes 786432 | tf_op jit(solution)/shard_map/cond/branch_1_fun/all_to_all | solution.py:268
  256.1 1.8 branch_1_fun.39
  257.8 9.5 %all-to-all-done.5.caches_ref = bf16[8,24,1024]{2,1,0:T(8,128)(2,1)S(1)} async-done(((bf16[8,24,1024]{2,1,0:T(8,128)(2,1)}), bf16[8,24,1024]{2,1,0:T(8,128)(2,1)S(1)}, u32[]{:S(2)}, u32[]{:S(2)}) %all-to-all-start.5) | async-done | bytes 393248 | tf_op jit(solution)/shard_map/cond/branch_1_fun/all_to_all | solution.py:268
  267.3 1.4 branch_1_fun.41
  268.7 1.2 select_select_fusion.2
  270.0 1.4 collective-permute-done.10.theirs_ref
  (60 shorter events, 5.9 us)
Async XLA Ops:
  0.6 2.6 copy-start
  1.5 3.3 %collective-permute-start = (f32[4,3072]{1,0:T(4,128)S(1)}, f32[4,3072]{1,0:T(4,128)S(1)}, u32[]{:S(2)}, u32[]{:S(2)}) collective-permute-start(f32[4,3072]{1,0:T(4,128)S(1)} %select_maximum_fusion.params_ref), channel_id=1, source_target_pairs={{0,8},{1,9},{2,10},{3,11},{4,12},{5,13},{6,14},{7,15},{8,0},{9,1},... | collective-permute-start | bytes 147464 | tf_op jit(solution)/shard_map/ppermute | solution.py:261
  2.0 2.9 %copy-start.1 = (bf16[1,256,3072]{2,1,0:T(8,128)(2,1)S(1)}, bf16[1,256,3072]{2,1,0:T(8,128)(2,1)}, u32[]{:S(2)}) copy-start(bf16[1,256,3072]{2,1,0:T(8,128)(2,1)} %param.40) | copy-start | bytes 4718596
  2.0 3.4 %copy-start.11 = (f32[1,3072]{1,0:T(1,128)S(1)}, f32[1,3072]{1,0:T(1,128)}, u32[]{:S(2)}) copy-start(f32[1,3072]{1,0:T(1,128)} %param.37) | copy-start | bytes 36868
  2.0 3.4 %copy-start.12 = (f32[1,3072]{1,0:T(1,128)S(1)}, f32[1,3072]{1,0:T(1,128)}, u32[]{:S(2)}) copy-start(f32[1,3072]{1,0:T(1,128)} %param.36) | copy-start | bytes 36868
  2.0 3.4 %copy-start.13 = (f32[1,3072]{1,0:T(1,128)S(1)}, f32[1,3072]{1,0:T(1,128)}, u32[]{:S(2)}) copy-start(f32[1,3072]{1,0:T(1,128)} %param.35) | copy-start | bytes 36868
  2.0 3.4 %copy-start.14 = (f32[1,2,128]{2,1,0:T(2,128)S(1)}, f32[1,2,128]{2,1,0:T(2,128)}, u32[]{:S(2)}) copy-start(f32[1,2,128]{2,1,0:T(2,128)} %param.38) | copy-start | bytes 3076
  4.8 33.9 %collective-permute-start.1 = (bf16[3,3072,256]{2,1,0:T(8,128)(2,1)}, bf16[3,3072,256]{2,1,0:T(8,128)(2,1)}, u32[]{:S(2)}, u32[]{:S(2)}) collective-permute-start(bf16[3,3072,256]{2,1,0:T(8,128)(2,1)} %bitcast.36), channel_id=1, source_target_pairs={{0,8},{1,9},{2,10},{3,11},{4,12},{5,13},{6,14},{7,15},{8,0},{9,1},... | collective-permute-start | bytes 14155784 | tf_op jit(solution)/shard_map/ppermute | solution.py:261
  4.9 33.8 %collective-permute-start.2 = (bf16[1,256,3072]{2,1,0:T(8,128)(2,1)S(1)}, bf16[1,256,3072]{2,1,0:T(8,128)(2,1)}, u32[]{:S(2)}, u32[]{:S(2)}) collective-permute-start(bf16[1,256,3072]{2,1,0:T(8,128)(2,1)S(1)} %copy-done.1), channel_id=1, source_target_pairs={{0,8},{1,9},{2,10},{3,11},{4,12},{5,13},{6,14},{7,15},{8,0},{9,1},... | collective-permute-start | bytes 4718600 | tf_op jit(solution)/shard_map/ppermute | solution.py:261
  5.5 31.9 %all-to-all-start.1 = ((bf16[8,24,3584]{2,1,0:T(8,128)(2,1)}), bf16[8,24,3584]{2,1,0:T(8,128)(2,1)}, u32[]{:S(2)}, u32[]{:S(2)}) async-start(bf16[8,24,3584]{2,1,0:T(8,128)(2,1)} %param.1), calls=%async_computation.1 | async-start | bytes 2752512 | tf_op jit(solution)/shard_map/cond/branch_1_fun/all_to_all | solution.py:268
  46.0 24.6 %all-to-all-start.6 = ((bf16[8,24,3072]{2,1,0:T(8,128)(2,1)}), bf16[8,24,3072]{2,1,0:T(8,128)(2,1)}, u32[]{:S(2)}, u32[]{:S(2)}) async-start(bf16[8,24,3072]{2,1,0:T(8,128)(2,1)} %get-tuple-element.414), calls=%async_computation.6 | async-start | bytes 2359296 | tf_op jit(solution)/shard_map/all_to_all | solution.py:268
  52.6 1.8 collective-permute-start.3
  74.1 22.9 %all-to-all-start.7 = ((bf16[8,24,3072]{2,1,0:T(8,128)(2,1)}), bf16[8,24,3072]{2,1,0:T(8,128)(2,1)}, u32[]{:S(2)}, u32[]{:S(2)}) async-start(bf16[8,24,3072]{2,1,0:T(8,128)(2,1)} %get-tuple-element.416), calls=%async_computation.7 | async-start | bytes 2359296 | tf_op jit(solution)/shard_map/all_to_all | solution.py:268
  78.4 18.6 %collective-permute-start.4 = (bf16[192,512]{1,0:T(8,128)(2,1)}, bf16[192,512]{1,0:T(8,128)(2,1)}, u32[]{:S(2)}, u32[]{:S(2)}) collective-permute-start(bf16[192,512]{1,0:T(8,128)(2,1)} %get-tuple-element.418), channel_id=1, source_target_pairs={{0,8},{1,9},{2,10},{3,11},{4,12},{5,13},{6,14},{7,15},{8,0},{9,1},... | collective-permute-start | bytes 589832 | tf_op jit(solution)/shard_map/ppermute | solution.py:261
  104.4 22.5 %copy-start.2 = (bf16[24,3072]{1,0:T(8,128)(2,1)S(1)}, bf16[24,3072]{1,0:T(8,128)(2,1)}, u32[]{:S(2)}) copy-start(bf16[24,3072]{1,0:T(8,128)(2,1)} %get-tuple-element.422) | copy-start | bytes 442372
  104.4 22.5 %all-to-all-start.8 = ((bf16[8,24,3072]{2,1,0:T(8,128)(2,1)}), bf16[8,24,3072]{2,1,0:T(8,128)(2,1)}, u32[]{:S(2)}, u32[]{:S(2)}) async-start(bf16[8,24,3072]{2,1,0:T(8,128)(2,1)} %get-tuple-element.420), calls=%async_computation.8 | async-start | bytes 2359296 | tf_op jit(solution)/shard_map/all_to_all | solution.py:268
  108.8 23.6 %collective-permute-start.5 = (bf16[2,192,256]{2,1,0:T(8,128)(2,1)}, bf16[2,192,256]{2,1,0:T(8,128)(2,1)}, u32[]{:S(2)}, u32[]{:S(2)}) collective-permute-start(bf16[2,192,256]{2,1,0:T(8,128)(2,1)} %get-tuple-element.421), channel_id=1, source_target_pairs={{0,8},{1,9},{2,10},{3,11},{4,12},{5,13},{6,14},{7,15},{8,0},{9,1},... | collective-permute-start | bytes 589832 | tf_op jit(solution)/shard_map/ppermute | solution.py:261
  129.0 6.4 %collective-permute-start.6 = (bf16[24,3072]{1,0:T(8,128)(2,1)}, bf16[24,3072]{1,0:T(8,128)(2,1)S(1)}, u32[]{:S(2)}, u32[]{:S(2)}) collective-permute-start(bf16[24,3072]{1,0:T(8,128)(2,1)} %get-tuple-element.491), channel_id=1, source_target_pairs={{0,16},{1,17},{2,18},{3,19},{4,20},{5,21},{6,22},{7,23}} | collective-permute-start | bytes 442376 | tf_op jit(solution)/shard_map/ppermute | solution.py:265
  135.4 0.7 copy-start.8
  138.0 1.3 copy-start.7
  138.0 1.3 collective-permute-start.7
  145.9 3.7 %copy-start.4 = (bf16[2,192,256]{2,1,0:T(8,128)(2,1)}, bf16[2,192,256]{2,1,0:T(8,128)(2,1)S(1)}, u32[]{:S(2)}) copy-start(bf16[2,192,256]{2,1,0:T(8,128)(2,1)S(1)} %get-tuple-element.425) | copy-start | bytes 589828
  146.0 31.5 %copy-start.9 = (bf16[24,3072]{1,0:T(8,128)(2,1)S(1)}, bf16[24,3072]{1,0:T(8,128)(2,1)}, u32[]{:S(2)}) copy-start(bf16[24,3072]{1,0:T(8,128)(2,1)} %copy-done.8) | copy-start | bytes 442372
  146.0 31.5 %all-to-all-start.9 = ((bf16[8,24,3072]{2,1,0:T(8,128)(2,1)}), bf16[8,24,3072]{2,1,0:T(8,128)(2,1)S(1)}, u32[]{:S(2)}, u32[]{:S(2)}) async-start(bf16[8,24,3072]{2,1,0:T(8,128)(2,1)} %get-tuple-element.424), calls=%async_computation.9 | async-start | bytes 2359296 | tf_op jit(solution)/shard_map/all_to_all | solution.py:268
  149.7 27.8 %collective-permute-start.8 = (bf16[2,192,256]{2,1,0:T(8,128)(2,1)S(1)}, bf16[2,192,256]{2,1,0:T(8,128)(2,1)}, u32[]{:S(2)}, u32[]{:S(2)}) collective-permute-start(bf16[2,192,256]{2,1,0:T(8,128)(2,1)S(1)} %get-tuple-element.425), channel_id=1, source_target_pairs={{0,8},{1,9},{2,10},{3,11},{4,12},{5,13},{6,14},{7,15},{8,0},{9,1},... | collective-permute-start | bytes 589832 | tf_op jit(solution)/shard_map/ppermute | solution.py:261
  220.5 0.7 copy-start.5
  220.5 5.0 %copy-start.10 = (bf16[2,192,256]{2,1,0:T(8,128)(2,1)}, bf16[2,192,256]{2,1,0:T(8,128)(2,1)S(1)}, u32[]{:S(2)}) copy-start(bf16[2,192,256]{2,1,0:T(8,128)(2,1)S(1)} %get-tuple-element.429) | copy-start | bytes 589828
  221.1 30.7 %all-to-all-start.11 = ((bf16[8,24,3072]{2,1,0:T(8,128)(2,1)}), bf16[8,24,3072]{2,1,0:T(8,128)(2,1)S(1)}, u32[]{:S(2)}, u32[]{:S(2)}) async-start(bf16[8,24,3072]{2,1,0:T(8,128)(2,1)} %get-tuple-element.431), calls=%async_computation.11 | async-start | bytes 2359296 | tf_op jit(solution)/shard_map/all_to_all | solution.py:268
  225.5 1.5 collective-permute-start.9
  227.0 0.7 copy-start.3
  252.6 14.7 %all-to-all-start.5 = ((bf16[8,24,1024]{2,1,0:T(8,128)(2,1)}), bf16[8,24,1024]{2,1,0:T(8,128)(2,1)S(1)}, u32[]{:S(2)}, u32[]{:S(2)}) async-start(bf16[8,24,1024]{2,1,0:T(8,128)(2,1)} %bitcast.22), calls=%async_computation.5 | async-start | bytes 786432 | tf_op jit(solution)/shard_map/cond/branch_1_fun/all_to_all | solution.py:268
  269.9 1.4 collective-permute-start.10
